TPU v7x, 32 devices: a whole 2x2x4 slice. The times are simulated.
32 devices in a mesh: batch: 8 (over z, y), freq: 4 (over x, core).
Axes of the slice: x: 2, y: 2, z: 4, core: 2. Of those that a mesh axis runs over, the one named last changes fastest.
Arguments:
- tokens: bfloat16 [1024, 8, 768], P('freq', 'batch'), may hold values from -6 to 6
- seg_ids: int32 [8, 1024], P('batch'), may hold values from 0 to 2, never falling along the last dimension, each value on 1 to 770 neighbouring positions
- cotangent: bfloat16 [1024, 8, 768], P('freq', 'batch'), may hold values from -6 to 6
- ln1_gain: float32 [768], replicated, may hold values from 0.25 to 1.75
- ln1_shift: float32 [768], replicated, may hold values from -3 to 3
- w_in: bfloat16 [768, 1536], replicated, may hold values from -0.21875 to 0.21875
- conv_taps: float32 [3, 1536], replicated, may hold values from -3 to 3
- freq_w1: float32 [64, 64], replicated, may hold values from -1 to 1
- freq_b1: float32 [64], replicated, may hold values from -3 to 3
- freq_w2: float32 [64, 1536], replicated, may hold values from -1 to 1
- cond_w: float32 [768, 64], replicated, may hold values from -0.625 to 0.625
- w_out: bfloat16 [768, 768], replicated, may hold values from -0.3125 to 0.3125
- ln2_gain: float32 [768], replicated, may hold values from 0.25 to 1.75
- ln2_shift: float32 [768], replicated, may hold values from -3 to 3
- w_gate: bfloat16 [768, 3072], replicated, may hold values from -0.21875 to 0.21875
- w_up: bfloat16 [768, 3072], replicated, may hold values from -0.21875 to 0.21875
- w_down: bfloat16 [3072, 768], replicated, may hold values from -0.15625 to 0.15625
Outputs:
- mixed_out: bfloat16 [1024, 8, 768], P('freq', 'batch')
- grad_tokens: float32 [1024, 8, 768], P('freq', 'batch')
- grad_ln1_gain: float32 [768], replicated
- grad_ln1_shift: float32 [768], replicated
- grad_w_in: float32 [768, 1536], P(None, ('batch', 'freq'))
- grad_conv_taps: float32 [3, 1536], replicated
- grad_freq_w1: float32 [64, 64], replicated
- grad_freq_b1: float32 [64], replicated
- grad_freq_w2: float32 [64, 1536], replicated
- grad_cond_w: float32 [768, 64], replicated
- grad_w_out: float32 [768, 768], P(None, ('batch', 'freq'))
- grad_ln2_gain: float32 [768], replicated
- grad_ln2_shift: float32 [768], replicated
- grad_w_gate: float32 [768, 3072], P(None, ('batch', 'freq'))
- grad_w_up: float32 [768, 3072], P(None, ('batch', 'freq'))
- grad_w_down: float32 [3072, 768], P(('batch', 'freq'))
Inputs may be any that keep to these rules, and one draw needn't show every extreme that they name: `seg_ids`: in each row the document numbers run 0, 1, .. 2 without falling, each present; one document of each row has exactly 770 tokens.
All inputs are finite; a program needn't handle non-finite values.
Results may differ from a plain program's by a relative error of at most 0.013.
Values may be sent and summed in bfloat16 or wider, within the bound.
No kernel may reach another device: no remote copies, remote signals or barrier semaphores. Data moves between devices by JAX's collectives and lax.ppermute only.
A program may use at most 128 MiB of HBM per device.

v0:
```python
import functools

import jax
import jax.numpy as jnp
import ml_dtypes
import numpy as np
from jax import lax
from jax.experimental import pallas as pl
from jax.experimental.pallas import tpu as pltpu
from jax.sharding import PartitionSpec as P

SEGS = 3
EPS = 1e-05
HIGH = lax.Precision.HIGHEST
F32 = jnp.float32
BF16 = jnp.bfloat16


def mm(a, b):
    return jnp.dot(a, b, preferred_element_type=F32)


def mm_nt(a, b):
    return lax.dot_general(a, b, (((1,), (1,)), ((), ())), preferred_element_type=F32)


def mm_tn(a, b):
    return lax.dot_general(a, b, (((0,), (0,)), ((), ())), preferred_element_type=F32)


def swap(value, axis, mask):
    count = lax.axis_size(axis)
    return lax.ppermute(value, axis, [(i, i ^ mask) for i in range(count)])


def pick(parts, index):
    return lax.dynamic_index_in_dim(parts, index, 0, keepdims=False)


def in_order(received, me):
    a, b, c, d = received
    low = (me & 1) == 1
    a, b = jnp.where(low, b, a), jnp.where(low, a, b)
    c, d = jnp.where(low, d, c), jnp.where(low, c, d)
    high = (me & 2) == 2
    a, c = jnp.where(high, c, a), jnp.where(high, a, c)
    b, d = jnp.where(high, d, b), jnp.where(high, b, d)
    return (a, b, c, d)


def trade(blocks, me):
    return [pick(blocks, me)] + [swap(pick(blocks, me ^ k), "freq", k) for k in (2, 3, 1)]


def trade_sorted(blocks, me):
    own, two, three, one = trade(blocks, me)
    return in_order((own, one, two, three), me)


def gather_freq(value, me):
    two = swap(value, "freq", 2)
    one = swap(value, "freq", 1)
    three = swap(two, "freq", 1)
    return (value, one, two, three)


def scatter_sum(value, order):
    bits = lax.axis_size("batch").bit_length() - 1
    me = lax.axis_index("batch")
    rest = value.shape[1:]
    value = value.reshape((2,) * bits + rest)
    left = list(range(bits - 1, -1, -1))
    for bit in order:
        dim = left.index(bit)
        mine = (me >> bit) & 1
        keep = lax.dynamic_index_in_dim(value, mine, dim, keepdims=False)
        give = lax.dynamic_index_in_dim(value, 1 - mine, dim, keepdims=False)
        got = swap(give, "batch", 1 << bit)
        total = keep.astype(F32) + got.astype(F32)
        left.remove(bit)
        value = total.astype(value.dtype) if left else total
    return value


def tables(length):
    index = np.arange(length, dtype=np.int64)
    angle = (index[:, None] * index[None, :] % (2 * length)) * (np.pi / length)
    return (
        np.cos(angle).astype(ml_dtypes.bfloat16),
        np.sin(angle).astype(ml_dtypes.bfloat16),
    )


def features(length, half):
    index = np.arange(length, dtype=np.int64)
    lags = (np.arange(half, dtype=np.int64) + 1) ** 2
    angle = (lags[:, None] * index[None, :] % (2 * length)) * (np.pi / length)
    return np.concatenate([np.cos(angle), np.sin(angle)], axis=0).astype(np.float32)


def normed(values):
    centered = values - jnp.mean(values, axis=-1, keepdims=True)
    scale = lax.rsqrt(jnp.mean(centered * centered, axis=-1, keepdims=True) + EPS)
    return centered * scale, scale


def norm_back(unit, scale, grad):
    return scale * (
        grad
        - jnp.mean(grad, axis=-1, keepdims=True)
        - unit * jnp.mean(grad * unit, axis=-1, keepdims=True)
    )


def shift_right(values):
    return jnp.pad(values, ((0, 0), (1, 0)))[:, :-1]


def shift_left(values):
    return jnp.pad(values, ((0, 0), (0, 1)))[:, 1:]


def plain_device(
    tokens,
    seg_ids,
    cotangent,
    ln1_gain,
    ln1_shift,
    w_in,
    conv_taps,
    freq_w1,
    freq_b1,
    freq_w2,
    cond_w,
    w_out,
    ln2_gain,
    ln2_shift,
    w_gate,
    w_up,
    w_down,
):
    quarter, _, channels = tokens.shape
    length = seg_ids.shape[1]
    ff = w_gate.shape[1]
    fs = lax.axis_size("freq")
    bs = lax.axis_size("batch")
    me = lax.axis_index("freq")
    width = channels // fs
    half = bs // 2
    step = channels // (half * fs)
    cos_table, sin_table = tables(length)
    feats = features(length, freq_w1.shape[0] // 2)

    x_own = tokens[:, 0]
    ct_own = cotangent[:, 0]
    ids = seg_ids
    x_parts = gather_freq(x_own, me)
    ct_parts = gather_freq(ct_own, me)

    w_in_t = (
        w_in.T.reshape(2, half, fs, step, channels)
        .transpose(2, 0, 1, 3, 4)
        .reshape(fs, 2 * width, channels)
    )
    w_in_mine = pick(w_in_t, me)
    w_out_p = (
        w_out.reshape(half, fs, step, channels).transpose(1, 0, 2, 3).reshape(channels, channels)
    )
    taps_mine = pick(
        conv_taps.reshape(3, 2, half, fs, step).transpose(3, 0, 1, 2, 4).reshape(fs, 3, 2 * width), me
    )[:, :, None]
    w2_mine = pick(
        freq_w2.reshape(-1, 2, half, fs, step).transpose(3, 0, 1, 2, 4).reshape(fs, -1, 2 * width), me
    )
    fw = ff // (bs * fs)
    wide = ff // fs

    def mine_rows(weight):
        return pick(
            weight.reshape(bs, fs, fw, channels).transpose(1, 0, 2, 3).reshape(fs, wide, channels), me
        )

    wg_mine, wu_mine, wd_mine = (mine_rows(w_gate.T), mine_rows(w_up.T), mine_rows(w_down))

    base = jnp.dot(freq_w1.T, feats, precision=HIGH) + freq_b1[:, None]

    x_row = jnp.concatenate(in_order(x_parts, me), axis=0).astype(F32)
    unit1, _ = normed(x_row)
    u1 = (unit1 * ln1_gain + ln1_shift).astype(BF16)
    n1 = unit1.astype(BF16)
    masks = (ids == jnp.arange(SEGS, dtype=jnp.int32)[:, None]).astype(F32)
    counts = jnp.sum(masks, axis=1, keepdims=True)
    mu = mm(masks.astype(BF16), u1) / counts
    mn = mm(masks.astype(BF16), n1) / counts
    cb = jnp.dot(mu, cond_w, precision=HIGH)
    p = mm_nt(w_in_mine, u1)
    same = (ids[:, 1:] == ids[:, :-1]).astype(F32)
    zero = jnp.zeros((1, 1), F32)
    prev = jnp.concatenate([zero, same], axis=1)
    nxt = jnp.concatenate([same, zero], axis=1)
    p_prev = shift_right(p) * prev
    p_next = shift_left(p) * nxt
    s = taps_mine[0] * p_prev + taps_mine[1] * p + taps_mine[2] * p_next
    q, v = s[:width], s[width:]

    pre = base[None] + cb[:, :, None]
    gate_pre = jax.nn.sigmoid(pre)
    hk = pre * gate_pre
    kk = jnp.einsum("kc,jkf->jcf", w2_mine, hk, precision=HIGH)
    kr, ki = kk[:, :width], kk[:, width:]
    vm = (v[None] * masks[:, None, :]).astype(BF16).reshape(SEGS * width, length)
    vr = mm(vm, cos_table).reshape(SEGS, width, length)
    vi = -mm(vm, sin_table).reshape(SEGS, width, length)
    weights = np.full((length,), 2.0 / (2 * length), np.float32)
    weights[0] = 1.0 / (2 * length)
    yr = ((kr * vr - ki * vi) * weights).astype(BF16).reshape(SEGS * width, length)
    yi = ((kr * vi + ki * vr) * weights).astype(BF16).reshape(SEGS * width, length)
    conv = (mm(yr, cos_table) - mm(yi, sin_table)).reshape(SEGS, width, length)
    c = jnp.sum(conv * masks[:, None, :], axis=0)
    z_mine = (q * c).astype(BF16)

    z_blocks = z_mine.reshape(width, fs, quarter).transpose(1, 0, 2)
    z_t = jnp.concatenate(trade_sorted(z_blocks, me), axis=0)

    x32 = x_own.astype(F32)
    ct32 = ct_own.astype(F32)
    h = x32 + mm_tn(z_t, w_out_p)
    unit2, scale2 = normed(h)
    u2 = (unit2 * ln2_gain + ln2_shift).astype(BF16)
    u2_parts = gather_freq(u2, me)
    g = mm(u2, w_gate)
    a = mm(u2, w_up)
    gh = mm_nt(ct_own, w_down)
    sg = jax.nn.sigmoid(g)
    silu = g * sg
    hid = (silu * a).astype(BF16)
    mixed_out = (h + mm(hid, w_down)).astype(BF16)
    gg = (gh * a * sg * (1.0 + g * (1.0 - sg))).astype(BF16)
    ga = (gh * silu).astype(BF16)
    gu2 = mm_nt(gg, w_gate) + mm_nt(ga, w_up)
    grad_ln2_gain = jnp.sum(gu2 * unit2, axis=0)
    grad_ln2_shift = jnp.sum(gu2, axis=0)
    big_g = ct32 + norm_back(unit2, scale2, gu2 * ln2_gain)
    gb = big_g.astype(BF16)
    gz_blocks = mm_nt(w_out_p, gb).astype(BF16).reshape(fs, width, quarter)
    gz = jnp.concatenate(trade_sorted(gz_blocks, me), axis=1).astype(F32)
    gb_parts = gather_freq(gb, me)

    u2_row = jnp.concatenate(u2_parts, axis=0)
    ct_row = jnp.concatenate(ct_parts, axis=0)
    g_t = mm_nt(wg_mine, u2_row)
    a_t = mm_nt(wu_mine, u2_row)
    gh_t = mm_nt(wd_mine, ct_row)
    sg_t = jax.nn.sigmoid(g_t)
    silu_t = g_t * sg_t
    hid_t = (silu_t * a_t).astype(BF16)
    gg_t = (gh_t * a_t * sg_t * (1.0 + g_t * (1.0 - sg_t))).astype(BF16)
    ga_t = (gh_t * silu_t).astype(BF16)
    d_gate = mm(gg_t, u2_row).astype(BF16)
    d_up = mm(ga_t, u2_row).astype(BF16)
    d_down = mm(hid_t, ct_row).astype(BF16)
    d_ff = jnp.stack([d_gate, d_up, d_down], axis=0).reshape(3, bs, fw, channels).transpose(1, 0, 2, 3)
    bits = bs.bit_length() - 1
    order_a = list(range(bits))
    order_b = [1, 0] + list(range(2, bits))
    cut = channels // 2
    ff_a = scatter_sum(d_ff[..., :cut], order_a)
    ff_b = scatter_sum(d_ff[..., cut:], order_b)
    d_ff = jnp.concatenate([ff_a, ff_b], axis=-1)

    gq = gz * c
    gc = gz * q
    gcm = (gc[None] * masks[:, None, :]).astype(BF16).reshape(SEGS * width, length)
    gyr = mm(gcm, cos_table).reshape(SEGS, width, length) * weights
    gyi = -mm(gcm, sin_table).reshape(SEGS, width, length) * weights
    gkr = gyr * vr + gyi * vi
    gki = gyi * vr - gyr * vi
    gvr = (kr * gyr + ki * gyi).astype(BF16).reshape(SEGS * width, length)
    gvi = (kr * gyi - ki * gyr).astype(BF16).reshape(SEGS * width, length)
    gv_all = (mm(gvr, cos_table) - mm(gvi, sin_table)).reshape(SEGS, width, length)
    gv = jnp.sum(gv_all * masks[:, None, :], axis=0)
    gs = jnp.concatenate([gq, gv], axis=0)
    d_taps = jnp.stack(
        [jnp.sum(gs * p_prev, axis=1), jnp.sum(gs * p, axis=1), jnp.sum(gs * p_next, axis=1)]
    )
    gp = (
        taps_mine[1] * gs
        + taps_mine[0] * shift_left(gs * prev)
        + taps_mine[2] * shift_right(gs * nxt)
    ).astype(BF16)

    gkk = jnp.concatenate([gkr, gki], axis=1)
    gkk_low = gkk.astype(BF16)
    hk_low = hk.astype(BF16)
    d_w2 = jnp.einsum("jkf,jcf->kc", hk_low, gkk_low, preferred_element_type=F32)
    gpre = jnp.einsum("kc,jcf->jkf", w2_mine.astype(BF16), gkk_low, preferred_element_type=F32)
    gpre = gpre * gate_pre * (1.0 + pre * (1.0 - gate_pre))
    d_w1 = jnp.einsum("ef,jkf->ek", feats, gpre, precision=HIGH)
    gcb = jnp.sum(gpre, axis=2)
    gcb_row = lax.psum(gcb, "freq")

    gp_blocks = gp.reshape(2 * width, fs, quarter).transpose(1, 0, 2)
    gp_t = jnp.concatenate(trade_sorted(gp_blocks, me), axis=0)

    u1_row = u1
    d_in = mm(gp, u1_row).astype(BF16).reshape(bs, 2 * width // bs, channels)
    d_in = scatter_sum(d_in, order_a)
    gb_row = jnp.concatenate(in_order(gb_parts, me), axis=0)
    d_out = mm(z_mine, gb_row)
    narrow = channels // bs
    d_out = scatter_sum(d_out.T.astype(BF16).reshape(bs, narrow, width), order_a)
    d_out = d_out.reshape(fs, narrow // fs, width)
    d_out = jnp.stack(trade_sorted(d_out, me), axis=0)
    d_out = (
        d_out.reshape(fs, narrow // fs, half, step).transpose(2, 0, 3, 1).reshape(channels, -1)
    )

    gmu_part = jnp.dot(gcb, cond_w.T, precision=HIGH)
    sum_gp = jnp.sum(gp.astype(F32), axis=1)
    w_mine32 = w_in_mine.astype(F32)
    d_shift1 = jnp.dot(sum_gp[None], w_mine32, precision=HIGH)[0] + jnp.sum(gmu_part, axis=0)
    d_gain1 = jnp.sum(mm(gp, n1) * w_mine32, axis=0) + jnp.sum(gmu_part * mn, axis=0)

    gmu = jnp.dot(gcb_row, cond_w.T, precision=HIGH) / counts
    own_masks = lax.dynamic_slice_in_dim(masks, me * quarter, quarter, 1)
    gu1 = mm_tn(gp_t, w_in_t.reshape(2 * channels, channels)) + lax.dot_general(
        own_masks, gmu, (((0,), (0,)), ((), ())), precision=HIGH
    )
    unit_own, scale_own = normed(x32)
    grad_tokens = big_g + norm_back(unit_own, scale_own, gu1 * ln1_gain)

    shared = [
        d_gain1,
        d_shift1,
        d_w1.reshape(-1),
        jnp.sum(gcb, axis=0),
        jnp.dot(mu.T, gcb, precision=HIGH).reshape(-1),
        grad_ln2_gain,
        grad_ln2_shift,
    ]
    owned = jnp.concatenate([d_taps, d_w2], axis=0)
    packed = jnp.concatenate(shared + [owned.reshape(-1)])
    for bit in range(bits):
        packed = packed + swap(packed, "batch", 1 << bit)
    split = packed.shape[0] - owned.size
    common, owned = packed[:split], packed[split:]
    common = common + swap(common, "freq", 1)
    common = common + swap(common, "freq", 2)
    owned = jnp.stack(in_order(gather_freq(owned, me), me), axis=0)
    owned = (
        owned.reshape(fs, -1, 2, half, step).transpose(1, 2, 3, 0, 4).reshape(-1, 2 * channels)
    )
    sizes = np.cumsum([part.size for part in shared])
    got = jnp.split(common, sizes[:-1])
    return (
        mixed_out[:, None],
        grad_tokens[:, None],
        got[0],
        got[1],
        d_in.T,
        owned[:3],
        got[2].reshape(freq_w1.shape),
        got[3],
        owned[3:],
        got[4].reshape(cond_w.shape),
        d_out,
        got[5],
        got[6],
        d_ff[0].T,
        d_ff[1].T,
        d_ff[2],
    )


VM = pl.BlockSpec(memory_space=pltpu.VMEM)
SM = pl.BlockSpec(memory_space=pltpu.SMEM)
HBM = pl.BlockSpec(memory_space=pl.ANY)
MIB = 1 << 20


def params():
    return pltpu.CompilerParams(vmem_limit_bytes=60 * MIB)


def cost(micros):
    return pl.CostEstimate(
        flops=int(micros * 1e9), bytes_accessed=int(micros * 3.5e6), transcendentals=0
    )


def shape(dims, dtype):
    return jax.ShapeDtypeStruct(dims, dtype)


def sigmoid(value):
    return 1.0 / (1.0 + jnp.exp(-value))


def dma_all(pairs, sems, first=0):
    copies = [
        pltpu.make_async_copy(source, target, sems.at[first + i])
        for i, (source, target) in enumerate(pairs)
    ]
    for copy in copies:
        copy.start()
    return copies


def one_hot_rows(me, rows, lanes, piece, fs):
    row = lax.broadcasted_iota(jnp.int32, (rows, lanes), 0)
    lane = lax.broadcasted_iota(jnp.int32, (rows, lanes), 1)
    block = jnp.zeros_like(row)
    for m in range(1, rows // piece):
        block = block + jnp.where(row >= m * piece, 1, 0)
    return jnp.where(lane == block * ((fs - 1) * piece) + me * piece + row, 1.0, 0.0)


def prepare_kernel(
    me_ref, w_in, freq_w2, conv_taps, freq_w1, freq_b1, feats,
    w_mine, w2x, w2t, taps, base, w1_aug, *, step, fs,
):
    lanes = w_in.shape[1] // 4
    rows = lanes // fs
    sel = one_hot_rows(me_ref[0], rows, lanes, step, fs)
    low = sel.astype(BF16)
    hidden = freq_w2.shape[0]
    for i in range(4):
        out = slice(i * rows, (i + 1) * rows)
        group = slice(i * lanes, (i + 1) * lanes)
        w_mine[out, :] = mm_nt(low, w_in[:, group]).astype(BF16)
        both = jnp.concatenate([freq_w2[:, group], conv_taps[:, group]], axis=0)
        mine = lax.dot_general(
            sel, both, (((1,), (1,)), ((), ())), precision=HIGH, preferred_element_type=F32
        )
        taps[out, :3] = mine[:, hidden:]
        mine = mine[:, :hidden]
        high = mine.astype(BF16)
        rest = (mine - high.astype(F32)).astype(BF16)
        w2x[out, :] = jnp.concatenate([high, high, rest], axis=1)
    w2t[...] = jnp.transpose(w2x[...][:, :hidden].astype(F32)).astype(BF16)
    w1_aug[...] = jnp.zeros_like(w1_aug)
    count = freq_w1.shape[0]
    w1_aug[:count, :] = freq_w1[...]
    w1_aug[count : count + 1, :] = freq_b1[...]
    base[...] = lax.dot_general(
        w1_aug[...], feats[...], (((0,), (0,)), ((), ())), precision=HIGH, preferred_element_type=F32
    )


def prepare(me, w_in, freq_w2, conv_taps, freq_w1, freq_b1, feats, step, fs):
    channels, both = w_in.shape
    hidden = freq_w2.shape[0]
    length = feats.shape[1]
    return pl.pallas_call(
        functools.partial(prepare_kernel, step=step, fs=fs),
        in_specs=[SM] + [VM] * 6,
        out_specs=[VM] * 5,
        out_shape=[
            shape((both // fs, channels), BF16),
            shape((both // fs, 3 * hidden), BF16),
            shape((hidden, both // fs), BF16),
            shape((both // fs, 8), F32),
            shape((hidden, length), F32),
        ],
        scratch_shapes=[pltpu.VMEM((feats.shape[0], hidden), F32)],
        compiler_params=params(),
        cost_estimate=cost(3),
        name="prepare",
    )(me, w_in, freq_w2, conv_taps, freq_w1, freq_b1[None], feats)


def select_kernel(me_ref, after, gate, up, gate_out, up_out, *, piece, fs):
    rows = gate_out.shape[0] // 2
    lanes = rows * fs
    sel = one_hot_rows(me_ref[0], rows, lanes, piece, fs).astype(BF16)
    for weight, out in ((gate, gate_out), (up, up_out)):
        for part in range(2):
            block = mm_nt(sel, weight[:, part * lanes : (part + 1) * lanes])
            out[part * rows : (part + 1) * rows, :] = block.astype(BF16)


def select_columns(me, after, w_gate, w_up, piece, fs):
    channels, ff = w_gate.shape
    big = ff // 4
    wide = pl.BlockSpec((channels, big), lambda i: (0, i))
    rows = pl.BlockSpec((big // fs, channels), lambda i: (i, 0))
    return pl.pallas_call(
        functools.partial(select_kernel, piece=piece, fs=fs),
        grid=(4,),
        in_specs=[SM, HBM, wide, wide],
        out_specs=[rows, rows],
        out_shape=[shape((ff // fs, channels), BF16)] * 2,
        compiler_params=params(),
        cost_estimate=cost(6),
        name="select_columns",
    )(me, after, w_gate, w_up)


def row_masks(ids):
    lane = lax.broadcasted_iota(jnp.int32, ids.shape, 1)
    length = ids.shape[1]
    prev = jnp.where((ids == pltpu.roll(ids, 1, 1)) & (lane > 0), 1.0, 0.0)
    nxt = jnp.where((ids == pltpu.roll(ids, length - 1, 1)) & (lane < length - 1), 1.0, 0.0)
    return prev, nxt


def bin_weights(start, width, length):
    lane = lax.broadcasted_iota(jnp.int32, (1, width), 1) + start
    return jnp.where(lane == 0, 0.5 / length, 1.0 / length)


def tile(index, size):
    return pl.ds(pl.multiple_of(index * size, size), size)


def hidden_tile(base, cb, j, lanes):
    pre = base[:, lanes] + cb[:, j : j + 1]
    return pre, sigmoid(pre)


def kernel_tile(w2x, hk):
    high = hk.astype(BF16)
    rest = (hk - high.astype(F32)).astype(BF16)
    return mm(w2x[...], jnp.concatenate([high, rest, high], axis=0))


def forward_kernel(
    me_ref, ids_at, x0, x1, x2, x3, ids_ref, norms, w, taps, base, w2x, condt, cos_hbm, sin_hbm,
    z0, z1, z2, z3, zrow_hbm, u1_hbm, n1_hbm, p_hbm, q_hbm, c_hbm, vr_hbm, vs_hbm, mu_out, mn_out, cb_out,
    cos, sin, z_row, u1, n1, p_out, q_out, c_out, vr_out, vs_out, p, q, vm, ycat, acc, sems,
):
    quarter = x0.shape[0]
    width, length = z_row.shape
    tiles = length // quarter
    me = me_ref[0]
    loads = dma_all([(cos_hbm, cos), (sin_hbm, sin)], sems)
    for k, x in enumerate((x0, x1, x2, x3)):
        values = x[...].astype(F32)
        unit, _ = normed(values)
        rows = tile(me ^ k, quarter)
        n1[rows, :] = unit.astype(BF16)
        u1[rows, :] = (unit * norms[0:1, :] + norms[1:2, :]).astype(BF16)
    stores = dma_all([(u1, u1_hbm), (n1, n1_hbm)], sems, 2)
    ids = ids_ref[...]
    number = lax.broadcasted_iota(jnp.int32, (8, length), 0)
    member = jnp.where(ids == number, 1.0, 0.0)
    counts = jnp.maximum(jnp.sum(member, axis=1, keepdims=True), 1.0)
    member_low = member.astype(BF16)
    mu = mm(member_low, u1[...]) / counts
    mu_out[...] = mu
    mn_out[...] = mm(member_low, n1[...]) / counts
    cb_out[...] = lax.dot_general(
        condt[...], mu, (((1,), (1,)), ((), ())), precision=HIGH, preferred_element_type=F32
    )
    prev, nxt = row_masks(ids)
    for t in range(tiles):
        at = slice(t * quarter, (t + 1) * quarter)
        p[:, at] = mm_nt(w[...], u1[at, :])
    chunk = width // 2
    for r in range(4):
        at = slice(r * chunk, (r + 1) * chunk)
        here = p[at, :]
        p_out[at, :] = here.astype(BF16)
        mixed = (
            taps[at, 0:1] * (pltpu.roll(here, 1, 1) * prev)
            + taps[at, 1:2] * here
            + taps[at, 2:3] * (pltpu.roll(here, length - 1, 1) * nxt)
        )
        if r < 2:
            q[at, :] = mixed
            q_out[at, :] = mixed.astype(BF16)
        else:
            for j in range(SEGS):
                lo = j * width + (r - 2) * chunk
                vm[lo : lo + chunk, :] = (mixed * member[j : j + 1, :]).astype(BF16)
    stores += dma_all([(p_out, p_hbm), (q_out, q_hbm)], sems, 4)
    for load in loads:
        load.wait()

    @pl.loop(0, tiles)
    def _(f):
        lanes = tile(f, quarter)
        upper = pl.ds(pl.multiple_of(f * quarter + length, quarter), quarter)
        weight = bin_weights(f * quarter, quarter, length)
        vr_all = mm(vm[...], cos[:, lanes])
        vs_all = mm(vm[...], sin[:, lanes])
        vr_out[:, lanes] = vr_all.astype(BF16)
        vs_out[:, lanes] = vs_all.astype(BF16)
        for j in range(SEGS):
            pre, gate = hidden_tile(base, cb_out, j, lanes)
            kk = kernel_tile(w2x, pre * gate)
            kr, ki = kk[:width] * weight, kk[width:] * weight
            at = slice(j * width, (j + 1) * width)
            vr, vs = vr_all[at], vs_all[at]
            ycat[at, lanes] = (kr * vr + ki * vs).astype(BF16)
            ycat[at, upper] = (kr * vs - ki * vr).astype(BF16)

    stores += dma_all([(vr_out, vr_hbm), (vs_out, vs_hbm)], sems, 6)
    for k, z_out in enumerate((z0, z1, z2, z3)):
        t = me ^ k
        lanes = tile(t, quarter)
        acc[...] = jnp.zeros_like(acc)
        ids_here = ids_ref[:, lanes]
        for j in range(SEGS):

            @pl.when((ids_at[0, t * quarter] <= j) & (ids_at[0, (t + 1) * quarter - 1] >= j))
            def _():
                at = slice(j * width, (j + 1) * width)
                part = mm(ycat[at, :length], cos[:, lanes]) + mm(ycat[at, length:], sin[:, lanes])
                acc[...] += jnp.where(ids_here == j, part, 0.0)

        c = acc[...]
        c_out[:, lanes] = c.astype(BF16)
        z = (q[:, lanes] * c).astype(BF16)
        z_out[...] = z
        z_row[:, lanes] = z
    stores += dma_all([(c_out, c_hbm), (z_row, zrow_hbm)], sems, 8)
    for store in stores:
        store.wait()


def forward_spectral(me, x_parts, ids, norms, w, taps, base, w2x, condt, cos, sin):
    quarter, channels = x_parts[0].shape
    length = ids.shape[1]
    width = w.shape[0] // 2
    saved = [
        (width, length),
        (length, channels),
        (length, channels),
        (2 * width, length),
        (width, length),
        (width, length),
        (SEGS * width, length),
        (SEGS * width, length),
    ]
    small = [
        shape((8, channels), F32),
        shape((8, channels), F32),
        shape((condt.shape[0], 8), F32),
    ]
    return pl.pallas_call(
        forward_kernel,
        in_specs=[SM, SM] + [VM] * 11 + [HBM, HBM],
        out_specs=[VM] * 4 + [HBM] * len(saved) + [VM] * 3,
        out_shape=[shape((width, quarter), BF16)] * 4 + [shape(dims, BF16) for dims in saved] + small,
        scratch_shapes=[pltpu.VMEM((length, length), BF16)] * 2
        + [pltpu.VMEM(dims, BF16) for dims in saved]
        + [
            pltpu.VMEM((2 * width, length), F32),
            pltpu.VMEM((width, length), F32),
            pltpu.VMEM((SEGS * width, length), BF16),
            pltpu.VMEM((SEGS * width, 2 * length), BF16),
            pltpu.VMEM((width, quarter), F32),
            pltpu.SemaphoreType.DMA((10,)),
        ],
        compiler_params=params(),
        cost_estimate=cost(15),
        name="forward_spectral",
    )(me, ids, *x_parts, ids, norms, w, taps, base, w2x, condt, cos, sin)


def backward_kernel(
    me_ref, ids_at, g0, g1, g2, g3, ids_ref, cb, taps, base, w2x, w2, feats,
    p_hbm, q_hbm, c_hbm, vr_hbm, vs_hbm, cos_hbm, sin_hbm, after,
    o0, o1, o2, o3, gp_hbm, d_taps, d_w2, d_w1, gcb,
    cos, sin, p, q, c, vr_in, vs_in, gp_row, gcm, gvcat, gs, acc, sems,
):
    width, quarter = g0.shape
    length = gp_row.shape[1]
    tiles = length // quarter
    hidden = base.shape[0]
    me = me_ref[0]
    loads = dma_all(
        [
            (c_hbm, c), (q_hbm, q), (cos_hbm, cos), (sin_hbm, sin),
            (vr_hbm, vr_in), (vs_hbm, vs_in), (p_hbm, p),
        ],
        sems,
    )
    loads[0].wait()
    loads[1].wait()
    for k, g in enumerate((g0, g1, g2, g3)):
        lanes = tile(me ^ k, quarter)
        gz = g[...].astype(F32)
        gs[:width, lanes] = gz * c[:, lanes].astype(F32)
        gc = gz * q[:, lanes].astype(F32)
        ids_here = ids_ref[:, lanes]
        for j in range(SEGS):
            gcm[j * width : (j + 1) * width, lanes] = jnp.where(ids_here == j, gc, 0.0).astype(BF16)
    d_w2[...] = jnp.zeros_like(d_w2)
    d_w1[...] = jnp.zeros_like(d_w1)
    gcb[...] = jnp.zeros_like(gcb)
    for load in loads[2:]:
        load.wait()

    @pl.loop(0, tiles)
    def _(f):
        lanes = tile(f, quarter)
        upper = pl.ds(pl.multiple_of(f * quarter + length, quarter), quarter)
        weight = bin_weights(f * quarter, quarter, length)
        gyr_all = mm(gcm[...], cos[:, lanes]) * weight
        gys_all = mm(gcm[...], sin[:, lanes]) * weight
        for j in range(SEGS):
            pre, gate = hidden_tile(base, cb, j, lanes)
            hk = pre * gate
            kk = kernel_tile(w2x, hk)
            kr, ki = kk[:width], kk[width:]
            at = slice(j * width, (j + 1) * width)
            gyr, gys = gyr_all[at], gys_all[at]
            vr, vs = vr_in[at, lanes].astype(F32), vs_in[at, lanes].astype(F32)
            gvcat[at, lanes] = (kr * gyr - ki * gys).astype(BF16)
            gvcat[at, upper] = (kr * gys + ki * gyr).astype(BF16)
            gkk = jnp.concatenate(
                [(gyr * vr + gys * vs).astype(BF16), (gyr * vs - gys * vr).astype(BF16)], axis=0
            )
            d_w2[...] += mm_nt(gkk, hk.astype(BF16))
            gpre = mm(w2[...], gkk) * (gate * (1.0 + pre * (1.0 - gate)))
            gcb[:, j : j + 1] += jnp.sum(gpre, axis=1, keepdims=True)
            d_w1[...] += mm_nt(feats[:, lanes], gpre.astype(BF16))

    for k in range(4):
        t = me ^ k
        lanes = tile(t, quarter)
        acc[...] = jnp.zeros_like(acc)
        ids_here = ids_ref[:, lanes]
        for j in range(SEGS):

            @pl.when((ids_at[0, t * quarter] <= j) & (ids_at[0, (t + 1) * quarter - 1] >= j))
            def _():
                at = slice(j * width, (j + 1) * width)
                part = mm(gvcat[at, :length], cos[:, lanes]) + mm(gvcat[at, length:], sin[:, lanes])
                acc[...] += jnp.where(ids_here == j, part, 0.0)

        gs[width:, lanes] = acc[...]
    prev, nxt = row_masks(ids_ref[...])
    chunk = width // 2
    for r in range(4):
        at = slice(r * chunk, (r + 1) * chunk)
        here = p[at, :].astype(F32)
        grad = gs[at, :]
        d_taps[at, 0:1] = jnp.sum(grad * (pltpu.roll(here, 1, 1) * prev), axis=1, keepdims=True)
        d_taps[at, 1:2] = jnp.sum(grad * here, axis=1, keepdims=True)
        d_taps[at, 2:3] = jnp.sum(
            grad * (pltpu.roll(here, length - 1, 1) * nxt), axis=1, keepdims=True
        )
        gp_row[at, :] = (
            taps[at, 1:2] * grad
            + taps[at, 0:1] * pltpu.roll(grad * prev, length - 1, 1)
            + taps[at, 2:3] * pltpu.roll(grad * nxt, 1, 1)
        ).astype(BF16)
    store = dma_all([(gp_row, gp_hbm)], sems, 7)[0]
    share = jnp.transpose(gcb[...])[:8, :]
    high = share.astype(BF16)
    rest = (share - high.astype(F32)).astype(BF16)
    extra = jnp.concatenate([high, rest], axis=0)
    extra = jnp.concatenate([extra, jnp.zeros((16, quarter - hidden), BF16)], axis=1)
    for k, out in enumerate((o0, o1, o2, o3)):
        out[: 2 * width, :] = gp_row[:, tile(me ^ k, quarter)]
        out[2 * width :, :] = extra
    store.wait()


def backward_spectral(
    me, gz_parts, ids, cb, taps, base, w2x, w2, feats, p, q, c, vr, vs, cos, sin, after
):
    width, quarter = gz_parts[0].shape
    length = ids.shape[1]
    hidden = base.shape[0]
    outs = [shape((2 * width + 16, quarter), BF16)] * 4 + [
        shape((2 * width, length), BF16),
        shape((2 * width, 128), F32),
        shape((2 * width, hidden), F32),
        shape((feats.shape[0], hidden), F32),
        shape((hidden, 128), F32),
    ]
    return pl.pallas_call(
        backward_kernel,
        in_specs=[SM, SM] + [VM] * 11 + [HBM] * 8,
        out_specs=[VM] * 4 + [HBM] + [VM] * 4,
        out_shape=outs,
        scratch_shapes=[
            pltpu.VMEM((length, length), BF16),
            pltpu.VMEM((length, length), BF16),
            pltpu.VMEM((2 * width, length), BF16),
            pltpu.VMEM((width, length), BF16),
            pltpu.VMEM((width, length), BF16),
            pltpu.VMEM((SEGS * width, length), BF16),
            pltpu.VMEM((SEGS * width, length), BF16),
            pltpu.VMEM((2 * width, length), BF16),
            pltpu.VMEM((SEGS * width, length), BF16),
            pltpu.VMEM((SEGS * width, 2 * length), BF16),
            pltpu.VMEM((2 * width, length), F32),
            pltpu.VMEM((width, quarter), F32),
            pltpu.SemaphoreType.DMA((8,)),
        ],
        compiler_params=params(),
        cost_estimate=cost(17),
        name="backward_spectral",
    )(
        me, ids, *gz_parts, ids, cb, taps, base, w2x, w2, feats, p, q, c, vr, vs, cos, sin, after
    )


def middle_kernel(me_ref, z0, z1, z2, z3, x, w_out, norms, after, h_out, u2_out, z_t, *, piece):
    me = me_ref[0]
    width = z0.shape[0]
    for k, z in enumerate((z0, z1, z2, z3)):
        for i in range(width // piece):
            at = pl.ds(pl.multiple_of((i * 4 + (me ^ k)) * piece, piece), piece)
            z_t[at, :] = z[i * piece : (i + 1) * piece, :]
    h = x[...].astype(F32) + mm(jnp.transpose(z_t[...]), w_out[...])
    h_out[...] = h
    unit, _ = normed(h)
    u2_out[...] = (unit * norms[2:3, :] + norms[3:4, :]).astype(BF16)


def middle(me, z_parts, x, w_out, norms, after, piece):
    quarter, channels = x.shape
    return pl.pallas_call(
        functools.partial(middle_kernel, piece=piece),
        in_specs=[SM] + [VM] * 7 + [HBM],
        out_specs=[VM] * 3,
        out_shape=[
            shape((quarter, channels), F32),
            shape((quarter, channels), BF16),
            shape((channels, quarter), BF16),
        ],
        compiler_params=params(),
        cost_estimate=cost(2),
        name="middle",
    )(me, *z_parts, x, w_out, norms, after)


def feed_kernel(
    me_ref, u2, h, ct, norms, w_out, gate, up, down,
    mixed, big_g, gb_out, g0, g1, g2, g3, sums, acc_out, acc_grad, gz_t, *, piece,
):
    i = pl.program_id(0)

    @pl.when(i == 0)
    def _():
        acc_out[...] = jnp.zeros_like(acc_out)
        acc_grad[...] = jnp.zeros_like(acc_grad)

    g = mm(u2[...], gate[...])
    a = mm(u2[...], up[...])
    gh = mm_nt(ct[...], down[...])
    sg = sigmoid(g)
    silu = g * sg
    hid = (silu * a).astype(BF16)
    gg = (gh * a * (sg * (1.0 + g * (1.0 - sg)))).astype(BF16)
    ga = (gh * silu).astype(BF16)
    acc_out[...] += mm(hid, down[...])
    acc_grad[...] += mm_nt(gg, gate[...]) + mm_nt(ga, up[...])

    @pl.when(i == pl.num_programs(0) - 1)
    def _():
        me = me_ref[0]
        width = g0.shape[0]
        here = h[...]
        mixed[...] = (here + acc_out[...]).astype(BF16)
        gu2 = acc_grad[...]
        unit, scale = normed(here)
        sums[0:1, :] = jnp.sum(gu2 * unit, axis=0, keepdims=True)
        sums[1:2, :] = jnp.sum(gu2, axis=0, keepdims=True)
        total = ct[...].astype(F32) + norm_back(unit, scale, gu2 * norms[2:3, :])
        big_g[...] = total
        low = total.astype(BF16)
        gb_out[...] = low
        gz_t[...] = mm_nt(w_out[...], low).astype(BF16)
        for k, out in enumerate((g0, g1, g2, g3)):
            for r in range(width // piece):
                at = pl.ds(pl.multiple_of((r * 4 + (me ^ k)) * piece, piece), piece)
                out[r * piece : (r + 1) * piece, :] = gz_t[at, :]


def feed_forward(me, u2, h, ct, norms, w_out, w_gate, w_up, w_down, piece):
    quarter, channels = u2.shape
    ff = w_gate.shape[1]
    block = 512

    def whole(*dims):
        return pl.BlockSpec(dims, lambda i: (0,) * len(dims))

    width = channels // 4
    outs = [
        ((quarter, channels), BF16),
        ((quarter, channels), F32),
        ((quarter, channels), BF16),
    ] + [((width, quarter), BF16)] * 4 + [((8, channels), F32)]
    return pl.pallas_call(
        functools.partial(feed_kernel, piece=piece),
        grid=(ff // block,),
        in_specs=[
            SM,
            whole(quarter, channels),
            whole(quarter, channels),
            whole(quarter, channels),
            whole(4, channels),
            whole(channels, channels),
            pl.BlockSpec((channels, block), lambda i: (0, i)),
            pl.BlockSpec((channels, block), lambda i: (0, i)),
            pl.BlockSpec((block, channels), lambda i: (i, 0)),
        ],
        out_specs=[whole(*dims) for dims, _ in outs],
        out_shape=[shape(*out) for out in outs],
        scratch_shapes=[
            pltpu.VMEM((quarter, channels), F32),
            pltpu.VMEM((quarter, channels), F32),
            pltpu.VMEM((channels, quarter), BF16),
        ],
        compiler_params=params(),
        cost_estimate=cost(13),
        name="feed_forward",
    )(me, u2, h, ct, norms, w_out, w_gate, w_up, w_down)


def hidden_grads_kernel(
    at_ref, u0, u1, u2, u3, c0, c1, c2, c3, gate, up, down, gb, z_in,
    keep_a, give_a, keep_b, give_b, t0, t1, t2, t3, z_out, u_row, c_row, d_all, gb_t, *, piece,
):
    quarter, channels = u0.shape
    i = pl.program_id(0)
    y, z = at_ref[1], at_ref[2]

    @pl.when(i == 0)
    def _():
        for k, (u, c) in enumerate(((u0, c0), (u1, c1), (u2, c2), (u3, c3))):
            u_row[k * quarter : (k + 1) * quarter, :] = u[...]
            c_row[k * quarter : (k + 1) * quarter, :] = c[...]

    @pl.when(i == pl.num_programs(0) - 1)
    def _():
        z_out[...] = z_in[...]
        gb_t[...] = jnp.transpose(gb[...].astype(F32))
        for k, out in enumerate((t0, t1, t2, t3)):
            parts = []
            for r in range(out.shape[0] // piece):
                lo = pl.multiple_of((r * 4 + (at_ref[0] ^ k)) * piece, piece)
                parts.append(gb_t[pl.ds(lo, piece), :])
            out[...] = jnp.concatenate(parts, axis=0).astype(BF16)

    rows = gate.shape[0]
    g = mm_nt(gate[...], u_row[...])
    a = mm_nt(up[...], u_row[...])
    gh = mm_nt(down[...].reshape(rows, channels), c_row[...])
    sg = sigmoid(g)
    silu = g * sg
    hid = (silu * a).astype(BF16)
    gg = (gh * a * (sg * (1.0 + g * (1.0 - sg)))).astype(BF16)
    ga = (gh * silu).astype(BF16)
    half = rows // 2
    for m, grad in enumerate((mm(gg, u_row[...]), mm(ga, u_row[...]), mm(hid, c_row[...]))):
        d_all[0, m] = grad[:half].astype(BF16)
        d_all[1, m] = grad[half:].astype(BF16)
    cut = channels // 2
    keep_a[0] = d_all[y, :, :, :cut]
    give_a[0] = d_all[1 - y, :, :, :cut]

    @pl.when((i & 1) == z)
    def _():
        keep_b[0] = d_all[:, :, :, cut:]

    @pl.when((i & 1) != z)
    def _():
        give_b[0] = d_all[:, :, :, cut:]


def hidden_grads(at, u2_parts, ct_parts, gate, up, down, gb, z_t):
    quarter, channels = u2_parts[0].shape
    wide = gate.shape[0]
    bs, fs, fw, _ = down.shape
    block = 2 * fw
    cut = channels // 2
    whole = pl.BlockSpec((quarter, channels), lambda i, at: (0, 0))
    tall = pl.BlockSpec((channels, quarter), lambda i, at: (0, 0))
    part = pl.BlockSpec((channels // fs, quarter), lambda i, at: (0, 0))
    rows = pl.BlockSpec((block, channels), lambda i, at: (i, 0))
    down_spec = pl.BlockSpec((2, 1, fw, channels), lambda i, at: (i, at[0], 0, 0))
    a_spec = pl.BlockSpec((1, 3, fw, cut), lambda i, at: (i, 0, 0, 0))
    b_spec = pl.BlockSpec((1, 2, 3, fw, cut), lambda i, at: (i // 2, 0, 0, 0, 0))
    return pl.pallas_call(
        functools.partial(hidden_grads_kernel, piece=channels // (bs * fs)),
        grid_spec=pltpu.PrefetchScalarGridSpec(
            num_scalar_prefetch=1,
            grid=(bs // 2,),
            in_specs=[whole] * 8 + [rows, rows, down_spec, whole, tall],
            out_specs=[a_spec, a_spec, b_spec, b_spec] + [part] * 4 + [tall],
            scratch_shapes=[
                pltpu.VMEM((4 * quarter, channels), BF16),
                pltpu.VMEM((4 * quarter, channels), BF16),
                pltpu.VMEM((2, 3, fw, channels), BF16),
                pltpu.VMEM((channels, quarter), F32),
            ],
        ),
        out_shape=[shape((bs // 2, 3, fw, cut), BF16)] * 2
        + [shape((bs // 4, 2, 3, fw, cut), BF16)] * 2
        + [shape((channels // fs, quarter), BF16)] * 4
        + [shape((channels, quarter), BF16)],
        compiler_params=params(),
        cost_estimate=cost(14),
        name="hidden_grads",
    )(at, *u2_parts, *ct_parts, gate, up, down, gb, z_t)


def halve_kernel(bit_ref, after, *refs, pairs):
    ins, outs = refs[: 2 * pairs], refs[2 * pairs :]
    for n in range(pairs):
        mine = bit_ref[n]
        keep, got = ins[2 * n], ins[2 * n + 1]
        next_keep, next_give = outs[2 * n], outs[2 * n + 1]
        for i in range(keep.shape[0]):
            for side, out in ((mine, next_keep), (1 - mine, next_give)):
                out[i] = (keep[i, side].astype(F32) + got[i, side].astype(F32)).astype(BF16)


def halve(bits, after, *sums):
    pairs = len(sums) // 2
    outs = []
    for n in range(pairs):
        dims = sums[2 * n].shape
        outs += [shape((dims[0],) + dims[2:], BF16)] * 2
    return pl.pallas_call(
        functools.partial(halve_kernel, pairs=pairs),
        in_specs=[SM, HBM] + [VM] * len(sums),
        out_specs=[VM] * len(outs),
        out_shape=outs,
        compiler_params=params(),
        cost_estimate=cost(2),
        name="halve",
    )(bits, after, *sums)


def join_kernel(bit_ref, after, keep_a, got_a, keep_b, got_b, keep, give):
    cut = keep_a.shape[-1]
    for side, out in ((bit_ref[0], keep), (1 - bit_ref[0], give)):
        for m in range(keep_a.shape[1]):
            for ours, theirs, lanes in ((keep_a, got_a, slice(0, cut)), (keep_b, got_b, slice(cut, 2 * cut))):
                total = ours[side, m].astype(F32) + theirs[side, m].astype(F32)
                out[m, :, lanes] = total.astype(BF16)


def join(bit, after, keep_a, got_a, keep_b, got_b):
    _, count, rows, cut = keep_a.shape
    return pl.pallas_call(
        join_kernel,
        in_specs=[SM, HBM] + [VM] * 4,
        out_specs=[VM] * 2,
        out_shape=[shape((count, rows, 2 * cut), BF16)] * 2,
        compiler_params=params(),
        cost_estimate=cost(2),
        name="join",
    )(bit, after, keep_a, got_a, keep_b, got_b)


def projection_kernel(
    at_ref, gp, u1, n1, w_mine, b0, b1, b2, b3, z0, z1, z2, z3, d_w2, d_w1, d_taps, gcb, condt, mu, mn,
    sums2, after, keep, give, packed, gb_row, z_row, d_in, d_out, *, layout,
):
    me, y = at_ref[0], at_ref[1]
    quarter = b0.shape[1]
    channels = u1.shape[1]
    width = b0.shape[0]
    for k, (b, z) in enumerate(((b0, z0), (b1, z1), (b2, z2), (b3, z3))):
        gb_row[:, k * quarter : (k + 1) * quarter] = b[...]
        z_row[:, k * quarter : (k + 1) * quarter] = z[...]
    d_in[...] = mm(gp[...], u1[...])
    d_out[...] = mm_nt(gb_row[...], z_row[...])
    blocks = 2 * keep.shape[0]
    first = 2 * width // blocks
    second = width // blocks
    for b in range(blocks // 2):
        for side, out in ((y, keep), (1 - y, give)):
            lo = pl.multiple_of((2 * b + side) * first, first)
            out[b, :first, :] = d_in[pl.ds(lo, first), :].astype(BF16)
            lo = pl.multiple_of((2 * b + side) * second, second)
            out[b, first:, :] = d_out[pl.ds(lo, second), :].astype(BF16)
    packed[...] = jnp.zeros_like(packed)
    packed[:width, :] = jnp.concatenate([d_w2[:width, :], d_w2[width:, :]], axis=1)
    taps_t = jnp.transpose(d_taps[...])
    gcb_t = jnp.transpose(gcb[...])[:8, :]
    gmu = lax.dot_general(
        gcb_t, condt[...], (((1,), (0,)), ((), ())), precision=HIGH, preferred_element_type=F32
    )
    gp_n = mm(gp[...], n1[...])
    w32 = w_mine[...].astype(F32)
    gain = jnp.sum(gp_n * w32, axis=0, keepdims=True) + jnp.sum(gmu * mn[...], axis=0, keepdims=True)
    total = jnp.sum(gp[...].astype(F32), axis=1, keepdims=True)
    shift = jnp.sum(total * w32, axis=0, keepdims=True) + jnp.sum(gmu, axis=0, keepdims=True)
    for i in range(3):
        for m in range(2 * width // 128):
            at = layout["taps"] + i * (2 * width // 128) + m
            packed[at : at + 1, :] = taps_t[i : i + 1, m * 128 : (m + 1) * 128]
    for i, row in enumerate((gain, shift, sums2[0:1, :], sums2[1:2, :])):
        for m in range(channels // 128):
            at = layout["ln"] + i * (channels // 128) + m
            packed[at : at + 1, :] = row[:, m * 128 : (m + 1) * 128]
    half = d_w1.shape[0] // 2
    packed[layout["w1"] : layout["w1"] + half, :] = jnp.concatenate(
        [d_w1[:half, :], d_w1[half:, :]], axis=1
    )
    zeros = jnp.zeros_like(gcb_t)
    row = at_ref[4]
    odd = (row & 1) == 1
    both = jnp.concatenate([jnp.where(odd, zeros, gcb_t), jnp.where(odd, gcb_t, zeros)], axis=1)
    packed[pl.ds(pl.multiple_of(layout["cb"] + 8 * (row >> 1), 8), 8), :] = both
    share = jnp.zeros((8, width), F32)
    for f in range(channels // width):
        share = share + jnp.where(me == f, mu[:, f * width : (f + 1) * width], 0.0)
    rest = jnp.concatenate([share[:SEGS, 128:], jnp.zeros((SEGS, 256 - width), F32)], axis=1)
    block = jnp.concatenate([share[:SEGS, :128], rest, jnp.zeros((8 - 2 * SEGS, 128), F32)], axis=0)
    packed[pl.ds(pl.multiple_of(layout["mu"] + 8 * row, 8), 8), :] = block


def packed_layout(width, channels, bs):
    taps = width
    ln = taps + 3 * (2 * width // 128)
    w1 = -(-(ln + 4 * (channels // 128)) // 8) * 8
    cb = w1 + 32
    mu = cb + 4 * bs
    return {"taps": taps, "ln": ln, "w1": w1, "cb": cb, "mu": mu, "rows": mu + 8 * bs}


def projection_grads(
    at, gp, u1, n1, w_mine, gb_parts, z_parts, d_w2, d_w1, d_taps, gcb, condt, mu, mn, sums2, after, bs
):
    length, channels = u1.shape
    width = gb_parts[0].shape[0]
    layout = packed_layout(width, channels, bs)
    return pl.pallas_call(
        functools.partial(projection_kernel, layout=layout),
        in_specs=[SM] + [VM] * 20 + [HBM],
        out_specs=[VM] * 3,
        out_shape=[shape((bs // 2, 3 * width // bs, channels), BF16)] * 2
        + [shape((layout["rows"], 128), F32)],
        scratch_shapes=[
            pltpu.VMEM((width, length), BF16),
            pltpu.VMEM((channels, length), BF16),
            pltpu.VMEM((2 * width, channels), F32),
            pltpu.VMEM((width, channels), F32),
        ],
        compiler_params=params(),
        cost_estimate=cost(4),
        name="projection_grads",
    )(
        at, gp, u1, n1, w_mine, *gb_parts, *z_parts, d_w2, d_w1, d_taps, gcb, condt, mu, mn, sums2, after
    )


def final_kernel(
    me_ref, p0, p1, p2, p3, x, big_g, norms, ids_row, condt, w_in, after, out, gp_t, *, piece
):
    me = me_ref[0]
    rows = gp_t.shape[0] // 4
    hidden = condt.shape[0]
    share = jnp.zeros((8, hidden), F32)
    for k, part in enumerate((p0, p1, p2, p3)):
        for i in range(rows // piece):
            at = pl.ds(pl.multiple_of((i * 4 + (me ^ k)) * piece, piece), piece)
            gp_t[at, :] = part[i * piece : (i + 1) * piece, :]
        extra = part[rows:, :hidden].astype(F32)
        share = share + extra[:8] + extra[8:]
    ids = ids_row[...]
    number = lax.broadcasted_iota(jnp.int32, (8, ids.shape[1]), 0)
    counts = jnp.sum(jnp.where(ids == number, 1.0, 0.0), axis=1, keepdims=True)
    gmu = lax.dot_general(
        share, condt[...], (((1,), (0,)), ((), ())), precision=HIGH, preferred_element_type=F32
    ) / jnp.maximum(counts, 1.0)
    gu1 = mm_nt(jnp.transpose(gp_t[...]), w_in[...])
    quarter = x.shape[0]
    own = jnp.broadcast_to(ids_row[:, tile(me, quarter)].astype(F32), (8, quarter))
    ids_own = jnp.transpose(own)[:, 0:1]
    for j in range(SEGS):
        gu1 = gu1 + jnp.where(ids_own == j, gmu[j : j + 1, :], 0.0)
    unit, scale = normed(x[...].astype(F32))
    out[...] = big_g[...] + norm_back(unit, scale, gu1 * norms[0:1, :])


def final(me, gp_parts, x, big_g, norms, ids, condt, w_in, after, piece):
    quarter, channels = x.shape
    return pl.pallas_call(
        functools.partial(final_kernel, piece=piece),
        in_specs=[SM] + [VM] * 10 + [HBM],
        out_specs=VM,
        out_shape=shape((quarter, channels), F32),
        scratch_shapes=[pltpu.VMEM((2 * channels, quarter), BF16)],
        compiler_params=params(),
        cost_estimate=cost(2),
        name="final",
    )(me, *gp_parts, x, big_g, norms, ids, condt, w_in, after)


def small_kernel(
    me_ref, j0, j1, j2, j3, w2, taps, ln, w1, b1, cond, wide, tap_t, cond_t, *, layout, step, width
):
    me = me_ref[0]
    parts = (j0, j1, j2, j3)
    hidden = w1.shape[0]
    half = width // step
    count = 2 * width // 128
    for k, part in enumerate(parts):
        who = me ^ k
        rows = jnp.concatenate(
            [
                jnp.concatenate([part[layout["taps"] + i * count + m : layout["taps"] + i * count + m + 1, :]
                                 for m in range(count)], axis=1)
                for i in range(3)
            ]
            + [jnp.zeros((125, 2 * width), F32)],
            axis=0,
        )
        tap_t[...] = jnp.transpose(rows)
        for side in range(2):
            for i in range(half):
                at = pl.ds(pl.multiple_of((side * half * 4 + i * 4 + who) * step, step), step)
                lo = i * step
                wide[at, :hidden] = part[lo : lo + step, side * hidden : (side + 1) * hidden]
                at2 = side * width + lo
                wide[at, hidden:] = tap_t[at2 : at2 + step, :hidden]
    whole = jnp.transpose(wide[...])
    w2[...] = whole[:hidden, :]
    taps[...] = whole[hidden : hidden + 3, :]

    def common(first, last):
        return (j0[first:last, :] + j1[first:last, :]) + (j2[first:last, :] + j3[first:last, :])

    lanes = ln.shape[1] // 128
    sums = common(layout["ln"], layout["ln"] + 4 * lanes)
    for i in range(4):
        for m in range(lanes):
            ln[i : i + 1, m * 128 : (m + 1) * 128] = sums[i * lanes + m : i * lanes + m + 1, :]
    both = common(layout["w1"], layout["w1"] + hidden // 2)
    w1[: hidden // 2, :] = both[:, :hidden]
    w1[hidden // 2 :, :] = both[:, hidden:]
    cb = common(layout["cb"], layout["mu"])
    shares = []
    for b in range(cb.shape[0] // 4):
        lo = 8 * (b // 2)
        shares.append(cb[lo : lo + 8, (b % 2) * hidden : (b % 2 + 1) * hidden])
    shares = jnp.concatenate(shares, axis=0)
    b1[...] = jnp.sum(shares, axis=0, keepdims=True)
    for k, part in enumerate(parts):
        rows = []
        for b in range(cb.shape[0] // 4):
            lo = layout["mu"] + 8 * b
            block = part[lo : lo + 8, :]
            rows.append(
                jnp.concatenate(
                    [
                        jnp.concatenate([block[:SEGS, :], jnp.zeros((8 - SEGS, 128), F32)], axis=0),
                        jnp.concatenate(
                            [block[SEGS : 2 * SEGS, : width - 128], jnp.zeros((8 - SEGS, width - 128), F32)],
                            axis=0,
                        ),
                    ],
                    axis=1,
                )
            )
        mu = jnp.concatenate(rows, axis=0)
        cond_t[tile(me ^ k, width), :] = lax.dot_general(
            jnp.transpose(mu), shares, (((1,), (0,)), ((), ())), precision=HIGH, preferred_element_type=F32
        )
    cond[...] = jnp.transpose(cond_t[...])


def small_grads(me, parts, hidden, channels, step, bs):
    width = channels // 4
    layout = packed_layout(width, channels, bs)
    return pl.pallas_call(
        functools.partial(small_kernel, layout=layout, step=step, width=width),
        in_specs=[SM] + [VM] * 4,
        out_specs=[VM] * 6,
        out_shape=[
            shape((hidden, 2 * channels), F32),
            shape((3, 2 * channels), F32),
            shape((4, channels), F32),
            shape((hidden, hidden), F32),
            shape((1, hidden), F32),
            shape((hidden, channels), F32),
        ],
        scratch_shapes=[
            pltpu.VMEM((2 * channels, 2 * hidden), F32),
            pltpu.VMEM((2 * width, 128), F32),
            pltpu.VMEM((channels, hidden), F32),
        ],
        compiler_params=params(),
        cost_estimate=cost(3),
        name="small_grads",
    )(me, *parts)


def trade_parts(parts):
    two, three, one = [swap(parts[k], "freq", k) for k in (2, 3, 1)]
    return (parts[0], one, two, three)


def tiled_device(
    tokens,
    seg_ids,
    cotangent,
    ln1_gain,
    ln1_shift,
    w_in,
    conv_taps,
    freq_w1,
    freq_b1,
    freq_w2,
    cond_w,
    w_out,
    ln2_gain,
    ln2_shift,
    w_gate,
    w_up,
    w_down,
):
    quarter, _, channels = tokens.shape
    length = seg_ids.shape[1]
    ff = w_gate.shape[1]
    fs = lax.axis_size("freq")
    bs = lax.axis_size("batch")
    me = lax.axis_index("freq")
    row = lax.axis_index("batch")
    width = channels // fs
    half = bs // 2
    step = channels // (half * fs)
    fw = ff // (bs * fs)
    cos_table, sin_table = tables(length)
    feats = features(length, freq_w1.shape[0] // 2)
    feats_aug = np.concatenate(
        [feats, np.ones((1, length), np.float32), np.zeros((7, length), np.float32)], axis=0
    )

    x_own = tokens[:, 0]
    ct_own = cotangent[:, 0]
    ids = seg_ids
    me1 = me.reshape(1)
    x_parts = gather_freq(x_own, me)
    ct_parts = gather_freq(ct_own, me)
    at = jnp.stack([me, row & 1, (row >> 1) & 1, (row >> 2) & 1, row]).astype(jnp.int32)
    norms = jnp.stack([ln1_gain, ln1_shift, ln2_gain, ln2_shift])
    condt = cond_w.T
    cos_c, sin_c = jnp.asarray(cos_table), jnp.asarray(sin_table)

    w_mine, w2x, w2t, taps, base = prepare(
        me1, w_in, freq_w2, conv_taps, freq_w1, freq_b1, jnp.asarray(feats_aug), step, fs
    )
    forward = forward_spectral(me1, x_parts, ids, norms, w_mine, taps, base, w2x, condt, cos_c, sin_c)
    z_parts, (z_row, u1, n1, p, q, c, vr, vs, mu, mn, cb) = forward[:4], forward[4:]
    z_got = trade_parts(z_parts)
    wg_mine, wu_mine = select_columns(me1, cb, w_gate, w_up, fw, fs)
    h, u2, z_t = middle(me1, z_got, x_own, w_out, norms, wg_mine, step)
    u2_parts = gather_freq(u2, me)
    fed = feed_forward(me1, u2, h, ct_own, norms, w_out, w_gate, w_up, w_down, step)
    mixed_out, big_g, gb, gz_parts, sums2 = fed[0], fed[1], fed[2], fed[3:7], fed[7]
    gz_got = trade_parts(gz_parts)

    hidden = hidden_grads(
        at, u2_parts, ct_parts, wg_mine, wu_mine, w_down.reshape(bs, fs, fw, channels), gb, z_t
    )
    keep_a, give_a, keep_b, give_b = hidden[:4]
    got_a = swap(give_a, "batch", 1)
    got_b = swap(give_b, "batch", 2)
    gb_got = trade_parts(hidden[4:8])
    z_all = gather_freq(hidden[8], me)

    back = backward_spectral(
        me1, gz_got, ids, cb, taps, base, w2x, w2t, jnp.asarray(feats).astype(BF16),
        p, q, c, vr, vs, cos_c, sin_c, give_a,
    )
    gp_parts, (gp, d_taps, d_w2, d_w1, gcb) = back[:4], back[4:]
    gp_got = trade_parts(gp_parts)

    def pairs(value):
        return value.reshape((value.shape[0] // 2, 2) + value.shape[1:])

    keep_a, give_a, keep_b, give_b = halve(
        jnp.stack([at[2], at[1]]), gp, pairs(keep_a), pairs(got_a), keep_b, got_b
    )
    got_a = swap(give_a, "batch", 2)
    got_b = swap(give_b, "batch", 1)

    keep, give, packed = projection_grads(
        at, gp, u1, n1, w_mine, gb_got, z_all, d_w2, d_w1, d_taps, gcb, condt, mu, mn, sums2, give_a, bs
    )
    got = swap(give, "batch", 1)
    grad_tokens = final(me1, gp_got, x_own, big_g, norms, ids, condt, w_in, packed, step)

    keep_ff, give_ff = join(at[3:4], grad_tokens, keep_a, got_a, keep_b, got_b)
    got_ff = swap(give_ff, "batch", 4)

    keep, give = halve(at[2:3], give_ff, pairs(keep), pairs(got))
    got = swap(give, "batch", 2)
    keep, give = halve(at[3:4], give_ff, pairs(keep), pairs(got))
    got = swap(give, "batch", 4)
    mine = keep[0].astype(F32) + got[0].astype(F32)
    first = 2 * width // bs

    for bit in range(bs.bit_length() - 1):
        packed = packed + swap(packed, "batch", 1 << bit)
    d_w2, d_taps, ln, d_w1, d_b1, d_cond = small_grads(
        me1, gather_freq(packed, me), freq_w1.shape[1], channels, step, bs
    )
    d_ff = keep_ff.astype(F32) + got_ff.astype(F32)
    return (
        mixed_out[:, None],
        grad_tokens[:, None],
        ln[0],
        ln[1],
        mine[:first].T,
        d_taps,
        d_w1,
        d_b1[0],
        d_w2,
        d_cond.T,
        mine[first:].T,
        ln[2],
        ln[3],
        d_ff[0].T,
        d_ff[1].T,
        d_ff[2],
    )


def per_device(*args):
    channels = args[0].shape[2]
    step = 2 * channels // (lax.axis_size("batch") * lax.axis_size("freq"))
    fits = lax.axis_size("batch") == 8 and lax.axis_size("freq") == 4 and step % 16 == 0
    return tiled_device(*args) if fits else plain_device(*args)


def solution(mesh):
    rows = P("freq", "batch", None)
    split = P(None, ("batch", "freq"))
    in_specs = (rows, P("batch", None), rows) + (P(),) * 14
    out_specs = (
        rows,
        rows,
        P(),
        P(),
        split,
        P(),
        P(),
        P(),
        P(),
        P(),
        split,
        P(),
        P(),
        split,
        split,
        P(("batch", "freq"), None),
    )
    return jax.shard_map(
        per_device, mesh=mesh, in_specs=in_specs, out_specs=out_specs, check_vma=False
    )
```

profile of v0, /device:TPU:2, one launch (start us, length us, event | category | flops | bytes accessed | tf_op | source)
XLA Modules:
  0.0 217.5 jit_solution(9873257472908777111)
XLA Ops:
  0.8 1.9 collective-permute-start.13
  5.5 7.4 %collective-permute-done.1.x2 = bf16[256,768]{1,0:T(8,128)(2,1)S(1)} collective-permute-done((bf16[256,768]{1,0:T(8,128)(2,1)}, bf16[256,768]{1,0:T(8,128)(2,1)S(1)}, u32[]{:S(2)}, u32[]{:S(2)}) %collective-permute-start.1) | collective-permute-done | bytes 393248 | tf_op jit(solution)/shard_map/ppermute | solution.py:33
  13.6 4.2 %prepare.1 = (bf16[384,768]{1,0:T(8,128)(2,1)}, bf16[384,192]{1,0:T(8,128)(2,1)}, bf16[64,384]{1,0:T(8,128)(2,1)}, f32[384,8]{1,0:T(8,128)}, f32[64,1024]{1,0:T(8,128)}) custom-call(s32[1]{0:T(128)} %bitcast.me_ref, bf16[768,1536]{1,0:T(8,128)(2,1)} %w_in.3, f32[64,1536]{1,0:T(8,128)} %freq_w2.1, f32[3,1536]{1,0:T(4,128)} %conv_taps.1, f32[64,64]{1,0:T(8,128)} %freq_w1.1, ...), custom_call_target="tpu_custom_call" | custom-call | flops 3000000000 | bytes 10500000 | tf_op jit(solution)/shard_map/prepare/pallas_call | solution.py:454
  18.7 15.5 %forward_spectral.1 = (bf16[192,256]{1,0:T(8,128)(2,1)}, bf16[192,256]{1,0:T(8,128)(2,1)}, bf16[192,256]{1,0:T(8,128)(2,1)}, bf16[192,256]{1,0:T(8,128)(2,1)}, b...) custom-call(s32[1]{0:T(128)} %bitcast.me_ref, ...), custom_call_target="tpu_custom_call" | custom-call | flops 15000000512 | bytes 52500000 | tf_op jit(solution)/shard_map/forward_spectral/pallas_call | solution.py:641
  36.1 6.9 %select_columns.1 = (bf16[768,768]{1,0:T(8,128)(2,1)}, bf16[768,768]{1,0:T(8,128)(2,1)}) custom-call(s32[1]{0:T(128)} %bitcast.me_ref, f32[64,8]{1,0:T(8,128)} %get-tuple-element.93.after.cb, bf16[768,3072]{1,0:T(8,128)(2,1)} %gate.3, bf16[768,3072]{1,0:T(8,128)(2,1)} %up.3), custom_call_target="tpu_custom_call" | custom-call | flops 6000000000 | bytes 21000000 | tf_op jit(solution)/shard_map/select_columns/pallas_call | solution.py:487
  43.7 3.2 %middle.1 = (f32[256,768]{1,0:T(8,128)}, bf16[256,768]{1,0:T(8,128)(2,1)}, bf16[768,256]{1,0:T(8,128)(2,1)}) custom-call(s32[1]{0:T(128)} %bitcast.me_ref, bf16[192,256]{1,0:T(8,128)(2,1)} %get-tuple-element.89.z0, bf16[192,256]{1,0:T(8,128)(2,1)} %copy-done.44, bf16[192,256]{1,0:T(8,128)(2,1)} %copy-done.45, bf16[192,256]{1,0:T(8,128)(2,1)} %copy-done.46, ...), custom_call_target="tpu_custom_call" | custom-call | flops 2000000000 | bytes 7000000 | tf_op jit(solution)/shard_map/middle/pallas_call | solution.py:819
  48.8 10.0 %collective-permute-done.10.u2 = bf16[256,768]{1,0:T(8,128)(2,1)S(1)} collective-permute-done((bf16[256,768]{1,0:T(8,128)(2,1)}, bf16[256,768]{1,0:T(8,128)(2,1)S(1)}, u32[]{:S(2)}, u32[]{:S(2)}) %collective-permute-start.10) | collective-permute-done | bytes 393248 | tf_op jit(solution)/shard_map/ppermute | solution.py:33
  58.9 14.5 %feed_forward.1 = (bf16[256,768]{1,0:T(8,128)(2,1)}, f32[256,768]{1,0:T(8,128)}, bf16[256,768]{1,0:T(8,128)(2,1)}, bf16[192,256]{1,0:T(8,128)(2,1)}, bf16[192,25...) custom-call(s32[1]{0:T(128)} %bitcast.me_ref, ...), custom_call_target="tpu_custom_call" | custom-call | flops 12999999488 | bytes 45500000 | tf_op jit(solution)/shard_map/feed_forward/pallas_call | solution.py:891
  74.6 16.3 %hidden_grads.1 = (bf16[4,3,96,384]{3,2,1,0:T(8,128)(2,1)}, bf16[4,3,96,384]{3,2,1,0:T(8,128)(2,1)}, bf16[2,2,3,96,384]{4,3,2,1,0:T(8,128)(2,1)}, bf16[2,2,3,96,...) custom-call(s32[5]{0:T(128)} %stack.43.at_ref, ...), custom_call_target="tpu_custom_call" | custom-call | flops 14000000000 | bytes 49000000 | tf_op jit(solution)/shard_map/hidden_grads/pallas_call | solution.py:982
  94.3 10.9 %collective-permute-done.7.g2 = bf16[192,256]{1,0:T(8,128)(2,1)S(1)} collective-permute-done((bf16[192,256]{1,0:T(8,128)(2,1)S(1)}, bf16[192,256]{1,0:T(8,128)(2,1)S(1)}, u32[]{:S(2)}, u32[]{:S(2)}) %collective-permute-start.7) | collective-permute-done | bytes 98336 | tf_op jit(solution)/shard_map/ppermute | solution.py:33
  108.4 19.0 %backward_spectral.1 = (bf16[400,256]{1,0:T(8,128)(2,1)}, bf16[400,256]{1,0:T(8,128)(2,1)}, bf16[400,256]{1,0:T(8,128)(2,1)}, bf16[400,256]{1,0:T(8,128)(2,1)}, ...) custom-call(s32[1]{0:T(128)} %bitcast.me_ref, ...), custom_call_target="tpu_custom_call" | custom-call | flops 16999999488 | bytes 59500000 | tf_op jit(solution)/shard_map/backward_spectral/pallas_call | solution.py:776
  129.3 3.5 %halve.3 = (bf16[2,3,96,384]{3,2,1,0:T(8,128)(2,1)}, bf16[2,3,96,384]{3,2,1,0:T(8,128)(2,1)}, bf16[2,3,96,384]{3,2,1,0:T(8,128)(2,1)}, bf16[2,3,96,384]{3,2,1,0:T(8,128)(2,1)}) custom-call(s32[2]{0:T(128)} %pad_add_fusion.bit_ref, bf16[384,1024]{1,0:T(8,128)(2,1)} %get-tuple-element.117.after.gp, bf16[2,2,3,96,384]{4,3,2,1,0:T(8,128)(2,1)} %bitcast.56, ...), custom_call_target="tpu_custom_call" | custom-call | flops 2000000000 | bytes 7000000 | tf_op jit(solution)/shard_map/halve/pallas_call | solution.py:1023
  139.1 5.7 %projection_grads.1 = (bf16[4,72,768]{2,1,0:T(8,128)(2,1)}, bf16[4,72,768]{2,1,0:T(8,128)(2,1)}, f32[360,128]{1,0:T(8,128)}) custom-call(s32[5]{0:T(128)} %stack.43.at_ref, bf16[384,1024]{1,0:T(8,128)(2,1)} %get-tuple-element.117.after.gp, bf16[1024,768]{1,0:T(8,128)(2,1)} %get-tuple-element.118.u1, bf16[1024,768]{1,0:T(8,128)(2,1)} %get-tuple-element.119.n1, ...), custom_call_target="tpu_custom_call" | custom-call | flops 4000000000 | bytes 14000000 | tf_op jit(solution)/shard_map/projection_grads/pallas_call | solution.py:1130
  147.6 4.7 %final.1.after = f32[256,768]{1,0:T(8,128)} custom-call(s32[1]{0:T(128)} %bitcast.me_ref, bf16[400,256]{1,0:T(8,128)(2,1)} %get-tuple-element.112.p0, bf16[400,256]{1,0:T(8,128)(2,1)} %copy-done.28, bf16[400,256]{1,0:T(8,128)(2,1)} %copy-done.29, bf16[400,256]{1,0:T(8,128)(2,1)} %copy-done.30, bf16[256,768]{1,0:T(8,128)(2,1)} %bitcast.50, ...), custom_call_target="tpu_custom_call" | custom-call | flops 2000000000 | bytes 7000000 | tf_op jit(solution)/shard_map/final/pallas_call | solution.py:1181
  152.3 10.1 %collective-permute-done.26 = f32[360,128]{1,0:T(8,128)S(1)} collective-permute-done((f32[360,128]{1,0:T(8,128)}, f32[360,128]{1,0:T(8,128)S(1)}, u32[]{:S(2)}, u32[]{:S(2)}) %collective-permute-start.26) | collective-permute-done | bytes 184352 | tf_op jit(solution)/shard_map/ppermute | solution.py:33
  164.6 2.5 %join.1 = (bf16[3,96,768]{2,1,0:T(8,128)(2,1)}, bf16[3,96,768]{2,1,0:T(8,128)(2,1)}) custom-call(s32[1]{0:T(128)} %bitcast.8.bit_ref, f32[256,768]{1,0:T(8,128)} %final.1.after, bf16[2,3,96,384]{3,2,1,0:T(8,128)(2,1)} %get-tuple-element.138.keep_a, bf16[2,3,96,384]{3,2,1,0:T(8,128)(2,1)} %copy-done.9, bf16[2,3,96,384]{3,2,1,0:T(8,128)(2,1)} %get-tuple-element.139.keep_b, ...), custom_call_target="tpu_custom_call" | custom-call | flops 2000000000 | bytes 7000000 | tf_op jit(solution)/shard_map/join/pallas_call | solution.py:1045
  167.9 2.0 halve.4
  170.7 2.7 %collective-permute-start.28 = (f32[360,128]{1,0:T(8,128)S(1)}, f32[360,128]{1,0:T(8,128)S(1)}, u32[]{:S(2)}, u32[]{:S(2)}) collective-permute-start(f32[360,128]{1,0:T(8,128)S(1)} %add.17), channel_id=1, source_target_pairs={{0,16},{4,20},{8,24},{12,28},{16,0},{20,4},{24,8},{28,12},{1,17},{... | collective-permute-start | bytes 552968 | tf_op jit(solution)/shard_map/ppermute | solution.py:33
  173.4 5.9 %collective-permute-done.28 = f32[360,128]{1,0:T(8,128)S(1)} collective-permute-done((f32[360,128]{1,0:T(8,128)S(1)}, f32[360,128]{1,0:T(8,128)S(1)}, u32[]{:S(2)}, u32[]{:S(2)}) %collective-permute-start.28) | collective-permute-done | bytes 184352 | tf_op jit(solution)/shard_map/ppermute | solution.py:33
  181.2 1.8 halve.5
  183.1 3.1 %collective-permute-start.36 = (bf16[1,72,768]{2,1,0:T(8,128)(2,1)}, bf16[1,72,768]{2,1,0:T(8,128)(2,1)S(1)}, u32[]{:S(2)}, u32[]{:S(2)}) collective-permute-start(bf16[1,72,768]{2,1,0:T(8,128)(2,1)} %get-tuple-element.147), channel_id=1, source_target_pairs={{0,16},{4,20},{8,24},{12,28},{16,0},{20,4},{24,8},{28,12},{1,17},{... | collective-permute-start | bytes 331784 | tf_op jit(solution)/shard_map/ppermute | solution.py:33
  186.2 1.7 copy.37
  191.4 19.1 %collective-permute-done.37 = bf16[3,96,768]{2,1,0:T(8,128)(2,1)S(1)} collective-permute-done((bf16[3,96,768]{2,1,0:T(8,128)(2,1)S(1)}, bf16[3,96,768]{2,1,0:T(8,128)(2,1)S(1)}, u32[]{:S(2)}, u32[]{:S(2)}) %collective-permute-start.37) | collective-permute-done | bytes 442400 | tf_op jit(solution)/shard_map/ppermute | solution.py:33
  212.9 3.2 %small_grads.1 = (f32[64,1536]{1,0:T(8,128)}, f32[3,1536]{1,0:T(4,128)}, f32[4,768]{1,0:T(4,128)}, f32[64,64]{1,0:T(8,128)}, f32[1,64]{1,0:T(1,128)}, /*index=5*/f32[64,768]{1,0:T(8,128)}) custom-call(s32[1]{0:T(128)} %bitcast.me_ref, f32[360,128]{1,0:T(8,128)} %copy-done.2, f32[360,128]{1,0:T(8,128)} %copy-done.32, f32[360,128]{1,0:T(8,128)} %copy-done.31, ...), custom_call_target="tpu_custom_call" | custom-call | flops 3000000000 | bytes 10500000 | tf_op jit(solution)/shard_map/small_grads/pallas_call | solution.py:1269
  (177 shorter events, 40.6 us)
Async XLA Ops:
  0.6 12.3 %collective-permute-start.1 = (bf16[256,768]{1,0:T(8,128)(2,1)}, bf16[256,768]{1,0:T(8,128)(2,1)S(1)}, u32[]{:S(2)}, u32[]{:S(2)}) collective-permute-start(bf16[256,768]{1,0:T(8,128)(2,1)} %bitcast.46), channel_id=1, source_target_pairs={{0,2},{1,3},{2,0},{3,1},{4,6},{5,7},{6,4},{7,5},{8,10},{9,11},{10,... | collective-permute-start | bytes 1179656 | tf_op jit(solution)/shard_map/ppermute | solution.py:33
  0.7 17.1 %collective-permute-start = (bf16[256,768]{1,0:T(8,128)(2,1)}, bf16[256,768]{1,0:T(8,128)(2,1)S(1)}, u32[]{:S(2)}, u32[]{:S(2)}) collective-permute-start(bf16[256,768]{1,0:T(8,128)(2,1)} %bitcast.47), channel_id=1, source_target_pairs={{0,1},{1,0},{2,3},{3,2},{4,5},{5,4},{6,7},{7,6},{8,9},{9,8},{10,11... | collective-permute-start | bytes 1179656 | tf_op jit(solution)/shard_map/ppermute | solution.py:33
  0.8 47.5 %collective-permute-start.13 = (bf16[256,768]{1,0:T(8,128)(2,1)}, bf16[256,768]{1,0:T(8,128)(2,1)S(1)}, u32[]{:S(2)}, u32[]{:S(2)}) collective-permute-start(bf16[256,768]{1,0:T(8,128)(2,1)} %bitcast.42), channel_id=1, source_target_pairs={{0,2},{1,3},{2,0},{3,1},{4,6},{5,7},{6,4},{7,5},{8,10},{9,11},{10,... | collective-permute-start | bytes 1179656 | tf_op jit(solution)/shard_map/ppermute | solution.py:33
  46.9 11.9 %collective-permute-start.10 = (bf16[256,768]{1,0:T(8,128)(2,1)}, bf16[256,768]{1,0:T(8,128)(2,1)S(1)}, u32[]{:S(2)}, u32[]{:S(2)}) collective-permute-start(bf16[256,768]{1,0:T(8,128)(2,1)} %get-tuple-element.95.u2.u0), channel_id=1, source_target_pairs={{0,2},{1,3},{2,0},{3,1},{4,6},{5,7},{6,4},{7,5},{8,10},{9,11},{10,... | collective-permute-start | bytes 1179656 | tf_op jit(solution)/shard_map/ppermute | solution.py:33
  47.5 25.9 %collective-permute-start.12 = (bf16[256,768]{1,0:T(8,128)(2,1)S(1)}, bf16[256,768]{1,0:T(8,128)(2,1)S(1)}, u32[]{:S(2)}, u32[]{:S(2)}) collective-permute-start(bf16[256,768]{1,0:T(8,128)(2,1)S(1)} %bitcast.45), channel_id=1, source_target_pairs={{0,1},{1,0},{2,3},{3,2},{4,5},{5,4},{6,7},{7,6},{8,9},{9,8},{10,11... | collective-permute-start | bytes 1179656 | tf_op jit(solution)/shard_map/ppermute | solution.py:33
  48.3 25.1 %collective-permute-start.14 = (bf16[256,768]{1,0:T(8,128)(2,1)S(1)}, bf16[256,768]{1,0:T(8,128)(2,1)S(1)}, u32[]{:S(2)}, u32[]{:S(2)}) collective-permute-start(bf16[256,768]{1,0:T(8,128)(2,1)S(1)} %collective-permute-done.13.c2), channel_id=1, source_target_pairs={{0,1},{1,0},{2,3},{3,2},{4,5},{5,4},{6,7},{7,6},{8,9},{9,8},{10,11... | collective-permute-start | bytes 1179656 | tf_op jit(solution)/shard_map/ppermute | solution.py:33
  48.7 24.8 %collective-permute-start.9 = (bf16[256,768]{1,0:T(8,128)(2,1)}, bf16[256,768]{1,0:T(8,128)(2,1)S(1)}, u32[]{:S(2)}, u32[]{:S(2)}) collective-permute-start(bf16[256,768]{1,0:T(8,128)(2,1)} %get-tuple-element.95.u2.u0), channel_id=1, source_target_pairs={{0,1},{1,0},{2,3},{3,2},{4,5},{5,4},{6,7},{7,6},{8,9},{9,8},{10,11... | collective-permute-start | bytes 1179656 | tf_op jit(solution)/shard_map/ppermute | solution.py:33
  58.9 14.6 %collective-permute-start.11 = (bf16[256,768]{1,0:T(8,128)(2,1)S(1)}, bf16[256,768]{1,0:T(8,128)(2,1)S(1)}, u32[]{:S(2)}, u32[]{:S(2)}) collective-permute-start(bf16[256,768]{1,0:T(8,128)(2,1)S(1)} %collective-permute-done.10.u2), channel_id=1, source_target_pairs={{0,1},{1,0},{2,3},{3,2},{4,5},{5,4},{6,7},{7,6},{8,9},{9,8},{10,11... | collective-permute-start | bytes 1179656 | tf_op jit(solution)/shard_map/ppermute | solution.py:33
  90.9 17.4 %collective-permute-start.22 = (bf16[768,256]{1,0:T(8,128)(2,1)}, bf16[768,256]{1,0:T(8,128)(2,1)S(1)}, u32[]{:S(2)}, u32[]{:S(2)}) collective-permute-start(bf16[768,256]{1,0:T(8,128)(2,1)} %get-tuple-element.124.z0), channel_id=1, source_target_pairs={{0,2},{1,3},{2,0},{3,1},{4,6},{5,7},{6,4},{7,5},{8,10},{9,11},{10,... | collective-permute-start | bytes 1179656 | tf_op jit(solution)/shard_map/ppermute | solution.py:33
  91.4 13.8 %collective-permute-start.7 = (bf16[192,256]{1,0:T(8,128)(2,1)S(1)}, bf16[192,256]{1,0:T(8,128)(2,1)S(1)}, u32[]{:S(2)}, u32[]{:S(2)}) collective-permute-start(bf16[192,256]{1,0:T(8,128)(2,1)S(1)} %copy-done.39), channel_id=1, source_target_pairs={{0,2},{1,3},{2,0},{3,1},{4,6},{5,7},{6,4},{7,5},{8,10},{9,11},{10,... | collective-permute-start | bytes 294920 | tf_op jit(solution)/shard_map/ppermute | solution.py:33
  93.1 13.7 %collective-permute-start.8 = (bf16[192,256]{1,0:T(8,128)(2,1)S(1)}, bf16[192,256]{1,0:T(8,128)(2,1)S(1)}, u32[]{:S(2)}, u32[]{:S(2)}) collective-permute-start(bf16[192,256]{1,0:T(8,128)(2,1)S(1)} %copy-done.38), channel_id=1, source_target_pairs={{0,3},{1,2},{2,1},{3,0},{4,7},{5,6},{6,5},{7,4},{8,11},{9,10},{10,... | collective-permute-start | bytes 294920 | tf_op jit(solution)/shard_map/ppermute | solution.py:33
  93.8 42.2 %collective-permute-start.21 = (bf16[768,256]{1,0:T(8,128)(2,1)}, bf16[768,256]{1,0:T(8,128)(2,1)S(1)}, u32[]{:S(2)}, u32[]{:S(2)}) collective-permute-start(bf16[768,256]{1,0:T(8,128)(2,1)} %get-tuple-element.124.z0), channel_id=1, source_target_pairs={{0,1},{1,0},{2,3},{3,2},{4,5},{5,4},{6,7},{7,6},{8,9},{9,8},{10,11... | collective-permute-start | bytes 1179656 | tf_op jit(solution)/shard_map/ppermute | solution.py:33
  94.2 38.7 %collective-permute-start.18 = (bf16[192,256]{1,0:T(8,128)(2,1)}, bf16[192,256]{1,0:T(8,128)(2,1)S(1)}, u32[]{:S(2)}, u32[]{:S(2)}) collective-permute-start(bf16[192,256]{1,0:T(8,128)(2,1)} %get-tuple-element.121), channel_id=1, source_target_pairs={{0,1},{1,0},{2,3},{3,2},{4,5},{5,4},{6,7},{7,6},{8,9},{9,8},{10,11... | collective-permute-start | bytes 294920 | tf_op jit(solution)/shard_map/ppermute | solution.py:33
  105.2 22.2 %collective-permute-start.25 = (bf16[2,2,3,96,384]{4,3,2,1,0:T(8,128)(2,1)}, bf16[2,2,3,96,384]{4,3,2,1,0:T(8,128)(2,1)S(1)}, u32[]{:S(2)}, u32[]{:S(2)}) collective-permute-start(bf16[2,2,3,96,384]{4,3,2,1,0:T(8,128)(2,1)} %get-tuple-element.134), channel_id=1, source_target_pairs={{0,8},{4,12},{8,0},{12,4},{16,24},{20,28},{24,16},{28,20},{1,9},{5... | collective-permute-start | bytes 2654216 | tf_op jit(solution)/shard_map/ppermute | solution.py:33
  106.8 21.5 %collective-permute-start.24 = (bf16[4,3,96,384]{3,2,1,0:T(8,128)(2,1)}, bf16[4,3,96,384]{3,2,1,0:T(8,128)(2,1)S(1)}, u32[]{:S(2)}, u32[]{:S(2)}) collective-permute-start(bf16[4,3,96,384]{3,2,1,0:T(8,128)(2,1)} %get-tuple-element.111.after), channel_id=1, source_target_pairs={{0,4},{4,0},{8,12},{12,8},{16,20},{20,16},{24,28},{28,24},{1,5},{5... | collective-permute-start | bytes 2654216 | tf_op jit(solution)/shard_map/ppermute | solution.py:33
  108.3 29.2 %collective-permute-start.23 = (bf16[768,256]{1,0:T(8,128)(2,1)S(1)}, bf16[768,256]{1,0:T(8,128)(2,1)S(1)}, u32[]{:S(2)}, u32[]{:S(2)}) collective-permute-start(bf16[768,256]{1,0:T(8,128)(2,1)S(1)} %collective-permute-done.22.z2), channel_id=1, source_target_pairs={{0,1},{1,0},{2,3},{3,2},{4,5},{5,4},{6,7},{7,6},{8,9},{9,8},{10,11... | collective-permute-start | bytes 1179656 | tf_op jit(solution)/shard_map/ppermute | solution.py:33
  135.4 11.5 %collective-permute-start.17 = (bf16[400,256]{1,0:T(8,128)(2,1)S(1)}, bf16[400,256]{1,0:T(8,128)(2,1)S(1)}, u32[]{:S(2)}, u32[]{:S(2)}) collective-permute-start(bf16[400,256]{1,0:T(8,128)(2,1)S(1)} %copy-done.25), channel_id=1, source_target_pairs={{0,3},{1,2},{2,1},{3,0},{4,7},{5,6},{6,5},{7,4},{8,11},{9,10},{10,... | collective-permute-start | bytes 614408 | tf_op jit(solution)/shard_map/ppermute | solution.py:33
  136.0 27.7 %collective-permute-start.33 = (bf16[2,3,96,384]{3,2,1,0:T(8,128)(2,1)}, bf16[2,3,96,384]{3,2,1,0:T(8,128)(2,1)S(1)}, u32[]{:S(2)}, u32[]{:S(2)}) collective-permute-start(bf16[2,3,96,384]{3,2,1,0:T(8,128)(2,1)} %get-tuple-element.140), channel_id=1, source_target_pairs={{0,4},{4,0},{8,12},{12,8},{16,20},{20,16},{24,28},{28,24},{1,5},{5... | collective-permute-start | bytes 1327112 | tf_op jit(solution)/shard_map/ppermute | solution.py:33
  137.5 26.2 %collective-permute-start.32 = (bf16[2,3,96,384]{3,2,1,0:T(8,128)(2,1)}, bf16[2,3,96,384]{3,2,1,0:T(8,128)(2,1)S(1)}, u32[]{:S(2)}, u32[]{:S(2)}) collective-permute-start(bf16[2,3,96,384]{3,2,1,0:T(8,128)(2,1)} %get-tuple-element.135.after), channel_id=1, source_target_pairs={{0,8},{4,12},{8,0},{12,4},{16,24},{20,28},{24,16},{28,20},{1,9},{5... | collective-permute-start | bytes 1327112 | tf_op jit(solution)/shard_map/ppermute | solution.py:33
  144.8 22.3 %collective-permute-start.34 = (bf16[4,72,768]{2,1,0:T(8,128)(2,1)}, bf16[4,72,768]{2,1,0:T(8,128)(2,1)S(1)}, u32[]{:S(2)}, u32[]{:S(2)}) collective-permute-start(bf16[4,72,768]{2,1,0:T(8,128)(2,1)} %get-tuple-element.143), channel_id=1, source_target_pairs={{0,4},{4,0},{8,12},{12,8},{16,20},{20,16},{24,28},{28,24},{1,5},{5... | collective-permute-start | bytes 1327112 | tf_op jit(solution)/shard_map/ppermute | solution.py:33
  145.4 17.0 %collective-permute-start.26 = (f32[360,128]{1,0:T(8,128)}, f32[360,128]{1,0:T(8,128)S(1)}, u32[]{:S(2)}, u32[]{:S(2)}) collective-permute-start(f32[360,128]{1,0:T(8,128)} %get-tuple-element.136.after), channel_id=1, source_target_pairs={{0,4},{4,0},{8,12},{12,8},{16,20},{20,16},{24,28},{28,24},{1,5},{5... | collective-permute-start | bytes 552968 | tf_op jit(solution)/shard_map/ppermute | solution.py:33
  187.9 22.6 %collective-permute-start.37 = (bf16[3,96,768]{2,1,0:T(8,128)(2,1)S(1)}, bf16[3,96,768]{2,1,0:T(8,128)(2,1)S(1)}, u32[]{:S(2)}, u32[]{:S(2)}) collective-permute-start(bf16[3,96,768]{2,1,0:T(8,128)(2,1)S(1)} %copy-done.8), channel_id=1, source_target_pairs={{0,16},{4,20},{8,24},{12,28},{16,0},{20,4},{24,8},{28,12},{1,17},{... | collective-permute-start | bytes 1327112 | tf_op jit(solution)/shard_map/ppermute | solution.py:33
  187.9 23.6 %collective-permute-start.29 = (f32[360,128]{1,0:T(8,128)S(1)}, f32[360,128]{1,0:T(8,128)S(1)}, u32[]{:S(2)}, u32[]{:S(2)}) collective-permute-start(f32[360,128]{1,0:T(8,128)S(1)} %add.18.j0), channel_id=1, source_target_pairs={{0,1},{1,0},{2,3},{3,2},{4,5},{5,4},{6,7},{7,6},{8,9},{9,8},{10,11... | collective-permute-start | bytes 552968 | tf_op jit(solution)/shard_map/ppermute | solution.py:33
  188.0 23.5 %collective-permute-start.31 = (f32[360,128]{1,0:T(8,128)S(1)}, f32[360,128]{1,0:T(8,128)S(1)}, u32[]{:S(2)}, u32[]{:S(2)}) collective-permute-start(f32[360,128]{1,0:T(8,128)S(1)} %collective-permute-done.30.j2), channel_id=1, source_target_pairs={{0,1},{1,0},{2,3},{3,2},{4,5},{5,4},{6,7},{7,6},{8,9},{9,8},{10,11... | collective-permute-start | bytes 552968 | tf_op jit(solution)/shard_map/ppermute | solution.py:33
  (61 other events, 422.2 us)
where the time goes:
time: 221 us; the launch traced here: 218 us
  Pallas kernels  103 us (47%)
  waiting for transfers between devices  65.8 us (30%)
  starting transfers between devices  29 us (13%)
  local copies, waits for them, and re-layouts  17.2 us (8%)
    ppermute x38, waiting for transfers between devices, swap(): return lax.ppermute(value, axis, [(i, i ^ mask) for i in range(count)])  65.8 us
    ppermute x38, starting transfers between devices, swap(): return lax.ppermute(value, axis, [(i, i ^ mask) for i in range(count)])  29 us
    pallas_call x1, Pallas kernels, backward_spectral(): pl.pallas_call(backward_kernel, in_specs=[SM, SM] + [VM] * 11 + [HBM] * 8...  19 us
    pallas_call x1, Pallas kernels, hidden_grads(): pl.pallas_call(functools.partial(hidden_grads_kernel, piece=channels // (...  16.3 us
    pallas_call x1, Pallas kernels, forward_spectral(): pl.pallas_call(forward_kernel, in_specs=[SM, SM] + [VM] * 11 + [HBM, HBM]...  15.5 us
    pallas_call x1, Pallas kernels, feed_forward(): pl.pallas_call(functools.partial(feed_kernel, piece=piece), grid=(ff // b...  14.5 us
    unnamed x95, local copies, waits for them, and re-layouts  10.1 us
    pallas_call x3, Pallas kernels, halve(): pl.pallas_call(functools.partial(halve_kernel, pairs=pairs), in_specs=[SM...  7.33 us
  transfers between devices with their start and end apart: 38, of which 9 were waited for; matrix products, arithmetic and copies ran while one was open for 4% of the time, Pallas kernels for 38%

commit v1 on v0

--- a/solution.py
+++ b/solution.py
@@ -384,7 +384,7 @@
 
 def cost(micros):
     return pl.CostEstimate(
-        flops=int(micros * 1e9), bytes_accessed=int(micros * 3.5e6), transcendentals=0
+        flops=int(micros * 1000000000.0), bytes_accessed=int(micros * 3500000.0), transcendentals=0
     )
 
 
@@ -404,6 +404,21 @@
     for copy in copies:
         copy.start()
     return copies
+
+
+def tie_kernel(value, after, out):
+    pass
+
+
+def tie(value, after):
+    return pl.pallas_call(
+        tie_kernel,
+        in_specs=[HBM, HBM],
+        out_specs=HBM,
+        out_shape=shape(value.shape, value.dtype),
+        input_output_aliases={0: 0},
+        name="tie",
+    )(value, after)
 
 
 def one_hot_rows(me, rows, lanes, piece, fs):
@@ -833,7 +848,7 @@
 
 def feed_kernel(
     me_ref, u2, h, ct, norms, w_out, gate, up, down,
-    mixed, big_g, gb_out, g0, g1, g2, g3, sums, acc_out, acc_grad, gz_t, *, piece,
+    mixed, big_g, g0, g1, g2, g3, t0, t1, t2, t3, sums, acc_out, acc_grad, gz_t, gb_t, *, piece, thin,
 ):
     i = pl.program_id(0)
 
@@ -866,15 +881,21 @@
         total = ct[...].astype(F32) + norm_back(unit, scale, gu2 * norms[2:3, :])
         big_g[...] = total
         low = total.astype(BF16)
-        gb_out[...] = low
         gz_t[...] = mm_nt(w_out[...], low).astype(BF16)
         for k, out in enumerate((g0, g1, g2, g3)):
             for r in range(width // piece):
                 at = pl.ds(pl.multiple_of((r * 4 + (me ^ k)) * piece, piece), piece)
                 out[r * piece : (r + 1) * piece, :] = gz_t[at, :]
-
-
-def feed_forward(me, u2, h, ct, norms, w_out, w_gate, w_up, w_down, piece):
+        gb_t[...] = jnp.transpose(total)
+        for k, out in enumerate((t0, t1, t2, t3)):
+            parts = []
+            for r in range(width // thin):
+                lo = pl.multiple_of((r * 4 + (me ^ k)) * thin, thin)
+                parts.append(gb_t[pl.ds(lo, thin), :])
+            out[...] = jnp.concatenate(parts, axis=0).astype(BF16)
+
+
+def feed_forward(me, u2, h, ct, norms, w_out, w_gate, w_up, w_down, piece, thin):
     quarter, channels = u2.shape
     ff = w_gate.shape[1]
     block = 512
@@ -886,10 +907,9 @@
     outs = [
         ((quarter, channels), BF16),
         ((quarter, channels), F32),
-        ((quarter, channels), BF16),
-    ] + [((width, quarter), BF16)] * 4 + [((8, channels), F32)]
+    ] + [((width, quarter), BF16)] * 8 + [((8, channels), F32)]
     return pl.pallas_call(
-        functools.partial(feed_kernel, piece=piece),
+        functools.partial(feed_kernel, piece=piece, thin=thin),
         grid=(ff // block,),
         in_specs=[
             SM,
@@ -908,6 +928,7 @@
             pltpu.VMEM((quarter, channels), F32),
             pltpu.VMEM((quarter, channels), F32),
             pltpu.VMEM((channels, quarter), BF16),
+            pltpu.VMEM((channels, quarter), F32),
         ],
         compiler_params=params(),
         cost_estimate=cost(13),
@@ -916,8 +937,8 @@
 
 
 def hidden_grads_kernel(
-    at_ref, u0, u1, u2, u3, c0, c1, c2, c3, gate, up, down, gb, z_in,
-    keep_a, give_a, keep_b, give_b, t0, t1, t2, t3, z_out, u_row, c_row, d_all, gb_t, *, piece,
+    at_ref, u0, u1, u2, u3, c0, c1, c2, c3, gate, up, down, after,
+    keep_a, give_a, keep_b, give_b, u_row, c_row, d_all,
 ):
     quarter, channels = u0.shape
     i = pl.program_id(0)
@@ -928,17 +949,6 @@
         for k, (u, c) in enumerate(((u0, c0), (u1, c1), (u2, c2), (u3, c3))):
             u_row[k * quarter : (k + 1) * quarter, :] = u[...]
             c_row[k * quarter : (k + 1) * quarter, :] = c[...]
-
-    @pl.when(i == pl.num_programs(0) - 1)
-    def _():
-        z_out[...] = z_in[...]
-        gb_t[...] = jnp.transpose(gb[...].astype(F32))
-        for k, out in enumerate((t0, t1, t2, t3)):
-            parts = []
-            for r in range(out.shape[0] // piece):
-                lo = pl.multiple_of((r * 4 + (at_ref[0] ^ k)) * piece, piece)
-                parts.append(gb_t[pl.ds(lo, piece), :])
-            out[...] = jnp.concatenate(parts, axis=0).astype(BF16)
 
     rows = gate.shape[0]
     g = mm_nt(gate[...], u_row[...])
@@ -966,47 +976,43 @@
         give_b[0] = d_all[:, :, :, cut:]
 
 
-def hidden_grads(at, u2_parts, ct_parts, gate, up, down, gb, z_t):
+def hidden_grads(at, u2_parts, ct_parts, gate, up, down, after):
     quarter, channels = u2_parts[0].shape
     wide = gate.shape[0]
     bs, fs, fw, _ = down.shape
     block = 2 * fw
     cut = channels // 2
     whole = pl.BlockSpec((quarter, channels), lambda i, at: (0, 0))
-    tall = pl.BlockSpec((channels, quarter), lambda i, at: (0, 0))
-    part = pl.BlockSpec((channels // fs, quarter), lambda i, at: (0, 0))
     rows = pl.BlockSpec((block, channels), lambda i, at: (i, 0))
     down_spec = pl.BlockSpec((2, 1, fw, channels), lambda i, at: (i, at[0], 0, 0))
     a_spec = pl.BlockSpec((1, 3, fw, cut), lambda i, at: (i, 0, 0, 0))
     b_spec = pl.BlockSpec((1, 2, 3, fw, cut), lambda i, at: (i // 2, 0, 0, 0, 0))
     return pl.pallas_call(
-        functools.partial(hidden_grads_kernel, piece=channels // (bs * fs)),
+        hidden_grads_kernel,
         grid_spec=pltpu.PrefetchScalarGridSpec(
             num_scalar_prefetch=1,
             grid=(bs // 2,),
-            in_specs=[whole] * 8 + [rows, rows, down_spec, whole, tall],
-            out_specs=[a_spec, a_spec, b_spec, b_spec] + [part] * 4 + [tall],
+            in_specs=[whole] * 8 + [rows, rows, down_spec, HBM],
+            out_specs=[a_spec, a_spec, b_spec, b_spec],
             scratch_shapes=[
                 pltpu.VMEM((4 * quarter, channels), BF16),
                 pltpu.VMEM((4 * quarter, channels), BF16),
                 pltpu.VMEM((2, 3, fw, channels), BF16),
-                pltpu.VMEM((channels, quarter), F32),
             ],
         ),
         out_shape=[shape((bs // 2, 3, fw, cut), BF16)] * 2
-        + [shape((bs // 4, 2, 3, fw, cut), BF16)] * 2
-        + [shape((channels // fs, quarter), BF16)] * 4
-        + [shape((channels, quarter), BF16)],
+        + [shape((bs // 4, 2, 3, fw, cut), BF16)] * 2,
         compiler_params=params(),
         cost_estimate=cost(14),
         name="hidden_grads",
-    )(at, *u2_parts, *ct_parts, gate, up, down, gb, z_t)
-
-
-def halve_kernel(bit_ref, after, *refs, pairs):
+    )(at, *u2_parts, *ct_parts, gate, up, down, after)
+
+
+def halve_kernel(at_ref, after, *refs, bits):
+    pairs = len(bits)
     ins, outs = refs[: 2 * pairs], refs[2 * pairs :]
     for n in range(pairs):
-        mine = bit_ref[n]
+        mine = at_ref[bits[n] + 1]
         keep, got = ins[2 * n], ins[2 * n + 1]
         next_keep, next_give = outs[2 * n], outs[2 * n + 1]
         for i in range(keep.shape[0]):
@@ -1014,33 +1020,32 @@
                 out[i] = (keep[i, side].astype(F32) + got[i, side].astype(F32)).astype(BF16)
 
 
-def halve(bits, after, *sums):
-    pairs = len(sums) // 2
+def halve(at, bits, after, *sums):
     outs = []
-    for n in range(pairs):
+    for n in range(len(bits)):
         dims = sums[2 * n].shape
         outs += [shape((dims[0],) + dims[2:], BF16)] * 2
     return pl.pallas_call(
-        functools.partial(halve_kernel, pairs=pairs),
+        functools.partial(halve_kernel, bits=bits),
         in_specs=[SM, HBM] + [VM] * len(sums),
         out_specs=[VM] * len(outs),
         out_shape=outs,
         compiler_params=params(),
         cost_estimate=cost(2),
         name="halve",
-    )(bits, after, *sums)
-
-
-def join_kernel(bit_ref, after, keep_a, got_a, keep_b, got_b, keep, give):
+    )(at, after, *sums)
+
+
+def join_kernel(at_ref, after, keep_a, got_a, keep_b, got_b, keep, give):
     cut = keep_a.shape[-1]
-    for side, out in ((bit_ref[0], keep), (1 - bit_ref[0], give)):
+    for side, out in ((at_ref[3], keep), (1 - at_ref[3], give)):
         for m in range(keep_a.shape[1]):
             for ours, theirs, lanes in ((keep_a, got_a, slice(0, cut)), (keep_b, got_b, slice(cut, 2 * cut))):
                 total = ours[side, m].astype(F32) + theirs[side, m].astype(F32)
                 out[m, :, lanes] = total.astype(BF16)
 
 
-def join(bit, after, keep_a, got_a, keep_b, got_b):
+def join(at, after, keep_a, got_a, keep_b, got_b):
     _, count, rows, cut = keep_a.shape
     return pl.pallas_call(
         join_kernel,
@@ -1050,12 +1055,12 @@
         compiler_params=params(),
         cost_estimate=cost(2),
         name="join",
-    )(bit, after, keep_a, got_a, keep_b, got_b)
+    )(at, after, keep_a, got_a, keep_b, got_b)
 
 
 def projection_kernel(
     at_ref, gp, u1, n1, w_mine, b0, b1, b2, b3, z0, z1, z2, z3, d_w2, d_w1, d_taps, gcb, condt, mu, mn,
-    sums2, after, keep, give, packed, gb_row, z_row, d_in, d_out, *, layout,
+    sums2, after, keep, give, packed_out, gb_row, z_row, d_in, d_out, packed, *, layout,
 ):
     me, y = at_ref[0], at_ref[1]
     quarter = b0.shape[1]
@@ -1110,6 +1115,7 @@
     rest = jnp.concatenate([share[:SEGS, 128:], jnp.zeros((SEGS, 256 - width), F32)], axis=1)
     block = jnp.concatenate([share[:SEGS, :128], rest, jnp.zeros((8 - 2 * SEGS, 128), F32)], axis=0)
     packed[pl.ds(pl.multiple_of(layout["mu"] + 8 * row, 8), 8), :] = block
+    packed_out[...] = packed[...].astype(BF16)
 
 
 def packed_layout(width, channels, bs):
@@ -1118,7 +1124,7 @@
     w1 = -(-(ln + 4 * (channels // 128)) // 8) * 8
     cb = w1 + 32
     mu = cb + 4 * bs
-    return {"taps": taps, "ln": ln, "w1": w1, "cb": cb, "mu": mu, "rows": mu + 8 * bs}
+    return {"taps": taps, "ln": ln, "w1": w1, "cb": cb, "mu": mu, "rows": -(-(mu + 8 * bs) // 16) * 16}
 
 
 def projection_grads(
@@ -1132,15 +1138,16 @@
         in_specs=[SM] + [VM] * 20 + [HBM],
         out_specs=[VM] * 3,
         out_shape=[shape((bs // 2, 3 * width // bs, channels), BF16)] * 2
-        + [shape((layout["rows"], 128), F32)],
+        + [shape((layout["rows"], 128), BF16)],
         scratch_shapes=[
             pltpu.VMEM((width, length), BF16),
             pltpu.VMEM((channels, length), BF16),
             pltpu.VMEM((2 * width, channels), F32),
             pltpu.VMEM((width, channels), F32),
+            pltpu.VMEM((layout["rows"], 128), F32),
         ],
         compiler_params=params(),
-        cost_estimate=cost(4),
+        cost_estimate=cost(6),
         name="projection_grads",
     )(
         at, gp, u1, n1, w_mine, *gb_parts, *z_parts, d_w2, d_w1, d_taps, gcb, condt, mu, mn, sums2, after
@@ -1185,7 +1192,7 @@
         out_shape=shape((quarter, channels), F32),
         scratch_shapes=[pltpu.VMEM((2 * channels, quarter), BF16)],
         compiler_params=params(),
-        cost_estimate=cost(2),
+        cost_estimate=cost(5),
         name="final",
     )(me, *gp_parts, x, big_g, norms, ids, condt, w_in, after)
 
@@ -1194,7 +1201,7 @@
     me_ref, j0, j1, j2, j3, w2, taps, ln, w1, b1, cond, wide, tap_t, cond_t, *, layout, step, width
 ):
     me = me_ref[0]
-    parts = (j0, j1, j2, j3)
+    parts = [part[...].astype(F32) for part in (j0, j1, j2, j3)]
     hidden = w1.shape[0]
     half = width // step
     count = 2 * width // 128
@@ -1222,7 +1229,8 @@
     taps[...] = whole[hidden : hidden + 3, :]
 
     def common(first, last):
-        return (j0[first:last, :] + j1[first:last, :]) + (j2[first:last, :] + j3[first:last, :])
+        a, b, c, d = [part[first:last, :] for part in parts]
+        return (a + b) + (c + d)
 
     lanes = ln.shape[1] // 128
     sums = common(layout["ln"], layout["ln"] + 4 * lanes)
@@ -1333,48 +1341,54 @@
     x_own = tokens[:, 0]
     ct_own = cotangent[:, 0]
     ids = seg_ids
-    me1 = me.reshape(1)
-    x_parts = gather_freq(x_own, me)
-    ct_parts = gather_freq(ct_own, me)
     at = jnp.stack([me, row & 1, (row >> 1) & 1, (row >> 2) & 1, row]).astype(jnp.int32)
     norms = jnp.stack([ln1_gain, ln1_shift, ln2_gain, ln2_shift])
     condt = cond_w.T
     cos_c, sin_c = jnp.asarray(cos_table), jnp.asarray(sin_table)
 
+    def gather_after(value, after):
+        two = swap(value, "freq", 2)
+        one = swap(value, "freq", 1)
+        two = tie(two, after)
+        return (value, one, two, swap(two, "freq", 1))
+
+    def pairs(value):
+        return value.reshape((value.shape[0] // 2, 2) + value.shape[1:])
+
     w_mine, w2x, w2t, taps, base = prepare(
-        me1, w_in, freq_w2, conv_taps, freq_w1, freq_b1, jnp.asarray(feats_aug), step, fs
-    )
-    forward = forward_spectral(me1, x_parts, ids, norms, w_mine, taps, base, w2x, condt, cos_c, sin_c)
+        at, w_in, freq_w2, conv_taps, freq_w1, freq_b1, jnp.asarray(feats_aug), step, fs
+    )
+    x_parts = gather_after(x_own, base)
+    forward = forward_spectral(at, x_parts, ids, norms, w_mine, taps, base, w2x, condt, cos_c, sin_c)
     z_parts, (z_row, u1, n1, p, q, c, vr, vs, mu, mn, cb) = forward[:4], forward[4:]
+    ct_parts = gather_after(ct_own, cb)
     z_got = trade_parts(z_parts)
-    wg_mine, wu_mine = select_columns(me1, cb, w_gate, w_up, fw, fs)
-    h, u2, z_t = middle(me1, z_got, x_own, w_out, norms, wg_mine, step)
-    u2_parts = gather_freq(u2, me)
-    fed = feed_forward(me1, u2, h, ct_own, norms, w_out, w_gate, w_up, w_down, step)
-    mixed_out, big_g, gb, gz_parts, sums2 = fed[0], fed[1], fed[2], fed[3:7], fed[7]
+    wg_mine, wu_mine = select_columns(at, cb, w_gate, w_up, fw, fs)
+    h, u2, z_t = middle(at, z_got, x_own, w_out, norms, wg_mine, step)
+    fed = feed_forward(
+        at, u2, h, ct_own, norms, w_out, w_gate, w_up, w_down, step, channels // (bs * fs)
+    )
+    mixed_out, big_g, gz_parts, gb_parts, sums2 = fed[0], fed[1], fed[2:6], fed[6:10], fed[10]
+    u2_parts = gather_after(u2, sums2)
     gz_got = trade_parts(gz_parts)
 
-    hidden = hidden_grads(
-        at, u2_parts, ct_parts, wg_mine, wu_mine, w_down.reshape(bs, fs, fw, channels), gb, z_t
-    )
-    keep_a, give_a, keep_b, give_b = hidden[:4]
+    keep_a, give_a, keep_b, give_b = hidden_grads(
+        at, u2_parts, ct_parts, wg_mine, wu_mine, w_down.reshape(bs, fs, fw, channels), sums2
+    )
     got_a = swap(give_a, "batch", 1)
     got_b = swap(give_b, "batch", 2)
-    gb_got = trade_parts(hidden[4:8])
-    z_all = gather_freq(hidden[8], me)
+    gb_got = trade_parts(gb_parts)
 
     back = backward_spectral(
-        me1, gz_got, ids, cb, taps, base, w2x, w2t, jnp.asarray(feats).astype(BF16),
+        at, gz_got, ids, cb, taps, base, w2x, w2t, jnp.asarray(feats).astype(BF16),
         p, q, c, vr, vs, cos_c, sin_c, give_a,
     )
     gp_parts, (gp, d_taps, d_w2, d_w1, gcb) = back[:4], back[4:]
     gp_got = trade_parts(gp_parts)
-
-    def pairs(value):
-        return value.reshape((value.shape[0] // 2, 2) + value.shape[1:])
+    z_all = gather_after(z_t, gcb)
 
     keep_a, give_a, keep_b, give_b = halve(
-        jnp.stack([at[2], at[1]]), gp, pairs(keep_a), pairs(got_a), keep_b, got_b
+        at, (1, 0), gp, pairs(keep_a), pairs(got_a), keep_b, got_b
     )
     got_a = swap(give_a, "batch", 2)
     got_b = swap(give_b, "batch", 1)
@@ -1383,22 +1397,25 @@
         at, gp, u1, n1, w_mine, gb_got, z_all, d_w2, d_w1, d_taps, gcb, condt, mu, mn, sums2, give_a, bs
     )
     got = swap(give, "batch", 1)
-    grad_tokens = final(me1, gp_got, x_own, big_g, norms, ids, condt, w_in, packed, step)
-
-    keep_ff, give_ff = join(at[3:4], grad_tokens, keep_a, got_a, keep_b, got_b)
+    keep_ff, give_ff = join(at, packed, keep_a, got_a, keep_b, got_b)
     got_ff = swap(give_ff, "batch", 4)
-
-    keep, give = halve(at[2:3], give_ff, pairs(keep), pairs(got))
+    grad_tokens = final(at, gp_got, x_own, big_g, norms, ids, condt, w_in, give_ff, step)
+
+    keep, give = halve(at, (1,), grad_tokens, pairs(keep), pairs(got))
     got = swap(give, "batch", 2)
-    keep, give = halve(at[3:4], give_ff, pairs(keep), pairs(got))
+    keep, give = halve(at, (2,), grad_tokens, pairs(keep), pairs(got))
     got = swap(give, "batch", 4)
     mine = keep[0].astype(F32) + got[0].astype(F32)
     first = 2 * width // bs
 
+    sent = packed
     for bit in range(bs.bit_length() - 1):
-        packed = packed + swap(packed, "batch", 1 << bit)
+        got_small = swap(sent, "batch", 1 << bit).astype(F32)
+        if bit == 0:
+            sent = tie(sent, grad_tokens)
+        sent = (sent.astype(F32) + got_small).astype(BF16)
     d_w2, d_taps, ln, d_w1, d_b1, d_cond = small_grads(
-        me1, gather_freq(packed, me), freq_w1.shape[1], channels, step, bs
+        at, gather_freq(sent, me), freq_w1.shape[1], channels, step, bs
     )
     d_ff = keep_ff.astype(F32) + got_ff.astype(F32)
     return (

time: 221 us -> 181 us (0.82)
  waiting for transfers between devices: 65.8 us -> 34.2 us
  starting transfers between devices: 29 us -> 25.6 us
    ppermute x38, waiting for transfers between devices: 65.8 us -> 34.2 us  [swap(): return lax.ppermute(value, axis, [(i, i ^ mask) for i in range(count)])]
    ppermute x38, starting transfers between devices: 29 us -> 25.6 us  [swap(): return lax.ppermute(value, axis, [(i, i ^ mask) for i in range(count)])]
    another operation x4, local copies, waits for them, and re-layouts: 2.76 us -> 0.02 us  [tiled_device(): norms = jnp.stack([ln1_gain, ln1_shift, ln2_gain, ln2_shift])]
    pallas_call x5 -> x10, Pallas kernels: 38.2 us -> 37.1 us  [the longest x1 15.4 us: hidden_grads(): pl.pallas_call(hidden_grads_kernel, grid_spec=pltpu.PrefetchScalarGridSpe...]
    unnamed x95 -> x97, local copies, waits for them, and re-layouts: 10.1 us -> 10.8 us
  transfers between devices with their start and end apart: 38 -> 38, of which waited for: 9 -> 8; matrix products, arithmetic and copies ran while one was open for 4% -> 4% of each run, Pallas kernels for 38% -> 57%
where the time goes in v1:
time: 181 us; the launch traced here: 179 us
  Pallas kernels  101 us (56%)
  waiting for transfers between devices  34.2 us (19%)
  starting transfers between devices  25.6 us (14%)
  local copies, waits for them, and re-layouts  15.2 us (8%)
    ppermute x38, waiting for transfers between devices, swap(): return lax.ppermute(value, axis, [(i, i ^ mask) for i in range(count)])  34.2 us
    ppermute x38, starting transfers between devices, swap(): return lax.ppermute(value, axis, [(i, i ^ mask) for i in range(count)])  25.6 us
    pallas_call x1, Pallas kernels, backward_spectral(): pl.pallas_call(backward_kernel, in_specs=[SM, SM] + [VM] * 11 + [HBM] * 8...  18.8 us
    pallas_call x1, Pallas kernels, hidden_grads(): pl.pallas_call(hidden_grads_kernel, grid_spec=pltpu.PrefetchScalarGridSpe...  15.4 us
    pallas_call x1, Pallas kernels, forward_spectral(): pl.pallas_call(forward_kernel, in_specs=[SM, SM] + [VM] * 11 + [HBM, HBM]...  15.4 us
    pallas_call x1, Pallas kernels, feed_forward(): pl.pallas_call(functools.partial(feed_kernel, piece=piece, thin=thin), gr...  14.5 us
    unnamed x97, local copies, waits for them, and re-layouts  10.8 us
    pallas_call x3, Pallas kernels, halve(): pl.pallas_call(functools.partial(halve_kernel, bits=bits), in_specs=[SM,...  7.21 us
  transfers between devices with their start and end apart: 38, of which 8 were waited for; matrix products, arithmetic and copies ran while one was open for 4% of the time, Pallas kernels for 57%

profile of v1, /device:TPU:2, one launch (start us, length us, event | category | flops | bytes accessed | tf_op | source)
XLA Modules:
  0.0 179.1 jit_solution(6114287009861236038)
XLA Ops:
  1.4 4.2 %prepare.1 = (bf16[384,768]{1,0:T(8,128)(2,1)}, bf16[384,192]{1,0:T(8,128)(2,1)}, bf16[64,384]{1,0:T(8,128)(2,1)}, f32[384,8]{1,0:T(8,128)}, f32[64,1024]{1,0:T(8,128)}) custom-call(s32[5]{0:T(128)} %stack.38.me_ref.at_ref, bf16[768,1536]{1,0:T(8,128)(2,1)} %w_in.3, f32[64,1536]{1,0:T(8,128)} %freq_w2.1, f32[3,1536]{1,0:T(4,128)} %conv_taps.1, ...), custom_call_target="tpu_custom_call" | custom-call | flops 3000000000 | bytes 10500000 | tf_op jit(solution)/shard_map/prepare/pallas_call | solution.py:469
  5.6 6.1 %collective-permute-done.1.value = bf16[256,768]{1,0:T(8,128)(2,1)S(1)} collective-permute-done((bf16[256,768]{1,0:T(8,128)(2,1)}, bf16[256,768]{1,0:T(8,128)(2,1)S(1)}, u32[]{:S(2)}, u32[]{:S(2)}) %collective-permute-start.1) | collective-permute-done | bytes 393248 | tf_op jit(solution)/shard_map/ppermute | solution.py:33
  15.7 15.4 %forward_spectral.1 = (bf16[192,256]{1,0:T(8,128)(2,1)}, bf16[192,256]{1,0:T(8,128)(2,1)}, bf16[192,256]{1,0:T(8,128)(2,1)}, bf16[192,256]{1,0:T(8,128)(2,1)}, b...) custom-call(s32[5]{0:T(128)} %stack.38.me_ref.at_ref, ...), custom_call_target="tpu_custom_call" | custom-call | flops 15000000512 | bytes 52500000 | tf_op jit(solution)/shard_map/forward_spectral/pallas_call | solution.py:656
  34.3 6.9 %select_columns.1 = (bf16[768,768]{1,0:T(8,128)(2,1)}, bf16[768,768]{1,0:T(8,128)(2,1)}) custom-call(s32[5]{0:T(128)} %stack.38.me_ref.at_ref, f32[64,8]{1,0:T(8,128)} %get-tuple-element.91.after.cb, bf16[768,3072]{1,0:T(8,128)(2,1)} %gate.3, bf16[768,3072]{1,0:T(8,128)(2,1)} %up.3), custom_call_target="tpu_custom_call" | custom-call | flops 6000000000 | bytes 21000000 | tf_op jit(solution)/shard_map/select_columns/pallas_call | solution.py:502
  41.9 3.2 %middle.1 = (f32[256,768]{1,0:T(8,128)}, bf16[256,768]{1,0:T(8,128)(2,1)}, bf16[768,256]{1,0:T(8,128)(2,1)}) custom-call(s32[5]{0:T(128)} %stack.38.me_ref.at_ref, bf16[192,256]{1,0:T(8,128)(2,1)} %get-tuple-element.87.z0, bf16[192,256]{1,0:T(8,128)(2,1)} %copy-done.42, bf16[192,256]{1,0:T(8,128)(2,1)} %copy-done.43, bf16[192,256]{1,0:T(8,128)(2,1)} %copy-done.44, ...), custom_call_target="tpu_custom_call" | custom-call | flops 2000000000 | bytes 7000000 | tf_op jit(solution)/shard_map/middle/pallas_call | solution.py:834
  46.1 14.5 %feed_forward.1 = (bf16[256,768]{1,0:T(8,128)(2,1)}, f32[256,768]{1,0:T(8,128)}, bf16[192,256]{1,0:T(8,128)(2,1)}, bf16[192,256]{1,0:T(8,128)(2,1)}, bf16[192,25...) custom-call(s32[5]{0:T(128)} %stack.38.me_ref.at_ref, ...), custom_call_target="tpu_custom_call" | custom-call | flops 12999999488 | bytes 45500000 | tf_op jit(solution)/shard_map/feed_forward/pallas_call | solution.py:911
  64.9 15.4 %hidden_grads.1 = (bf16[4,3,96,384]{3,2,1,0:T(8,128)(2,1)}, bf16[4,3,96,384]{3,2,1,0:T(8,128)(2,1)}, bf16[2,2,3,96,384]{4,3,2,1,0:T(8,128)(2,1)}, bf16[2,2,3,96,384]{4,3,2,1,0:T(8,128)(2,1)}) custom-call(s32[5]{0:T(128)} %stack.38.me_ref.at_ref, bf16[256,768]{1,0:T(8,128)(2,1)} %get-tuple-element.93.u2.u0, bf16[256,768]{1,0:T(8,128)(2,1)} %copy-done.25, ...), custom_call_target="tpu_custom_call" | custom-call | flops 14000000000 | bytes 49000000 | tf_op jit(solution)/shard_map/hidden_grads/pallas_call | solution.py:990
  80.3 1.6 collective-permute-start.24
  81.9 1.6 collective-permute-start.25
  84.1 18.8 %backward_spectral.1 = (bf16[400,256]{1,0:T(8,128)(2,1)}, bf16[400,256]{1,0:T(8,128)(2,1)}, bf16[400,256]{1,0:T(8,128)(2,1)}, bf16[400,256]{1,0:T(8,128)(2,1)}, ...) custom-call(s32[5]{0:T(128)} %stack.38.me_ref.at_ref, ...), custom_call_target="tpu_custom_call" | custom-call | flops 16999999488 | bytes 59500000 | tf_op jit(solution)/shard_map/backward_spectral/pallas_call | solution.py:791
  106.2 3.4 %halve.3 = (bf16[2,3,96,384]{3,2,1,0:T(8,128)(2,1)}, bf16[2,3,96,384]{3,2,1,0:T(8,128)(2,1)}, bf16[2,3,96,384]{3,2,1,0:T(8,128)(2,1)}, bf16[2,3,96,384]{3,2,1,0:T(8,128)(2,1)}) custom-call(s32[5]{0:T(128)} %stack.38.me_ref.at_ref, bf16[384,1024]{1,0:T(8,128)(2,1)} %get-tuple-element.114.after.gp, bf16[2,2,3,96,384]{4,3,2,1,0:T(8,128)(2,1)} %bitcast.56, ...), custom_call_target="tpu_custom_call" | custom-call | flops 2000000000 | bytes 7000000 | tf_op jit(solution)/shard_map/halve/pallas_call | solution.py:1028
  113.0 5.7 %projection_grads.1 = (bf16[4,72,768]{2,1,0:T(8,128)(2,1)}, bf16[4,72,768]{2,1,0:T(8,128)(2,1)}, bf16[368,128]{1,0:T(8,128)(2,1)}) custom-call(s32[5]{0:T(128)} %stack.38.me_ref.at_ref, bf16[384,1024]{1,0:T(8,128)(2,1)} %get-tuple-element.114.after.gp, bf16[1024,768]{1,0:T(8,128)(2,1)} %get-tuple-element.115.u1, bf16[1024,768]{1,0:T(8,128)(2,1)} %get-tuple-element.116.n1, ...), custom_call_target="tpu_custom_call" | custom-call | flops 6000000000 | bytes 21000000 | tf_op jit(solution)/shard_map/projection_grads/pallas_call | solution.py:1136
  118.7 5.9 %collective-permute-done.26.got_a = bf16[2,3,96,384]{3,2,1,0:T(8,128)(2,1)S(1)} collective-permute-done((bf16[2,3,96,384]{3,2,1,0:T(8,128)(2,1)}, bf16[2,3,96,384]{3,2,1,0:T(8,128)(2,1)S(1)}, u32[]{:S(2)}, u32[]{:S(2)}) %collective-permute-start.26) | collective-permute-done | bytes 442400 | tf_op jit(solution)/shard_map/ppermute | solution.py:33
  126.7 2.5 %join.1 = (bf16[3,96,768]{2,1,0:T(8,128)(2,1)}, bf16[3,96,768]{2,1,0:T(8,128)(2,1)}) custom-call(s32[5]{0:T(128)} %stack.38.me_ref.at_ref, bf16[368,128]{1,0:T(8,128)(2,1)} %get-tuple-element.132.after.value, bf16[2,3,96,384]{3,2,1,0:T(8,128)(2,1)} %get-tuple-element.133.keep_a, bf16[2,3,96,384]{3,2,1,0:T(8,128)(2,1)} %copy-done.15, ...), custom_call_target="tpu_custom_call" | custom-call | flops 2000000000 | bytes 7000000 | tf_op jit(solution)/shard_map/join/pallas_call | solution.py:1050
  130.0 4.7 %final.1.after = f32[256,768]{1,0:T(8,128)} custom-call(s32[5]{0:T(128)} %stack.38.me_ref.at_ref, bf16[400,256]{1,0:T(8,128)(2,1)} %get-tuple-element.109.p0, bf16[400,256]{1,0:T(8,128)(2,1)} %copy-done.31, bf16[400,256]{1,0:T(8,128)(2,1)} %copy-done.32, bf16[400,256]{1,0:T(8,128)(2,1)} %copy-done.33, bf16[256,768]{1,0:T(8,128)(2,1)} %bitcast.50, ...), custom_call_target="tpu_custom_call" | custom-call | flops 5000000000 | bytes 17500000 | tf_op jit(solution)/shard_map/final/pallas_call | solution.py:1188
  136.2 2.6 %collective-permute-done.34 = bf16[4,72,768]{2,1,0:T(8,128)(2,1)S(1)} collective-permute-done((bf16[4,72,768]{2,1,0:T(8,128)(2,1)}, bf16[4,72,768]{2,1,0:T(8,128)(2,1)S(1)}, u32[]{:S(2)}, u32[]{:S(2)}) %collective-permute-start.34) | collective-permute-done | bytes 442400 | tf_op jit(solution)/shard_map/ppermute | solution.py:33
  139.5 2.0 %halve.4 = (bf16[2,72,768]{2,1,0:T(8,128)(2,1)}, bf16[2,72,768]{2,1,0:T(8,128)(2,1)}) custom-call(s32[5]{0:T(128)} %stack.38.me_ref.at_ref, f32[256,768]{1,0:T(8,128)} %final.1.after, bf16[2,2,72,768]{3,2,1,0:T(8,128)(2,1)} %bitcast.57, bf16[2,2,72,768]{3,2,1,0:T(8,128)(2,1)} %bitcast.41), custom_call_target="tpu_custom_call" | custom-call | flops 2000000000 | bytes 7000000 | tf_op jit(solution)/shard_map/halve/pallas_call | solution.py:1028
  142.0 2.6 %collective-permute-start.30 = (bf16[368,128]{1,0:T(8,128)(2,1)S(1)}, bf16[368,128]{1,0:T(8,128)(2,1)S(1)}, u32[]{:S(2)}, u32[]{:S(2)}) collective-permute-start(bf16[368,128]{1,0:T(8,128)(2,1)S(1)} %add_convert_fusion.1), channel_id=1, source_target_pairs={{0,16},{4,20},{8,24},{12,28},{16,0},{20,4},{24,8},{28,12},{1,17},{... | collective-permute-start | bytes 282632 | tf_op jit(solution)/shard_map/ppermute | solution.py:33
  144.6 5.4 %collective-permute-done.35 = bf16[2,72,768]{2,1,0:T(8,128)(2,1)S(1)} collective-permute-done((bf16[2,72,768]{2,1,0:T(8,128)(2,1)}, bf16[2,72,768]{2,1,0:T(8,128)(2,1)S(1)}, u32[]{:S(2)}, u32[]{:S(2)}) %collective-permute-start.35) | collective-permute-done | bytes 221216 | tf_op jit(solution)/shard_map/ppermute | solution.py:33
  150.7 1.9 %halve.5 = (bf16[1,72,768]{2,1,0:T(8,128)(2,1)}, bf16[1,72,768]{2,1,0:T(8,128)(2,1)}) custom-call(s32[5]{0:T(128)} %stack.38.me_ref.at_ref, f32[256,768]{1,0:T(8,128)} %final.1.after, bf16[1,2,72,768]{3,2,1,0:T(8,128)(2,1)} %bitcast.59, bf16[1,2,72,768]{3,2,1,0:T(8,128)(2,1)} %bitcast.51), custom_call_target="tpu_custom_call" | custom-call | flops 2000000000 | bytes 7000000 | tf_op jit(solution)/shard_map/halve/pallas_call | solution.py:1028
  156.3 1.7 copy.42
  158.9 9.9 %collective-permute-done.36 = bf16[1,72,768]{2,1,0:T(8,128)(2,1)S(1)} collective-permute-done((bf16[1,72,768]{2,1,0:T(8,128)(2,1)}, bf16[1,72,768]{2,1,0:T(8,128)(2,1)S(1)}, u32[]{:S(2)}, u32[]{:S(2)}) %collective-permute-start.36) | collective-permute-done | bytes 110624 | tf_op jit(solution)/shard_map/ppermute | solution.py:33
  171.3 2.8 %small_grads.1 = (f32[64,1536]{1,0:T(8,128)}, f32[3,1536]{1,0:T(4,128)}, f32[4,768]{1,0:T(4,128)}, f32[64,64]{1,0:T(8,128)}, f32[1,64]{1,0:T(1,128)}, /*index=5*/f32[64,768]{1,0:T(8,128)}) custom-call(s32[5]{0:T(128)} %stack.38.me_ref.at_ref, bf16[368,128]{1,0:T(8,128)(2,1)} %copy-done.7, bf16[368,128]{1,0:T(8,128)(2,1)} %copy-done.46, ...), custom_call_target="tpu_custom_call" | custom-call | flops 3000000000 | bytes 10500000 | tf_op jit(solution)/shard_map/small_grads/pallas_call | solution.py:1277
  175.6 2.5 %collective-permute-done.37 = bf16[3,96,768]{2,1,0:T(8,128)(2,1)S(1)} collective-permute-done((bf16[3,96,768]{2,1,0:T(8,128)(2,1)S(1)}, bf16[3,96,768]{2,1,0:T(8,128)(2,1)S(1)}, u32[]{:S(2)}, u32[]{:S(2)}) %collective-permute-start.37) | collective-permute-done | bytes 442400 | tf_op jit(solution)/shard_map/ppermute | solution.py:33
  (183 shorter events, 36.9 us)
Async XLA Ops:
  0.7 13.3 %collective-permute-start = (bf16[256,768]{1,0:T(8,128)(2,1)}, bf16[256,768]{1,0:T(8,128)(2,1)S(1)}, u32[]{:S(2)}, u32[]{:S(2)}) collective-permute-start(bf16[256,768]{1,0:T(8,128)(2,1)} %bitcast.47), channel_id=1, source_target_pairs={{0,1},{1,0},{2,3},{3,2},{4,5},{5,4},{6,7},{7,6},{8,9},{9,8},{10,11... | collective-permute-start | bytes 1179656 | tf_op jit(solution)/shard_map/ppermute | solution.py:33
  12.5 49.3 %collective-permute-start.12 = (bf16[256,768]{1,0:T(8,128)(2,1)S(1)}, bf16[256,768]{1,0:T(8,128)(2,1)S(1)}, u32[]{:S(2)}, u32[]{:S(2)}) collective-permute-start(bf16[256,768]{1,0:T(8,128)(2,1)S(1)} %bitcast.44), channel_id=1, source_target_pairs={{0,1},{1,0},{2,3},{3,2},{4,5},{5,4},{6,7},{7,6},{8,9},{9,8},{10,11... | collective-permute-start | bytes 1179656 | tf_op jit(solution)/shard_map/ppermute | solution.py:33
  13.0 20.0 %collective-permute-start.13 = (bf16[256,768]{1,0:T(8,128)(2,1)S(1)}, bf16[256,768]{1,0:T(8,128)(2,1)S(1)}, u32[]{:S(2)}, u32[]{:S(2)}) collective-permute-start(bf16[256,768]{1,0:T(8,128)(2,1)S(1)} %bitcast.45), channel_id=1, source_target_pairs={{0,2},{1,3},{2,0},{3,1},{4,6},{5,7},{6,4},{7,5},{8,10},{9,11},{10,... | collective-permute-start | bytes 1179656 | tf_op jit(solution)/shard_map/ppermute | solution.py:33
  33.8 29.1 %collective-permute-start.14 = (bf16[256,768]{1,0:T(8,128)(2,1)}, bf16[256,768]{1,0:T(8,128)(2,1)S(1)}, u32[]{:S(2)}, u32[]{:S(2)}) collective-permute-start(bf16[256,768]{1,0:T(8,128)(2,1)} %tie.7.c2), channel_id=1, source_target_pairs={{0,1},{1,0},{2,3},{3,2},{4,5},{5,4},{6,7},{7,6},{8,9},{9,8},{10,11... | collective-permute-start | bytes 1179656 | tf_op jit(solution)/shard_map/ppermute | solution.py:33
  45.1 17.9 %collective-permute-start.9 = (bf16[256,768]{1,0:T(8,128)(2,1)}, bf16[256,768]{1,0:T(8,128)(2,1)S(1)}, u32[]{:S(2)}, u32[]{:S(2)}) collective-permute-start(bf16[256,768]{1,0:T(8,128)(2,1)} %get-tuple-element.93.u2.u0), channel_id=1, source_target_pairs={{0,1},{1,0},{2,3},{3,2},{4,5},{5,4},{6,7},{7,6},{8,9},{9,8},{10,11... | collective-permute-start | bytes 1179656 | tf_op jit(solution)/shard_map/ppermute | solution.py:33
  45.2 15.4 %collective-permute-start.10 = (bf16[256,768]{1,0:T(8,128)(2,1)}, bf16[256,768]{1,0:T(8,128)(2,1)S(1)}, u32[]{:S(2)}, u32[]{:S(2)}) collective-permute-start(bf16[256,768]{1,0:T(8,128)(2,1)} %get-tuple-element.93.u2.u0), channel_id=1, source_target_pairs={{0,2},{1,3},{2,0},{3,1},{4,6},{5,7},{6,4},{7,5},{8,10},{9,11},{10,... | collective-permute-start | bytes 1179656 | tf_op jit(solution)/shard_map/ppermute | solution.py:33
  61.4 50.3 %collective-permute-start.21 = (bf16[768,256]{1,0:T(8,128)(2,1)S(1)}, bf16[768,256]{1,0:T(8,128)(2,1)S(1)}, u32[]{:S(2)}, u32[]{:S(2)}) collective-permute-start(bf16[768,256]{1,0:T(8,128)(2,1)S(1)} %copy-done.19), channel_id=1, source_target_pairs={{0,1},{1,0},{2,3},{3,2},{4,5},{5,4},{6,7},{7,6},{8,9},{9,8},{10,11... | collective-permute-start | bytes 1179656 | tf_op jit(solution)/shard_map/ppermute | solution.py:33
  61.8 41.1 %collective-permute-start.22 = (bf16[768,256]{1,0:T(8,128)(2,1)S(1)}, bf16[768,256]{1,0:T(8,128)(2,1)S(1)}, u32[]{:S(2)}, u32[]{:S(2)}) collective-permute-start(bf16[768,256]{1,0:T(8,128)(2,1)S(1)} %copy-done.19), channel_id=1, source_target_pairs={{0,2},{1,3},{2,0},{3,1},{4,6},{5,7},{6,4},{7,5},{8,10},{9,11},{10,... | collective-permute-start | bytes 1179656 | tf_op jit(solution)/shard_map/ppermute | solution.py:33
  63.0 17.3 %collective-permute-start.6 = (bf16[192,256]{1,0:T(8,128)(2,1)}, bf16[192,256]{1,0:T(8,128)(2,1)S(1)}, u32[]{:S(2)}, u32[]{:S(2)}) collective-permute-start(bf16[192,256]{1,0:T(8,128)(2,1)} %get-tuple-element.97), channel_id=1, source_target_pairs={{0,1},{1,0},{2,3},{3,2},{4,5},{5,4},{6,7},{7,6},{8,9},{9,8},{10,11... | collective-permute-start | bytes 294920 | tf_op jit(solution)/shard_map/ppermute | solution.py:33
  63.0 18.9 %collective-permute-start.7 = (bf16[192,256]{1,0:T(8,128)(2,1)}, bf16[192,256]{1,0:T(8,128)(2,1)S(1)}, u32[]{:S(2)}, u32[]{:S(2)}) collective-permute-start(bf16[192,256]{1,0:T(8,128)(2,1)} %get-tuple-element.98), channel_id=1, source_target_pairs={{0,2},{1,3},{2,0},{3,1},{4,6},{5,7},{6,4},{7,5},{8,10},{9,11},{10,... | collective-permute-start | bytes 294920 | tf_op jit(solution)/shard_map/ppermute | solution.py:33
  64.0 19.5 %collective-permute-start.8 = (bf16[192,256]{1,0:T(8,128)(2,1)}, bf16[192,256]{1,0:T(8,128)(2,1)S(1)}, u32[]{:S(2)}, u32[]{:S(2)}) collective-permute-start(bf16[192,256]{1,0:T(8,128)(2,1)} %get-tuple-element.99), channel_id=1, source_target_pairs={{0,3},{1,2},{2,1},{3,0},{4,7},{5,6},{6,5},{7,4},{8,11},{9,10},{10,... | collective-permute-start | bytes 294920 | tf_op jit(solution)/shard_map/ppermute | solution.py:33
  80.3 23.9 %collective-permute-start.24 = (bf16[4,3,96,384]{3,2,1,0:T(8,128)(2,1)}, bf16[4,3,96,384]{3,2,1,0:T(8,128)(2,1)S(1)}, u32[]{:S(2)}, u32[]{:S(2)}) collective-permute-start(bf16[4,3,96,384]{3,2,1,0:T(8,128)(2,1)} %get-tuple-element.108.after), channel_id=1, source_target_pairs={{0,4},{4,0},{8,12},{12,8},{16,20},{20,16},{24,28},{28,24},{1,5},{5... | collective-permute-start | bytes 2654216 | tf_op jit(solution)/shard_map/ppermute | solution.py:33
  81.9 23.4 %collective-permute-start.25 = (bf16[2,2,3,96,384]{4,3,2,1,0:T(8,128)(2,1)}, bf16[2,2,3,96,384]{4,3,2,1,0:T(8,128)(2,1)S(1)}, u32[]{:S(2)}, u32[]{:S(2)}) collective-permute-start(bf16[2,2,3,96,384]{4,3,2,1,0:T(8,128)(2,1)} %get-tuple-element.130), channel_id=1, source_target_pairs={{0,8},{4,12},{8,0},{12,4},{16,24},{20,28},{24,16},{28,20},{1,9},{5... | collective-permute-start | bytes 2654216 | tf_op jit(solution)/shard_map/ppermute | solution.py:33
  109.6 19.6 %collective-permute-start.15 = (bf16[400,256]{1,0:T(8,128)(2,1)}, bf16[400,256]{1,0:T(8,128)(2,1)S(1)}, u32[]{:S(2)}, u32[]{:S(2)}) collective-permute-start(bf16[400,256]{1,0:T(8,128)(2,1)} %get-tuple-element.110), channel_id=1, source_target_pairs={{0,1},{1,0},{2,3},{3,2},{4,5},{5,4},{6,7},{7,6},{8,9},{9,8},{10,11... | collective-permute-start | bytes 614408 | tf_op jit(solution)/shard_map/ppermute | solution.py:33
  110.0 19.2 %collective-permute-start.16 = (bf16[400,256]{1,0:T(8,128)(2,1)S(1)}, bf16[400,256]{1,0:T(8,128)(2,1)S(1)}, u32[]{:S(2)}, u32[]{:S(2)}) collective-permute-start(bf16[400,256]{1,0:T(8,128)(2,1)S(1)} %copy-done.30), channel_id=1, source_target_pairs={{0,2},{1,3},{2,0},{3,1},{4,6},{5,7},{6,4},{7,5},{8,10},{9,11},{10,... | collective-permute-start | bytes 614408 | tf_op jit(solution)/shard_map/ppermute | solution.py:33
  111.0 18.2 %collective-permute-start.17 = (bf16[400,256]{1,0:T(8,128)(2,1)S(1)}, bf16[400,256]{1,0:T(8,128)(2,1)S(1)}, u32[]{:S(2)}, u32[]{:S(2)}) collective-permute-start(bf16[400,256]{1,0:T(8,128)(2,1)S(1)} %copy-done.29), channel_id=1, source_target_pairs={{0,3},{1,2},{2,1},{3,0},{4,7},{5,6},{6,5},{7,4},{8,11},{9,10},{10,... | collective-permute-start | bytes 614408 | tf_op jit(solution)/shard_map/ppermute | solution.py:33
  111.7 12.9 %collective-permute-start.26 = (bf16[2,3,96,384]{3,2,1,0:T(8,128)(2,1)}, bf16[2,3,96,384]{3,2,1,0:T(8,128)(2,1)S(1)}, u32[]{:S(2)}, u32[]{:S(2)}) collective-permute-start(bf16[2,3,96,384]{3,2,1,0:T(8,128)(2,1)} %get-tuple-element.131.after), channel_id=1, source_target_pairs={{0,8},{4,12},{8,0},{12,4},{16,24},{20,28},{24,16},{28,20},{1,9},{5... | collective-permute-start | bytes 1327112 | tf_op jit(solution)/shard_map/ppermute | solution.py:33
  112.2 12.9 %collective-permute-start.27 = (bf16[2,3,96,384]{3,2,1,0:T(8,128)(2,1)}, bf16[2,3,96,384]{3,2,1,0:T(8,128)(2,1)S(1)}, u32[]{:S(2)}, u32[]{:S(2)}) collective-permute-start(bf16[2,3,96,384]{3,2,1,0:T(8,128)(2,1)} %get-tuple-element.135), channel_id=1, source_target_pairs={{0,4},{4,0},{8,12},{12,8},{16,20},{20,16},{24,28},{28,24},{1,5},{5... | collective-permute-start | bytes 1327112 | tf_op jit(solution)/shard_map/ppermute | solution.py:33
  125.1 13.6 %collective-permute-start.34 = (bf16[4,72,768]{2,1,0:T(8,128)(2,1)}, bf16[4,72,768]{2,1,0:T(8,128)(2,1)S(1)}, u32[]{:S(2)}, u32[]{:S(2)}) collective-permute-start(bf16[4,72,768]{2,1,0:T(8,128)(2,1)} %get-tuple-element.139), channel_id=1, source_target_pairs={{0,4},{4,0},{8,12},{12,8},{16,20},{20,16},{24,28},{28,24},{1,5},{5... | collective-permute-start | bytes 1327112 | tf_op jit(solution)/shard_map/ppermute | solution.py:33
  142.0 12.2 %collective-permute-start.30 = (bf16[368,128]{1,0:T(8,128)(2,1)S(1)}, bf16[368,128]{1,0:T(8,128)(2,1)S(1)}, u32[]{:S(2)}, u32[]{:S(2)}) collective-permute-start(bf16[368,128]{1,0:T(8,128)(2,1)S(1)} %add_convert_fusion.1), channel_id=1, source_target_pairs={{0,16},{4,20},{8,24},{12,28},{16,0},{20,4},{24,8},{28,12},{1,17},{... | collective-permute-start | bytes 282632 | tf_op jit(solution)/shard_map/ppermute | solution.py:33
  152.6 16.1 %collective-permute-start.36 = (bf16[1,72,768]{2,1,0:T(8,128)(2,1)}, bf16[1,72,768]{2,1,0:T(8,128)(2,1)S(1)}, u32[]{:S(2)}, u32[]{:S(2)}) collective-permute-start(bf16[1,72,768]{2,1,0:T(8,128)(2,1)} %get-tuple-element.143), channel_id=1, source_target_pairs={{0,16},{4,20},{8,24},{12,28},{16,0},{20,4},{24,8},{28,12},{1,17},{... | collective-permute-start | bytes 331784 | tf_op jit(solution)/shard_map/ppermute | solution.py:33
  154.9 23.2 %collective-permute-start.37 = (bf16[3,96,768]{2,1,0:T(8,128)(2,1)S(1)}, bf16[3,96,768]{2,1,0:T(8,128)(2,1)S(1)}, u32[]{:S(2)}, u32[]{:S(2)}) collective-permute-start(bf16[3,96,768]{2,1,0:T(8,128)(2,1)S(1)} %copy-done.14), channel_id=1, source_target_pairs={{0,16},{4,20},{8,24},{12,28},{16,0},{20,4},{24,8},{28,12},{1,17},{... | collective-permute-start | bytes 1327112 | tf_op jit(solution)/shard_map/ppermute | solution.py:33
  158.0 12.1 %collective-permute-start.31 = (bf16[368,128]{1,0:T(8,128)(2,1)S(1)}, bf16[368,128]{1,0:T(8,128)(2,1)S(1)}, u32[]{:S(2)}, u32[]{:S(2)}) collective-permute-start(bf16[368,128]{1,0:T(8,128)(2,1)S(1)} %add_convert_fusion.j0), channel_id=1, source_target_pairs={{0,1},{1,0},{2,3},{3,2},{4,5},{5,4},{6,7},{7,6},{8,9},{9,8},{10,11... | collective-permute-start | bytes 282632 | tf_op jit(solution)/shard_map/ppermute | solution.py:33
  158.9 11.2 %collective-permute-start.33 = (bf16[368,128]{1,0:T(8,128)(2,1)S(1)}, bf16[368,128]{1,0:T(8,128)(2,1)S(1)}, u32[]{:S(2)}, u32[]{:S(2)}) collective-permute-start(bf16[368,128]{1,0:T(8,128)(2,1)S(1)} %collective-permute-done.32.j2), channel_id=1, source_target_pairs={{0,1},{1,0},{2,3},{3,2},{4,5},{5,4},{6,7},{7,6},{8,9},{9,8},{10,11... | collective-permute-start | bytes 282632 | tf_op jit(solution)/shard_map/ppermute | solution.py:33
  (62 other events, 324.0 us)

commit v2 on v1

--- a/solution.py
+++ b/solution.py
@@ -378,8 +378,8 @@
 MIB = 1 << 20
 
 
-def params():
-    return pltpu.CompilerParams(vmem_limit_bytes=60 * MIB)
+def params(mib):
+    return pltpu.CompilerParams(vmem_limit_bytes=mib * MIB)
 
 
 def cost(micros):
@@ -389,7 +389,20 @@
 
 
 def shape(dims, dtype):
-    return jax.ShapeDtypeStruct(dims, dtype)
+    return pltpu.VMEM(dims, dtype)
+
+
+def far(dims, dtype):
+    return pltpu.HBM(dims, dtype)
+
+
+def in_hbm(*values):
+    kept = tuple(pltpu.with_memory_space_constraint(value, pltpu.HBM) for value in values)
+    return kept if len(kept) > 1 else kept[0]
+
+
+def in_vmem(value):
+    return pltpu.with_memory_space_constraint(value, pltpu.VMEM)
 
 
 def sigmoid(value):
@@ -415,8 +428,9 @@
         tie_kernel,
         in_specs=[HBM, HBM],
         out_specs=HBM,
-        out_shape=shape(value.shape, value.dtype),
+        out_shape=jax.ShapeDtypeStruct(value.shape, value.dtype),
         input_output_aliases={0: 0},
+        compiler_params=params(1),
         name="tie",
     )(value, after)
 
@@ -431,9 +445,10 @@
 
 
 def prepare_kernel(
-    me_ref, w_in, freq_w2, conv_taps, freq_w1, freq_b1, feats,
-    w_mine, w2x, w2t, taps, base, w1_aug, *, step, fs,
+    me_ref, w_in, freq_w2, conv_taps, freq_w1, freq_b1, feats, cos_far, sin_far, norms,
+    w_mine, w2x, w2t, taps, base, cos, sin, w1_aug, sems, *, step, fs,
 ):
+    loads = dma_all([(cos_far, cos), (sin_far, sin)], sems)
     lanes = w_in.shape[1] // 4
     rows = lanes // fs
     sel = one_hot_rows(me_ref[0], rows, lanes, step, fs)
@@ -460,28 +475,35 @@
     base[...] = lax.dot_general(
         w1_aug[...], feats[...], (((0,), (0,)), ((), ())), precision=HIGH, preferred_element_type=F32
     )
-
-
-def prepare(me, w_in, freq_w2, conv_taps, freq_w1, freq_b1, feats, step, fs):
+    for load in loads:
+        load.wait()
+
+
+def prepare(me, w_in, freq_w2, conv_taps, freq_w1, freq_b1, feats, cos, sin, norms, step, fs):
     channels, both = w_in.shape
     hidden = freq_w2.shape[0]
     length = feats.shape[1]
     return pl.pallas_call(
         functools.partial(prepare_kernel, step=step, fs=fs),
-        in_specs=[SM] + [VM] * 6,
-        out_specs=[VM] * 5,
+        in_specs=[SM] + [VM] * 6 + [HBM] * 3,
+        out_specs=[VM] * 7,
         out_shape=[
             shape((both // fs, channels), BF16),
             shape((both // fs, 3 * hidden), BF16),
             shape((hidden, both // fs), BF16),
             shape((both // fs, 8), F32),
             shape((hidden, length), F32),
+            shape((length, length), BF16),
+            shape((length, length), BF16),
         ],
-        scratch_shapes=[pltpu.VMEM((feats.shape[0], hidden), F32)],
-        compiler_params=params(),
+        scratch_shapes=[
+            pltpu.VMEM((feats.shape[0], hidden), F32),
+            pltpu.SemaphoreType.DMA((2,)),
+        ],
+        compiler_params=params(24),
         cost_estimate=cost(3),
         name="prepare",
-    )(me, w_in, freq_w2, conv_taps, freq_w1, freq_b1[None], feats)
+    )(me, in_hbm(w_in), freq_w2, conv_taps, freq_w1, freq_b1[None], in_hbm(feats), in_hbm(cos), in_hbm(sin), norms)
 
 
 def select_kernel(me_ref, after, gate, up, gate_out, up_out, *, piece, fs):
@@ -504,11 +526,11 @@
         grid=(4,),
         in_specs=[SM, HBM, wide, wide],
         out_specs=[rows, rows],
-        out_shape=[shape((ff // fs, channels), BF16)] * 2,
-        compiler_params=params(),
+        out_shape=[far((ff // fs, channels), BF16)] * 2,
+        compiler_params=params(24),
         cost_estimate=cost(6),
         name="select_columns",
-    )(me, after, w_gate, w_up)
+    )(me, after, in_hbm(w_gate), in_hbm(w_up))
 
 
 def row_masks(ids):
@@ -540,22 +562,20 @@
 
 
 def forward_kernel(
-    me_ref, ids_at, x0, x1, x2, x3, ids_ref, norms, w, taps, base, w2x, condt, cos_hbm, sin_hbm,
-    z0, z1, z2, z3, zrow_hbm, u1_hbm, n1_hbm, p_hbm, q_hbm, c_hbm, vr_hbm, vs_hbm, mu_out, mn_out, cb_out,
-    cos, sin, z_row, u1, n1, p_out, q_out, c_out, vr_out, vs_out, p, q, vm, ycat, acc, sems,
+    me_ref, ids_at, x0, x1, x2, x3, ids_ref, norms, w, taps, base, w2x, condt, cos, sin,
+    z0, z1, z2, z3, u1, n1, p_out, q_out, c_out, vr_out, vs_out, mu_out, mn_out, cb_out,
+    p, q, vm, ycat, acc,
 ):
     quarter = x0.shape[0]
-    width, length = z_row.shape
+    width, length = q_out.shape
     tiles = length // quarter
     me = me_ref[0]
-    loads = dma_all([(cos_hbm, cos), (sin_hbm, sin)], sems)
     for k, x in enumerate((x0, x1, x2, x3)):
         values = x[...].astype(F32)
         unit, _ = normed(values)
         rows = tile(me ^ k, quarter)
         n1[rows, :] = unit.astype(BF16)
         u1[rows, :] = (unit * norms[0:1, :] + norms[1:2, :]).astype(BF16)
-    stores = dma_all([(u1, u1_hbm), (n1, n1_hbm)], sems, 2)
     ids = ids_ref[...]
     number = lax.broadcasted_iota(jnp.int32, (8, length), 0)
     member = jnp.where(ids == number, 1.0, 0.0)
@@ -588,9 +608,6 @@
             for j in range(SEGS):
                 lo = j * width + (r - 2) * chunk
                 vm[lo : lo + chunk, :] = (mixed * member[j : j + 1, :]).astype(BF16)
-    stores += dma_all([(p_out, p_hbm), (q_out, q_hbm)], sems, 4)
-    for load in loads:
-        load.wait()
 
     @pl.loop(0, tiles)
     def _(f):
@@ -610,7 +627,6 @@
             ycat[at, lanes] = (kr * vr + ki * vs).astype(BF16)
             ycat[at, upper] = (kr * vs - ki * vr).astype(BF16)
 
-    stores += dma_all([(vr_out, vr_hbm), (vs_out, vs_hbm)], sems, 6)
     for k, z_out in enumerate((z0, z1, z2, z3)):
         t = me ^ k
         lanes = tile(t, quarter)
@@ -628,10 +644,6 @@
         c_out[:, lanes] = c.astype(BF16)
         z = (q[:, lanes] * c).astype(BF16)
         z_out[...] = z
-        z_row[:, lanes] = z
-    stores += dma_all([(c_out, c_hbm), (z_row, zrow_hbm)], sems, 8)
-    for store in stores:
-        store.wait()
 
 
 def forward_spectral(me, x_parts, ids, norms, w, taps, base, w2x, condt, cos, sin):
@@ -639,7 +651,6 @@
     length = ids.shape[1]
     width = w.shape[0] // 2
     saved = [
-        (width, length),
         (length, channels),
         (length, channels),
         (2 * width, length),
@@ -655,20 +666,17 @@
     ]
     return pl.pallas_call(
         forward_kernel,
-        in_specs=[SM, SM] + [VM] * 11 + [HBM, HBM],
-        out_specs=[VM] * 4 + [HBM] * len(saved) + [VM] * 3,
+        in_specs=[SM, SM] + [VM] * 13,
+        out_specs=[VM] * (7 + len(saved)),
         out_shape=[shape((width, quarter), BF16)] * 4 + [shape(dims, BF16) for dims in saved] + small,
-        scratch_shapes=[pltpu.VMEM((length, length), BF16)] * 2
-        + [pltpu.VMEM(dims, BF16) for dims in saved]
-        + [
+        scratch_shapes=[
             pltpu.VMEM((2 * width, length), F32),
             pltpu.VMEM((width, length), F32),
             pltpu.VMEM((SEGS * width, length), BF16),
             pltpu.VMEM((SEGS * width, 2 * length), BF16),
             pltpu.VMEM((width, quarter), F32),
-            pltpu.SemaphoreType.DMA((10,)),
         ],
-        compiler_params=params(),
+        compiler_params=params(26),
         cost_estimate=cost(15),
         name="forward_spectral",
     )(me, ids, *x_parts, ids, norms, w, taps, base, w2x, condt, cos, sin)
@@ -676,24 +684,15 @@
 
 def backward_kernel(
     me_ref, ids_at, g0, g1, g2, g3, ids_ref, cb, taps, base, w2x, w2, feats,
-    p_hbm, q_hbm, c_hbm, vr_hbm, vs_hbm, cos_hbm, sin_hbm, after,
-    o0, o1, o2, o3, gp_hbm, d_taps, d_w2, d_w1, gcb,
-    cos, sin, p, q, c, vr_in, vs_in, gp_row, gcm, gvcat, gs, acc, sems,
+    p, q, c, vr_in, vs_in, cos, sin, after,
+    o0, o1, o2, o3, gp_row, d_taps, d_w2, d_w1, gcb,
+    gcm, gvcat, gs, acc,
 ):
     width, quarter = g0.shape
     length = gp_row.shape[1]
     tiles = length // quarter
     hidden = base.shape[0]
     me = me_ref[0]
-    loads = dma_all(
-        [
-            (c_hbm, c), (q_hbm, q), (cos_hbm, cos), (sin_hbm, sin),
-            (vr_hbm, vr_in), (vs_hbm, vs_in), (p_hbm, p),
-        ],
-        sems,
-    )
-    loads[0].wait()
-    loads[1].wait()
     for k, g in enumerate((g0, g1, g2, g3)):
         lanes = tile(me ^ k, quarter)
         gz = g[...].astype(F32)
@@ -705,8 +704,6 @@
     d_w2[...] = jnp.zeros_like(d_w2)
     d_w1[...] = jnp.zeros_like(d_w1)
     gcb[...] = jnp.zeros_like(gcb)
-    for load in loads[2:]:
-        load.wait()
 
     @pl.loop(0, tiles)
     def _(f):
@@ -763,7 +760,6 @@
             + taps[at, 0:1] * pltpu.roll(grad * prev, length - 1, 1)
             + taps[at, 2:3] * pltpu.roll(grad * nxt, 1, 1)
         ).astype(BF16)
-    store = dma_all([(gp_row, gp_hbm)], sems, 7)[0]
     share = jnp.transpose(gcb[...])[:8, :]
     high = share.astype(BF16)
     rest = (share - high.astype(F32)).astype(BF16)
@@ -772,7 +768,6 @@
     for k, out in enumerate((o0, o1, o2, o3)):
         out[: 2 * width, :] = gp_row[:, tile(me ^ k, quarter)]
         out[2 * width :, :] = extra
-    store.wait()
 
 
 def backward_spectral(
@@ -790,25 +785,16 @@
     ]
     return pl.pallas_call(
         backward_kernel,
-        in_specs=[SM, SM] + [VM] * 11 + [HBM] * 8,
-        out_specs=[VM] * 4 + [HBM] + [VM] * 4,
+        in_specs=[SM, SM] + [VM] * 18 + [HBM],
+        out_specs=[VM] * 9,
         out_shape=outs,
         scratch_shapes=[
-            pltpu.VMEM((length, length), BF16),
-            pltpu.VMEM((length, length), BF16),
-            pltpu.VMEM((2 * width, length), BF16),
-            pltpu.VMEM((width, length), BF16),
-            pltpu.VMEM((width, length), BF16),
-            pltpu.VMEM((SEGS * width, length), BF16),
-            pltpu.VMEM((SEGS * width, length), BF16),
-            pltpu.VMEM((2 * width, length), BF16),
             pltpu.VMEM((SEGS * width, length), BF16),
             pltpu.VMEM((SEGS * width, 2 * length), BF16),
             pltpu.VMEM((2 * width, length), F32),
             pltpu.VMEM((width, quarter), F32),
-            pltpu.SemaphoreType.DMA((8,)),
         ],
-        compiler_params=params(),
+        compiler_params=params(26),
         cost_estimate=cost(17),
         name="backward_spectral",
     )(
@@ -840,10 +826,10 @@
             shape((quarter, channels), BF16),
             shape((channels, quarter), BF16),
         ],
-        compiler_params=params(),
+        compiler_params=params(24),
         cost_estimate=cost(2),
         name="middle",
-    )(me, *z_parts, x, w_out, norms, after)
+    )(me, *z_parts, x, in_hbm(w_out), norms, after)
 
 
 def feed_kernel(
@@ -900,9 +886,6 @@
     ff = w_gate.shape[1]
     block = 512
 
-    def whole(*dims):
-        return pl.BlockSpec(dims, lambda i: (0,) * len(dims))
-
     width = channels // 4
     outs = [
         ((quarter, channels), BF16),
@@ -913,27 +896,27 @@
         grid=(ff // block,),
         in_specs=[
             SM,
-            whole(quarter, channels),
-            whole(quarter, channels),
-            whole(quarter, channels),
-            whole(4, channels),
-            whole(channels, channels),
+            VM,
+            VM,
+            VM,
+            VM,
+            VM,
             pl.BlockSpec((channels, block), lambda i: (0, i)),
             pl.BlockSpec((channels, block), lambda i: (0, i)),
             pl.BlockSpec((block, channels), lambda i: (i, 0)),
         ],
-        out_specs=[whole(*dims) for dims, _ in outs],
-        out_shape=[shape(*out) for out in outs],
+        out_specs=[VM] * len(outs),
+        out_shape=[far(*outs[0])] + [shape(*out) for out in outs[1:]],
         scratch_shapes=[
             pltpu.VMEM((quarter, channels), F32),
             pltpu.VMEM((quarter, channels), F32),
             pltpu.VMEM((channels, quarter), BF16),
             pltpu.VMEM((channels, quarter), F32),
         ],
-        compiler_params=params(),
+        compiler_params=params(28),
         cost_estimate=cost(13),
         name="feed_forward",
-    )(me, u2, h, ct, norms, w_out, w_gate, w_up, w_down)
+    )(me, u2, h, ct, norms, in_hbm(w_out), in_hbm(w_gate), in_hbm(w_up), in_hbm(w_down))
 
 
 def hidden_grads_kernel(
@@ -982,7 +965,6 @@
     bs, fs, fw, _ = down.shape
     block = 2 * fw
     cut = channels // 2
-    whole = pl.BlockSpec((quarter, channels), lambda i, at: (0, 0))
     rows = pl.BlockSpec((block, channels), lambda i, at: (i, 0))
     down_spec = pl.BlockSpec((2, 1, fw, channels), lambda i, at: (i, at[0], 0, 0))
     a_spec = pl.BlockSpec((1, 3, fw, cut), lambda i, at: (i, 0, 0, 0))
@@ -992,7 +974,7 @@
         grid_spec=pltpu.PrefetchScalarGridSpec(
             num_scalar_prefetch=1,
             grid=(bs // 2,),
-            in_specs=[whole] * 8 + [rows, rows, down_spec, HBM],
+            in_specs=[VM] * 8 + [rows, rows, down_spec, HBM],
             out_specs=[a_spec, a_spec, b_spec, b_spec],
             scratch_shapes=[
                 pltpu.VMEM((4 * quarter, channels), BF16),
@@ -1002,10 +984,10 @@
         ),
         out_shape=[shape((bs // 2, 3, fw, cut), BF16)] * 2
         + [shape((bs // 4, 2, 3, fw, cut), BF16)] * 2,
-        compiler_params=params(),
+        compiler_params=params(30),
         cost_estimate=cost(14),
         name="hidden_grads",
-    )(at, *u2_parts, *ct_parts, gate, up, down, after)
+    )(at, *u2_parts, *ct_parts, in_hbm(gate), in_hbm(up), in_hbm(down), after)
 
 
 def halve_kernel(at_ref, after, *refs, bits):
@@ -1030,7 +1012,7 @@
         in_specs=[SM, HBM] + [VM] * len(sums),
         out_specs=[VM] * len(outs),
         out_shape=outs,
-        compiler_params=params(),
+        compiler_params=params(24),
         cost_estimate=cost(2),
         name="halve",
     )(at, after, *sums)
@@ -1052,10 +1034,26 @@
         in_specs=[SM, HBM] + [VM] * 4,
         out_specs=[VM] * 2,
         out_shape=[shape((count, rows, 2 * cut), BF16)] * 2,
-        compiler_params=params(),
+        compiler_params=params(24),
         cost_estimate=cost(2),
         name="join",
     )(at, after, keep_a, got_a, keep_b, got_b)
+
+
+def add_kernel(ours, theirs, after, out):
+    out[...] = (ours[...].astype(F32) + theirs[...].astype(F32)).astype(out.dtype)
+
+
+def add(ours, theirs, after, dtype):
+    return pl.pallas_call(
+        add_kernel,
+        in_specs=[VM, VM, HBM],
+        out_specs=VM,
+        out_shape=shape(ours.shape, dtype),
+        compiler_params=params(8),
+        cost_estimate=cost(1),
+        name="add",
+    )(ours, theirs, after)
 
 
 def projection_kernel(
@@ -1146,7 +1144,7 @@
             pltpu.VMEM((width, channels), F32),
             pltpu.VMEM((layout["rows"], 128), F32),
         ],
-        compiler_params=params(),
+        compiler_params=params(24),
         cost_estimate=cost(6),
         name="projection_grads",
     )(
@@ -1189,12 +1187,12 @@
         functools.partial(final_kernel, piece=piece),
         in_specs=[SM] + [VM] * 10 + [HBM],
         out_specs=VM,
-        out_shape=shape((quarter, channels), F32),
+        out_shape=far((quarter, channels), F32),
         scratch_shapes=[pltpu.VMEM((2 * channels, quarter), BF16)],
-        compiler_params=params(),
+        compiler_params=params(24),
         cost_estimate=cost(5),
         name="final",
-    )(me, *gp_parts, x, big_g, norms, ids, condt, w_in, after)
+    )(me, *gp_parts, x, big_g, norms, ids, condt, in_hbm(w_in), after)
 
 
 def small_kernel(
@@ -1279,19 +1277,19 @@
         in_specs=[SM] + [VM] * 4,
         out_specs=[VM] * 6,
         out_shape=[
-            shape((hidden, 2 * channels), F32),
-            shape((3, 2 * channels), F32),
-            shape((4, channels), F32),
-            shape((hidden, hidden), F32),
-            shape((1, hidden), F32),
-            shape((hidden, channels), F32),
+            far((hidden, 2 * channels), F32),
+            far((3, 2 * channels), F32),
+            far((4, channels), F32),
+            far((hidden, hidden), F32),
+            far((1, hidden), F32),
+            far((hidden, channels), F32),
         ],
         scratch_shapes=[
             pltpu.VMEM((2 * channels, 2 * hidden), F32),
             pltpu.VMEM((2 * width, 128), F32),
             pltpu.VMEM((channels, hidden), F32),
         ],
-        compiler_params=params(),
+        compiler_params=params(24),
         cost_estimate=cost(3),
         name="small_grads",
     )(me, *parts)
@@ -1355,12 +1353,12 @@
     def pairs(value):
         return value.reshape((value.shape[0] // 2, 2) + value.shape[1:])
 
-    w_mine, w2x, w2t, taps, base = prepare(
-        at, w_in, freq_w2, conv_taps, freq_w1, freq_b1, jnp.asarray(feats_aug), step, fs
+    w_mine, w2x, w2t, taps, base, cos_c, sin_c = prepare(
+        at, w_in, freq_w2, conv_taps, freq_w1, freq_b1, jnp.asarray(feats_aug), cos_c, sin_c, norms, step, fs
     )
     x_parts = gather_after(x_own, base)
     forward = forward_spectral(at, x_parts, ids, norms, w_mine, taps, base, w2x, condt, cos_c, sin_c)
-    z_parts, (z_row, u1, n1, p, q, c, vr, vs, mu, mn, cb) = forward[:4], forward[4:]
+    z_parts, (u1, n1, p, q, c, vr, vs, mu, mn, cb) = forward[:4], forward[4:]
     ct_parts = gather_after(ct_own, cb)
     z_got = trade_parts(z_parts)
     wg_mine, wu_mine = select_columns(at, cb, w_gate, w_up, fw, fs)
@@ -1410,10 +1408,7 @@
 
     sent = packed
     for bit in range(bs.bit_length() - 1):
-        got_small = swap(sent, "batch", 1 << bit).astype(F32)
-        if bit == 0:
-            sent = tie(sent, grad_tokens)
-        sent = (sent.astype(F32) + got_small).astype(BF16)
+        sent = add(sent, swap(sent, "batch", 1 << bit), grad_tokens, BF16)
     d_w2, d_taps, ln, d_w1, d_b1, d_cond = small_grads(
         at, gather_freq(sent, me), freq_w1.shape[1], channels, step, bs
     )

time: 181 us -> 166 us (0.917)
  Pallas kernels: 101 us -> 76 us
  waiting for transfers between devices: 34.2 us -> 46.9 us
    ppermute x38, waiting for transfers between devices: 34.2 us -> 46.9 us  [swap(): return lax.ppermute(value, axis, [(i, i ^ mask) for i in range(count)])]
    pallas_call x2 -> x5, Pallas kernels: 34.2 us -> 24.6 us  [the longest x1 13.5 us: backward_spectral(): pl.pallas_call(backward_kernel, in_specs=[SM, SM] + [VM] * 18 + [HBM], ou...]
    pallas_call x3, Pallas kernels: 7.21 us -> 2.26 us  [halve(): pl.pallas_call(functools.partial(halve_kernel, bits=bits), in_specs=[SM,...]
    unnamed x97 -> x25, local copies, waits for them, and re-layouts: 10.8 us -> 7.25 us
    pallas_call x1, Pallas kernels: 5.74 us -> 2.66 us  [projection_grads(): pl.pallas_call(functools.partial(projection_kernel, layout=layout), in_sp...]
    another operation x4, local copies, waits for them, and re-layouts: 0.02 us -> 2.76 us  [tiled_device(): norms = jnp.stack([ln1_gain, ln1_shift, ln2_gain, ln2_shift])]
    pallas_call x1, Pallas kernels: 15.4 us -> 13 us  [hidden_grads(): pl.pallas_call(hidden_grads_kernel, grid_spec=pltpu.PrefetchScalarGridSpe...]
  transfers between devices with their start and end apart: 38 -> 38, of which waited for: 8 -> 13; matrix products, arithmetic and copies ran while one was open for 4% -> 4% of each run, Pallas kernels for 57% -> 46%
where the time goes in v2:
time: 166 us; the launch traced here: 165 us
  Pallas kernels  76 us (46%)
  waiting for transfers between devices  46.9 us (28%)
  starting transfers between devices  27.3 us (16%)
  local copies, waits for them, and re-layouts  13.8 us (8%)
    ppermute x38, waiting for transfers between devices, swap(): return lax.ppermute(value, axis, [(i, i ^ mask) for i in range(count)])  46.9 us
    ppermute x38, starting transfers between devices, swap(): return lax.ppermute(value, axis, [(i, i ^ mask) for i in range(count)])  27.3 us
    pallas_call x1, Pallas kernels, backward_spectral(): pl.pallas_call(backward_kernel, in_specs=[SM, SM] + [VM] * 18 + [HBM], ou...  13.5 us
    pallas_call x1, Pallas kernels, feed_forward(): pl.pallas_call(functools.partial(feed_kernel, piece=piece, thin=thin), gr...  13.4 us
    pallas_call x1, Pallas kernels, hidden_grads(): pl.pallas_call(hidden_grads_kernel, grid_spec=pltpu.PrefetchScalarGridSpe...  13 us
    pallas_call x1, Pallas kernels, forward_spectral(): pl.pallas_call(forward_kernel, in_specs=[SM, SM] + [VM] * 13, out_specs=[...  11 us
    unnamed x25, local copies, waits for them, and re-layouts  7.25 us
    pallas_call x1, Pallas kernels, select_columns(): pl.pallas_call(functools.partial(select_kernel, piece=piece, fs=fs), grid...  6.92 us
  transfers between devices with their start and end apart: 38, of which 13 were waited for; matrix products, arithmetic and copies ran while one was open for 4% of the time, Pallas kernels for 46%

profile of v2, /device:TPU:2, one launch (start us, length us, event | category | flops | bytes accessed | tf_op | source)
XLA Modules:
  0.0 165.1 jit_solution(662878877397591637)
XLA Ops:
  6.8 4.0 %prepare.1 = (bf16[384,768]{1,0:T(8,128)(2,1)S(1)}, bf16[384,192]{1,0:T(8,128)(2,1)S(1)}, bf16[64,384]{1,0:T(8,128)(2,1)S(1)}, f32[384,8]{1,0:T(8,128)S(1)}, f32...) custom-call(s32[5]{0:T(128)S(1)} %stack.38.me_ref.at_ref, ...), custom_call_target="tpu_custom_call" | custom-call | flops 3000000000 | bytes 10500000 | tf_op jit(solution)/shard_map/prepare/pallas_call | solution.py:486
  14.2 11.0 %forward_spectral.1 = (bf16[192,256]{1,0:T(8,128)(2,1)S(1)}, bf16[192,256]{1,0:T(8,128)(2,1)S(1)}, bf16[192,256]{1,0:T(8,128)(2,1)S(1)}, bf16[192,256]{1,0:T(8,1...) custom-call(s32[5]{0:T(128)S(1)} %stack.38.me_ref.at_ref, ...), custom_call_target="tpu_custom_call" | custom-call | flops 15000000512 | bytes 52500000 | tf_op jit(solution)/shard_map/forward_spectral/pallas_call | solution.py:667
  27.6 6.9 %select_columns.1 = (bf16[768,768]{1,0:T(8,128)(2,1)}, bf16[768,768]{1,0:T(8,128)(2,1)}) custom-call(s32[5]{0:T(128)S(1)} %stack.38.me_ref.at_ref, f32[64,8]{1,0:T(8,128)S(1)} %get-tuple-element.95.after.cb, bf16[768,3072]{1,0:T(8,128)(2,1)} %gate.3, bf16[768,3072]{1,0:T(8,128)(2,1)} %up.3), custom_call_target="tpu_custom_call" | custom-call | flops 6000000000 | bytes 21000000 | tf_op jit(solution)/shard_map/select_columns/pallas_call | solution.py:524
  35.8 2.0 %middle.1 = (f32[256,768]{1,0:T(8,128)S(1)}, bf16[256,768]{1,0:T(8,128)(2,1)S(1)}, bf16[768,256]{1,0:T(8,128)(2,1)S(1)}) custom-call(s32[5]{0:T(128)S(1)} %stack.38.me_ref.at_ref, bf16[192,256]{1,0:T(8,128)(2,1)S(1)} %get-tuple-element.91.z0, bf16[192,256]{1,0:T(8,128)(2,1)S(1)} %collective-permute-done.3.z1, ...), custom_call_target="tpu_custom_call" | custom-call | flops 2000000000 | bytes 7000000 | tf_op jit(solution)/shard_map/middle/pallas_call | solution.py:820
  38.8 13.4 %feed_forward.1 = (bf16[256,768]{1,0:T(8,128)(2,1)}, f32[256,768]{1,0:T(8,128)S(1)}, bf16[192,256]{1,0:T(8,128)(2,1)S(1)}, bf16[192,256]{1,0:T(8,128)(2,1)S(1)},...) custom-call(s32[5]{0:T(128)S(1)} %stack.38.me_ref.at_ref, ...), custom_call_target="tpu_custom_call" | custom-call | flops 12999999488 | bytes 45500000 | tf_op jit(solution)/shard_map/feed_forward/pallas_call | solution.py:894
  55.8 13.0 %hidden_grads.1 = (bf16[4,3,96,384]{3,2,1,0:T(8,128)(2,1)S(1)}, bf16[4,3,96,384]{3,2,1,0:T(8,128)(2,1)S(1)}, bf16[2,2,3,96,384]{4,3,2,1,0:T(8,128)(2,1)S(1)}, bf16[2,2,3,96,384]{4,3,2,1,0:T(8,128)(2,1)S(1)}) custom-call(s32[5]{0:T(128)S(1)} %stack.38.me_ref.at_ref, bf16[256,768]{1,0:T(8,128)(2,1)S(1)} %get-tuple-element.97.u2.u0, ...), custom_call_target="tpu_custom_call" | custom-call | flops 14000000000 | bytes 49000000 | tf_op jit(solution)/shard_map/hidden_grads/pallas_call | solution.py:972
  72.1 13.5 %backward_spectral.1 = (bf16[400,256]{1,0:T(8,128)(2,1)S(1)}, bf16[400,256]{1,0:T(8,128)(2,1)S(1)}, bf16[400,256]{1,0:T(8,128)(2,1)S(1)}, bf16[400,256]{1,0:T(8,...) custom-call(s32[5]{0:T(128)S(1)} %stack.38.me_ref.at_ref, ...), custom_call_target="tpu_custom_call" | custom-call | flops 16999999488 | bytes 59500000 | tf_op jit(solution)/shard_map/backward_spectral/pallas_call | solution.py:786
  86.2 4.6 %collective-permute-done.24 = bf16[4,3,96,384]{3,2,1,0:T(8,128)(2,1)S(1)} collective-permute-done((bf16[4,3,96,384]{3,2,1,0:T(8,128)(2,1)S(1)}, bf16[4,3,96,384]{3,2,1,0:T(8,128)(2,1)S(1)}, u32[]{:S(2)}, u32[]{:S(2)}) %collective-permute-start.24) | collective-permute-done | bytes 884768 | tf_op jit(solution)/shard_map/ppermute | solution.py:33
  94.1 1.8 %collective-permute-done.19.b2 = bf16[192,256]{1,0:T(8,128)(2,1)S(1)} collective-permute-done((bf16[192,256]{1,0:T(8,128)(2,1)S(1)}, bf16[192,256]{1,0:T(8,128)(2,1)S(1)}, u32[]{:S(2)}, u32[]{:S(2)}) %collective-permute-start.19) | collective-permute-done | bytes 98336 | tf_op jit(solution)/shard_map/ppermute | solution.py:33
  99.7 1.7 %collective-permute-start.27 = (bf16[2,3,96,384]{3,2,1,0:T(8,128)(2,1)S(1)}, bf16[2,3,96,384]{3,2,1,0:T(8,128)(2,1)S(1)}, u32[]{:S(2)}, u32[]{:S(2)}) collective-permute-start(bf16[2,3,96,384]{3,2,1,0:T(8,128)(2,1)S(1)} %get-tuple-element.139), channel_id=1, source_target_pairs={{0,4},{4,0},{8,12},{12,8},{16,20},{20,16},{24,28},{28,24},{1,5},{5... | collective-permute-start | bytes 1327112 | tf_op jit(solution)/shard_map/ppermute | solution.py:33
  101.4 2.7 %projection_grads.1 = (bf16[4,72,768]{2,1,0:T(8,128)(2,1)S(1)}, bf16[4,72,768]{2,1,0:T(8,128)(2,1)S(1)}, bf16[368,128]{1,0:T(8,128)(2,1)S(1)}) custom-call(s32[5]{0:T(128)S(1)} %stack.38.me_ref.at_ref, bf16[384,1024]{1,0:T(8,128)(2,1)S(1)} %get-tuple-element.118.after.gp, bf16[1024,768]{1,0:T(8,128)(2,1)S(1)} %get-tuple-element.119.u1, ...), custom_call_target="tpu_custom_call" | custom-call | flops 6000000000 | bytes 21000000 | tf_op jit(solution)/shard_map/projection_grads/pallas_call | solution.py:1134
  104.1 6.0 %collective-permute-done.26.got_a = bf16[2,3,96,384]{3,2,1,0:T(8,128)(2,1)S(1)} collective-permute-done((bf16[2,3,96,384]{3,2,1,0:T(8,128)(2,1)S(1)}, bf16[2,3,96,384]{3,2,1,0:T(8,128)(2,1)S(1)}, u32[]{:S(2)}, u32[]{:S(2)}) %collective-permute-start.26) | collective-permute-done | bytes 442400 | tf_op jit(solution)/shard_map/ppermute | solution.py:33
  110.2 1.8 %collective-permute-start.28 = (bf16[368,128]{1,0:T(8,128)(2,1)S(1)}, bf16[368,128]{1,0:T(8,128)(2,1)S(1)}, u32[]{:S(2)}, u32[]{:S(2)}) collective-permute-start(bf16[368,128]{1,0:T(8,128)(2,1)S(1)} %get-tuple-element.136.after.ours), channel_id=1, source_target_pairs={{0,4},{4,0},{8,12},{12,8},{16,20},{20,16},{24,28},{28,24},{1,5},{5... | collective-permute-start | bytes 282632 | tf_op jit(solution)/shard_map/ppermute | solution.py:33
  114.1 4.0 %final.1.after = f32[256,768]{1,0:T(8,128)} custom-call(s32[5]{0:T(128)S(1)} %stack.38.me_ref.at_ref, bf16[400,256]{1,0:T(8,128)(2,1)S(1)} %get-tuple-element.113.p0, bf16[400,256]{1,0:T(8,128)(2,1)S(1)} %collective-permute-done.15.p1, bf16[400,256]{1,0:T(8,128)(2,1)S(1)} %collective-permute-done.16.p2, bf16[400,256]{1,0:T(8,128)(2,1)S(1)} %collective-permute-done.17.p3, ...), custom_call_target="tpu_custom_call" | custom-call | flops 5000000000 | bytes 17500000 | tf_op jit(solution)/shard_map/final/pallas_call | solution.py:1186
  118.1 5.9 %collective-permute-done.34 = bf16[4,72,768]{2,1,0:T(8,128)(2,1)S(1)} collective-permute-done((bf16[4,72,768]{2,1,0:T(8,128)(2,1)S(1)}, bf16[4,72,768]{2,1,0:T(8,128)(2,1)S(1)}, u32[]{:S(2)}, u32[]{:S(2)}) %collective-permute-start.34) | collective-permute-done | bytes 442400 | tf_op jit(solution)/shard_map/ppermute | solution.py:33
  125.8 1.7 %collective-permute-start.35 = (bf16[2,72,768]{2,1,0:T(8,128)(2,1)S(1)}, bf16[2,72,768]{2,1,0:T(8,128)(2,1)S(1)}, u32[]{:S(2)}, u32[]{:S(2)}) collective-permute-start(bf16[2,72,768]{2,1,0:T(8,128)(2,1)S(1)} %get-tuple-element.145), channel_id=1, source_target_pairs={{0,8},{4,12},{8,0},{12,4},{16,24},{20,28},{24,16},{28,20},{1,9},{5... | collective-permute-start | bytes 663560 | tf_op jit(solution)/shard_map/ppermute | solution.py:33
  128.0 6.1 %collective-permute-done.29.theirs = bf16[368,128]{1,0:T(8,128)(2,1)S(1)} collective-permute-done((bf16[368,128]{1,0:T(8,128)(2,1)S(1)}, bf16[368,128]{1,0:T(8,128)(2,1)S(1)}, u32[]{:S(2)}, u32[]{:S(2)}) %collective-permute-start.29) | collective-permute-done | bytes 94240 | tf_op jit(solution)/shard_map/ppermute | solution.py:33
  134.1 2.5 %collective-permute-start.30 = (bf16[368,128]{1,0:T(8,128)(2,1)S(1)}, bf16[368,128]{1,0:T(8,128)(2,1)S(1)}, u32[]{:S(2)}, u32[]{:S(2)}) collective-permute-start(bf16[368,128]{1,0:T(8,128)(2,1)S(1)} %add.19.ours), channel_id=1, source_target_pairs={{0,16},{4,20},{8,24},{12,28},{16,0},{20,4},{24,8},{28,12},{1,17},{... | collective-permute-start | bytes 282632 | tf_op jit(solution)/shard_map/ppermute | solution.py:33
  137.8 5.1 %collective-permute-done.30.theirs = bf16[368,128]{1,0:T(8,128)(2,1)S(1)} collective-permute-done((bf16[368,128]{1,0:T(8,128)(2,1)S(1)}, bf16[368,128]{1,0:T(8,128)(2,1)S(1)}, u32[]{:S(2)}, u32[]{:S(2)}) %collective-permute-start.30) | collective-permute-done | bytes 94240 | tf_op jit(solution)/shard_map/ppermute | solution.py:33
  143.1 1.7 %copy.41 = f32[256,1,768]{2,1,0:T(1,128)} copy(f32[256,1,768]{2,0,1:T(8,128)S(1)} %bitcast.38) | data formatting | bytes 1572864
  144.8 2.8 %collective-permute-done.32.j2 = bf16[368,128]{1,0:T(8,128)(2,1)S(1)} collective-permute-done((bf16[368,128]{1,0:T(8,128)(2,1)S(1)}, bf16[368,128]{1,0:T(8,128)(2,1)S(1)}, u32[]{:S(2)}, u32[]{:S(2)}) %collective-permute-start.32) | collective-permute-done | bytes 94240 | tf_op jit(solution)/shard_map/ppermute | solution.py:33
  147.5 3.6 %collective-permute-done.36 = bf16[1,72,768]{2,1,0:T(8,128)(2,1)S(1)} collective-permute-done((bf16[1,72,768]{2,1,0:T(8,128)(2,1)S(1)}, bf16[1,72,768]{2,1,0:T(8,128)(2,1)S(1)}, u32[]{:S(2)}, u32[]{:S(2)}) %collective-permute-start.36) | collective-permute-done | bytes 110624 | tf_op jit(solution)/shard_map/ppermute | solution.py:33
  152.5 2.3 %small_grads.1 = (f32[64,1536]{1,0:T(8,128)}, f32[3,1536]{1,0:T(4,128)}, f32[4,768]{1,0:T(4,128)}, f32[64,64]{1,0:T(8,128)}, f32[1,64]{1,0:T(1,128)}, /*index=5*/f32[64,768]{1,0:T(8,128)}) custom-call(s32[5]{0:T(128)S(1)} %stack.38.me_ref.at_ref, bf16[368,128]{1,0:T(8,128)(2,1)S(1)} %add.20.j0, bf16[368,128]{1,0:T(8,128)(2,1)S(1)} %collective-permute-done.31.j1, ...), custom_call_target="tpu_custom_call" | custom-call | flops 3000000000 | bytes 10500000 | tf_op jit(solution)/shard_map/small_grads/pallas_call | solution.py:1275
  156.3 7.8 %collective-permute-done.37 = bf16[3,96,768]{2,1,0:T(8,128)(2,1)S(1)} collective-permute-done((bf16[3,96,768]{2,1,0:T(8,128)(2,1)S(1)}, bf16[3,96,768]{2,1,0:T(8,128)(2,1)S(1)}, u32[]{:S(2)}, u32[]{:S(2)}) %collective-permute-start.37) | collective-permute-done | bytes 442400 | tf_op jit(solution)/shard_map/ppermute | solution.py:33
  (110 shorter events, 38.2 us)
Async XLA Ops:
  0.6 12.8 %collective-permute-start = (bf16[256,768]{1,0:T(8,128)(2,1)}, bf16[256,768]{1,0:T(8,128)(2,1)S(1)}, u32[]{:S(2)}, u32[]{:S(2)}) collective-permute-start(bf16[256,768]{1,0:T(8,128)(2,1)} %bitcast.45), channel_id=1, source_target_pairs={{0,1},{1,0},{2,3},{3,2},{4,5},{5,4},{6,7},{7,6},{8,9},{9,8},{10,11... | collective-permute-start | bytes 1179656 | tf_op jit(solution)/shard_map/ppermute | solution.py:33
  0.7 11.7 %collective-permute-start.1 = (bf16[256,768]{1,0:T(8,128)(2,1)}, bf16[256,768]{1,0:T(8,128)(2,1)S(1)}, u32[]{:S(2)}, u32[]{:S(2)}) collective-permute-start(bf16[256,768]{1,0:T(8,128)(2,1)} %bitcast.46), channel_id=1, source_target_pairs={{0,2},{1,3},{2,0},{3,1},{4,6},{5,7},{6,4},{7,5},{8,10},{9,11},{10,... | collective-permute-start | bytes 1179656 | tf_op jit(solution)/shard_map/ppermute | solution.py:33
  12.5 40.3 %collective-permute-start.12 = (bf16[256,768]{1,0:T(8,128)(2,1)S(1)}, bf16[256,768]{1,0:T(8,128)(2,1)S(1)}, u32[]{:S(2)}, u32[]{:S(2)}) collective-permute-start(bf16[256,768]{1,0:T(8,128)(2,1)S(1)} %bitcast.41), channel_id=1, source_target_pairs={{0,1},{1,0},{2,3},{3,2},{4,5},{5,4},{6,7},{7,6},{8,9},{9,8},{10,11... | collective-permute-start | bytes 1179656 | tf_op jit(solution)/shard_map/ppermute | solution.py:33
  13.0 14.1 %collective-permute-start.13 = (bf16[256,768]{1,0:T(8,128)(2,1)S(1)}, bf16[256,768]{1,0:T(8,128)(2,1)S(1)}, u32[]{:S(2)}, u32[]{:S(2)}) collective-permute-start(bf16[256,768]{1,0:T(8,128)(2,1)S(1)} %bitcast.42), channel_id=1, source_target_pairs={{0,2},{1,3},{2,0},{3,1},{4,6},{5,7},{6,4},{7,5},{8,10},{9,11},{10,... | collective-permute-start | bytes 1179656 | tf_op jit(solution)/shard_map/ppermute | solution.py:33
  27.1 26.8 %collective-permute-start.14 = (bf16[256,768]{1,0:T(8,128)(2,1)S(1)}, bf16[256,768]{1,0:T(8,128)(2,1)S(1)}, u32[]{:S(2)}, u32[]{:S(2)}) collective-permute-start(bf16[256,768]{1,0:T(8,128)(2,1)S(1)} %tie.6.c2), channel_id=1, source_target_pairs={{0,1},{1,0},{2,3},{3,2},{4,5},{5,4},{6,7},{7,6},{8,9},{9,8},{10,11... | collective-permute-start | bytes 1179656 | tf_op jit(solution)/shard_map/ppermute | solution.py:33
  37.8 16.1 %collective-permute-start.9 = (bf16[256,768]{1,0:T(8,128)(2,1)S(1)}, bf16[256,768]{1,0:T(8,128)(2,1)S(1)}, u32[]{:S(2)}, u32[]{:S(2)}) collective-permute-start(bf16[256,768]{1,0:T(8,128)(2,1)S(1)} %get-tuple-element.97.u2.u0), channel_id=1, source_target_pairs={{0,1},{1,0},{2,3},{3,2},{4,5},{5,4},{6,7},{7,6},{8,9},{9,8},{10,11... | collective-permute-start | bytes 1179656 | tf_op jit(solution)/shard_map/ppermute | solution.py:33
  38.0 14.3 %collective-permute-start.10 = (bf16[256,768]{1,0:T(8,128)(2,1)S(1)}, bf16[256,768]{1,0:T(8,128)(2,1)S(1)}, u32[]{:S(2)}, u32[]{:S(2)}) collective-permute-start(bf16[256,768]{1,0:T(8,128)(2,1)S(1)} %get-tuple-element.97.u2.u0), channel_id=1, source_target_pairs={{0,2},{1,3},{2,0},{3,1},{4,6},{5,7},{6,4},{7,5},{8,10},{9,11},{10,... | collective-permute-start | bytes 1179656 | tf_op jit(solution)/shard_map/ppermute | solution.py:33
  52.3 45.9 %collective-permute-start.21 = (bf16[768,256]{1,0:T(8,128)(2,1)S(1)}, bf16[768,256]{1,0:T(8,128)(2,1)S(1)}, u32[]{:S(2)}, u32[]{:S(2)}) collective-permute-start(bf16[768,256]{1,0:T(8,128)(2,1)S(1)} %get-tuple-element.125.z0), channel_id=1, source_target_pairs={{0,1},{1,0},{2,3},{3,2},{4,5},{5,4},{6,7},{7,6},{8,9},{9,8},{10,11... | collective-permute-start | bytes 1179656 | tf_op jit(solution)/shard_map/ppermute | solution.py:33
  52.7 32.9 %collective-permute-start.22 = (bf16[768,256]{1,0:T(8,128)(2,1)S(1)}, bf16[768,256]{1,0:T(8,128)(2,1)S(1)}, u32[]{:S(2)}, u32[]{:S(2)}) collective-permute-start(bf16[768,256]{1,0:T(8,128)(2,1)S(1)} %get-tuple-element.125.z0), channel_id=1, source_target_pairs={{0,2},{1,3},{2,0},{3,1},{4,6},{5,7},{6,4},{7,5},{8,10},{9,11},{10,... | collective-permute-start | bytes 1179656 | tf_op jit(solution)/shard_map/ppermute | solution.py:33
  53.9 14.9 %collective-permute-start.6 = (bf16[192,256]{1,0:T(8,128)(2,1)S(1)}, bf16[192,256]{1,0:T(8,128)(2,1)S(1)}, u32[]{:S(2)}, u32[]{:S(2)}) collective-permute-start(bf16[192,256]{1,0:T(8,128)(2,1)S(1)} %get-tuple-element.101), channel_id=1, source_target_pairs={{0,1},{1,0},{2,3},{3,2},{4,5},{5,4},{6,7},{7,6},{8,9},{9,8},{10,11... | collective-permute-start | bytes 294920 | tf_op jit(solution)/shard_map/ppermute | solution.py:33
  53.9 16.5 %collective-permute-start.7 = (bf16[192,256]{1,0:T(8,128)(2,1)S(1)}, bf16[192,256]{1,0:T(8,128)(2,1)S(1)}, u32[]{:S(2)}, u32[]{:S(2)}) collective-permute-start(bf16[192,256]{1,0:T(8,128)(2,1)S(1)} %get-tuple-element.102), channel_id=1, source_target_pairs={{0,2},{1,3},{2,0},{3,1},{4,6},{5,7},{6,4},{7,5},{8,10},{9,11},{10,... | collective-permute-start | bytes 294920 | tf_op jit(solution)/shard_map/ppermute | solution.py:33
  54.9 17.2 %collective-permute-start.8 = (bf16[192,256]{1,0:T(8,128)(2,1)S(1)}, bf16[192,256]{1,0:T(8,128)(2,1)S(1)}, u32[]{:S(2)}, u32[]{:S(2)}) collective-permute-start(bf16[192,256]{1,0:T(8,128)(2,1)S(1)} %get-tuple-element.103), channel_id=1, source_target_pairs={{0,3},{1,2},{2,1},{3,0},{4,7},{5,6},{6,5},{7,4},{8,11},{9,10},{10,... | collective-permute-start | bytes 294920 | tf_op jit(solution)/shard_map/ppermute | solution.py:33
  68.9 22.0 %collective-permute-start.24 = (bf16[4,3,96,384]{3,2,1,0:T(8,128)(2,1)S(1)}, bf16[4,3,96,384]{3,2,1,0:T(8,128)(2,1)S(1)}, u32[]{:S(2)}, u32[]{:S(2)}) collective-permute-start(bf16[4,3,96,384]{3,2,1,0:T(8,128)(2,1)S(1)} %get-tuple-element.112.after), channel_id=1, source_target_pairs={{0,4},{4,0},{8,12},{12,8},{16,20},{20,16},{24,28},{28,24},{1,5},{5... | collective-permute-start | bytes 2654216 | tf_op jit(solution)/shard_map/ppermute | solution.py:33
  70.5 21.6 %collective-permute-start.25 = (bf16[2,2,3,96,384]{4,3,2,1,0:T(8,128)(2,1)S(1)}, bf16[2,2,3,96,384]{4,3,2,1,0:T(8,128)(2,1)S(1)}, u32[]{:S(2)}, u32[]{:S(2)}) collective-permute-start(bf16[2,2,3,96,384]{4,3,2,1,0:T(8,128)(2,1)S(1)} %get-tuple-element.134), channel_id=1, source_target_pairs={{0,8},{4,12},{8,0},{12,4},{16,24},{20,28},{24,16},{28,20},{1,9},{5... | collective-permute-start | bytes 2654216 | tf_op jit(solution)/shard_map/ppermute | solution.py:33
  85.6 14.1 %collective-permute-start.23 = (bf16[768,256]{1,0:T(8,128)(2,1)S(1)}, bf16[768,256]{1,0:T(8,128)(2,1)S(1)}, u32[]{:S(2)}, u32[]{:S(2)}) collective-permute-start(bf16[768,256]{1,0:T(8,128)(2,1)S(1)} %tie.7.z2), channel_id=1, source_target_pairs={{0,1},{1,0},{2,3},{3,2},{4,5},{5,4},{6,7},{7,6},{8,9},{9,8},{10,11... | collective-permute-start | bytes 1179656 | tf_op jit(solution)/shard_map/ppermute | solution.py:33
  93.1 21.0 %collective-permute-start.15 = (bf16[400,256]{1,0:T(8,128)(2,1)S(1)}, bf16[400,256]{1,0:T(8,128)(2,1)S(1)}, u32[]{:S(2)}, u32[]{:S(2)}) collective-permute-start(bf16[400,256]{1,0:T(8,128)(2,1)S(1)} %get-tuple-element.114), channel_id=1, source_target_pairs={{0,1},{1,0},{2,3},{3,2},{4,5},{5,4},{6,7},{7,6},{8,9},{9,8},{10,11... | collective-permute-start | bytes 614408 | tf_op jit(solution)/shard_map/ppermute | solution.py:33
  95.9 18.2 %collective-permute-start.16 = (bf16[400,256]{1,0:T(8,128)(2,1)S(1)}, bf16[400,256]{1,0:T(8,128)(2,1)S(1)}, u32[]{:S(2)}, u32[]{:S(2)}) collective-permute-start(bf16[400,256]{1,0:T(8,128)(2,1)S(1)} %get-tuple-element.115), channel_id=1, source_target_pairs={{0,2},{1,3},{2,0},{3,1},{4,6},{5,7},{6,4},{7,5},{8,10},{9,11},{10,... | collective-permute-start | bytes 614408 | tf_op jit(solution)/shard_map/ppermute | solution.py:33
  97.1 17.0 %collective-permute-start.17 = (bf16[400,256]{1,0:T(8,128)(2,1)S(1)}, bf16[400,256]{1,0:T(8,128)(2,1)S(1)}, u32[]{:S(2)}, u32[]{:S(2)}) collective-permute-start(bf16[400,256]{1,0:T(8,128)(2,1)S(1)} %get-tuple-element.116), channel_id=1, source_target_pairs={{0,3},{1,2},{2,1},{3,0},{4,7},{5,6},{6,5},{7,4},{8,11},{9,10},{10,... | collective-permute-start | bytes 614408 | tf_op jit(solution)/shard_map/ppermute | solution.py:33
  98.2 12.0 %collective-permute-start.26 = (bf16[2,3,96,384]{3,2,1,0:T(8,128)(2,1)S(1)}, bf16[2,3,96,384]{3,2,1,0:T(8,128)(2,1)S(1)}, u32[]{:S(2)}, u32[]{:S(2)}) collective-permute-start(bf16[2,3,96,384]{3,2,1,0:T(8,128)(2,1)S(1)} %get-tuple-element.135.after), channel_id=1, source_target_pairs={{0,8},{4,12},{8,0},{12,4},{16,24},{20,28},{24,16},{28,20},{1,9},{5... | collective-permute-start | bytes 1327112 | tf_op jit(solution)/shard_map/ppermute | solution.py:33
  99.7 12.2 %collective-permute-start.27 = (bf16[2,3,96,384]{3,2,1,0:T(8,128)(2,1)S(1)}, bf16[2,3,96,384]{3,2,1,0:T(8,128)(2,1)S(1)}, u32[]{:S(2)}, u32[]{:S(2)}) collective-permute-start(bf16[2,3,96,384]{3,2,1,0:T(8,128)(2,1)S(1)} %get-tuple-element.139), channel_id=1, source_target_pairs={{0,4},{4,0},{8,12},{12,8},{16,20},{20,16},{24,28},{28,24},{1,5},{5... | collective-permute-start | bytes 1327112 | tf_op jit(solution)/shard_map/ppermute | solution.py:33
  110.2 17.3 %collective-permute-start.28 = (bf16[368,128]{1,0:T(8,128)(2,1)S(1)}, bf16[368,128]{1,0:T(8,128)(2,1)S(1)}, u32[]{:S(2)}, u32[]{:S(2)}) collective-permute-start(bf16[368,128]{1,0:T(8,128)(2,1)S(1)} %get-tuple-element.136.after.ours), channel_id=1, source_target_pairs={{0,4},{4,0},{8,12},{12,8},{16,20},{20,16},{24,28},{28,24},{1,5},{5... | collective-permute-start | bytes 282632 | tf_op jit(solution)/shard_map/ppermute | solution.py:33
  112.0 12.0 %collective-permute-start.34 = (bf16[4,72,768]{2,1,0:T(8,128)(2,1)S(1)}, bf16[4,72,768]{2,1,0:T(8,128)(2,1)S(1)}, u32[]{:S(2)}, u32[]{:S(2)}) collective-permute-start(bf16[4,72,768]{2,1,0:T(8,128)(2,1)S(1)} %get-tuple-element.143), channel_id=1, source_target_pairs={{0,4},{4,0},{8,12},{12,8},{16,20},{20,16},{24,28},{28,24},{1,5},{5... | collective-permute-start | bytes 1327112 | tf_op jit(solution)/shard_map/ppermute | solution.py:33
  137.2 14.0 %collective-permute-start.36 = (bf16[1,72,768]{2,1,0:T(8,128)(2,1)S(1)}, bf16[1,72,768]{2,1,0:T(8,128)(2,1)S(1)}, u32[]{:S(2)}, u32[]{:S(2)}) collective-permute-start(bf16[1,72,768]{2,1,0:T(8,128)(2,1)S(1)} %get-tuple-element.147), channel_id=1, source_target_pairs={{0,16},{4,20},{8,24},{12,28},{16,0},{20,4},{24,8},{28,12},{1,17},{... | collective-permute-start | bytes 331784 | tf_op jit(solution)/shard_map/ppermute | solution.py:33
  143.0 21.1 %collective-permute-start.37 = (bf16[3,96,768]{2,1,0:T(8,128)(2,1)S(1)}, bf16[3,96,768]{2,1,0:T(8,128)(2,1)S(1)}, u32[]{:S(2)}, u32[]{:S(2)}) collective-permute-start(bf16[3,96,768]{2,1,0:T(8,128)(2,1)S(1)} %get-tuple-element.140.after), channel_id=1, source_target_pairs={{0,16},{4,20},{8,24},{12,28},{16,0},{20,4},{24,8},{28,12},{1,17},{... | collective-permute-start | bytes 1327112 | tf_op jit(solution)/shard_map/ppermute | solution.py:33
  (26 other events, 150.7 us)

commit v3 on v2

--- a/solution.py
+++ b/solution.py
@@ -419,20 +419,21 @@
     return copies
 
 
-def tie_kernel(value, after, out):
+def tie_kernel(*refs):
     pass
 
 
-def tie(value, after):
+def tie(values, after):
+    count = len(values)
     return pl.pallas_call(
         tie_kernel,
-        in_specs=[HBM, HBM],
-        out_specs=HBM,
-        out_shape=jax.ShapeDtypeStruct(value.shape, value.dtype),
-        input_output_aliases={0: 0},
+        in_specs=[HBM] * (count + 1),
+        out_specs=[HBM] * count,
+        out_shape=[jax.ShapeDtypeStruct(value.shape, value.dtype) for value in values],
+        input_output_aliases={i: i for i in range(count)},
         compiler_params=params(1),
         name="tie",
-    )(value, after)
+    )(*values, after)
 
 
 def one_hot_rows(me, rows, lanes, piece, fs):
@@ -445,10 +446,10 @@
 
 
 def prepare_kernel(
-    me_ref, w_in, freq_w2, conv_taps, freq_w1, freq_b1, feats, cos_far, sin_far, norms,
-    w_mine, w2x, w2t, taps, base, cos, sin, w1_aug, sems, *, step, fs,
+    me_ref, w_in, freq_w2, conv_taps, freq_w1, freq_b1, feats, waves_far, norms,
+    w_mine, w2x, w2t, taps, base, waves, w1_aug, sems, *, step, fs,
 ):
-    loads = dma_all([(cos_far, cos), (sin_far, sin)], sems)
+    loads = dma_all([(waves_far, waves)], sems)
     lanes = w_in.shape[1] // 4
     rows = lanes // fs
     sel = one_hot_rows(me_ref[0], rows, lanes, step, fs)
@@ -479,58 +480,57 @@
         load.wait()
 
 
-def prepare(me, w_in, freq_w2, conv_taps, freq_w1, freq_b1, feats, cos, sin, norms, step, fs):
+def prepare(me, w_in, freq_w2, conv_taps, freq_w1, freq_b1, feats, waves, norms, step, fs):
     channels, both = w_in.shape
     hidden = freq_w2.shape[0]
     length = feats.shape[1]
     return pl.pallas_call(
         functools.partial(prepare_kernel, step=step, fs=fs),
-        in_specs=[SM] + [VM] * 6 + [HBM] * 3,
-        out_specs=[VM] * 7,
+        in_specs=[SM] + [VM] * 6 + [HBM] * 2,
+        out_specs=[VM] * 6,
         out_shape=[
             shape((both // fs, channels), BF16),
             shape((both // fs, 3 * hidden), BF16),
             shape((hidden, both // fs), BF16),
             shape((both // fs, 8), F32),
             shape((hidden, length), F32),
-            shape((length, length), BF16),
-            shape((length, length), BF16),
+            shape((2 * length, length), BF16),
         ],
         scratch_shapes=[
             pltpu.VMEM((feats.shape[0], hidden), F32),
-            pltpu.SemaphoreType.DMA((2,)),
+            pltpu.SemaphoreType.DMA((1,)),
         ],
         compiler_params=params(24),
         cost_estimate=cost(3),
         name="prepare",
-    )(me, in_hbm(w_in), freq_w2, conv_taps, freq_w1, freq_b1[None], in_hbm(feats), in_hbm(cos), in_hbm(sin), norms)
-
-
-def select_kernel(me_ref, after, gate, up, gate_out, up_out, *, piece, fs):
-    rows = gate_out.shape[0] // 2
-    lanes = rows * fs
-    sel = one_hot_rows(me_ref[0], rows, lanes, piece, fs).astype(BF16)
-    for weight, out in ((gate, gate_out), (up, up_out)):
-        for part in range(2):
-            block = mm_nt(sel, weight[:, part * lanes : (part + 1) * lanes])
-            out[part * rows : (part + 1) * rows, :] = block.astype(BF16)
-
-
-def select_columns(me, after, w_gate, w_up, piece, fs):
+    )(me, *in_hbm(w_in, freq_w2, conv_taps, freq_w1), freq_b1[None], in_hbm(feats), in_hbm(waves), norms)
+
+
+def select_kernel(at_ref, after, gate, up, gate_out, up_out, *, fs):
+    rows = gate_out.shape[0]
+    sel = one_hot_rows(at_ref[0], rows, rows * fs, rows, fs).astype(BF16)
+    gate_out[...] = mm_nt(sel, gate[...]).astype(BF16)
+    up_out[...] = mm_nt(sel, up[...]).astype(BF16)
+
+
+def select_columns(at, after, w_gate, w_up, bs, fs):
     channels, ff = w_gate.shape
-    big = ff // 4
-    wide = pl.BlockSpec((channels, big), lambda i: (0, i))
-    rows = pl.BlockSpec((big // fs, channels), lambda i: (i, 0))
+    lanes = ff // bs
+    wide = pl.BlockSpec((channels, lanes), lambda i, at: (0, (i // 2) * 4 + at[2] * 2 + i % 2))
+    rows = pl.BlockSpec((lanes // fs, channels), lambda i, at: (i, 0))
     return pl.pallas_call(
-        functools.partial(select_kernel, piece=piece, fs=fs),
-        grid=(4,),
-        in_specs=[SM, HBM, wide, wide],
-        out_specs=[rows, rows],
-        out_shape=[far((ff // fs, channels), BF16)] * 2,
-        compiler_params=params(24),
-        cost_estimate=cost(6),
+        functools.partial(select_kernel, fs=fs),
+        grid_spec=pltpu.PrefetchScalarGridSpec(
+            num_scalar_prefetch=1,
+            grid=(bs // 2,),
+            in_specs=[HBM, wide, wide],
+            out_specs=[rows, rows],
+        ),
+        out_shape=[shape((ff // (2 * fs), channels), BF16)] * 2,
+        compiler_params=params(20),
+        cost_estimate=cost(5),
         name="select_columns",
-    )(me, after, in_hbm(w_gate), in_hbm(w_up))
+    )(at, after, in_hbm(w_gate), in_hbm(w_up))
 
 
 def row_masks(ids):
@@ -562,7 +562,7 @@
 
 
 def forward_kernel(
-    me_ref, ids_at, x0, x1, x2, x3, ids_ref, norms, w, taps, base, w2x, condt, cos, sin,
+    me_ref, ids_at, x0, x1, x2, x3, ids_ref, norms, w, taps, base, w2x, condt, waves,
     z0, z1, z2, z3, u1, n1, p_out, q_out, c_out, vr_out, vs_out, mu_out, mn_out, cb_out,
     p, q, vm, ycat, acc,
 ):
@@ -614,8 +614,8 @@
         lanes = tile(f, quarter)
         upper = pl.ds(pl.multiple_of(f * quarter + length, quarter), quarter)
         weight = bin_weights(f * quarter, quarter, length)
-        vr_all = mm(vm[...], cos[:, lanes])
-        vs_all = mm(vm[...], sin[:, lanes])
+        vr_all = mm(vm[...], waves[:length, lanes])
+        vs_all = mm(vm[...], waves[length:, lanes])
         vr_out[:, lanes] = vr_all.astype(BF16)
         vs_out[:, lanes] = vs_all.astype(BF16)
         for j in range(SEGS):
@@ -637,7 +637,7 @@
             @pl.when((ids_at[0, t * quarter] <= j) & (ids_at[0, (t + 1) * quarter - 1] >= j))
             def _():
                 at = slice(j * width, (j + 1) * width)
-                part = mm(ycat[at, :length], cos[:, lanes]) + mm(ycat[at, length:], sin[:, lanes])
+                part = mm(ycat[at, :], waves[:, lanes])
                 acc[...] += jnp.where(ids_here == j, part, 0.0)
 
         c = acc[...]
@@ -646,7 +646,7 @@
         z_out[...] = z
 
 
-def forward_spectral(me, x_parts, ids, norms, w, taps, base, w2x, condt, cos, sin):
+def forward_spectral(me, x_parts, ids, norms, w, taps, base, w2x, condt, waves):
     quarter, channels = x_parts[0].shape
     length = ids.shape[1]
     width = w.shape[0] // 2
@@ -666,7 +666,7 @@
     ]
     return pl.pallas_call(
         forward_kernel,
-        in_specs=[SM, SM] + [VM] * 13,
+        in_specs=[SM, SM] + [VM] * 12,
         out_specs=[VM] * (7 + len(saved)),
         out_shape=[shape((width, quarter), BF16)] * 4 + [shape(dims, BF16) for dims in saved] + small,
         scratch_shapes=[
@@ -679,12 +679,12 @@
         compiler_params=params(26),
         cost_estimate=cost(15),
         name="forward_spectral",
-    )(me, ids, *x_parts, ids, norms, w, taps, base, w2x, condt, cos, sin)
+    )(me, ids, *x_parts, ids, norms, w, taps, base, w2x, condt, waves)
 
 
 def backward_kernel(
     me_ref, ids_at, g0, g1, g2, g3, ids_ref, cb, taps, base, w2x, w2, feats,
-    p, q, c, vr_in, vs_in, cos, sin, after,
+    p, q, c, vr_in, vs_in, waves, after,
     o0, o1, o2, o3, gp_row, d_taps, d_w2, d_w1, gcb,
     gcm, gvcat, gs, acc,
 ):
@@ -710,8 +710,8 @@
         lanes = tile(f, quarter)
         upper = pl.ds(pl.multiple_of(f * quarter + length, quarter), quarter)
         weight = bin_weights(f * quarter, quarter, length)
-        gyr_all = mm(gcm[...], cos[:, lanes]) * weight
-        gys_all = mm(gcm[...], sin[:, lanes]) * weight
+        gyr_all = mm(gcm[...], waves[:length, lanes]) * weight
+        gys_all = mm(gcm[...], waves[length:, lanes]) * weight
         for j in range(SEGS):
             pre, gate = hidden_tile(base, cb, j, lanes)
             hk = pre * gate
@@ -740,7 +740,7 @@
             @pl.when((ids_at[0, t * quarter] <= j) & (ids_at[0, (t + 1) * quarter - 1] >= j))
             def _():
                 at = slice(j * width, (j + 1) * width)
-                part = mm(gvcat[at, :length], cos[:, lanes]) + mm(gvcat[at, length:], sin[:, lanes])
+                part = mm(gvcat[at, :], waves[:, lanes])
                 acc[...] += jnp.where(ids_here == j, part, 0.0)
 
         gs[width:, lanes] = acc[...]
@@ -771,7 +771,7 @@
 
 
 def backward_spectral(
-    me, gz_parts, ids, cb, taps, base, w2x, w2, feats, p, q, c, vr, vs, cos, sin, after
+    me, gz_parts, ids, cb, taps, base, w2x, w2, feats, p, q, c, vr, vs, waves, after
 ):
     width, quarter = gz_parts[0].shape
     length = ids.shape[1]
@@ -785,7 +785,7 @@
     ]
     return pl.pallas_call(
         backward_kernel,
-        in_specs=[SM, SM] + [VM] * 18 + [HBM],
+        in_specs=[SM, SM] + [VM] * 17 + [HBM],
         out_specs=[VM] * 9,
         out_shape=outs,
         scratch_shapes=[
@@ -798,7 +798,7 @@
         cost_estimate=cost(17),
         name="backward_spectral",
     )(
-        me, ids, *gz_parts, ids, cb, taps, base, w2x, w2, feats, p, q, c, vr, vs, cos, sin, after
+        me, ids, *gz_parts, ids, cb, taps, base, w2x, w2, feats, p, q, c, vr, vs, waves, after
     )
 
 
@@ -834,7 +834,7 @@
 
 def feed_kernel(
     me_ref, u2, h, ct, norms, w_out, gate, up, down,
-    mixed, big_g, g0, g1, g2, g3, t0, t1, t2, t3, sums, acc_out, acc_grad, gz_t, gb_t, *, piece, thin,
+    mixed, big_g, g0, g1, g2, g3, t_own, t_other, sums, acc_out, acc_grad, gz_t, gb_t, *, piece, thin,
 ):
     i = pl.program_id(0)
 
@@ -873,11 +873,12 @@
                 at = pl.ds(pl.multiple_of((r * 4 + (me ^ k)) * piece, piece), piece)
                 out[r * piece : (r + 1) * piece, :] = gz_t[at, :]
         gb_t[...] = jnp.transpose(total)
-        for k, out in enumerate((t0, t1, t2, t3)):
+        for core, out in ((me & 1, t_own), (1 - (me & 1), t_other)):
             parts = []
-            for r in range(width // thin):
-                lo = pl.multiple_of((r * 4 + (me ^ k)) * thin, thin)
-                parts.append(gb_t[pl.ds(lo, thin), :])
+            for x in range(2):
+                for r in range(width // thin):
+                    lo = pl.multiple_of((r * 4 + 2 * x + core) * thin, thin)
+                    parts.append(gb_t[pl.ds(lo, thin), :])
             out[...] = jnp.concatenate(parts, axis=0).astype(BF16)
 
 
@@ -890,7 +891,7 @@
     outs = [
         ((quarter, channels), BF16),
         ((quarter, channels), F32),
-    ] + [((width, quarter), BF16)] * 8 + [((8, channels), F32)]
+    ] + [((width, quarter), BF16)] * 4 + [((2 * width, quarter), BF16)] * 2 + [((8, channels), F32)]
     return pl.pallas_call(
         functools.partial(feed_kernel, piece=piece, thin=thin),
         grid=(ff // block,),
@@ -919,79 +920,88 @@
     )(me, u2, h, ct, norms, in_hbm(w_out), in_hbm(w_gate), in_hbm(w_up), in_hbm(w_down))
 
 
-def hidden_grads_kernel(
-    at_ref, u0, u1, u2, u3, c0, c1, c2, c3, gate, up, down, after,
-    keep_a, give_a, keep_b, give_b, u_row, c_row, d_all,
-):
-    quarter, channels = u0.shape
-    i = pl.program_id(0)
-    y, z = at_ref[1], at_ref[2]
-
-    @pl.when(i == 0)
-    def _():
-        for k, (u, c) in enumerate(((u0, c0), (u1, c1), (u2, c2), (u3, c3))):
-            u_row[k * quarter : (k + 1) * quarter, :] = u[...]
-            c_row[k * quarter : (k + 1) * quarter, :] = c[...]
-
+def hidden_grads_kernel(at_ref, *refs):
+    u_parts, c_parts, refs = refs[:8], refs[8:16], refs[16:]
+    gate, up, gt_own, gt_got, z_own, z_got, down, after, *refs = refs
+    keep_a, give_a, keep_b, give_b, keep_o, give_o, rights, lefts, d_all, d_out = refs
+    quarter, channels = u_parts[0].shape
+    y, z = at_ref[1], at_ref[3]
     rows = gate.shape[0]
-    g = mm_nt(gate[...], u_row[...])
-    a = mm_nt(up[...], u_row[...])
-    gh = mm_nt(down[...].reshape(rows, channels), c_row[...])
-    sg = sigmoid(g)
-    silu = g * sg
-    hid = (silu * a).astype(BF16)
-    gg = (gh * a * (sg * (1.0 + g * (1.0 - sg)))).astype(BF16)
-    ga = (gh * silu).astype(BF16)
-    half = rows // 2
-    for m, grad in enumerate((mm(gg, u_row[...]), mm(ga, u_row[...]), mm(hid, c_row[...]))):
-        d_all[0, m] = grad[:half].astype(BF16)
-        d_all[1, m] = grad[half:].astype(BF16)
-    cut = channels // 2
-    keep_a[0] = d_all[y, :, :, :cut]
-    give_a[0] = d_all[1 - y, :, :, :cut]
-
-    @pl.when((i & 1) == z)
-    def _():
-        keep_b[0] = d_all[:, :, :, cut:]
-
-    @pl.when((i & 1) != z)
-    def _():
-        give_b[0] = d_all[:, :, :, cut:]
-
-
-def hidden_grads(at, u2_parts, ct_parts, gate, up, down, after):
+    for k in range(8):
+        at = slice(k * quarter, (k + 1) * quarter)
+        rights[0, at, :] = u_parts[k][...]
+        rights[1, at, :] = c_parts[k][...]
+    span = 2 * quarter
+
+    @pl.loop(0, 4)
+    def _(k):
+        at = tile(k, span)
+        g = mm_nt(gate[...], rights[0, at, :])
+        a = mm_nt(up[...], rights[0, at, :])
+        gh = mm_nt(down[...].reshape(rows, channels), rights[1, at, :])
+        sg = sigmoid(g)
+        silu = g * sg
+        lefts[0, :, at] = (gh * a * (sg * (1.0 + g * (1.0 - sg)))).astype(BF16)
+        lefts[1, :, at] = (gh * silu).astype(BF16)
+        lefts[2, :, at] = (silu * a).astype(BF16)
+
+    d_out[...] = mm_nt(gt_own[...], z_own[...]) + mm_nt(gt_got[...], z_got[...])
+    half = keep_o.shape[0]
+    x = at_ref[0] >> 1
+    keep_o[...] = d_out[tile(x, half), :].astype(BF16)
+    give_o[...] = d_out[tile(1 - x, half), :].astype(BF16)
+    fw = rows // 4
+    cut = keep_a.shape[-1]
+
+    @pl.loop(0, 3)
+    def _(m):
+        grad = mm(lefts[m], rights[m >> 1]).astype(BF16)
+        for i in range(4):
+            d_all[i, m] = grad[i * fw : (i + 1) * fw]
+
+    for i in range(2):
+        keep_a[i] = d_all[2 * i + y, :, :, :cut]
+        give_a[i] = d_all[2 * i + 1 - y, :, :, :cut]
+        keep_b[i] = d_all[2 * z + i, :, :, cut:]
+        give_b[i] = d_all[2 * (1 - z) + i, :, :, cut:]
+
+
+def hidden_grads(at, u2_parts, ct_parts, gate, up, gt_own, gt_got, z_own, z_got, down, after):
     quarter, channels = u2_parts[0].shape
     wide = gate.shape[0]
     bs, fs, fw, _ = down.shape
-    block = 2 * fw
-    cut = channels // 2
-    rows = pl.BlockSpec((block, channels), lambda i, at: (i, 0))
-    down_spec = pl.BlockSpec((2, 1, fw, channels), lambda i, at: (i, at[0], 0, 0))
-    a_spec = pl.BlockSpec((1, 3, fw, cut), lambda i, at: (i, 0, 0, 0))
-    b_spec = pl.BlockSpec((1, 2, 3, fw, cut), lambda i, at: (i // 2, 0, 0, 0, 0))
+    cut = 2 * channels // 3
+    down = down.reshape(2, 2, 2, fs, fw, channels)
+    down_spec = pl.BlockSpec((2, 1, 2, 1, fw, channels), lambda i, at: (0, at[2], 0, at[0], 0, 0))
     return pl.pallas_call(
         hidden_grads_kernel,
         grid_spec=pltpu.PrefetchScalarGridSpec(
             num_scalar_prefetch=1,
-            grid=(bs // 2,),
-            in_specs=[VM] * 8 + [rows, rows, down_spec, HBM],
-            out_specs=[a_spec, a_spec, b_spec, b_spec],
+            grid=(1,),
+            in_specs=[VM] * 22 + [down_spec, HBM],
+            out_specs=[VM] * 6,
             scratch_shapes=[
-                pltpu.VMEM((4 * quarter, channels), BF16),
-                pltpu.VMEM((4 * quarter, channels), BF16),
-                pltpu.VMEM((2, 3, fw, channels), BF16),
+                pltpu.VMEM((2, 8 * quarter, channels), BF16),
+                pltpu.VMEM((3, wide, 8 * quarter), BF16),
+                pltpu.VMEM((4, 3, fw, channels), BF16),
+                pltpu.VMEM((2 * channels // fs, channels), F32),
             ],
         ),
-        out_shape=[shape((bs // 2, 3, fw, cut), BF16)] * 2
-        + [shape((bs // 4, 2, 3, fw, cut), BF16)] * 2,
-        compiler_params=params(30),
+        out_shape=[shape((2, 3, fw, cut), BF16)] * 2
+        + [shape((2, 3, fw, channels - cut), BF16)] * 2
+        + [shape((channels // fs, channels), BF16)] * 2,
+        compiler_params=params(34),
         cost_estimate=cost(14),
         name="hidden_grads",
-    )(at, *u2_parts, *ct_parts, in_hbm(gate), in_hbm(up), in_hbm(down), after)
-
-
-def halve_kernel(at_ref, after, *refs, bits):
+    )(at, *u2_parts, *ct_parts, gate, up, gt_own, gt_got, z_own, z_got, in_hbm(down), after)
+
+
+def halve_kernel(at_ref, after, *refs, bits, extra):
     pairs = len(bits)
+    if extra:
+        ours, theirs, out = refs[2 * pairs], refs[2 * pairs + 1], refs[-1]
+        out[...] = (ours[...].astype(F32) + theirs[...].astype(F32)).astype(BF16)
+        refs = refs[: 2 * pairs] + refs[2 * pairs + 2 : -1]
     ins, outs = refs[: 2 * pairs], refs[2 * pairs :]
     for n in range(pairs):
         mine = at_ref[bits[n] + 1]
@@ -1004,40 +1014,62 @@
 
 def halve(at, bits, after, *sums):
     outs = []
+    extra = len(sums) > 2 * len(bits)
     for n in range(len(bits)):
         dims = sums[2 * n].shape
         outs += [shape((dims[0],) + dims[2:], BF16)] * 2
+    if extra:
+        outs.append(shape(sums[-1].shape, BF16))
     return pl.pallas_call(
-        functools.partial(halve_kernel, bits=bits),
+        functools.partial(halve_kernel, bits=bits, extra=extra),
         in_specs=[SM, HBM] + [VM] * len(sums),
         out_specs=[VM] * len(outs),
         out_shape=outs,
         compiler_params=params(24),
-        cost_estimate=cost(2),
+        cost_estimate=cost(0.3),
         name="halve",
     )(at, after, *sums)
 
 
-def join_kernel(at_ref, after, keep_a, got_a, keep_b, got_b, keep, give):
+def join_kernel(at_ref, after, keep_a, got_a, keep_b, got_b, ours, theirs, keep, give, total):
+    total[...] = (ours[...].astype(F32) + theirs[...].astype(F32)).astype(BF16)
     cut = keep_a.shape[-1]
     for side, out in ((at_ref[3], keep), (1 - at_ref[3], give)):
-        for m in range(keep_a.shape[1]):
-            for ours, theirs, lanes in ((keep_a, got_a, slice(0, cut)), (keep_b, got_b, slice(cut, 2 * cut))):
-                total = ours[side, m].astype(F32) + theirs[side, m].astype(F32)
-                out[m, :, lanes] = total.astype(BF16)
-
-
-def join(at, after, keep_a, got_a, keep_b, got_b):
+        out[:, :cut] = (keep_a[side].astype(F32) + got_a[side].astype(F32)).astype(BF16)
+        out[:, cut:] = (keep_b[side].astype(F32) + got_b[side].astype(F32)).astype(BF16)
+
+
+def join(at, after, keep_a, got_a, keep_b, got_b, ours, theirs):
+    _, rows, cut = keep_a.shape
+    return pl.pallas_call(
+        join_kernel,
+        in_specs=[SM, HBM] + [VM] * 6,
+        out_specs=[VM] * 3,
+        out_shape=[shape((rows, cut + keep_b.shape[-1]), BF16)] * 2 + [shape(ours.shape, BF16)],
+        compiler_params=params(12),
+        cost_estimate=cost(0.3),
+        name="join",
+    )(at, after, keep_a, got_a, keep_b, got_b, ours, theirs)
+
+
+def hidden_last_kernel(keep_a, got_a, keep_b, got_b, after, *outs):
+    cut = keep_a.shape[-1]
+    for m, out in enumerate(outs):
+        out[:, :cut] = keep_a[0, m].astype(F32) + got_a[0, m].astype(F32)
+        out[:, cut:] = keep_b[0, m].astype(F32) + got_b[0, m].astype(F32)
+
+
+def hidden_last(keep_a, got_a, keep_b, got_b, after):
     _, count, rows, cut = keep_a.shape
     return pl.pallas_call(
-        join_kernel,
-        in_specs=[SM, HBM] + [VM] * 4,
-        out_specs=[VM] * 2,
-        out_shape=[shape((count, rows, 2 * cut), BF16)] * 2,
-        compiler_params=params(24),
-        cost_estimate=cost(2),
-        name="join",
-    )(at, after, keep_a, got_a, keep_b, got_b)
+        hidden_last_kernel,
+        in_specs=[VM] * 4 + [HBM],
+        out_specs=[VM] * count,
+        out_shape=[far((rows, cut + keep_b.shape[-1]), F32)] * count,
+        compiler_params=params(12),
+        cost_estimate=cost(0.3),
+        name="hidden_last",
+    )(keep_a, got_a, keep_b, got_b, after)
 
 
 def add_kernel(ours, theirs, after, out):
@@ -1051,33 +1083,38 @@
         out_specs=VM,
         out_shape=shape(ours.shape, dtype),
         compiler_params=params(8),
-        cost_estimate=cost(1),
+        cost_estimate=cost(0.3),
         name="add",
     )(ours, theirs, after)
 
 
 def projection_kernel(
-    at_ref, gp, u1, n1, w_mine, b0, b1, b2, b3, z0, z1, z2, z3, d_w2, d_w1, d_taps, gcb, condt, mu, mn,
-    sums2, after, keep, give, packed_out, gb_row, z_row, d_in, d_out, packed, *, layout,
+    at_ref, gp, u1, n1, w_mine, keep_o, got_o, d_w2, d_w1, d_taps, gcb, condt, mu, mn,
+    sums2, after, keep_a, give_a, keep_b, give_b, packed_out, d_in, d_out, packed, *, layout,
 ):
-    me, y = at_ref[0], at_ref[1]
-    quarter = b0.shape[1]
+    me, y, zbit = at_ref[0], at_ref[1], at_ref[2]
     channels = u1.shape[1]
-    width = b0.shape[0]
-    for k, (b, z) in enumerate(((b0, z0), (b1, z1), (b2, z2), (b3, z3))):
-        gb_row[:, k * quarter : (k + 1) * quarter] = b[...]
-        z_row[:, k * quarter : (k + 1) * quarter] = z[...]
+    width = keep_o.shape[0]
     d_in[...] = mm(gp[...], u1[...])
-    d_out[...] = mm_nt(gb_row[...], z_row[...])
-    blocks = 2 * keep.shape[0]
+    d_out[...] = keep_o[...].astype(F32) + got_o[...].astype(F32)
+    blocks = 2 * keep_a.shape[0]
     first = 2 * width // blocks
     second = width // blocks
+    cut = 2 * channels // 3
+
+    def put(out, block, lanes):
+        lo = pl.multiple_of(block * first, first)
+        out[:first, :] = d_in[pl.ds(lo, first), lanes].astype(BF16)
+        lo = pl.multiple_of(block * second, second)
+        out[first:, :] = d_out[pl.ds(lo, second), lanes].astype(BF16)
+
     for b in range(blocks // 2):
-        for side, out in ((y, keep), (1 - y, give)):
-            lo = pl.multiple_of((2 * b + side) * first, first)
-            out[b, :first, :] = d_in[pl.ds(lo, first), :].astype(BF16)
-            lo = pl.multiple_of((2 * b + side) * second, second)
-            out[b, first:, :] = d_out[pl.ds(lo, second), :].astype(BF16)
+        put(keep_a.at[b], 2 * b + y, slice(0, cut))
+        put(give_a.at[b], 2 * b + 1 - y, slice(0, cut))
+    for b in range(blocks // 4):
+        for i in range(2):
+            put(keep_b.at[b, i], 4 * b + 2 * zbit + i, slice(cut, channels))
+            put(give_b.at[b, i], 4 * b + 2 * (1 - zbit) + i, slice(cut, channels))
     packed[...] = jnp.zeros_like(packed)
     packed[:width, :] = jnp.concatenate([d_w2[:width, :], d_w2[width:, :]], axis=1)
     taps_t = jnp.transpose(d_taps[...])
@@ -1126,29 +1163,28 @@
 
 
 def projection_grads(
-    at, gp, u1, n1, w_mine, gb_parts, z_parts, d_w2, d_w1, d_taps, gcb, condt, mu, mn, sums2, after, bs
+    at, gp, u1, n1, w_mine, keep_o, got_o, d_w2, d_w1, d_taps, gcb, condt, mu, mn, sums2, after, bs
 ):
     length, channels = u1.shape
-    width = gb_parts[0].shape[0]
+    width = keep_o.shape[0]
     layout = packed_layout(width, channels, bs)
     return pl.pallas_call(
         functools.partial(projection_kernel, layout=layout),
-        in_specs=[SM] + [VM] * 20 + [HBM],
-        out_specs=[VM] * 3,
-        out_shape=[shape((bs // 2, 3 * width // bs, channels), BF16)] * 2
+        in_specs=[SM] + [VM] * 14 + [HBM],
+        out_specs=[VM] * 5,
+        out_shape=[shape((bs // 2, 3 * width // bs, 2 * channels // 3), BF16)] * 2
+        + [shape((bs // 4, 2, 3 * width // bs, channels // 3), BF16)] * 2
         + [shape((layout["rows"], 128), BF16)],
         scratch_shapes=[
-            pltpu.VMEM((width, length), BF16),
-            pltpu.VMEM((channels, length), BF16),
             pltpu.VMEM((2 * width, channels), F32),
             pltpu.VMEM((width, channels), F32),
             pltpu.VMEM((layout["rows"], 128), F32),
         ],
         compiler_params=params(24),
-        cost_estimate=cost(6),
+        cost_estimate=cost(2),
         name="projection_grads",
     )(
-        at, gp, u1, n1, w_mine, *gb_parts, *z_parts, d_w2, d_w1, d_taps, gcb, condt, mu, mn, sums2, after
+        at, gp, u1, n1, w_mine, keep_o, got_o, d_w2, d_w1, d_taps, gcb, condt, mu, mn, sums2, after
     )
 
 
@@ -1187,16 +1223,16 @@
         functools.partial(final_kernel, piece=piece),
         in_specs=[SM] + [VM] * 10 + [HBM],
         out_specs=VM,
-        out_shape=far((quarter, channels), F32),
+        out_shape=shape((quarter, channels), F32),
         scratch_shapes=[pltpu.VMEM((2 * channels, quarter), BF16)],
         compiler_params=params(24),
-        cost_estimate=cost(5),
+        cost_estimate=cost(1),
         name="final",
     )(me, *gp_parts, x, big_g, norms, ids, condt, in_hbm(w_in), after)
 
 
 def small_kernel(
-    me_ref, j0, j1, j2, j3, w2, taps, ln, w1, b1, cond, wide, tap_t, cond_t, *, layout, step, width
+    me_ref, j0, j1, j2, j3, w2, taps, ln0, ln1, ln2, ln3, w1, b1, cond, wide, tap_t, cond_t, *, layout, step, width
 ):
     me = me_ref[0]
     parts = [part[...].astype(F32) for part in (j0, j1, j2, j3)]
@@ -1230,11 +1266,11 @@
         a, b, c, d = [part[first:last, :] for part in parts]
         return (a + b) + (c + d)
 
-    lanes = ln.shape[1] // 128
+    lanes = ln0.shape[0] // 128
     sums = common(layout["ln"], layout["ln"] + 4 * lanes)
-    for i in range(4):
-        for m in range(lanes):
-            ln[i : i + 1, m * 128 : (m + 1) * 128] = sums[i * lanes + m : i * lanes + m + 1, :]
+    for i, out in enumerate((ln0, ln1, ln2, ln3)):
+        row = jnp.concatenate([sums[i * lanes + m : i * lanes + m + 1, :] for m in range(lanes)], axis=1)
+        out[...] = row.reshape(out.shape)
     both = common(layout["w1"], layout["w1"] + hidden // 2)
     w1[: hidden // 2, :] = both[:, :hidden]
     w1[hidden // 2 :, :] = both[:, hidden:]
@@ -1275,11 +1311,14 @@
     return pl.pallas_call(
         functools.partial(small_kernel, layout=layout, step=step, width=width),
         in_specs=[SM] + [VM] * 4,
-        out_specs=[VM] * 6,
+        out_specs=[VM] * 9,
         out_shape=[
             far((hidden, 2 * channels), F32),
             far((3, 2 * channels), F32),
-            far((4, channels), F32),
+            far((channels,), F32),
+            far((channels,), F32),
+            far((channels,), F32),
+            far((channels,), F32),
             far((hidden, hidden), F32),
             far((1, hidden), F32),
             far((hidden, channels), F32),
@@ -1330,7 +1369,7 @@
     half = bs // 2
     step = channels // (half * fs)
     fw = ff // (bs * fs)
-    cos_table, sin_table = tables(length)
+    table = np.concatenate(tables(length), axis=0)
     feats = features(length, freq_w1.shape[0] // 2)
     feats_aug = np.concatenate(
         [feats, np.ones((1, length), np.float32), np.zeros((7, length), np.float32)], axis=0
@@ -1340,79 +1379,100 @@
     ct_own = cotangent[:, 0]
     ids = seg_ids
     at = jnp.stack([me, row & 1, (row >> 1) & 1, (row >> 2) & 1, row]).astype(jnp.int32)
-    norms = jnp.stack([ln1_gain, ln1_shift, ln2_gain, ln2_shift])
+    norms = jnp.concatenate([ln1_gain, ln1_shift, ln2_gain, ln2_shift]).reshape(4, channels)
     condt = cond_w.T
-    cos_c, sin_c = jnp.asarray(cos_table), jnp.asarray(sin_table)
 
     def gather_after(value, after):
         two = swap(value, "freq", 2)
         one = swap(value, "freq", 1)
-        two = tie(two, after)
+        (two,) = tie([two], after)
         return (value, one, two, swap(two, "freq", 1))
+
+    def gather_wide(value, after):
+        count = bs * fs
+        parts = (
+            value,
+            swap(value, "freq", 2),
+            swap(value, "batch", 2),
+            lax.ppermute(value, ("batch", "freq"), [(i, i ^ (2 * fs + 2)) for i in range(count)]),
+        )
+        parts = parts[:1] + tuple(tie(parts[1:], after))
+        return parts + tuple(swap(part, "freq", 1) for part in parts)
 
     def pairs(value):
         return value.reshape((value.shape[0] // 2, 2) + value.shape[1:])
 
-    w_mine, w2x, w2t, taps, base, cos_c, sin_c = prepare(
-        at, w_in, freq_w2, conv_taps, freq_w1, freq_b1, jnp.asarray(feats_aug), cos_c, sin_c, norms, step, fs
+    w_mine, w2x, w2t, taps, base, waves = prepare(
+        at, w_in, freq_w2, conv_taps, freq_w1, freq_b1, jnp.asarray(feats_aug), jnp.asarray(table), norms, step, fs
     )
     x_parts = gather_after(x_own, base)
-    forward = forward_spectral(at, x_parts, ids, norms, w_mine, taps, base, w2x, condt, cos_c, sin_c)
+    forward = forward_spectral(at, x_parts, ids, norms, w_mine, taps, base, w2x, condt, waves)
     z_parts, (u1, n1, p, q, c, vr, vs, mu, mn, cb) = forward[:4], forward[4:]
-    ct_parts = gather_after(ct_own, cb)
+    ct_x = swap(ct_own, "freq", 2)
+    ct_z = swap(ct_own, "batch", 2)
     z_got = trade_parts(z_parts)
-    wg_mine, wu_mine = select_columns(at, cb, w_gate, w_up, fw, fs)
+    wg_mine, wu_mine = select_columns(at, cb, w_gate, w_up, bs, fs)
+    (ct_x,) = tie([ct_x], cb)
+    ct_parts = (ct_own, ct_x, ct_z, swap(ct_x, "batch", 2))
     h, u2, z_t = middle(at, z_got, x_own, w_out, norms, wg_mine, step)
     fed = feed_forward(
         at, u2, h, ct_own, norms, w_out, w_gate, w_up, w_down, step, channels // (bs * fs)
     )
-    mixed_out, big_g, gz_parts, gb_parts, sums2 = fed[0], fed[1], fed[2:6], fed[6:10], fed[10]
-    u2_parts = gather_after(u2, sums2)
+    mixed_out, big_g, gz_parts, gt_own, gt_other, sums2 = fed[0], fed[1], fed[2:6], *fed[6:]
+    u2_parts = gather_wide(u2, sums2)
+    ct_parts = ct_parts + tuple(swap(part, "freq", 1) for part in tie(ct_parts, sums2))
     gz_got = trade_parts(gz_parts)
 
-    keep_a, give_a, keep_b, give_b = hidden_grads(
-        at, u2_parts, ct_parts, wg_mine, wu_mine, w_down.reshape(bs, fs, fw, channels), sums2
+    gt_got = swap(gt_other, "freq", 1)
+    z_got = swap(z_t, "freq", 1)
+    keep_a, give_a, keep_b, give_b, keep_o, give_o = hidden_grads(
+        at, u2_parts, ct_parts, wg_mine, wu_mine, gt_own, gt_got, z_t, z_got,
+        w_down.reshape(bs, fs, fw, channels), sums2,
     )
     got_a = swap(give_a, "batch", 1)
-    got_b = swap(give_b, "batch", 2)
-    gb_got = trade_parts(gb_parts)
+    got_b = swap(give_b, "batch", 4)
+    got_o = swap(give_o, "freq", 2)
 
     back = backward_spectral(
         at, gz_got, ids, cb, taps, base, w2x, w2t, jnp.asarray(feats).astype(BF16),
-        p, q, c, vr, vs, cos_c, sin_c, give_a,
+        p, q, c, vr, vs, waves, give_a,
     )
     gp_parts, (gp, d_taps, d_w2, d_w1, gcb) = back[:4], back[4:]
     gp_got = trade_parts(gp_parts)
-    z_all = gather_after(z_t, gcb)
 
     keep_a, give_a, keep_b, give_b = halve(
-        at, (1, 0), gp, pairs(keep_a), pairs(got_a), keep_b, got_b
-    )
-    got_a = swap(give_a, "batch", 2)
+        at, (2, 0), gp, keep_a[None], got_a[None], keep_b[None], got_b[None]
+    )
+    got_a = swap(give_a, "batch", 4)
     got_b = swap(give_b, "batch", 1)
 
-    keep, give, packed = projection_grads(
-        at, gp, u1, n1, w_mine, gb_got, z_all, d_w2, d_w1, d_taps, gcb, condt, mu, mn, sums2, give_a, bs
-    )
-    got = swap(give, "batch", 1)
-    keep_ff, give_ff = join(at, packed, keep_a, got_a, keep_b, got_b)
-    got_ff = swap(give_ff, "batch", 4)
-    grad_tokens = final(at, gp_got, x_own, big_g, norms, ids, condt, w_in, give_ff, step)
-
-    keep, give = halve(at, (1,), grad_tokens, pairs(keep), pairs(got))
-    got = swap(give, "batch", 2)
-    keep, give = halve(at, (2,), grad_tokens, pairs(keep), pairs(got))
+    proj = projection_grads(
+        at, gp, u1, n1, w_mine, keep_o, got_o, d_w2, d_w1, d_taps, gcb, condt, mu, mn, sums2, give_a, bs
+    )
+    p_keep_a, p_give_a, p_keep_b, p_give_b, packed = proj
+    p_got_a = swap(p_give_a, "batch", 1)
+    p_got_b = swap(p_give_b, "batch", 2)
+    got_packed = swap(packed, "batch", 1)
+    grad_tokens = final(at, gp_got, x_own, big_g, norms, ids, condt, w_in, packed, step)
+
+    p_keep_a, p_give_a, p_keep_b, p_give_b, packed = halve(
+        at, (1, 0), grad_tokens, pairs(p_keep_a), pairs(p_got_a), p_keep_b, p_got_b, packed, got_packed
+    )
+    p_got_a = swap(p_give_a, "batch", 2)
+    p_got_b = swap(p_give_b, "batch", 1)
+    got_packed = swap(packed, "batch", 2)
+    d_gate, d_up, d_down = hidden_last(keep_a, got_a, keep_b, got_b, packed)
+    keep, give, packed = join(
+        at, d_down, p_keep_a, p_got_a, p_keep_b, p_got_b, packed, got_packed
+    )
     got = swap(give, "batch", 4)
-    mine = keep[0].astype(F32) + got[0].astype(F32)
+    sent = add(packed, swap(packed, "batch", 4), give, BF16)
+    mine = keep.astype(F32) + got.astype(F32)
     first = 2 * width // bs
 
-    sent = packed
-    for bit in range(bs.bit_length() - 1):
-        sent = add(sent, swap(sent, "batch", 1 << bit), grad_tokens, BF16)
-    d_w2, d_taps, ln, d_w1, d_b1, d_cond = small_grads(
+    d_w2, d_taps, *ln, d_w1, d_b1, d_cond = small_grads(
         at, gather_freq(sent, me), freq_w1.shape[1], channels, step, bs
     )
-    d_ff = keep_ff.astype(F32) + got_ff.astype(F32)
     return (
         mixed_out[:, None],
         grad_tokens[:, None],
@@ -1427,9 +1487,9 @@
         mine[first:].T,
         ln[2],
         ln[3],
-        d_ff[0].T,
-        d_ff[1].T,
-        d_ff[2],
+        d_gate.T,
+        d_up.T,
+        d_down,
     )
 
 

time: 166 us -> 141 us (0.85); the launches traced: 165 us -> 138 us
  waiting for transfers between devices: 46.9 us -> 30.6 us
  local copies, waits for them, and re-layouts: 13.8 us -> 4.85 us
  Pallas kernels: 76 us -> 71.2 us
  starting transfers between devices: 27.3 us -> 29.8 us
    ppermute x38 -> x43, waiting for transfers between devices: 46.9 us -> 30.6 us  [swap(): return lax.ppermute(value, axis, [(i, i ^ mask) for i in range(count)])]
    unnamed x25 -> x19, local copies, waits for them, and re-layouts: 7.25 us -> 3.44 us
    another operation x4 -> x0, local copies, waits for them, and re-layouts: 2.76 us -> none  [tiled_device(): norms = jnp.stack([ln1_gain, ln1_shift, ln2_gain, ln2_shift])]
    pallas_call x11, Pallas kernels: 34.4 us -> 32.2 us  [the longest x1 13.6 us: backward_spectral(): pl.pallas_call(backward_kernel, in_specs=[SM, SM] + [VM] * 17 + [HBM], ou...]
    ppermute x38 -> x43, starting transfers between devices: 27.3 us -> 28.9 us  [swap(): return lax.ppermute(value, axis, [(i, i ^ mask) for i in range(count)])]
  transfers between devices with their start and end apart: 38 -> 44, of which waited for: 13 -> 20; matrix products, arithmetic and copies ran while one was open for 4% -> 3% of each run, Pallas kernels for 46% -> 49%
where the time goes in v3:
time: 141 us; the launch traced here: 138 us
  Pallas kernels  71.2 us (50%)
  waiting for transfers between devices  30.6 us (22%)
  starting transfers between devices  29.8 us (21%)
  local copies, waits for them, and re-layouts  4.85 us (3%)
    ppermute x43, waiting for transfers between devices, swap(): return lax.ppermute(value, axis, [(i, i ^ mask) for i in range(count)])  30.6 us
    ppermute x43, starting transfers between devices, swap(): return lax.ppermute(value, axis, [(i, i ^ mask) for i in range(count)])  28.9 us
    pallas_call x1, Pallas kernels, backward_spectral(): pl.pallas_call(backward_kernel, in_specs=[SM, SM] + [VM] * 17 + [HBM], ou...  13.6 us
    pallas_call x1, Pallas kernels, feed_forward(): pl.pallas_call(functools.partial(feed_kernel, piece=piece, thin=thin), gr...  13.5 us
    pallas_call x1, Pallas kernels, hidden_grads(): pl.pallas_call(hidden_grads_kernel, grid_spec=pltpu.PrefetchScalarGridSpe...  11.7 us
    pallas_call x1, Pallas kernels, forward_spectral(): pl.pallas_call(forward_kernel, in_specs=[SM, SM] + [VM] * 12, out_specs=[...  10.9 us
    pallas_call x1, Pallas kernels, select_columns(): pl.pallas_call(functools.partial(select_kernel, fs=fs), grid_spec=pltpu.P...  4.7 us
    pallas_call x1, Pallas kernels, prepare(): pl.pallas_call(functools.partial(prepare_kernel, step=step, fs=fs), in_sp...  4.08 us
  transfers between devices with their start and end apart: 44, of which 20 were waited for; matrix products, arithmetic and copies ran while one was open for 3% of the time, Pallas kernels for 49%

profile of v3, /device:TPU:2, one launch (start us, length us, event | category | flops | bytes accessed | tf_op | source)
XLA Modules:
  0.0 138.2 jit_solution(3422679827101930516)
XLA Ops:
  0.8 2.0 %collective-permute-start.17 = (bf16[256,768]{1,0:T(8,128)(2,1)}, bf16[256,768]{1,0:T(8,128)(2,1)S(1)}, u32[]{:S(2)}, u32[]{:S(2)}) collective-permute-start(bf16[256,768]{1,0:T(8,128)(2,1)} %bitcast.34), channel_id=1, source_target_pairs={{0,8},{4,12},{8,0},{12,4},{16,24},{20,28},{24,16},{28,20},{1,9},{5... | collective-permute-start | bytes 1179656 | tf_op jit(solution)/shard_map/ppermute | solution.py:33
  4.3 4.1 %prepare.1 = (bf16[384,768]{1,0:T(8,128)(2,1)S(1)}, bf16[384,192]{1,0:T(8,128)(2,1)S(1)}, bf16[64,384]{1,0:T(8,128)(2,1)S(1)}, f32[384,8]{1,0:T(8,128)S(1)}, f32...) custom-call(s32[5]{0:T(128)S(1)} %stack.23.me_ref.at_ref, bf16[768,1536]{1,0:T(8,128)(2,1)} %w_in.3, ...), custom_call_target="tpu_custom_call" | custom-call | flops 3000000000 | bytes 10500000 | tf_op jit(solution)/shard_map/prepare/pallas_call | solution.py:487
  8.5 3.3 %collective-permute-done.1.refs_0_ = bf16[256,768]{1,0:T(8,128)(2,1)S(1)} collective-permute-done((bf16[256,768]{1,0:T(8,128)(2,1)}, bf16[256,768]{1,0:T(8,128)(2,1)S(1)}, u32[]{:S(2)}, u32[]{:S(2)}) %collective-permute-start.1) | collective-permute-done | bytes 393248 | tf_op jit(solution)/shard_map/ppermute | solution.py:33
  13.5 10.9 %forward_spectral.1 = (bf16[192,256]{1,0:T(8,128)(2,1)S(1)}, bf16[192,256]{1,0:T(8,128)(2,1)S(1)}, bf16[192,256]{1,0:T(8,128)(2,1)S(1)}, bf16[192,256]{1,0:T(8,1...) custom-call(s32[5]{0:T(128)S(1)} %stack.23.me_ref.at_ref, ...), custom_call_target="tpu_custom_call" | custom-call | flops 15000000512 | bytes 52500000 | tf_op jit(solution)/shard_map/forward_spectral/pallas_call | solution.py:667
  24.5 1.6 %collective-permute-start.18 = (bf16[256,768]{1,0:T(8,128)(2,1)S(1)}, bf16[256,768]{1,0:T(8,128)(2,1)S(1)}, u32[]{:S(2)}, u32[]{:S(2)}) collective-permute-start(bf16[256,768]{1,0:T(8,128)(2,1)S(1)} %tie.6.refs_9_), channel_id=1, source_target_pairs={{0,8},{4,12},{8,0},{12,4},{16,24},{20,28},{24,16},{28,20},{1,9},{5... | collective-permute-start | bytes 1179656 | tf_op jit(solution)/shard_map/ppermute | solution.py:33
  28.0 4.7 %select_columns.1 = (bf16[384,768]{1,0:T(8,128)(2,1)S(1)}, bf16[384,768]{1,0:T(8,128)(2,1)S(1)}) custom-call(s32[5]{0:T(128)S(1)} %stack.23.me_ref.at_ref, f32[64,8]{1,0:T(8,128)S(1)} %get-tuple-element.110.after.refs_1_.cb, bf16[768,3072]{1,0:T(8,128)(2,1)} %gate.3, bf16[768,3072]{1,0:T(8,128)(2,1)} %up.3), custom_call_target="tpu_custom_call" | custom-call | flops 5000000000 | bytes 17500000 | tf_op jit(solution)/shard_map/select_columns/pallas_call | solution.py:521
  33.1 2.0 %middle.1 = (f32[256,768]{1,0:T(8,128)S(1)}, bf16[256,768]{1,0:T(8,128)(2,1)S(1)}, bf16[768,256]{1,0:T(8,128)(2,1)S(1)}) custom-call(s32[5]{0:T(128)S(1)} %stack.23.me_ref.at_ref, bf16[192,256]{1,0:T(8,128)(2,1)S(1)} %get-tuple-element.106.z0, bf16[192,256]{1,0:T(8,128)(2,1)S(1)} %collective-permute-done.3.z1, ...), custom_call_target="tpu_custom_call" | custom-call | flops 2000000000 | bytes 7000000 | tf_op jit(solution)/shard_map/middle/pallas_call | solution.py:820
  39.2 13.5 %feed_forward.1 = (bf16[256,768]{1,0:T(8,128)(2,1)}, f32[256,768]{1,0:T(8,128)S(1)}, bf16[192,256]{1,0:T(8,128)(2,1)S(1)}, bf16[192,256]{1,0:T(8,128)(2,1)S(1)},...) custom-call(s32[5]{0:T(128)S(1)} %stack.23.me_ref.at_ref, ...), custom_call_target="tpu_custom_call" | custom-call | flops 12999999488 | bytes 45500000 | tf_op jit(solution)/shard_map/feed_forward/pallas_call | solution.py:895
  53.3 2.4 %collective-permute-done.10.refs_1_ = bf16[256,768]{1,0:T(8,128)(2,1)S(1)} collective-permute-done((bf16[256,768]{1,0:T(8,128)(2,1)S(1)}, bf16[256,768]{1,0:T(8,128)(2,1)S(1)}, u32[]{:S(2)}, u32[]{:S(2)}) %collective-permute-start.10) | collective-permute-done | bytes 393248 | tf_op jit(solution)/shard_map/ppermute | solution.py:33
  61.7 11.7 %hidden_grads.1 = (bf16[2,3,96,512]{3,2,1,0:T(8,128)(2,1)S(1)}, bf16[2,3,96,512]{3,2,1,0:T(8,128)(2,1)S(1)}, bf16[2,3,96,256]{3,2,1,0:T(8,128)(2,1)S(1)}, bf16[2...) custom-call(s32[5]{0:T(128)S(1)} %stack.23.me_ref.at_ref, ...), custom_call_target="tpu_custom_call" | custom-call | flops 14000000000 | bytes 49000000 | tf_op jit(solution)/shard_map/hidden_grads/pallas_call | solution.py:976
  74.5 2.6 %collective-permute-start.30 = (bf16[2,3,96,256]{3,2,1,0:T(8,128)(2,1)S(1)}, bf16[2,3,96,256]{3,2,1,0:T(8,128)(2,1)S(1)}, u32[]{:S(2)}, u32[]{:S(2)}) collective-permute-start(bf16[2,3,96,256]{3,2,1,0:T(8,128)(2,1)S(1)} %get-tuple-element.156), channel_id=1, source_target_pairs={{0,16},{4,20},{8,24},{12,28},{16,0},{20,4},{24,8},{28,12},{1,17},{... | collective-permute-start | bytes 884744 | tf_op jit(solution)/shard_map/ppermute | solution.py:33
  78.6 13.6 %backward_spectral.1 = (bf16[400,256]{1,0:T(8,128)(2,1)S(1)}, bf16[400,256]{1,0:T(8,128)(2,1)S(1)}, bf16[400,256]{1,0:T(8,128)(2,1)S(1)}, bf16[400,256]{1,0:T(8,...) custom-call(s32[5]{0:T(128)S(1)} %stack.23.me_ref.at_ref, ...), custom_call_target="tpu_custom_call" | custom-call | flops 16999999488 | bytes 59500000 | tf_op jit(solution)/shard_map/backward_spectral/pallas_call | solution.py:786
  94.9 2.2 %projection_grads.1 = (bf16[4,72,512]{2,1,0:T(8,128)(2,1)S(1)}, bf16[4,72,512]{2,1,0:T(8,128)(2,1)S(1)}, bf16[2,2,72,256]{3,2,1,0:T(8,128)(2,1)S(1)}, bf16[2,2,7...) custom-call(s32[5]{0:T(128)S(1)} %stack.23.me_ref.at_ref, bf16[384,1024]{1,0:T(8,128)(2,1)S(1)} %get-tuple-element.143.after.gp, ...), custom_call_target="tpu_custom_call" | custom-call | flops 2000000000 | bytes 7000000 | tf_op jit(solution)/shard_map/projection_grads/pallas_call | solution.py:1171
  98.6 1.6 %collective-permute-done.26.p2 = bf16[400,256]{1,0:T(8,128)(2,1)S(1)} collective-permute-done((bf16[400,256]{1,0:T(8,128)(2,1)S(1)}, bf16[400,256]{1,0:T(8,128)(2,1)S(1)}, u32[]{:S(2)}, u32[]{:S(2)}) %collective-permute-start.26) | collective-permute-done | bytes 204832 | tf_op jit(solution)/shard_map/ppermute | solution.py:33
  100.8 2.9 %collective-permute-done.27.p3 = bf16[400,256]{1,0:T(8,128)(2,1)S(1)} collective-permute-done((bf16[400,256]{1,0:T(8,128)(2,1)S(1)}, bf16[400,256]{1,0:T(8,128)(2,1)S(1)}, u32[]{:S(2)}, u32[]{:S(2)}) %collective-permute-start.27) | collective-permute-done | bytes 204832 | tf_op jit(solution)/shard_map/ppermute | solution.py:33
  104.3 3.1 %final.1.after = f32[256,768]{1,0:T(8,128)S(1)} custom-call(s32[5]{0:T(128)S(1)} %stack.23.me_ref.at_ref, bf16[400,256]{1,0:T(8,128)(2,1)S(1)} %get-tuple-element.138.p0, bf16[400,256]{1,0:T(8,128)(2,1)S(1)} %collective-permute-done.25.p1, bf16[400,256]{1,0:T(8,128)(2,1)S(1)} %collective-permute-done.26.p2, bf16[400,256]{1,0:T(8,128)(2,1)S(1)} %collective-permute-done.27.p3, ...), custom_call_target="tpu_custom_call" | custom-call | flops 1000000000 | bytes 3500000 | tf_op jit(solution)/shard_map/final/pallas_call | solution.py:1222
  107.4 1.7 %collective-permute-done.35.refs_5_ = bf16[368,128]{1,0:T(8,128)(2,1)S(1)} collective-permute-done((bf16[368,128]{1,0:T(8,128)(2,1)S(1)}, bf16[368,128]{1,0:T(8,128)(2,1)S(1)}, u32[]{:S(2)}, u32[]{:S(2)}) %collective-permute-start.35) | collective-permute-done | bytes 94240 | tf_op jit(solution)/shard_map/ppermute | solution.py:33
  112.4 1.9 %collective-permute-done.31.got_a = bf16[1,3,96,512]{3,2,1,0:T(8,128)(2,1)S(1)} collective-permute-done((bf16[1,3,96,512]{3,2,1,0:T(8,128)(2,1)S(1)}, bf16[1,3,96,512]{3,2,1,0:T(8,128)(2,1)S(1)}, u32[]{:S(2)}, u32[]{:S(2)}) %collective-permute-start.31) | collective-permute-done | bytes 294944 | tf_op jit(solution)/shard_map/ppermute | solution.py:33
  116.2 3.1 %collective-permute-done.38.theirs = bf16[368,128]{1,0:T(8,128)(2,1)S(1)} collective-permute-done((bf16[368,128]{1,0:T(8,128)(2,1)S(1)}, bf16[368,128]{1,0:T(8,128)(2,1)S(1)}, u32[]{:S(2)}, u32[]{:S(2)}) %collective-permute-start.38) | collective-permute-done | bytes 94240 | tf_op jit(solution)/shard_map/ppermute | solution.py:33
  121.0 2.9 %collective-permute-start.43 = (bf16[72,768]{1,0:T(8,128)(2,1)S(1)}, bf16[72,768]{1,0:T(8,128)(2,1)S(1)}, u32[]{:S(2)}, u32[]{:S(2)}) collective-permute-start(bf16[72,768]{1,0:T(8,128)(2,1)S(1)} %get-tuple-element.173.after), channel_id=1, source_target_pairs={{0,16},{4,20},{8,24},{12,28},{16,0},{20,4},{24,8},{28,12},{1,17},{... | collective-permute-start | bytes 331784 | tf_op jit(solution)/shard_map/ppermute | solution.py:33
  123.9 1.7 %copy.45 = f32[256,1,768]{2,1,0:T(1,128)} copy(f32[256,1,768]{2,0,1:T(8,128)S(1)} %bitcast.26) | data formatting | bytes 1572864
  125.6 4.4 %collective-permute-done.39.theirs = bf16[368,128]{1,0:T(8,128)(2,1)S(1)} collective-permute-done((bf16[368,128]{1,0:T(8,128)(2,1)S(1)}, bf16[368,128]{1,0:T(8,128)(2,1)S(1)}, u32[]{:S(2)}, u32[]{:S(2)}) %collective-permute-start.39) | collective-permute-done | bytes 94240 | tf_op jit(solution)/shard_map/ppermute | solution.py:33
  132.9 1.7 %collective-permute-done.41.j2 = bf16[368,128]{1,0:T(8,128)(2,1)S(1)} collective-permute-done((bf16[368,128]{1,0:T(8,128)(2,1)S(1)}, bf16[368,128]{1,0:T(8,128)(2,1)S(1)}, u32[]{:S(2)}, u32[]{:S(2)}) %collective-permute-start.41) | collective-permute-done | bytes 94240 | tf_op jit(solution)/shard_map/ppermute | solution.py:33
  135.9 2.3 %small_grads.1 = (f32[64,1536]{1,0:T(8,128)}, f32[3,1536]{1,0:T(4,128)}, f32[768]{0:T(1024)}, f32[768]{0:T(1024)}, f32[768]{0:T(1024)}, /*index=5*/f32[768]{0:T(...) custom-call(s32[5]{0:T(128)S(1)} %stack.23.me_ref.at_ref, bf16[368,128]{1,0:T(8,128)(2,1)S(1)} %add.6.j0, ...), custom_call_target="tpu_custom_call" | custom-call | flops 3000000000 | bytes 10500000 | tf_op jit(solution)/shard_map/small_grads/pallas_call | solution.py:1311
  (108 shorter events, 35.2 us)
Async XLA Ops:
  0.6 11.1 %collective-permute-start.1 = (bf16[256,768]{1,0:T(8,128)(2,1)}, bf16[256,768]{1,0:T(8,128)(2,1)S(1)}, u32[]{:S(2)}, u32[]{:S(2)}) collective-permute-start(bf16[256,768]{1,0:T(8,128)(2,1)} %bitcast.29), channel_id=1, source_target_pairs={{0,2},{1,3},{2,0},{3,1},{4,6},{5,7},{6,4},{7,5},{8,10},{9,11},{10,... | collective-permute-start | bytes 1179656 | tf_op jit(solution)/shard_map/ppermute | solution.py:33
  0.7 12.1 %collective-permute-start = (bf16[256,768]{1,0:T(8,128)(2,1)}, bf16[256,768]{1,0:T(8,128)(2,1)S(1)}, u32[]{:S(2)}, u32[]{:S(2)}) collective-permute-start(bf16[256,768]{1,0:T(8,128)(2,1)} %bitcast.30), channel_id=1, source_target_pairs={{0,1},{1,0},{2,3},{3,2},{4,5},{5,4},{6,7},{7,6},{8,9},{9,8},{10,11... | collective-permute-start | bytes 1179656 | tf_op jit(solution)/shard_map/ppermute | solution.py:33
  0.8 12.0 %collective-permute-start.17 = (bf16[256,768]{1,0:T(8,128)(2,1)}, bf16[256,768]{1,0:T(8,128)(2,1)S(1)}, u32[]{:S(2)}, u32[]{:S(2)}) collective-permute-start(bf16[256,768]{1,0:T(8,128)(2,1)} %bitcast.34), channel_id=1, source_target_pairs={{0,8},{4,12},{8,0},{12,4},{16,24},{20,28},{24,16},{28,20},{1,9},{5... | collective-permute-start | bytes 1179656 | tf_op jit(solution)/shard_map/ppermute | solution.py:33
  11.8 12.7 %collective-permute-start.16 = (bf16[256,768]{1,0:T(8,128)(2,1)S(1)}, bf16[256,768]{1,0:T(8,128)(2,1)S(1)}, u32[]{:S(2)}, u32[]{:S(2)}) collective-permute-start(bf16[256,768]{1,0:T(8,128)(2,1)S(1)} %bitcast.35), channel_id=1, source_target_pairs={{0,2},{1,3},{2,0},{3,1},{4,6},{5,7},{6,4},{7,5},{8,10},{9,11},{10,... | collective-permute-start | bytes 1179656 | tf_op jit(solution)/shard_map/ppermute | solution.py:33
  24.5 28.2 %collective-permute-start.18 = (bf16[256,768]{1,0:T(8,128)(2,1)S(1)}, bf16[256,768]{1,0:T(8,128)(2,1)S(1)}, u32[]{:S(2)}, u32[]{:S(2)}) collective-permute-start(bf16[256,768]{1,0:T(8,128)(2,1)S(1)} %tie.6.refs_9_), channel_id=1, source_target_pairs={{0,8},{4,12},{8,0},{12,4},{16,24},{20,28},{24,16},{28,20},{1,9},{5... | collective-permute-start | bytes 1179656 | tf_op jit(solution)/shard_map/ppermute | solution.py:33
  35.1 23.1 %collective-permute-start.12 = (bf16[256,768]{1,0:T(8,128)(2,1)S(1)}, bf16[256,768]{1,0:T(8,128)(2,1)S(1)}, u32[]{:S(2)}, u32[]{:S(2)}) collective-permute-start(bf16[256,768]{1,0:T(8,128)(2,1)S(1)} %get-tuple-element.112.u2.refs_0_), channel_id=1, source_target_pairs={{0,1},{1,0},{2,3},{3,2},{4,5},{5,4},{6,7},{7,6},{8,9},{9,8},{10,11... | collective-permute-start | bytes 1179656 | tf_op jit(solution)/shard_map/ppermute | solution.py:33
  35.7 17.1 %collective-permute-start.11 = (bf16[256,768]{1,0:T(8,128)(2,1)S(1)}, bf16[256,768]{1,0:T(8,128)(2,1)S(1)}, u32[]{:S(2)}, u32[]{:S(2)}) collective-permute-start(bf16[256,768]{1,0:T(8,128)(2,1)S(1)} %get-tuple-element.112.u2.refs_0_), channel_id=1, source_target_pairs={{0,10},{1,11},{2,8},{3,9},{4,14},{5,15},{6,12},{7,13},{8,2},{9,3},... | collective-permute-start | bytes 1179656 | tf_op jit(solution)/shard_map/ppermute | solution.py:1397
  36.6 19.1 %collective-permute-start.10 = (bf16[256,768]{1,0:T(8,128)(2,1)S(1)}, bf16[256,768]{1,0:T(8,128)(2,1)S(1)}, u32[]{:S(2)}, u32[]{:S(2)}) collective-permute-start(bf16[256,768]{1,0:T(8,128)(2,1)S(1)} %get-tuple-element.112.u2.refs_0_), channel_id=1, source_target_pairs={{0,8},{4,12},{8,0},{12,4},{16,24},{20,28},{24,16},{28,20},{1,9},{5... | collective-permute-start | bytes 1179656 | tf_op jit(solution)/shard_map/ppermute | solution.py:33
  38.2 17.9 %collective-permute-start.9 = (bf16[256,768]{1,0:T(8,128)(2,1)S(1)}, bf16[256,768]{1,0:T(8,128)(2,1)S(1)}, u32[]{:S(2)}, u32[]{:S(2)}) collective-permute-start(bf16[256,768]{1,0:T(8,128)(2,1)S(1)} %get-tuple-element.112.u2.refs_0_), channel_id=1, source_target_pairs={{0,2},{1,3},{2,0},{3,1},{4,6},{5,7},{6,4},{7,5},{8,10},{9,11},{10,... | collective-permute-start | bytes 1179656 | tf_op jit(solution)/shard_map/ppermute | solution.py:33
  59.5 17.6 %collective-permute-start.6 = (bf16[192,256]{1,0:T(8,128)(2,1)S(1)}, bf16[192,256]{1,0:T(8,128)(2,1)S(1)}, u32[]{:S(2)}, u32[]{:S(2)}) collective-permute-start(bf16[192,256]{1,0:T(8,128)(2,1)S(1)} %get-tuple-element.116), channel_id=1, source_target_pairs={{0,1},{1,0},{2,3},{3,2},{4,5},{5,4},{6,7},{7,6},{8,9},{9,8},{10,11... | collective-permute-start | bytes 294920 | tf_op jit(solution)/shard_map/ppermute | solution.py:33
  60.0 18.6 %collective-permute-start.7 = (bf16[192,256]{1,0:T(8,128)(2,1)S(1)}, bf16[192,256]{1,0:T(8,128)(2,1)S(1)}, u32[]{:S(2)}, u32[]{:S(2)}) collective-permute-start(bf16[192,256]{1,0:T(8,128)(2,1)S(1)} %get-tuple-element.117), channel_id=1, source_target_pairs={{0,2},{1,3},{2,0},{3,1},{4,6},{5,7},{6,4},{7,5},{8,10},{9,11},{10,... | collective-permute-start | bytes 294920 | tf_op jit(solution)/shard_map/ppermute | solution.py:33
  61.0 17.6 %collective-permute-start.8 = (bf16[192,256]{1,0:T(8,128)(2,1)S(1)}, bf16[192,256]{1,0:T(8,128)(2,1)S(1)}, u32[]{:S(2)}, u32[]{:S(2)}) collective-permute-start(bf16[192,256]{1,0:T(8,128)(2,1)S(1)} %get-tuple-element.118), channel_id=1, source_target_pairs={{0,3},{1,2},{2,1},{3,0},{4,7},{5,6},{6,5},{7,4},{8,11},{9,10},{10,... | collective-permute-start | bytes 294920 | tf_op jit(solution)/shard_map/ppermute | solution.py:33
  73.5 21.4 %collective-permute-start.28 = (bf16[192,768]{1,0:T(8,128)(2,1)S(1)}, bf16[192,768]{1,0:T(8,128)(2,1)S(1)}, u32[]{:S(2)}, u32[]{:S(2)}) collective-permute-start(bf16[192,768]{1,0:T(8,128)(2,1)S(1)} %get-tuple-element.147), channel_id=1, source_target_pairs={{0,2},{1,3},{2,0},{3,1},{4,6},{5,7},{6,4},{7,5},{8,10},{9,11},{10,... | collective-permute-start | bytes 884744 | tf_op jit(solution)/shard_map/ppermute | solution.py:33
  74.5 18.9 %collective-permute-start.30 = (bf16[2,3,96,256]{3,2,1,0:T(8,128)(2,1)S(1)}, bf16[2,3,96,256]{3,2,1,0:T(8,128)(2,1)S(1)}, u32[]{:S(2)}, u32[]{:S(2)}) collective-permute-start(bf16[2,3,96,256]{3,2,1,0:T(8,128)(2,1)S(1)} %get-tuple-element.156), channel_id=1, source_target_pairs={{0,16},{4,20},{8,24},{12,28},{16,0},{20,4},{24,8},{28,12},{1,17},{... | collective-permute-start | bytes 884744 | tf_op jit(solution)/shard_map/ppermute | solution.py:33
  77.1 17.0 %collective-permute-start.29 = (bf16[2,3,96,512]{3,2,1,0:T(8,128)(2,1)S(1)}, bf16[2,3,96,512]{3,2,1,0:T(8,128)(2,1)S(1)}, u32[]{:S(2)}, u32[]{:S(2)}) collective-permute-start(bf16[2,3,96,512]{3,2,1,0:T(8,128)(2,1)S(1)} %get-tuple-element.137.after), channel_id=1, source_target_pairs={{0,4},{4,0},{8,12},{12,8},{16,20},{20,16},{24,28},{28,24},{1,5},{5... | collective-permute-start | bytes 1769480 | tf_op jit(solution)/shard_map/ppermute | solution.py:33
  93.4 10.3 %collective-permute-start.27 = (bf16[400,256]{1,0:T(8,128)(2,1)S(1)}, bf16[400,256]{1,0:T(8,128)(2,1)S(1)}, u32[]{:S(2)}, u32[]{:S(2)}) collective-permute-start(bf16[400,256]{1,0:T(8,128)(2,1)S(1)} %get-tuple-element.141), channel_id=1, source_target_pairs={{0,3},{1,2},{2,1},{3,0},{4,7},{5,6},{6,5},{7,4},{8,11},{9,10},{10,... | collective-permute-start | bytes 614408 | tf_op jit(solution)/shard_map/ppermute | solution.py:33
  97.2 11.9 %collective-permute-start.33 = (bf16[4,72,512]{2,1,0:T(8,128)(2,1)S(1)}, bf16[4,72,512]{2,1,0:T(8,128)(2,1)S(1)}, u32[]{:S(2)}, u32[]{:S(2)}) collective-permute-start(bf16[4,72,512]{2,1,0:T(8,128)(2,1)S(1)} %get-tuple-element.163), channel_id=1, source_target_pairs={{0,4},{4,0},{8,12},{12,8},{16,20},{20,16},{24,28},{28,24},{1,5},{5... | collective-permute-start | bytes 884744 | tf_op jit(solution)/shard_map/ppermute | solution.py:33
  97.8 11.3 %collective-permute-start.34 = (bf16[2,2,72,256]{3,2,1,0:T(8,128)(2,1)S(1)}, bf16[2,2,72,256]{3,2,1,0:T(8,128)(2,1)S(1)}, u32[]{:S(2)}, u32[]{:S(2)}) collective-permute-start(bf16[2,2,72,256]{3,2,1,0:T(8,128)(2,1)S(1)} %get-tuple-element.165), channel_id=1, source_target_pairs={{0,8},{4,12},{8,0},{12,4},{16,24},{20,28},{24,16},{28,20},{1,9},{5... | collective-permute-start | bytes 442376 | tf_op jit(solution)/shard_map/ppermute | solution.py:33
  98.2 16.1 %collective-permute-start.31 = (bf16[1,3,96,512]{3,2,1,0:T(8,128)(2,1)S(1)}, bf16[1,3,96,512]{3,2,1,0:T(8,128)(2,1)S(1)}, u32[]{:S(2)}, u32[]{:S(2)}) collective-permute-start(bf16[1,3,96,512]{3,2,1,0:T(8,128)(2,1)S(1)} %get-tuple-element.157.after), channel_id=1, source_target_pairs={{0,16},{4,20},{8,24},{12,28},{16,0},{20,4},{24,8},{28,12},{1,17},{... | collective-permute-start | bytes 884744 | tf_op jit(solution)/shard_map/ppermute | solution.py:33
  100.2 8.8 %collective-permute-start.35 = (bf16[368,128]{1,0:T(8,128)(2,1)S(1)}, bf16[368,128]{1,0:T(8,128)(2,1)S(1)}, u32[]{:S(2)}, u32[]{:S(2)}) collective-permute-start(bf16[368,128]{1,0:T(8,128)(2,1)S(1)} %get-tuple-element.158.after.refs_4_), channel_id=1, source_target_pairs={{0,4},{4,0},{8,12},{12,8},{16,20},{20,16},{24,28},{28,24},{1,5},{5... | collective-permute-start | bytes 282632 | tf_op jit(solution)/shard_map/ppermute | solution.py:33
  109.8 9.6 %collective-permute-start.36 = (bf16[2,72,512]{2,1,0:T(8,128)(2,1)S(1)}, bf16[2,72,512]{2,1,0:T(8,128)(2,1)S(1)}, u32[]{:S(2)}, u32[]{:S(2)}) collective-permute-start(bf16[2,72,512]{2,1,0:T(8,128)(2,1)S(1)} %get-tuple-element.169), channel_id=1, source_target_pairs={{0,8},{4,12},{8,0},{12,4},{16,24},{20,28},{24,16},{28,20},{1,9},{5... | collective-permute-start | bytes 442376 | tf_op jit(solution)/shard_map/ppermute | solution.py:33
  110.3 9.0 %collective-permute-start.38 = (bf16[368,128]{1,0:T(8,128)(2,1)S(1)}, bf16[368,128]{1,0:T(8,128)(2,1)S(1)}, u32[]{:S(2)}, u32[]{:S(2)}) collective-permute-start(bf16[368,128]{1,0:T(8,128)(2,1)S(1)} %get-tuple-element.166.after.ours), channel_id=1, source_target_pairs={{0,8},{4,12},{8,0},{12,4},{16,24},{20,28},{24,16},{28,20},{1,9},{5... | collective-permute-start | bytes 282632 | tf_op jit(solution)/shard_map/ppermute | solution.py:33
  120.9 9.1 %collective-permute-start.39 = (bf16[368,128]{1,0:T(8,128)(2,1)S(1)}, bf16[368,128]{1,0:T(8,128)(2,1)S(1)}, u32[]{:S(2)}, u32[]{:S(2)}) collective-permute-start(bf16[368,128]{1,0:T(8,128)(2,1)S(1)} %get-tuple-element.172.ours), channel_id=1, source_target_pairs={{0,16},{4,20},{8,24},{12,28},{16,0},{20,4},{24,8},{28,12},{1,17},{... | collective-permute-start | bytes 282632 | tf_op jit(solution)/shard_map/ppermute | solution.py:33
  121.0 11.3 %collective-permute-start.43 = (bf16[72,768]{1,0:T(8,128)(2,1)S(1)}, bf16[72,768]{1,0:T(8,128)(2,1)S(1)}, u32[]{:S(2)}, u32[]{:S(2)}) collective-permute-start(bf16[72,768]{1,0:T(8,128)(2,1)S(1)} %get-tuple-element.173.after), channel_id=1, source_target_pairs={{0,16},{4,20},{8,24},{12,28},{16,0},{20,4},{24,8},{28,12},{1,17},{... | collective-permute-start | bytes 331784 | tf_op jit(solution)/shard_map/ppermute | solution.py:33
  (27 other events, 127.1 us)

commit v4 on v3

--- a/solution.py
+++ b/solution.py
@@ -609,11 +609,13 @@
                 lo = j * width + (r - 2) * chunk
                 vm[lo : lo + chunk, :] = (mixed * member[j : j + 1, :]).astype(BF16)
 
-    @pl.loop(0, tiles)
+    span = 2 * quarter
+
+    @pl.loop(0, length // span)
     def _(f):
-        lanes = tile(f, quarter)
-        upper = pl.ds(pl.multiple_of(f * quarter + length, quarter), quarter)
-        weight = bin_weights(f * quarter, quarter, length)
+        lanes = tile(f, span)
+        upper = pl.ds(pl.multiple_of(f * span + length, span), span)
+        weight = bin_weights(f * span, span, length)
         vr_all = mm(vm[...], waves[:length, lanes])
         vs_all = mm(vm[...], waves[length:, lanes])
         vr_out[:, lanes] = vr_all.astype(BF16)
@@ -705,11 +707,13 @@
     d_w1[...] = jnp.zeros_like(d_w1)
     gcb[...] = jnp.zeros_like(gcb)
 
-    @pl.loop(0, tiles)
+    span = 2 * quarter
+
+    @pl.loop(0, length // span)
     def _(f):
-        lanes = tile(f, quarter)
-        upper = pl.ds(pl.multiple_of(f * quarter + length, quarter), quarter)
-        weight = bin_weights(f * quarter, quarter, length)
+        lanes = tile(f, span)
+        upper = pl.ds(pl.multiple_of(f * span + length, span), span)
+        weight = bin_weights(f * span, span, length)
         gyr_all = mm(gcm[...], waves[:length, lanes]) * weight
         gys_all = mm(gcm[...], waves[length:, lanes]) * weight
         for j in range(SEGS):
@@ -996,12 +1000,8 @@
     )(at, *u2_parts, *ct_parts, gate, up, gt_own, gt_got, z_own, z_got, in_hbm(down), after)
 
 
-def halve_kernel(at_ref, after, *refs, bits, extra):
+def halve_kernel(at_ref, after, *refs, bits):
     pairs = len(bits)
-    if extra:
-        ours, theirs, out = refs[2 * pairs], refs[2 * pairs + 1], refs[-1]
-        out[...] = (ours[...].astype(F32) + theirs[...].astype(F32)).astype(BF16)
-        refs = refs[: 2 * pairs] + refs[2 * pairs + 2 : -1]
     ins, outs = refs[: 2 * pairs], refs[2 * pairs :]
     for n in range(pairs):
         mine = at_ref[bits[n] + 1]
@@ -1014,14 +1014,11 @@
 
 def halve(at, bits, after, *sums):
     outs = []
-    extra = len(sums) > 2 * len(bits)
     for n in range(len(bits)):
         dims = sums[2 * n].shape
         outs += [shape((dims[0],) + dims[2:], BF16)] * 2
-    if extra:
-        outs.append(shape(sums[-1].shape, BF16))
     return pl.pallas_call(
-        functools.partial(halve_kernel, bits=bits, extra=extra),
+        functools.partial(halve_kernel, bits=bits),
         in_specs=[SM, HBM] + [VM] * len(sums),
         out_specs=[VM] * len(outs),
         out_shape=outs,
@@ -1031,28 +1028,97 @@
     )(at, after, *sums)
 
 
-def join_kernel(at_ref, after, keep_a, got_a, keep_b, got_b, ours, theirs, keep, give, total):
-    total[...] = (ours[...].astype(F32) + theirs[...].astype(F32)).astype(BF16)
-    cut = keep_a.shape[-1]
+def load_riders(blocks, first, rows):
+    parts = []
+    for i in range(blocks.shape[0]):
+        for m in range(blocks.shape[2] // 128):
+            parts.append(blocks[i, first : first + rows, m * 128 : (m + 1) * 128].astype(F32))
+    return jnp.concatenate(parts, axis=0)
+
+
+def store_riders(block, packed, i, first, rows):
+    columns = block.shape[1] // 128
+    for m in range(columns):
+        lo = (columns * i + m) * rows
+        block[first : first + rows, m * 128 : (m + 1) * 128] = packed[lo : lo + rows, :]
+
+
+def stage_kernel(
+    at_ref, after, keep_a, got_a, keep_b, got_b, ours,
+    next_keep_a, next_give_a, next_keep_b, next_give_b, total, joined, block,
+):
+    y, z = at_ref[1], at_ref[2]
+    tall, rows = keep_a.shape[2], next_give_a.shape[1]
+    flat = got_a.shape[2]
+    columns = got_a.shape[3] // 128
+    riders = joined.shape[0] // (4 * columns)
+    start = flat - riders
+    for i in range(2):
+        for k in range(2):
+            for m in range(columns):
+                lo = (columns * (2 * i + k) + m) * riders
+                piece = got_a[i, k, start:flat, m * 128 : (m + 1) * 128]
+                joined[lo : lo + riders, :] = ours[lo : lo + riders, :].astype(F32) + piece.astype(F32)
+    total[...] = joined[...].astype(BF16)
+    for i in range(2):
+        next_keep_a[i] = (keep_a[i, z].astype(F32) + got_a[i, z, :tall].astype(F32)).astype(BF16)
+        block[...] = jnp.zeros_like(block)
+        block[:tall, :] = keep_a[i, 1 - z].astype(F32) + got_a[i, 1 - z, :tall].astype(F32)
+        store_riders(block, joined, i, rows - 2 * riders, 2 * riders)
+        next_give_a[i] = block[...].astype(BF16)
+        for side, out in ((y, next_keep_b), (1 - y, next_give_b)):
+            out[i] = (keep_b[i, side].astype(F32) + got_b[i, side].astype(F32)).astype(BF16)
+
+
+def stage(at, after, keep_a, got_a, keep_b, got_b, ours):
+    _, _, tall, lanes = keep_a.shape
+    narrow = keep_b.shape[-1]
+    riders = ours.shape[0] // (4 * (lanes // 128))
+    rows = got_a.shape[2] + riders
+    return pl.pallas_call(
+        stage_kernel,
+        in_specs=[SM, HBM] + [VM] * 5,
+        out_specs=[VM] * 5,
+        out_shape=[
+            shape((2, tall, lanes), BF16),
+            shape((2, rows, lanes), BF16),
+            shape((2, tall, narrow), BF16),
+            shape((2, tall, narrow), BF16),
+            shape(ours.shape, BF16),
+        ],
+        scratch_shapes=[pltpu.VMEM(ours.shape, F32), pltpu.VMEM((rows, lanes), F32)],
+        compiler_params=params(12),
+        cost_estimate=cost(0.3),
+        name="stage",
+    )(at, after, keep_a, got_a, keep_b, got_b, ours)
+
+
+def join_kernel(at_ref, after, keep_a, got_a, keep_b, got_b, ours, keep, give, total):
+    tall, cut = keep_a.shape[1:]
+    riders = ours.shape[0] // (2 * (cut // 128))
+    start = got_a.shape[1] - riders
+    total[...] = (ours[...].astype(F32) + load_riders(got_a, start, riders)).astype(BF16)
     for side, out in ((at_ref[3], keep), (1 - at_ref[3], give)):
-        out[:, :cut] = (keep_a[side].astype(F32) + got_a[side].astype(F32)).astype(BF16)
+        out[:, :cut] = (keep_a[side].astype(F32) + got_a[side, :tall].astype(F32)).astype(BF16)
         out[:, cut:] = (keep_b[side].astype(F32) + got_b[side].astype(F32)).astype(BF16)
 
 
-def join(at, after, keep_a, got_a, keep_b, got_b, ours, theirs):
+def join(at, after, keep_a, got_a, keep_b, got_b, ours):
     _, rows, cut = keep_a.shape
     return pl.pallas_call(
         join_kernel,
-        in_specs=[SM, HBM] + [VM] * 6,
+        in_specs=[SM, HBM] + [VM] * 5,
         out_specs=[VM] * 3,
         out_shape=[shape((rows, cut + keep_b.shape[-1]), BF16)] * 2 + [shape(ours.shape, BF16)],
         compiler_params=params(12),
         cost_estimate=cost(0.3),
         name="join",
-    )(at, after, keep_a, got_a, keep_b, got_b, ours, theirs)
+    )(at, after, keep_a, got_a, keep_b, got_b, ours)
 
 
 def hidden_last_kernel(keep_a, got_a, keep_b, got_b, after, *outs):
+    *outs, token = outs
+    token[...] = jnp.zeros_like(token)
     cut = keep_a.shape[-1]
     for m, out in enumerate(outs):
         out[:, :cut] = keep_a[0, m].astype(F32) + got_a[0, m].astype(F32)
@@ -1064,8 +1130,8 @@
     return pl.pallas_call(
         hidden_last_kernel,
         in_specs=[VM] * 4 + [HBM],
-        out_specs=[VM] * count,
-        out_shape=[far((rows, cut + keep_b.shape[-1]), F32)] * count,
+        out_specs=[VM] * (count + 1),
+        out_shape=[far((rows, cut + keep_b.shape[-1]), F32)] * count + [shape((8, 128), F32)],
         compiler_params=params(12),
         cost_estimate=cost(0.3),
         name="hidden_last",
@@ -1090,7 +1156,7 @@
 
 def projection_kernel(
     at_ref, gp, u1, n1, w_mine, keep_o, got_o, d_w2, d_w1, d_taps, gcb, condt, mu, mn,
-    sums2, after, keep_a, give_a, keep_b, give_b, packed_out, d_in, d_out, packed, *, layout,
+    sums2, after, keep_a, give_a, keep_b, give_b, packed_out, d_in, d_out, packed, sheet, *, layout,
 ):
     me, y, zbit = at_ref[0], at_ref[1], at_ref[2]
     channels = u1.shape[1]
@@ -1100,7 +1166,7 @@
     blocks = 2 * keep_a.shape[0]
     first = 2 * width // blocks
     second = width // blocks
-    cut = 2 * channels // 3
+    cut = channels // 2
 
     def put(out, block, lanes):
         lo = pl.multiple_of(block * first, first)
@@ -1110,7 +1176,6 @@
 
     for b in range(blocks // 2):
         put(keep_a.at[b], 2 * b + y, slice(0, cut))
-        put(give_a.at[b], 2 * b + 1 - y, slice(0, cut))
     for b in range(blocks // 4):
         for i in range(2):
             put(keep_b.at[b, i], 4 * b + 2 * zbit + i, slice(cut, channels))
@@ -1151,6 +1216,15 @@
     block = jnp.concatenate([share[:SEGS, :128], rest, jnp.zeros((8 - 2 * SEGS, 128), F32)], axis=0)
     packed[pl.ds(pl.multiple_of(layout["mu"] + 8 * row, 8), 8), :] = block
     packed_out[...] = packed[...].astype(BF16)
+    riders = packed.shape[0] // (4 * (cut // 128))
+    for b in range(blocks // 2):
+        sheet[...] = jnp.zeros_like(sheet)
+        lo = pl.multiple_of((2 * b + 1 - y) * first, first)
+        sheet[:first, :] = d_in[pl.ds(lo, first), :cut]
+        lo = pl.multiple_of((2 * b + 1 - y) * second, second)
+        sheet[first : first + second, :] = d_out[pl.ds(lo, second), :cut]
+        store_riders(sheet, packed, b, sheet.shape[0] - riders, riders)
+        give_a[b] = sheet[...].astype(BF16)
 
 
 def packed_layout(width, channels, bs):
@@ -1159,7 +1233,7 @@
     w1 = -(-(ln + 4 * (channels // 128)) // 8) * 8
     cb = w1 + 32
     mu = cb + 4 * bs
-    return {"taps": taps, "ln": ln, "w1": w1, "cb": cb, "mu": mu, "rows": -(-(mu + 8 * bs) // 16) * 16}
+    return {"taps": taps, "ln": ln, "w1": w1, "cb": cb, "mu": mu, "rows": -(-(mu + 8 * bs) // 128) * 128}
 
 
 def projection_grads(
@@ -1168,17 +1242,23 @@
     length, channels = u1.shape
     width = keep_o.shape[0]
     layout = packed_layout(width, channels, bs)
+    tall = 3 * width // bs
+    flat = -(-tall // 16) * 16 + layout["rows"] // (4 * (channels // 256))
     return pl.pallas_call(
         functools.partial(projection_kernel, layout=layout),
         in_specs=[SM] + [VM] * 14 + [HBM],
         out_specs=[VM] * 5,
-        out_shape=[shape((bs // 2, 3 * width // bs, 2 * channels // 3), BF16)] * 2
-        + [shape((bs // 4, 2, 3 * width // bs, channels // 3), BF16)] * 2
+        out_shape=[
+            shape((bs // 2, tall, channels // 2), BF16),
+            shape((bs // 2, flat, channels // 2), BF16),
+        ]
+        + [shape((bs // 4, 2, 3 * width // bs, channels // 2), BF16)] * 2
         + [shape((layout["rows"], 128), BF16)],
         scratch_shapes=[
             pltpu.VMEM((2 * width, channels), F32),
             pltpu.VMEM((width, channels), F32),
             pltpu.VMEM((layout["rows"], 128), F32),
+            pltpu.VMEM((flat, channels // 2), F32),
         ],
         compiler_params=params(24),
         cost_estimate=cost(2),
@@ -1226,7 +1306,7 @@
         out_shape=shape((quarter, channels), F32),
         scratch_shapes=[pltpu.VMEM((2 * channels, quarter), BF16)],
         compiler_params=params(24),
-        cost_estimate=cost(1),
+        cost_estimate=cost(0.3),
         name="final",
     )(me, *gp_parts, x, big_g, norms, ids, condt, in_hbm(w_in), after)
 
@@ -1452,19 +1532,14 @@
     p_keep_a, p_give_a, p_keep_b, p_give_b, packed = proj
     p_got_a = swap(p_give_a, "batch", 1)
     p_got_b = swap(p_give_b, "batch", 2)
-    got_packed = swap(packed, "batch", 1)
-    grad_tokens = final(at, gp_got, x_own, big_g, norms, ids, condt, w_in, packed, step)
-
-    p_keep_a, p_give_a, p_keep_b, p_give_b, packed = halve(
-        at, (1, 0), grad_tokens, pairs(p_keep_a), pairs(p_got_a), p_keep_b, p_got_b, packed, got_packed
+    p_keep_a, p_give_a, p_keep_b, p_give_b, packed = stage(
+        at, p_give_a, pairs(p_keep_a), pairs(p_got_a), p_keep_b, p_got_b, packed
     )
     p_got_a = swap(p_give_a, "batch", 2)
     p_got_b = swap(p_give_b, "batch", 1)
-    got_packed = swap(packed, "batch", 2)
-    d_gate, d_up, d_down = hidden_last(keep_a, got_a, keep_b, got_b, packed)
-    keep, give, packed = join(
-        at, d_down, p_keep_a, p_got_a, p_keep_b, p_got_b, packed, got_packed
-    )
+    d_gate, d_up, d_down, token = hidden_last(keep_a, got_a, keep_b, got_b, packed)
+    keep, give, packed = join(at, token, p_keep_a, p_got_a, p_keep_b, p_got_b, packed)
+    grad_tokens = final(at, gp_got, x_own, big_g, norms, ids, condt, w_in, packed, step)
     got = swap(give, "batch", 4)
     sent = add(packed, swap(packed, "batch", 4), give, BF16)
     mine = keep.astype(F32) + got.astype(F32)

time: 141 us -> 136 us (0.965)
  starting transfers between devices: 29.8 us -> 28.2 us
    ppermute x43 -> x41, starting transfers between devices: 28.9 us -> 27.3 us  [swap(): return lax.ppermute(value, axis, [(i, i ^ mask) for i in range(count)])]
    ppermute x43 -> x41, waiting for transfers between devices: 30.6 us -> 29.2 us  [swap(): return lax.ppermute(value, axis, [(i, i ^ mask) for i in range(count)])]
    unnamed x19 -> x17, local copies, waits for them, and re-layouts: 3.44 us -> 2.48 us
  transfers between devices with their start and end apart: 44 -> 42, of which waited for: 20 -> 19; matrix products, arithmetic and copies ran while one was open for 3% -> 3% of each run, Pallas kernels for 49% -> 49%
where the time goes in v4:
time: 136 us; the launch traced here: 133 us
  Pallas kernels  70.3 us (52%)
  waiting for transfers between devices  29.2 us (21%)
  starting transfers between devices  28.2 us (21%)
  local copies, waits for them, and re-layouts  3.88 us (3%)
    ppermute x41, waiting for transfers between devices, swap(): return lax.ppermute(value, axis, [(i, i ^ mask) for i in range(count)])  29.2 us
    ppermute x41, starting transfers between devices, swap(): return lax.ppermute(value, axis, [(i, i ^ mask) for i in range(count)])  27.3 us
    pallas_call x1, Pallas kernels, feed_forward(): pl.pallas_call(functools.partial(feed_kernel, piece=piece, thin=thin), gr...  13.5 us
    pallas_call x1, Pallas kernels, backward_spectral(): pl.pallas_call(backward_kernel, in_specs=[SM, SM] + [VM] * 17 + [HBM], ou...  13 us
    pallas_call x1, Pallas kernels, hidden_grads(): pl.pallas_call(hidden_grads_kernel, grid_spec=pltpu.PrefetchScalarGridSpe...  11.7 us
    pallas_call x1, Pallas kernels, forward_spectral(): pl.pallas_call(forward_kernel, in_specs=[SM, SM] + [VM] * 12, out_specs=[...  10.6 us
    pallas_call x1, Pallas kernels, select_columns(): pl.pallas_call(functools.partial(select_kernel, fs=fs), grid_spec=pltpu.P...  4.7 us
    pallas_call x1, Pallas kernels, prepare(): pl.pallas_call(functools.partial(prepare_kernel, step=step, fs=fs), in_sp...  4.08 us
  transfers between devices with their start and end apart: 42, of which 19 were waited for; matrix products, arithmetic and copies ran while one was open for 3% of the time, Pallas kernels for 49%

profile of v4, /device:TPU:2, one launch (start us, length us, event | category | flops | bytes accessed | tf_op | source)
XLA Modules:
  0.0 133.3 jit_solution(15576180646888589128)
XLA Ops:
  0.8 2.0 %collective-permute-start.17 = (bf16[256,768]{1,0:T(8,128)(2,1)}, bf16[256,768]{1,0:T(8,128)(2,1)S(1)}, u32[]{:S(2)}, u32[]{:S(2)}) collective-permute-start(bf16[256,768]{1,0:T(8,128)(2,1)} %bitcast.34), channel_id=1, source_target_pairs={{0,8},{4,12},{8,0},{12,4},{16,24},{20,28},{24,16},{28,20},{1,9},{5... | collective-permute-start | bytes 1179656 | tf_op jit(solution)/shard_map/ppermute | solution.py:33
  4.3 4.1 %prepare.1 = (bf16[384,768]{1,0:T(8,128)(2,1)S(1)}, bf16[384,192]{1,0:T(8,128)(2,1)S(1)}, bf16[64,384]{1,0:T(8,128)(2,1)S(1)}, f32[384,8]{1,0:T(8,128)S(1)}, f32...) custom-call(s32[5]{0:T(128)S(1)} %stack.23.me_ref.at_ref, bf16[768,1536]{1,0:T(8,128)(2,1)} %w_in.3, ...), custom_call_target="tpu_custom_call" | custom-call | flops 3000000000 | bytes 10500000 | tf_op jit(solution)/shard_map/prepare/pallas_call | solution.py:487
  8.5 3.3 %collective-permute-done.1.refs_0_ = bf16[256,768]{1,0:T(8,128)(2,1)S(1)} collective-permute-done((bf16[256,768]{1,0:T(8,128)(2,1)}, bf16[256,768]{1,0:T(8,128)(2,1)S(1)}, u32[]{:S(2)}, u32[]{:S(2)}) %collective-permute-start.1) | collective-permute-done | bytes 393248 | tf_op jit(solution)/shard_map/ppermute | solution.py:33
  13.5 10.6 %forward_spectral.1 = (bf16[192,256]{1,0:T(8,128)(2,1)S(1)}, bf16[192,256]{1,0:T(8,128)(2,1)S(1)}, bf16[192,256]{1,0:T(8,128)(2,1)S(1)}, bf16[192,256]{1,0:T(8,1...) custom-call(s32[5]{0:T(128)S(1)} %stack.23.me_ref.at_ref, ...), custom_call_target="tpu_custom_call" | custom-call | flops 15000000512 | bytes 52500000 | tf_op jit(solution)/shard_map/forward_spectral/pallas_call | solution.py:669
  24.2 1.6 %collective-permute-start.18 = (bf16[256,768]{1,0:T(8,128)(2,1)S(1)}, bf16[256,768]{1,0:T(8,128)(2,1)S(1)}, u32[]{:S(2)}, u32[]{:S(2)}) collective-permute-start(bf16[256,768]{1,0:T(8,128)(2,1)S(1)} %tie.6.refs_9_), channel_id=1, source_target_pairs={{0,8},{4,12},{8,0},{12,4},{16,24},{20,28},{24,16},{28,20},{1,9},{5... | collective-permute-start | bytes 1179656 | tf_op jit(solution)/shard_map/ppermute | solution.py:33
  27.7 4.7 %select_columns.1 = (bf16[384,768]{1,0:T(8,128)(2,1)S(1)}, bf16[384,768]{1,0:T(8,128)(2,1)S(1)}) custom-call(s32[5]{0:T(128)S(1)} %stack.23.me_ref.at_ref, f32[64,8]{1,0:T(8,128)S(1)} %get-tuple-element.111.after.refs_1_.cb, bf16[768,3072]{1,0:T(8,128)(2,1)} %gate.3, bf16[768,3072]{1,0:T(8,128)(2,1)} %up.3), custom_call_target="tpu_custom_call" | custom-call | flops 5000000000 | bytes 17500000 | tf_op jit(solution)/shard_map/select_columns/pallas_call | solution.py:521
  32.8 2.0 %middle.1 = (f32[256,768]{1,0:T(8,128)S(1)}, bf16[256,768]{1,0:T(8,128)(2,1)S(1)}, bf16[768,256]{1,0:T(8,128)(2,1)S(1)}) custom-call(s32[5]{0:T(128)S(1)} %stack.23.me_ref.at_ref, bf16[192,256]{1,0:T(8,128)(2,1)S(1)} %get-tuple-element.107.z0, bf16[192,256]{1,0:T(8,128)(2,1)S(1)} %collective-permute-done.3.z1, ...), custom_call_target="tpu_custom_call" | custom-call | flops 2000000000 | bytes 7000000 | tf_op jit(solution)/shard_map/middle/pallas_call | solution.py:824
  36.3 1.6 %collective-permute-start.10 = (bf16[256,768]{1,0:T(8,128)(2,1)S(1)}, bf16[256,768]{1,0:T(8,128)(2,1)S(1)}, u32[]{:S(2)}, u32[]{:S(2)}) collective-permute-start(bf16[256,768]{1,0:T(8,128)(2,1)S(1)} %get-tuple-element.113.u2.refs_0_), channel_id=1, source_target_pairs={{0,8},{4,12},{8,0},{12,4},{16,24},{20,28},{24,16},{28,20},{1,9},{5... | collective-permute-start | bytes 1179656 | tf_op jit(solution)/shard_map/ppermute | solution.py:33
  38.9 13.5 %feed_forward.1 = (bf16[256,768]{1,0:T(8,128)(2,1)}, f32[256,768]{1,0:T(8,128)S(1)}, bf16[192,256]{1,0:T(8,128)(2,1)S(1)}, bf16[192,256]{1,0:T(8,128)(2,1)S(1)},...) custom-call(s32[5]{0:T(128)S(1)} %stack.23.me_ref.at_ref, ...), custom_call_target="tpu_custom_call" | custom-call | flops 12999999488 | bytes 45500000 | tf_op jit(solution)/shard_map/feed_forward/pallas_call | solution.py:899
  53.0 2.4 %collective-permute-done.10.refs_1_ = bf16[256,768]{1,0:T(8,128)(2,1)S(1)} collective-permute-done((bf16[256,768]{1,0:T(8,128)(2,1)S(1)}, bf16[256,768]{1,0:T(8,128)(2,1)S(1)}, u32[]{:S(2)}, u32[]{:S(2)}) %collective-permute-start.10) | collective-permute-done | bytes 393248 | tf_op jit(solution)/shard_map/ppermute | solution.py:33
  61.4 11.7 %hidden_grads.1 = (bf16[2,3,96,512]{3,2,1,0:T(8,128)(2,1)S(1)}, bf16[2,3,96,512]{3,2,1,0:T(8,128)(2,1)S(1)}, bf16[2,3,96,256]{3,2,1,0:T(8,128)(2,1)S(1)}, bf16[2...) custom-call(s32[5]{0:T(128)S(1)} %stack.23.me_ref.at_ref, ...), custom_call_target="tpu_custom_call" | custom-call | flops 14000000000 | bytes 49000000 | tf_op jit(solution)/shard_map/hidden_grads/pallas_call | solution.py:980
  73.2 2.7 %collective-permute-start.29 = (bf16[2,3,96,256]{3,2,1,0:T(8,128)(2,1)S(1)}, bf16[2,3,96,256]{3,2,1,0:T(8,128)(2,1)S(1)}, u32[]{:S(2)}, u32[]{:S(2)}) collective-permute-start(bf16[2,3,96,256]{3,2,1,0:T(8,128)(2,1)S(1)} %get-tuple-element.147), channel_id=1, source_target_pairs={{0,16},{4,20},{8,24},{12,28},{16,0},{20,4},{24,8},{28,12},{1,17},{... | collective-permute-start | bytes 884744 | tf_op jit(solution)/shard_map/ppermute | solution.py:33
  76.8 1.5 %collective-permute-start.28 = (bf16[2,3,96,512]{3,2,1,0:T(8,128)(2,1)S(1)}, bf16[2,3,96,512]{3,2,1,0:T(8,128)(2,1)S(1)}, u32[]{:S(2)}, u32[]{:S(2)}) collective-permute-start(bf16[2,3,96,512]{3,2,1,0:T(8,128)(2,1)S(1)} %get-tuple-element.138.after), channel_id=1, source_target_pairs={{0,4},{4,0},{8,12},{12,8},{16,20},{20,16},{24,28},{28,24},{1,5},{5... | collective-permute-start | bytes 1769480 | tf_op jit(solution)/shard_map/ppermute | solution.py:33
  78.3 13.0 %backward_spectral.1 = (bf16[400,256]{1,0:T(8,128)(2,1)S(1)}, bf16[400,256]{1,0:T(8,128)(2,1)S(1)}, bf16[400,256]{1,0:T(8,128)(2,1)S(1)}, bf16[400,256]{1,0:T(8,...) custom-call(s32[5]{0:T(128)S(1)} %stack.23.me_ref.at_ref, ...), custom_call_target="tpu_custom_call" | custom-call | flops 16999999488 | bytes 59500000 | tf_op jit(solution)/shard_map/backward_spectral/pallas_call | solution.py:790
  92.7 2.2 %projection_grads.1 = (bf16[4,72,384]{2,1,0:T(8,128)(2,1)S(1)}, bf16[4,112,384]{2,1,0:T(8,128)(2,1)S(1)}, bf16[2,2,72,384]{3,2,1,0:T(8,128)(2,1)S(1)}, bf16[2,2,...) custom-call(s32[5]{0:T(128)S(1)} %stack.23.me_ref.at_ref, bf16[384,1024]{1,0:T(8,128)(2,1)S(1)} %get-tuple-element.144.after.gp, ...), custom_call_target="tpu_custom_call" | custom-call | flops 2000000000 | bytes 7000000 | tf_op jit(solution)/shard_map/projection_grads/pallas_call | solution.py:1247
  95.0 1.6 %collective-permute-start.33 = (bf16[4,112,384]{2,1,0:T(8,128)(2,1)S(1)}, bf16[4,112,384]{2,1,0:T(8,128)(2,1)S(1)}, u32[]{:S(2)}, u32[]{:S(2)}) collective-permute-start(bf16[4,112,384]{2,1,0:T(8,128)(2,1)S(1)} %get-tuple-element.162.after), channel_id=1, source_target_pairs={{0,4},{4,0},{8,12},{12,8},{16,20},{20,16},{24,28},{28,24},{1,5},{5... | collective-permute-start | bytes 1032200 | tf_op jit(solution)/shard_map/ppermute | solution.py:33
  98.0 8.3 %collective-permute-done.34.got_b = bf16[2,2,72,384]{3,2,1,0:T(8,128)(2,1)S(1)} collective-permute-done((bf16[2,2,72,384]{3,2,1,0:T(8,128)(2,1)S(1)}, bf16[2,2,72,384]{3,2,1,0:T(8,128)(2,1)S(1)}, u32[]{:S(2)}, u32[]{:S(2)}) %collective-permute-start.34) | collective-permute-done | bytes 221216 | tf_op jit(solution)/shard_map/ppermute | solution.py:33
  109.5 2.4 %collective-permute-done.30.got_a = bf16[1,3,96,512]{3,2,1,0:T(8,128)(2,1)S(1)} collective-permute-done((bf16[1,3,96,512]{3,2,1,0:T(8,128)(2,1)S(1)}, bf16[1,3,96,512]{3,2,1,0:T(8,128)(2,1)S(1)}, u32[]{:S(2)}, u32[]{:S(2)}) %collective-permute-start.30) | collective-permute-done | bytes 294944 | tf_op jit(solution)/shard_map/ppermute | solution.py:33
  112.8 2.9 %collective-permute-done.35.got_a = bf16[2,144,384]{2,1,0:T(8,128)(2,1)S(1)} collective-permute-done((bf16[2,144,384]{2,1,0:T(8,128)(2,1)S(1)}, bf16[2,144,384]{2,1,0:T(8,128)(2,1)S(1)}, u32[]{:S(2)}, u32[]{:S(2)}) %collective-permute-start.35) | collective-permute-done | bytes 221216 | tf_op jit(solution)/shard_map/ppermute | solution.py:33
  116.4 2.9 %collective-permute-start.41 = (bf16[72,768]{1,0:T(8,128)(2,1)S(1)}, bf16[72,768]{1,0:T(8,128)(2,1)S(1)}, u32[]{:S(2)}, u32[]{:S(2)}) collective-permute-start(bf16[72,768]{1,0:T(8,128)(2,1)S(1)} %get-tuple-element.174.after), channel_id=1, source_target_pairs={{0,16},{4,20},{8,24},{12,28},{16,0},{20,4},{24,8},{28,12},{1,17},{... | collective-permute-start | bytes 331784 | tf_op jit(solution)/shard_map/ppermute | solution.py:33
  119.9 3.1 %final.1 = f32[256,768]{1,0:T(8,128)S(1)} custom-call(s32[5]{0:T(128)S(1)} %stack.23.me_ref.at_ref, bf16[400,256]{1,0:T(8,128)(2,1)S(1)} %get-tuple-element.139.p0, bf16[400,256]{1,0:T(8,128)(2,1)S(1)} %collective-permute-done.25.p1, bf16[400,256]{1,0:T(8,128)(2,1)S(1)} %collective-permute-done.26.p2, bf16[400,256]{1,0:T(8,128)(2,1)S(1)} %collective-permute-done.27.p3, ...), custom_call_target="tpu_custom_call" | custom-call | flops 300000000 | bytes 1050000 | tf_op jit(solution)/shard_map/final/pallas_call | solution.py:1302
  123.0 1.7 %copy.45 = f32[256,1,768]{2,1,0:T(1,128)} copy(f32[256,1,768]{2,0,1:T(8,128)S(1)} %bitcast.26) | data formatting | bytes 1572864
  127.8 1.9 %collective-permute-done.39.j2 = bf16[384,128]{1,0:T(8,128)(2,1)S(1)} collective-permute-done((bf16[384,128]{1,0:T(8,128)(2,1)S(1)}, bf16[384,128]{1,0:T(8,128)(2,1)S(1)}, u32[]{:S(2)}, u32[]{:S(2)}) %collective-permute-start.39) | collective-permute-done | bytes 98336 | tf_op jit(solution)/shard_map/ppermute | solution.py:33
  131.0 2.3 %small_grads.1 = (f32[64,1536]{1,0:T(8,128)}, f32[3,1536]{1,0:T(4,128)}, f32[768]{0:T(1024)}, f32[768]{0:T(1024)}, f32[768]{0:T(1024)}, /*index=5*/f32[768]{0:T(...) custom-call(s32[5]{0:T(128)S(1)} %stack.23.me_ref.at_ref, bf16[384,128]{1,0:T(8,128)(2,1)S(1)} %add.6.j0, ...), custom_call_target="tpu_custom_call" | custom-call | flops 3000000000 | bytes 10500000 | tf_op jit(solution)/shard_map/small_grads/pallas_call | solution.py:1391
  (102 shorter events, 28.2 us)
Async XLA Ops:
  0.6 11.1 %collective-permute-start.1 = (bf16[256,768]{1,0:T(8,128)(2,1)}, bf16[256,768]{1,0:T(8,128)(2,1)S(1)}, u32[]{:S(2)}, u32[]{:S(2)}) collective-permute-start(bf16[256,768]{1,0:T(8,128)(2,1)} %bitcast.29), channel_id=1, source_target_pairs={{0,2},{1,3},{2,0},{3,1},{4,6},{5,7},{6,4},{7,5},{8,10},{9,11},{10,... | collective-permute-start | bytes 1179656 | tf_op jit(solution)/shard_map/ppermute | solution.py:33
  0.7 12.1 %collective-permute-start = (bf16[256,768]{1,0:T(8,128)(2,1)}, bf16[256,768]{1,0:T(8,128)(2,1)S(1)}, u32[]{:S(2)}, u32[]{:S(2)}) collective-permute-start(bf16[256,768]{1,0:T(8,128)(2,1)} %bitcast.30), channel_id=1, source_target_pairs={{0,1},{1,0},{2,3},{3,2},{4,5},{5,4},{6,7},{7,6},{8,9},{9,8},{10,11... | collective-permute-start | bytes 1179656 | tf_op jit(solution)/shard_map/ppermute | solution.py:33
  0.8 12.0 %collective-permute-start.17 = (bf16[256,768]{1,0:T(8,128)(2,1)}, bf16[256,768]{1,0:T(8,128)(2,1)S(1)}, u32[]{:S(2)}, u32[]{:S(2)}) collective-permute-start(bf16[256,768]{1,0:T(8,128)(2,1)} %bitcast.34), channel_id=1, source_target_pairs={{0,8},{4,12},{8,0},{12,4},{16,24},{20,28},{24,16},{28,20},{1,9},{5... | collective-permute-start | bytes 1179656 | tf_op jit(solution)/shard_map/ppermute | solution.py:33
  11.8 12.3 %collective-permute-start.16 = (bf16[256,768]{1,0:T(8,128)(2,1)S(1)}, bf16[256,768]{1,0:T(8,128)(2,1)S(1)}, u32[]{:S(2)}, u32[]{:S(2)}) collective-permute-start(bf16[256,768]{1,0:T(8,128)(2,1)S(1)} %bitcast.35), channel_id=1, source_target_pairs={{0,2},{1,3},{2,0},{3,1},{4,6},{5,7},{6,4},{7,5},{8,10},{9,11},{10,... | collective-permute-start | bytes 1179656 | tf_op jit(solution)/shard_map/ppermute | solution.py:33
  24.2 28.2 %collective-permute-start.18 = (bf16[256,768]{1,0:T(8,128)(2,1)S(1)}, bf16[256,768]{1,0:T(8,128)(2,1)S(1)}, u32[]{:S(2)}, u32[]{:S(2)}) collective-permute-start(bf16[256,768]{1,0:T(8,128)(2,1)S(1)} %tie.6.refs_9_), channel_id=1, source_target_pairs={{0,8},{4,12},{8,0},{12,4},{16,24},{20,28},{24,16},{28,20},{1,9},{5... | collective-permute-start | bytes 1179656 | tf_op jit(solution)/shard_map/ppermute | solution.py:33
  34.8 23.1 %collective-permute-start.12 = (bf16[256,768]{1,0:T(8,128)(2,1)S(1)}, bf16[256,768]{1,0:T(8,128)(2,1)S(1)}, u32[]{:S(2)}, u32[]{:S(2)}) collective-permute-start(bf16[256,768]{1,0:T(8,128)(2,1)S(1)} %get-tuple-element.113.u2.refs_0_), channel_id=1, source_target_pairs={{0,1},{1,0},{2,3},{3,2},{4,5},{5,4},{6,7},{7,6},{8,9},{9,8},{10,11... | collective-permute-start | bytes 1179656 | tf_op jit(solution)/shard_map/ppermute | solution.py:33
  35.4 17.1 %collective-permute-start.11 = (bf16[256,768]{1,0:T(8,128)(2,1)S(1)}, bf16[256,768]{1,0:T(8,128)(2,1)S(1)}, u32[]{:S(2)}, u32[]{:S(2)}) collective-permute-start(bf16[256,768]{1,0:T(8,128)(2,1)S(1)} %get-tuple-element.113.u2.refs_0_), channel_id=1, source_target_pairs={{0,10},{1,11},{2,8},{3,9},{4,14},{5,15},{6,12},{7,13},{8,2},{9,3},... | collective-permute-start | bytes 1179656 | tf_op jit(solution)/shard_map/ppermute | solution.py:1477
  36.3 19.1 %collective-permute-start.10 = (bf16[256,768]{1,0:T(8,128)(2,1)S(1)}, bf16[256,768]{1,0:T(8,128)(2,1)S(1)}, u32[]{:S(2)}, u32[]{:S(2)}) collective-permute-start(bf16[256,768]{1,0:T(8,128)(2,1)S(1)} %get-tuple-element.113.u2.refs_0_), channel_id=1, source_target_pairs={{0,8},{4,12},{8,0},{12,4},{16,24},{20,28},{24,16},{28,20},{1,9},{5... | collective-permute-start | bytes 1179656 | tf_op jit(solution)/shard_map/ppermute | solution.py:33
  37.9 17.9 %collective-permute-start.9 = (bf16[256,768]{1,0:T(8,128)(2,1)S(1)}, bf16[256,768]{1,0:T(8,128)(2,1)S(1)}, u32[]{:S(2)}, u32[]{:S(2)}) collective-permute-start(bf16[256,768]{1,0:T(8,128)(2,1)S(1)} %get-tuple-element.113.u2.refs_0_), channel_id=1, source_target_pairs={{0,2},{1,3},{2,0},{3,1},{4,6},{5,7},{6,4},{7,5},{8,10},{9,11},{10,... | collective-permute-start | bytes 1179656 | tf_op jit(solution)/shard_map/ppermute | solution.py:33
  59.2 17.6 %collective-permute-start.6 = (bf16[192,256]{1,0:T(8,128)(2,1)S(1)}, bf16[192,256]{1,0:T(8,128)(2,1)S(1)}, u32[]{:S(2)}, u32[]{:S(2)}) collective-permute-start(bf16[192,256]{1,0:T(8,128)(2,1)S(1)} %get-tuple-element.117), channel_id=1, source_target_pairs={{0,1},{1,0},{2,3},{3,2},{4,5},{5,4},{6,7},{7,6},{8,9},{9,8},{10,11... | collective-permute-start | bytes 294920 | tf_op jit(solution)/shard_map/ppermute | solution.py:33
  59.7 18.6 %collective-permute-start.7 = (bf16[192,256]{1,0:T(8,128)(2,1)S(1)}, bf16[192,256]{1,0:T(8,128)(2,1)S(1)}, u32[]{:S(2)}, u32[]{:S(2)}) collective-permute-start(bf16[192,256]{1,0:T(8,128)(2,1)S(1)} %get-tuple-element.118), channel_id=1, source_target_pairs={{0,2},{1,3},{2,0},{3,1},{4,6},{5,7},{6,4},{7,5},{8,10},{9,11},{10,... | collective-permute-start | bytes 294920 | tf_op jit(solution)/shard_map/ppermute | solution.py:33
  60.7 17.6 %collective-permute-start.8 = (bf16[192,256]{1,0:T(8,128)(2,1)S(1)}, bf16[192,256]{1,0:T(8,128)(2,1)S(1)}, u32[]{:S(2)}, u32[]{:S(2)}) collective-permute-start(bf16[192,256]{1,0:T(8,128)(2,1)S(1)} %get-tuple-element.119), channel_id=1, source_target_pairs={{0,3},{1,2},{2,1},{3,0},{4,7},{5,6},{6,5},{7,4},{8,11},{9,10},{10,... | collective-permute-start | bytes 294920 | tf_op jit(solution)/shard_map/ppermute | solution.py:33
  73.2 18.1 %collective-permute-start.29 = (bf16[2,3,96,256]{3,2,1,0:T(8,128)(2,1)S(1)}, bf16[2,3,96,256]{3,2,1,0:T(8,128)(2,1)S(1)}, u32[]{:S(2)}, u32[]{:S(2)}) collective-permute-start(bf16[2,3,96,256]{3,2,1,0:T(8,128)(2,1)S(1)} %get-tuple-element.147), channel_id=1, source_target_pairs={{0,16},{4,20},{8,24},{12,28},{16,0},{20,4},{24,8},{28,12},{1,17},{... | collective-permute-start | bytes 884744 | tf_op jit(solution)/shard_map/ppermute | solution.py:33
  75.8 16.9 %collective-permute-start.32 = (bf16[192,768]{1,0:T(8,128)(2,1)S(1)}, bf16[192,768]{1,0:T(8,128)(2,1)S(1)}, u32[]{:S(2)}, u32[]{:S(2)}) collective-permute-start(bf16[192,768]{1,0:T(8,128)(2,1)S(1)} %get-tuple-element.155), channel_id=1, source_target_pairs={{0,2},{1,3},{2,0},{3,1},{4,6},{5,7},{6,4},{7,5},{8,10},{9,11},{10,... | collective-permute-start | bytes 884744 | tf_op jit(solution)/shard_map/ppermute | solution.py:33
  76.8 15.2 %collective-permute-start.28 = (bf16[2,3,96,512]{3,2,1,0:T(8,128)(2,1)S(1)}, bf16[2,3,96,512]{3,2,1,0:T(8,128)(2,1)S(1)}, u32[]{:S(2)}, u32[]{:S(2)}) collective-permute-start(bf16[2,3,96,512]{3,2,1,0:T(8,128)(2,1)S(1)} %get-tuple-element.138.after), channel_id=1, source_target_pairs={{0,4},{4,0},{8,12},{12,8},{16,20},{20,16},{24,28},{28,24},{1,5},{5... | collective-permute-start | bytes 1769480 | tf_op jit(solution)/shard_map/ppermute | solution.py:33
  95.0 11.3 %collective-permute-start.33 = (bf16[4,112,384]{2,1,0:T(8,128)(2,1)S(1)}, bf16[4,112,384]{2,1,0:T(8,128)(2,1)S(1)}, u32[]{:S(2)}, u32[]{:S(2)}) collective-permute-start(bf16[4,112,384]{2,1,0:T(8,128)(2,1)S(1)} %get-tuple-element.162.after), channel_id=1, source_target_pairs={{0,4},{4,0},{8,12},{12,8},{16,20},{20,16},{24,28},{28,24},{1,5},{5... | collective-permute-start | bytes 1032200 | tf_op jit(solution)/shard_map/ppermute | solution.py:33
  96.6 9.7 %collective-permute-start.34 = (bf16[2,2,72,384]{3,2,1,0:T(8,128)(2,1)S(1)}, bf16[2,2,72,384]{3,2,1,0:T(8,128)(2,1)S(1)}, u32[]{:S(2)}, u32[]{:S(2)}) collective-permute-start(bf16[2,2,72,384]{3,2,1,0:T(8,128)(2,1)S(1)} %get-tuple-element.165), channel_id=1, source_target_pairs={{0,8},{4,12},{8,0},{12,4},{16,24},{20,28},{24,16},{28,20},{1,9},{5... | collective-permute-start | bytes 663560 | tf_op jit(solution)/shard_map/ppermute | solution.py:33
  97.0 14.8 %collective-permute-start.30 = (bf16[1,3,96,512]{3,2,1,0:T(8,128)(2,1)S(1)}, bf16[1,3,96,512]{3,2,1,0:T(8,128)(2,1)S(1)}, u32[]{:S(2)}, u32[]{:S(2)}) collective-permute-start(bf16[1,3,96,512]{3,2,1,0:T(8,128)(2,1)S(1)} %get-tuple-element.149.after), channel_id=1, source_target_pairs={{0,16},{4,20},{8,24},{12,28},{16,0},{20,4},{24,8},{28,12},{1,17},{... | collective-permute-start | bytes 884744 | tf_op jit(solution)/shard_map/ppermute | solution.py:33
  97.5 10.9 %collective-permute-start.31 = (bf16[1,3,96,256]{3,2,1,0:T(8,128)(2,1)S(1)}, bf16[1,3,96,256]{3,2,1,0:T(8,128)(2,1)S(1)}, u32[]{:S(2)}, u32[]{:S(2)}) collective-permute-start(bf16[1,3,96,256]{3,2,1,0:T(8,128)(2,1)S(1)} %get-tuple-element.151), channel_id=1, source_target_pairs={{0,4},{4,0},{8,12},{12,8},{16,20},{20,16},{24,28},{28,24},{1,5},{5... | collective-permute-start | bytes 442376 | tf_op jit(solution)/shard_map/ppermute | solution.py:33
  107.0 8.8 %collective-permute-start.35 = (bf16[2,144,384]{2,1,0:T(8,128)(2,1)S(1)}, bf16[2,144,384]{2,1,0:T(8,128)(2,1)S(1)}, u32[]{:S(2)}, u32[]{:S(2)}) collective-permute-start(bf16[2,144,384]{2,1,0:T(8,128)(2,1)S(1)} %get-tuple-element.170), channel_id=1, source_target_pairs={{0,8},{4,12},{8,0},{12,4},{16,24},{20,28},{24,16},{28,20},{1,9},{5... | collective-permute-start | bytes 663560 | tf_op jit(solution)/shard_map/ppermute | solution.py:33
  108.4 10.9 %collective-permute-start.25 = (bf16[400,256]{1,0:T(8,128)(2,1)S(1)}, bf16[400,256]{1,0:T(8,128)(2,1)S(1)}, u32[]{:S(2)}, u32[]{:S(2)}) collective-permute-start(bf16[400,256]{1,0:T(8,128)(2,1)S(1)} %get-tuple-element.140), channel_id=1, source_target_pairs={{0,1},{1,0},{2,3},{3,2},{4,5},{5,4},{6,7},{7,6},{8,9},{9,8},{10,11... | collective-permute-start | bytes 614408 | tf_op jit(solution)/shard_map/ppermute | solution.py:33
  108.4 10.9 %collective-permute-start.26 = (bf16[400,256]{1,0:T(8,128)(2,1)S(1)}, bf16[400,256]{1,0:T(8,128)(2,1)S(1)}, u32[]{:S(2)}, u32[]{:S(2)}) collective-permute-start(bf16[400,256]{1,0:T(8,128)(2,1)S(1)} %get-tuple-element.141), channel_id=1, source_target_pairs={{0,2},{1,3},{2,0},{3,1},{4,6},{5,7},{6,4},{7,5},{8,10},{9,11},{10,... | collective-permute-start | bytes 614408 | tf_op jit(solution)/shard_map/ppermute | solution.py:33
  116.4 8.4 %collective-permute-start.37 = (bf16[384,128]{1,0:T(8,128)(2,1)S(1)}, bf16[384,128]{1,0:T(8,128)(2,1)S(1)}, u32[]{:S(2)}, u32[]{:S(2)}) collective-permute-start(bf16[384,128]{1,0:T(8,128)(2,1)S(1)} %get-tuple-element.173.after.ours), channel_id=1, source_target_pairs={{0,16},{4,20},{8,24},{12,28},{16,0},{20,4},{24,8},{28,12},{1,17},{... | collective-permute-start | bytes 294920 | tf_op jit(solution)/shard_map/ppermute | solution.py:33
  116.4 10.6 %collective-permute-start.41 = (bf16[72,768]{1,0:T(8,128)(2,1)S(1)}, bf16[72,768]{1,0:T(8,128)(2,1)S(1)}, u32[]{:S(2)}, u32[]{:S(2)}) collective-permute-start(bf16[72,768]{1,0:T(8,128)(2,1)S(1)} %get-tuple-element.174.after), channel_id=1, source_target_pairs={{0,16},{4,20},{8,24},{12,28},{16,0},{20,4},{24,8},{28,12},{1,17},{... | collective-permute-start | bytes 331784 | tf_op jit(solution)/shard_map/ppermute | solution.py:33
  (24 other events, 113.6 us)

commit v5 on v4

--- a/solution.py
+++ b/solution.py
@@ -423,17 +423,17 @@
     pass
 
 
-def tie(values, after):
+def tie(values, *after):
     count = len(values)
     return pl.pallas_call(
         tie_kernel,
-        in_specs=[HBM] * (count + 1),
+        in_specs=[HBM] * (count + len(after)),
         out_specs=[HBM] * count,
         out_shape=[jax.ShapeDtypeStruct(value.shape, value.dtype) for value in values],
         input_output_aliases={i: i for i in range(count)},
         compiler_params=params(1),
         name="tie",
-    )(*values, after)
+    )(*values, *after)
 
 
 def one_hot_rows(me, rows, lanes, piece, fs):
@@ -446,10 +446,12 @@
 
 
 def prepare_kernel(
-    me_ref, w_in, freq_w2, conv_taps, freq_w1, freq_b1, feats, waves_far, norms,
-    w_mine, w2x, w2t, taps, base, waves, w1_aug, sems, *, step, fs,
+    me_ref, w_in, freq_w2, conv_taps, freq_w1, freq_b1, feats, waves_far, w_far, x_far, cond_far, norms,
+    w_mine, w2x, w2t, taps, base, waves, w_near, x_near, cond_near, w1_aug, sems, *, step, fs,
 ):
-    loads = dma_all([(waves_far, waves)], sems)
+    loads = dma_all(
+        [(waves_far, waves), (w_far, w_near), (x_far, x_near), (cond_far, cond_near)], sems
+    )
     lanes = w_in.shape[1] // 4
     rows = lanes // fs
     sel = one_hot_rows(me_ref[0], rows, lanes, step, fs)
@@ -480,14 +482,14 @@
         load.wait()
 
 
-def prepare(me, w_in, freq_w2, conv_taps, freq_w1, freq_b1, feats, waves, norms, step, fs):
+def prepare(me, w_in, freq_w2, conv_taps, freq_w1, freq_b1, feats, waves, w_out, x, condt, norms, step, fs):
     channels, both = w_in.shape
     hidden = freq_w2.shape[0]
     length = feats.shape[1]
     return pl.pallas_call(
         functools.partial(prepare_kernel, step=step, fs=fs),
-        in_specs=[SM] + [VM] * 6 + [HBM] * 2,
-        out_specs=[VM] * 6,
+        in_specs=[SM] + [VM] * 6 + [HBM] * 5,
+        out_specs=[VM] * 9,
         out_shape=[
             shape((both // fs, channels), BF16),
             shape((both // fs, 3 * hidden), BF16),
@@ -495,42 +497,50 @@
             shape((both // fs, 8), F32),
             shape((hidden, length), F32),
             shape((2 * length, length), BF16),
+            shape(w_out.shape, BF16),
+            shape(x.shape, BF16),
+            shape(condt.shape, F32),
         ],
         scratch_shapes=[
             pltpu.VMEM((feats.shape[0], hidden), F32),
-            pltpu.SemaphoreType.DMA((1,)),
+            pltpu.SemaphoreType.DMA((4,)),
         ],
         compiler_params=params(24),
         cost_estimate=cost(3),
         name="prepare",
-    )(me, *in_hbm(w_in, freq_w2, conv_taps, freq_w1), freq_b1[None], in_hbm(feats), in_hbm(waves), norms)
-
-
-def select_kernel(at_ref, after, gate, up, gate_out, up_out, *, fs):
+    )(me, *in_hbm(w_in, freq_w2, conv_taps, freq_w1), freq_b1[None], in_hbm(feats), in_hbm(waves), *in_hbm(w_out, x, condt), norms)
+
+
+def select_kernel(at_ref, after, gate, up, down, gate_out, up_out, down_out, *, fs):
+    down_out[...] = down[0, 0]
     rows = gate_out.shape[0]
     sel = one_hot_rows(at_ref[0], rows, rows * fs, rows, fs).astype(BF16)
     gate_out[...] = mm_nt(sel, gate[...]).astype(BF16)
     up_out[...] = mm_nt(sel, up[...]).astype(BF16)
 
 
-def select_columns(at, after, w_gate, w_up, bs, fs):
+def select_columns(at, after, w_gate, w_up, w_down, bs, fs):
     channels, ff = w_gate.shape
     lanes = ff // bs
     wide = pl.BlockSpec((channels, lanes), lambda i, at: (0, (i // 2) * 4 + at[2] * 2 + i % 2))
     rows = pl.BlockSpec((lanes // fs, channels), lambda i, at: (i, 0))
+    down = pl.BlockSpec(
+        (1, 1, lanes // fs, channels),
+        lambda i, at: ((i // 2) * 4 + at[2] * 2 + i % 2, at[0], 0, 0),
+    )
     return pl.pallas_call(
         functools.partial(select_kernel, fs=fs),
         grid_spec=pltpu.PrefetchScalarGridSpec(
             num_scalar_prefetch=1,
             grid=(bs // 2,),
-            in_specs=[HBM, wide, wide],
-            out_specs=[rows, rows],
+            in_specs=[HBM, wide, wide, down],
+            out_specs=[rows, rows, rows],
         ),
-        out_shape=[shape((ff // (2 * fs), channels), BF16)] * 2,
+        out_shape=[shape((ff // (2 * fs), channels), BF16)] * 3,
         compiler_params=params(20),
         cost_estimate=cost(5),
         name="select_columns",
-    )(at, after, in_hbm(w_gate), in_hbm(w_up))
+    )(at, after, in_hbm(w_gate), in_hbm(w_up), in_hbm(w_down.reshape(bs, fs, lanes // fs, channels)))
 
 
 def row_masks(ids):
@@ -833,7 +843,7 @@
         compiler_params=params(24),
         cost_estimate=cost(2),
         name="middle",
-    )(me, *z_parts, x, in_hbm(w_out), norms, after)
+    )(me, *z_parts, x, w_out, norms, after)
 
 
 def feed_kernel(
@@ -921,7 +931,7 @@
         compiler_params=params(28),
         cost_estimate=cost(13),
         name="feed_forward",
-    )(me, u2, h, ct, norms, in_hbm(w_out), in_hbm(w_gate), in_hbm(w_up), in_hbm(w_down))
+    )(me, u2, h, ct, norms, w_out, in_hbm(w_gate), in_hbm(w_up), in_hbm(w_down))
 
 
 def hidden_grads_kernel(at_ref, *refs):
@@ -942,7 +952,7 @@
         at = tile(k, span)
         g = mm_nt(gate[...], rights[0, at, :])
         a = mm_nt(up[...], rights[0, at, :])
-        gh = mm_nt(down[...].reshape(rows, channels), rights[1, at, :])
+        gh = mm_nt(down[...], rights[1, at, :])
         sg = sigmoid(g)
         silu = g * sg
         lefts[0, :, at] = (gh * a * (sg * (1.0 + g * (1.0 - sg)))).astype(BF16)
@@ -973,16 +983,15 @@
 def hidden_grads(at, u2_parts, ct_parts, gate, up, gt_own, gt_got, z_own, z_got, down, after):
     quarter, channels = u2_parts[0].shape
     wide = gate.shape[0]
-    bs, fs, fw, _ = down.shape
+    fw = wide // 4
+    fs = 4
     cut = 2 * channels // 3
-    down = down.reshape(2, 2, 2, fs, fw, channels)
-    down_spec = pl.BlockSpec((2, 1, 2, 1, fw, channels), lambda i, at: (0, at[2], 0, at[0], 0, 0))
     return pl.pallas_call(
         hidden_grads_kernel,
         grid_spec=pltpu.PrefetchScalarGridSpec(
             num_scalar_prefetch=1,
             grid=(1,),
-            in_specs=[VM] * 22 + [down_spec, HBM],
+            in_specs=[VM] * 23 + [HBM],
             out_specs=[VM] * 6,
             scratch_shapes=[
                 pltpu.VMEM((2, 8 * quarter, channels), BF16),
@@ -997,7 +1006,7 @@
         compiler_params=params(34),
         cost_estimate=cost(14),
         name="hidden_grads",
-    )(at, *u2_parts, *ct_parts, gate, up, gt_own, gt_got, z_own, z_got, in_hbm(down), after)
+    )(at, *u2_parts, *ct_parts, gate, up, gt_own, gt_got, z_own, z_got, down, after)
 
 
 def halve_kernel(at_ref, after, *refs, bits):
@@ -1468,7 +1477,7 @@
         (two,) = tie([two], after)
         return (value, one, two, swap(two, "freq", 1))
 
-    def gather_wide(value, after):
+    def gather_wide(value, *after):
         count = bs * fs
         parts = (
             value,
@@ -1476,38 +1485,40 @@
             swap(value, "batch", 2),
             lax.ppermute(value, ("batch", "freq"), [(i, i ^ (2 * fs + 2)) for i in range(count)]),
         )
-        parts = parts[:1] + tuple(tie(parts[1:], after))
+        parts = parts[:1] + tuple(tie(parts[1:], *after))
         return parts + tuple(swap(part, "freq", 1) for part in parts)
 
     def pairs(value):
         return value.reshape((value.shape[0] // 2, 2) + value.shape[1:])
 
-    w_mine, w2x, w2t, taps, base, waves = prepare(
-        at, w_in, freq_w2, conv_taps, freq_w1, freq_b1, jnp.asarray(feats_aug), jnp.asarray(table), norms, step, fs
+    w_mine, w2x, w2t, taps, base, waves, w_near, x_near, condt = prepare(
+        at, w_in, freq_w2, conv_taps, freq_w1, freq_b1, jnp.asarray(feats_aug), jnp.asarray(table), w_out,
+        x_own, condt, norms, step, fs
     )
     x_parts = gather_after(x_own, base)
+    x_parts = (x_near,) + x_parts[1:]
     forward = forward_spectral(at, x_parts, ids, norms, w_mine, taps, base, w2x, condt, waves)
     z_parts, (u1, n1, p, q, c, vr, vs, mu, mn, cb) = forward[:4], forward[4:]
     ct_x = swap(ct_own, "freq", 2)
     ct_z = swap(ct_own, "batch", 2)
     z_got = trade_parts(z_parts)
-    wg_mine, wu_mine = select_columns(at, cb, w_gate, w_up, bs, fs)
+    wg_mine, wu_mine, wd_mine = select_columns(at, cb, w_gate, w_up, w_down, bs, fs)
     (ct_x,) = tie([ct_x], cb)
     ct_parts = (ct_own, ct_x, ct_z, swap(ct_x, "batch", 2))
-    h, u2, z_t = middle(at, z_got, x_own, w_out, norms, wg_mine, step)
+    h, u2, z_t = middle(at, z_got, x_near, w_near, norms, wg_mine, step)
     fed = feed_forward(
-        at, u2, h, ct_own, norms, w_out, w_gate, w_up, w_down, step, channels // (bs * fs)
+        at, u2, h, ct_own, norms, w_near, w_gate, w_up, w_down, step, channels // (bs * fs)
     )
     mixed_out, big_g, gz_parts, gt_own, gt_other, sums2 = fed[0], fed[1], fed[2:6], *fed[6:]
-    u2_parts = gather_wide(u2, sums2)
+    gt_got = swap(gt_other, "freq", 1)
     ct_parts = ct_parts + tuple(swap(part, "freq", 1) for part in tie(ct_parts, sums2))
+    u2_parts = gather_wide(u2, sums2, ct_parts[4])
     gz_got = trade_parts(gz_parts)
 
-    gt_got = swap(gt_other, "freq", 1)
     z_got = swap(z_t, "freq", 1)
     keep_a, give_a, keep_b, give_b, keep_o, give_o = hidden_grads(
         at, u2_parts, ct_parts, wg_mine, wu_mine, gt_own, gt_got, z_t, z_got,
-        w_down.reshape(bs, fs, fw, channels), sums2,
+        wd_mine, sums2,
     )
     got_a = swap(give_a, "batch", 1)
     got_b = swap(give_b, "batch", 4)
@@ -1542,6 +1553,7 @@
     grad_tokens = final(at, gp_got, x_own, big_g, norms, ids, condt, w_in, packed, step)
     got = swap(give, "batch", 4)
     sent = add(packed, swap(packed, "batch", 4), give, BF16)
+    (grad_tokens,) = tie([grad_tokens], sent)
     mine = keep.astype(F32) + got.astype(F32)
     first = 2 * width // bs
 

time: 136 us -> 133 us (0.978)
  Pallas kernels: 70.3 us -> 68.4 us
  transfers between devices with their start and end apart: 42 -> 42, of which waited for: 19 -> 17; matrix products, arithmetic and copies ran while one was open for 3% -> 3% of each run, Pallas kernels for 49% -> 49%
where the time goes in v5:
time: 133 us; the launch traced here: 131 us
  Pallas kernels  68.4 us (51%)
  waiting for transfers between devices  28.8 us (22%)
  starting transfers between devices  28 us (21%)
  local copies, waits for them, and re-layouts  3.88 us (3%)
    ppermute x41, waiting for transfers between devices, swap(): return lax.ppermute(value, axis, [(i, i ^ mask) for i in range(count)])  28.8 us
    ppermute x41, starting transfers between devices, swap(): return lax.ppermute(value, axis, [(i, i ^ mask) for i in range(count)])  27 us
    pallas_call x1, Pallas kernels, feed_forward(): pl.pallas_call(functools.partial(feed_kernel, piece=piece, thin=thin), gr...  12.9 us
    pallas_call x1, Pallas kernels, backward_spectral(): pl.pallas_call(backward_kernel, in_specs=[SM, SM] + [VM] * 17 + [HBM], ou...  12.9 us
    pallas_call x1, Pallas kernels, hidden_grads(): pl.pallas_call(hidden_grads_kernel, grid_spec=pltpu.PrefetchScalarGridSpe...  10.8 us
    pallas_call x1, Pallas kernels, forward_spectral(): pl.pallas_call(forward_kernel, in_specs=[SM, SM] + [VM] * 12, out_specs=[...  10.5 us
    pallas_call x1, Pallas kernels, select_columns(): pl.pallas_call(functools.partial(select_kernel, fs=fs), grid_spec=pltpu.P...  4.82 us
    pallas_call x1, Pallas kernels, prepare(): pl.pallas_call(functools.partial(prepare_kernel, step=step, fs=fs), in_sp...  4.57 us
  transfers between devices with their start and end apart: 42, of which 17 were waited for; matrix products, arithmetic and copies ran while one was open for 3% of the time, Pallas kernels for 49%

profile of v5, /device:TPU:2, one launch (start us, length us, event | category | flops | bytes accessed | tf_op | source)
XLA Modules:
  0.0 130.7 jit_solution(15069401351723570389)
XLA Ops:
  0.8 2.0 %collective-permute-start.13 = (bf16[256,768]{1,0:T(8,128)(2,1)}, bf16[256,768]{1,0:T(8,128)(2,1)S(1)}, u32[]{:S(2)}, u32[]{:S(2)}) collective-permute-start(bf16[256,768]{1,0:T(8,128)(2,1)} %bitcast.33), channel_id=1, source_target_pairs={{0,8},{4,12},{8,0},{12,4},{16,24},{20,28},{24,16},{28,20},{1,9},{5... | collective-permute-start | bytes 1179656 | tf_op jit(solution)/shard_map/ppermute | solution.py:33
  4.3 4.6 %prepare.1 = (bf16[384,768]{1,0:T(8,128)(2,1)S(1)}, bf16[384,192]{1,0:T(8,128)(2,1)S(1)}, bf16[64,384]{1,0:T(8,128)(2,1)S(1)}, f32[384,8]{1,0:T(8,128)S(1)}, f32...) custom-call(s32[5]{0:T(128)S(1)} %stack.23.me_ref.at_ref, ...), custom_call_target="tpu_custom_call" | custom-call | flops 3000000000 | bytes 10500000 | tf_op jit(solution)/shard_map/prepare/pallas_call | solution.py:489
  8.9 2.9 %collective-permute-done.1.refs_0_ = bf16[256,768]{1,0:T(8,128)(2,1)S(1)} collective-permute-done((bf16[256,768]{1,0:T(8,128)(2,1)}, bf16[256,768]{1,0:T(8,128)(2,1)S(1)}, u32[]{:S(2)}, u32[]{:S(2)}) %collective-permute-start.1) | collective-permute-done | bytes 393248 | tf_op jit(solution)/shard_map/ppermute | solution.py:33
  13.5 10.5 %forward_spectral.1 = (bf16[192,256]{1,0:T(8,128)(2,1)S(1)}, bf16[192,256]{1,0:T(8,128)(2,1)S(1)}, bf16[192,256]{1,0:T(8,128)(2,1)S(1)}, bf16[192,256]{1,0:T(8,1...) custom-call(s32[5]{0:T(128)S(1)} %stack.23.me_ref.at_ref, ...), custom_call_target="tpu_custom_call" | custom-call | flops 15000000512 | bytes 52500000 | tf_op jit(solution)/shard_map/forward_spectral/pallas_call | solution.py:679
  24.1 1.6 %collective-permute-start.14 = (bf16[256,768]{1,0:T(8,128)(2,1)S(1)}, bf16[256,768]{1,0:T(8,128)(2,1)S(1)}, u32[]{:S(2)}, u32[]{:S(2)}) collective-permute-start(bf16[256,768]{1,0:T(8,128)(2,1)S(1)} %tie.6.refs_9_), channel_id=1, source_target_pairs={{0,8},{4,12},{8,0},{12,4},{16,24},{20,28},{24,16},{28,20},{1,9},{5... | collective-permute-start | bytes 1179656 | tf_op jit(solution)/shard_map/ppermute | solution.py:33
  27.6 4.8 %select_columns.1 = (bf16[384,768]{1,0:T(8,128)(2,1)S(1)}, bf16[384,768]{1,0:T(8,128)(2,1)S(1)}, bf16[384,768]{1,0:T(8,128)(2,1)S(1)}) custom-call(s32[5]{0:T(128)S(1)} %stack.23.me_ref.at_ref, f32[64,8]{1,0:T(8,128)S(1)} %get-tuple-element.118.after.refs_1_.cb, bf16[768,3072]{1,0:T(8,128)(2,1)} %gate.3, bf16[768,3072]{1,0:T(8,128)(2,1)} %up.3, ...), custom_call_target="tpu_custom_call" | custom-call | flops 5000000000 | bytes 17500000 | tf_op jit(solution)/shard_map/select_columns/pallas_call | solution.py:531
  35.0 1.6 %collective-permute-start.10 = (bf16[256,768]{1,0:T(8,128)(2,1)S(1)}, bf16[256,768]{1,0:T(8,128)(2,1)S(1)}, u32[]{:S(2)}, u32[]{:S(2)}) collective-permute-start(bf16[256,768]{1,0:T(8,128)(2,1)S(1)} %get-tuple-element.120.u2.refs_0_), channel_id=1, source_target_pairs={{0,8},{4,12},{8,0},{12,4},{16,24},{20,28},{24,16},{28,20},{1,9},{5... | collective-permute-start | bytes 1179656 | tf_op jit(solution)/shard_map/ppermute | solution.py:33
  37.5 12.9 %feed_forward.1 = (bf16[256,768]{1,0:T(8,128)(2,1)}, f32[256,768]{1,0:T(8,128)S(1)}, bf16[192,256]{1,0:T(8,128)(2,1)S(1)}, bf16[192,256]{1,0:T(8,128)(2,1)S(1)},...) custom-call(s32[5]{0:T(128)S(1)} %stack.23.me_ref.at_ref, ...), custom_call_target="tpu_custom_call" | custom-call | flops 12999999488 | bytes 45500000 | tf_op jit(solution)/shard_map/feed_forward/pallas_call | solution.py:909
  51.1 3.4 %collective-permute-done.10.refs_1_ = bf16[256,768]{1,0:T(8,128)(2,1)S(1)} collective-permute-done((bf16[256,768]{1,0:T(8,128)(2,1)S(1)}, bf16[256,768]{1,0:T(8,128)(2,1)S(1)}, u32[]{:S(2)}, u32[]{:S(2)}) %collective-permute-start.10) | collective-permute-done | bytes 393248 | tf_op jit(solution)/shard_map/ppermute | solution.py:33
  59.9 10.8 %hidden_grads.1 = (bf16[2,3,96,512]{3,2,1,0:T(8,128)(2,1)S(1)}, bf16[2,3,96,512]{3,2,1,0:T(8,128)(2,1)S(1)}, bf16[2,3,96,256]{3,2,1,0:T(8,128)(2,1)S(1)}, bf16[2...) custom-call(s32[5]{0:T(128)S(1)} %stack.23.me_ref.at_ref, ...), custom_call_target="tpu_custom_call" | custom-call | flops 14000000000 | bytes 49000000 | tf_op jit(solution)/shard_map/hidden_grads/pallas_call | solution.py:989
  70.7 2.6 %collective-permute-start.29 = (bf16[2,3,96,256]{3,2,1,0:T(8,128)(2,1)S(1)}, bf16[2,3,96,256]{3,2,1,0:T(8,128)(2,1)S(1)}, u32[]{:S(2)}, u32[]{:S(2)}) collective-permute-start(bf16[2,3,96,256]{3,2,1,0:T(8,128)(2,1)S(1)} %get-tuple-element.155), channel_id=1, source_target_pairs={{0,16},{4,20},{8,24},{12,28},{16,0},{20,4},{24,8},{28,12},{1,17},{... | collective-permute-start | bytes 884744 | tf_op jit(solution)/shard_map/ppermute | solution.py:33
  74.3 1.5 %collective-permute-start.28 = (bf16[2,3,96,512]{3,2,1,0:T(8,128)(2,1)S(1)}, bf16[2,3,96,512]{3,2,1,0:T(8,128)(2,1)S(1)}, u32[]{:S(2)}, u32[]{:S(2)}) collective-permute-start(bf16[2,3,96,512]{3,2,1,0:T(8,128)(2,1)S(1)} %get-tuple-element.146.after), channel_id=1, source_target_pairs={{0,4},{4,0},{8,12},{12,8},{16,20},{20,16},{24,28},{28,24},{1,5},{5... | collective-permute-start | bytes 1769480 | tf_op jit(solution)/shard_map/ppermute | solution.py:33
  75.9 12.9 %backward_spectral.1 = (bf16[400,256]{1,0:T(8,128)(2,1)S(1)}, bf16[400,256]{1,0:T(8,128)(2,1)S(1)}, bf16[400,256]{1,0:T(8,128)(2,1)S(1)}, bf16[400,256]{1,0:T(8,...) custom-call(s32[5]{0:T(128)S(1)} %stack.23.me_ref.at_ref, ...), custom_call_target="tpu_custom_call" | custom-call | flops 16999999488 | bytes 59500000 | tf_op jit(solution)/shard_map/backward_spectral/pallas_call | solution.py:800
  90.3 2.2 %projection_grads.1 = (bf16[4,72,384]{2,1,0:T(8,128)(2,1)S(1)}, bf16[4,112,384]{2,1,0:T(8,128)(2,1)S(1)}, bf16[2,2,72,384]{3,2,1,0:T(8,128)(2,1)S(1)}, bf16[2,2,...) custom-call(s32[5]{0:T(128)S(1)} %stack.23.me_ref.at_ref, bf16[384,1024]{1,0:T(8,128)(2,1)S(1)} %get-tuple-element.152.after.gp, ...), custom_call_target="tpu_custom_call" | custom-call | flops 2000000000 | bytes 7000000 | tf_op jit(solution)/shard_map/projection_grads/pallas_call | solution.py:1256
  92.5 1.6 %collective-permute-start.33 = (bf16[4,112,384]{2,1,0:T(8,128)(2,1)S(1)}, bf16[4,112,384]{2,1,0:T(8,128)(2,1)S(1)}, u32[]{:S(2)}, u32[]{:S(2)}) collective-permute-start(bf16[4,112,384]{2,1,0:T(8,128)(2,1)S(1)} %get-tuple-element.170.after), channel_id=1, source_target_pairs={{0,4},{4,0},{8,12},{12,8},{16,20},{20,16},{24,28},{28,24},{1,5},{5... | collective-permute-start | bytes 1032200 | tf_op jit(solution)/shard_map/ppermute | solution.py:33
  95.6 8.2 %collective-permute-done.34.got_b = bf16[2,2,72,384]{3,2,1,0:T(8,128)(2,1)S(1)} collective-permute-done((bf16[2,2,72,384]{3,2,1,0:T(8,128)(2,1)S(1)}, bf16[2,2,72,384]{3,2,1,0:T(8,128)(2,1)S(1)}, u32[]{:S(2)}, u32[]{:S(2)}) %collective-permute-start.34) | collective-permute-done | bytes 221216 | tf_op jit(solution)/shard_map/ppermute | solution.py:33
  104.5 1.4 %collective-permute-start.36 = (bf16[2,72,384]{2,1,0:T(8,128)(2,1)S(1)}, bf16[2,72,384]{2,1,0:T(8,128)(2,1)S(1)}, u32[]{:S(2)}, u32[]{:S(2)}) collective-permute-start(bf16[2,72,384]{2,1,0:T(8,128)(2,1)S(1)} %get-tuple-element.180), channel_id=1, source_target_pairs={{0,4},{4,0},{8,12},{12,8},{16,20},{20,16},{24,28},{28,24},{1,5},{5... | collective-permute-start | bytes 331784 | tf_op jit(solution)/shard_map/ppermute | solution.py:33
  107.0 2.4 %collective-permute-done.30.got_a = bf16[1,3,96,512]{3,2,1,0:T(8,128)(2,1)S(1)} collective-permute-done((bf16[1,3,96,512]{3,2,1,0:T(8,128)(2,1)S(1)}, bf16[1,3,96,512]{3,2,1,0:T(8,128)(2,1)S(1)}, u32[]{:S(2)}, u32[]{:S(2)}) %collective-permute-start.30) | collective-permute-done | bytes 294944 | tf_op jit(solution)/shard_map/ppermute | solution.py:33
  110.4 3.0 %collective-permute-done.35.got_a = bf16[2,144,384]{2,1,0:T(8,128)(2,1)S(1)} collective-permute-done((bf16[2,144,384]{2,1,0:T(8,128)(2,1)S(1)}, bf16[2,144,384]{2,1,0:T(8,128)(2,1)S(1)}, u32[]{:S(2)}, u32[]{:S(2)}) %collective-permute-start.35) | collective-permute-done | bytes 221216 | tf_op jit(solution)/shard_map/ppermute | solution.py:33
  114.0 2.9 %collective-permute-start.41 = (bf16[72,768]{1,0:T(8,128)(2,1)S(1)}, bf16[72,768]{1,0:T(8,128)(2,1)S(1)}, u32[]{:S(2)}, u32[]{:S(2)}) collective-permute-start(bf16[72,768]{1,0:T(8,128)(2,1)S(1)} %get-tuple-element.182.after), channel_id=1, source_target_pairs={{0,16},{4,20},{8,24},{12,28},{16,0},{20,4},{24,8},{28,12},{1,17},{... | collective-permute-start | bytes 331784 | tf_op jit(solution)/shard_map/ppermute | solution.py:33
  117.5 3.1 %final.1.refs_0_ = f32[256,768]{1,0:T(8,128)S(1)} custom-call(s32[5]{0:T(128)S(1)} %stack.23.me_ref.at_ref, bf16[400,256]{1,0:T(8,128)(2,1)S(1)} %get-tuple-element.147.p0, bf16[400,256]{1,0:T(8,128)(2,1)S(1)} %collective-permute-done.25.p1, bf16[400,256]{1,0:T(8,128)(2,1)S(1)} %collective-permute-done.26.p2, ...), custom_call_target="tpu_custom_call" | custom-call | flops 300000000 | bytes 1050000 | tf_op jit(solution)/shard_map/final/pallas_call | solution.py:1311
  120.6 1.8 %collective-permute-done.37.theirs = bf16[384,128]{1,0:T(8,128)(2,1)S(1)} collective-permute-done((bf16[384,128]{1,0:T(8,128)(2,1)S(1)}, bf16[384,128]{1,0:T(8,128)(2,1)S(1)}, u32[]{:S(2)}, u32[]{:S(2)}) %collective-permute-start.37) | collective-permute-done | bytes 98336 | tf_op jit(solution)/shard_map/ppermute | solution.py:33
  123.4 1.7 %copy.46 = f32[256,1,768]{2,1,0:T(1,128)} copy(f32[256,1,768]{2,0,1:T(8,128)S(1)} %bitcast.26) | data formatting | bytes 1572864
  128.4 2.3 %small_grads.1 = (f32[64,1536]{1,0:T(8,128)}, f32[3,1536]{1,0:T(4,128)}, f32[768]{0:T(1024)}, f32[768]{0:T(1024)}, f32[768]{0:T(1024)}, /*index=5*/f32[768]{0:T(...) custom-call(s32[5]{0:T(128)S(1)} %stack.23.me_ref.at_ref, bf16[384,128]{1,0:T(8,128)(2,1)S(1)} %add.6.refs_1_.j0, ...), custom_call_target="tpu_custom_call" | custom-call | flops 3000000000 | bytes 10500000 | tf_op jit(solution)/shard_map/small_grads/pallas_call | solution.py:1400
  (101 shorter events, 27.1 us)
Async XLA Ops:
  0.6 11.1 %collective-permute-start.1 = (bf16[256,768]{1,0:T(8,128)(2,1)}, bf16[256,768]{1,0:T(8,128)(2,1)S(1)}, u32[]{:S(2)}, u32[]{:S(2)}) collective-permute-start(bf16[256,768]{1,0:T(8,128)(2,1)} %bitcast.29), channel_id=1, source_target_pairs={{0,2},{1,3},{2,0},{3,1},{4,6},{5,7},{6,4},{7,5},{8,10},{9,11},{10,... | collective-permute-start | bytes 1179656 | tf_op jit(solution)/shard_map/ppermute | solution.py:33
  0.7 12.1 %collective-permute-start = (bf16[256,768]{1,0:T(8,128)(2,1)}, bf16[256,768]{1,0:T(8,128)(2,1)S(1)}, u32[]{:S(2)}, u32[]{:S(2)}) collective-permute-start(bf16[256,768]{1,0:T(8,128)(2,1)} %bitcast.30), channel_id=1, source_target_pairs={{0,1},{1,0},{2,3},{3,2},{4,5},{5,4},{6,7},{7,6},{8,9},{9,8},{10,11... | collective-permute-start | bytes 1179656 | tf_op jit(solution)/shard_map/ppermute | solution.py:33
  0.8 12.0 %collective-permute-start.13 = (bf16[256,768]{1,0:T(8,128)(2,1)}, bf16[256,768]{1,0:T(8,128)(2,1)S(1)}, u32[]{:S(2)}, u32[]{:S(2)}) collective-permute-start(bf16[256,768]{1,0:T(8,128)(2,1)} %bitcast.33), channel_id=1, source_target_pairs={{0,8},{4,12},{8,0},{12,4},{16,24},{20,28},{24,16},{28,20},{1,9},{5... | collective-permute-start | bytes 1179656 | tf_op jit(solution)/shard_map/ppermute | solution.py:33
  11.8 12.2 %collective-permute-start.12 = (bf16[256,768]{1,0:T(8,128)(2,1)S(1)}, bf16[256,768]{1,0:T(8,128)(2,1)S(1)}, u32[]{:S(2)}, u32[]{:S(2)}) collective-permute-start(bf16[256,768]{1,0:T(8,128)(2,1)S(1)} %bitcast.34), channel_id=1, source_target_pairs={{0,2},{1,3},{2,0},{3,1},{4,6},{5,7},{6,4},{7,5},{8,10},{9,11},{10,... | collective-permute-start | bytes 1179656 | tf_op jit(solution)/shard_map/ppermute | solution.py:33
  24.1 26.3 %collective-permute-start.14 = (bf16[256,768]{1,0:T(8,128)(2,1)S(1)}, bf16[256,768]{1,0:T(8,128)(2,1)S(1)}, u32[]{:S(2)}, u32[]{:S(2)}) collective-permute-start(bf16[256,768]{1,0:T(8,128)(2,1)S(1)} %tie.6.refs_9_), channel_id=1, source_target_pairs={{0,8},{4,12},{8,0},{12,4},{16,24},{20,28},{24,16},{28,20},{1,9},{5... | collective-permute-start | bytes 1179656 | tf_op jit(solution)/shard_map/ppermute | solution.py:33
  34.0 17.1 %collective-permute-start.11 = (bf16[256,768]{1,0:T(8,128)(2,1)S(1)}, bf16[256,768]{1,0:T(8,128)(2,1)S(1)}, u32[]{:S(2)}, u32[]{:S(2)}) collective-permute-start(bf16[256,768]{1,0:T(8,128)(2,1)S(1)} %get-tuple-element.120.u2.refs_0_), channel_id=1, source_target_pairs={{0,10},{1,11},{2,8},{3,9},{4,14},{5,15},{6,12},{7,13},{8,2},{9,3},... | collective-permute-start | bytes 1179656 | tf_op jit(solution)/shard_map/ppermute | solution.py:1486
  35.0 19.6 %collective-permute-start.10 = (bf16[256,768]{1,0:T(8,128)(2,1)S(1)}, bf16[256,768]{1,0:T(8,128)(2,1)S(1)}, u32[]{:S(2)}, u32[]{:S(2)}) collective-permute-start(bf16[256,768]{1,0:T(8,128)(2,1)S(1)} %get-tuple-element.120.u2.refs_0_), channel_id=1, source_target_pairs={{0,8},{4,12},{8,0},{12,4},{16,24},{20,28},{24,16},{28,20},{1,9},{5... | collective-permute-start | bytes 1179656 | tf_op jit(solution)/shard_map/ppermute | solution.py:33
  36.5 18.3 %collective-permute-start.9 = (bf16[256,768]{1,0:T(8,128)(2,1)S(1)}, bf16[256,768]{1,0:T(8,128)(2,1)S(1)}, u32[]{:S(2)}, u32[]{:S(2)}) collective-permute-start(bf16[256,768]{1,0:T(8,128)(2,1)S(1)} %get-tuple-element.120.u2.refs_0_), channel_id=1, source_target_pairs={{0,2},{1,3},{2,0},{3,1},{4,6},{5,7},{6,4},{7,5},{8,10},{9,11},{10,... | collective-permute-start | bytes 1179656 | tf_op jit(solution)/shard_map/ppermute | solution.py:33
  57.6 16.8 %collective-permute-start.6 = (bf16[192,256]{1,0:T(8,128)(2,1)S(1)}, bf16[192,256]{1,0:T(8,128)(2,1)S(1)}, u32[]{:S(2)}, u32[]{:S(2)}) collective-permute-start(bf16[192,256]{1,0:T(8,128)(2,1)S(1)} %get-tuple-element.124), channel_id=1, source_target_pairs={{0,1},{1,0},{2,3},{3,2},{4,5},{5,4},{6,7},{7,6},{8,9},{9,8},{10,11... | collective-permute-start | bytes 294920 | tf_op jit(solution)/shard_map/ppermute | solution.py:33
  58.2 17.6 %collective-permute-start.7 = (bf16[192,256]{1,0:T(8,128)(2,1)S(1)}, bf16[192,256]{1,0:T(8,128)(2,1)S(1)}, u32[]{:S(2)}, u32[]{:S(2)}) collective-permute-start(bf16[192,256]{1,0:T(8,128)(2,1)S(1)} %get-tuple-element.125), channel_id=1, source_target_pairs={{0,2},{1,3},{2,0},{3,1},{4,6},{5,7},{6,4},{7,5},{8,10},{9,11},{10,... | collective-permute-start | bytes 294920 | tf_op jit(solution)/shard_map/ppermute | solution.py:33
  59.2 16.6 %collective-permute-start.8 = (bf16[192,256]{1,0:T(8,128)(2,1)S(1)}, bf16[192,256]{1,0:T(8,128)(2,1)S(1)}, u32[]{:S(2)}, u32[]{:S(2)}) collective-permute-start(bf16[192,256]{1,0:T(8,128)(2,1)S(1)} %get-tuple-element.126), channel_id=1, source_target_pairs={{0,3},{1,2},{2,1},{3,0},{4,7},{5,6},{6,5},{7,4},{8,11},{9,10},{10,... | collective-permute-start | bytes 294920 | tf_op jit(solution)/shard_map/ppermute | solution.py:33
  70.7 18.0 %collective-permute-start.29 = (bf16[2,3,96,256]{3,2,1,0:T(8,128)(2,1)S(1)}, bf16[2,3,96,256]{3,2,1,0:T(8,128)(2,1)S(1)}, u32[]{:S(2)}, u32[]{:S(2)}) collective-permute-start(bf16[2,3,96,256]{3,2,1,0:T(8,128)(2,1)S(1)} %get-tuple-element.155), channel_id=1, source_target_pairs={{0,16},{4,20},{8,24},{12,28},{16,0},{20,4},{24,8},{28,12},{1,17},{... | collective-permute-start | bytes 884744 | tf_op jit(solution)/shard_map/ppermute | solution.py:33
  73.4 16.9 %collective-permute-start.32 = (bf16[192,768]{1,0:T(8,128)(2,1)S(1)}, bf16[192,768]{1,0:T(8,128)(2,1)S(1)}, u32[]{:S(2)}, u32[]{:S(2)}) collective-permute-start(bf16[192,768]{1,0:T(8,128)(2,1)S(1)} %get-tuple-element.163), channel_id=1, source_target_pairs={{0,2},{1,3},{2,0},{3,1},{4,6},{5,7},{6,4},{7,5},{8,10},{9,11},{10,... | collective-permute-start | bytes 884744 | tf_op jit(solution)/shard_map/ppermute | solution.py:33
  74.3 15.2 %collective-permute-start.28 = (bf16[2,3,96,512]{3,2,1,0:T(8,128)(2,1)S(1)}, bf16[2,3,96,512]{3,2,1,0:T(8,128)(2,1)S(1)}, u32[]{:S(2)}, u32[]{:S(2)}) collective-permute-start(bf16[2,3,96,512]{3,2,1,0:T(8,128)(2,1)S(1)} %get-tuple-element.146.after), channel_id=1, source_target_pairs={{0,4},{4,0},{8,12},{12,8},{16,20},{20,16},{24,28},{28,24},{1,5},{5... | collective-permute-start | bytes 1769480 | tf_op jit(solution)/shard_map/ppermute | solution.py:33
  92.5 11.2 %collective-permute-start.33 = (bf16[4,112,384]{2,1,0:T(8,128)(2,1)S(1)}, bf16[4,112,384]{2,1,0:T(8,128)(2,1)S(1)}, u32[]{:S(2)}, u32[]{:S(2)}) collective-permute-start(bf16[4,112,384]{2,1,0:T(8,128)(2,1)S(1)} %get-tuple-element.170.after), channel_id=1, source_target_pairs={{0,4},{4,0},{8,12},{12,8},{16,20},{20,16},{24,28},{28,24},{1,5},{5... | collective-permute-start | bytes 1032200 | tf_op jit(solution)/shard_map/ppermute | solution.py:33
  94.1 9.7 %collective-permute-start.34 = (bf16[2,2,72,384]{3,2,1,0:T(8,128)(2,1)S(1)}, bf16[2,2,72,384]{3,2,1,0:T(8,128)(2,1)S(1)}, u32[]{:S(2)}, u32[]{:S(2)}) collective-permute-start(bf16[2,2,72,384]{3,2,1,0:T(8,128)(2,1)S(1)} %get-tuple-element.173), channel_id=1, source_target_pairs={{0,8},{4,12},{8,0},{12,4},{16,24},{20,28},{24,16},{28,20},{1,9},{5... | collective-permute-start | bytes 663560 | tf_op jit(solution)/shard_map/ppermute | solution.py:33
  94.6 14.8 %collective-permute-start.30 = (bf16[1,3,96,512]{3,2,1,0:T(8,128)(2,1)S(1)}, bf16[1,3,96,512]{3,2,1,0:T(8,128)(2,1)S(1)}, u32[]{:S(2)}, u32[]{:S(2)}) collective-permute-start(bf16[1,3,96,512]{3,2,1,0:T(8,128)(2,1)S(1)} %get-tuple-element.157.after), channel_id=1, source_target_pairs={{0,16},{4,20},{8,24},{12,28},{16,0},{20,4},{24,8},{28,12},{1,17},{... | collective-permute-start | bytes 884744 | tf_op jit(solution)/shard_map/ppermute | solution.py:33
  95.1 10.9 %collective-permute-start.31 = (bf16[1,3,96,256]{3,2,1,0:T(8,128)(2,1)S(1)}, bf16[1,3,96,256]{3,2,1,0:T(8,128)(2,1)S(1)}, u32[]{:S(2)}, u32[]{:S(2)}) collective-permute-start(bf16[1,3,96,256]{3,2,1,0:T(8,128)(2,1)S(1)} %get-tuple-element.159), channel_id=1, source_target_pairs={{0,4},{4,0},{8,12},{12,8},{16,20},{20,16},{24,28},{28,24},{1,5},{5... | collective-permute-start | bytes 442376 | tf_op jit(solution)/shard_map/ppermute | solution.py:33
  104.5 8.9 %collective-permute-start.35 = (bf16[2,144,384]{2,1,0:T(8,128)(2,1)S(1)}, bf16[2,144,384]{2,1,0:T(8,128)(2,1)S(1)}, u32[]{:S(2)}, u32[]{:S(2)}) collective-permute-start(bf16[2,144,384]{2,1,0:T(8,128)(2,1)S(1)} %get-tuple-element.178), channel_id=1, source_target_pairs={{0,8},{4,12},{8,0},{12,4},{16,24},{20,28},{24,16},{28,20},{1,9},{5... | collective-permute-start | bytes 663560 | tf_op jit(solution)/shard_map/ppermute | solution.py:33
  106.0 11.0 %collective-permute-start.25 = (bf16[400,256]{1,0:T(8,128)(2,1)S(1)}, bf16[400,256]{1,0:T(8,128)(2,1)S(1)}, u32[]{:S(2)}, u32[]{:S(2)}) collective-permute-start(bf16[400,256]{1,0:T(8,128)(2,1)S(1)} %get-tuple-element.148), channel_id=1, source_target_pairs={{0,1},{1,0},{2,3},{3,2},{4,5},{5,4},{6,7},{7,6},{8,9},{9,8},{10,11... | collective-permute-start | bytes 614408 | tf_op jit(solution)/shard_map/ppermute | solution.py:33
  106.0 11.0 %collective-permute-start.26 = (bf16[400,256]{1,0:T(8,128)(2,1)S(1)}, bf16[400,256]{1,0:T(8,128)(2,1)S(1)}, u32[]{:S(2)}, u32[]{:S(2)}) collective-permute-start(bf16[400,256]{1,0:T(8,128)(2,1)S(1)} %get-tuple-element.149), channel_id=1, source_target_pairs={{0,2},{1,3},{2,0},{3,1},{4,6},{5,7},{6,4},{7,5},{8,10},{9,11},{10,... | collective-permute-start | bytes 614408 | tf_op jit(solution)/shard_map/ppermute | solution.py:33
  109.4 8.1 %collective-permute-start.27 = (bf16[400,256]{1,0:T(8,128)(2,1)S(1)}, bf16[400,256]{1,0:T(8,128)(2,1)S(1)}, u32[]{:S(2)}, u32[]{:S(2)}) collective-permute-start(bf16[400,256]{1,0:T(8,128)(2,1)S(1)} %get-tuple-element.150), channel_id=1, source_target_pairs={{0,3},{1,2},{2,1},{3,0},{4,7},{5,6},{6,5},{7,4},{8,11},{9,10},{10,... | collective-permute-start | bytes 614408 | tf_op jit(solution)/shard_map/ppermute | solution.py:33
  114.0 8.5 %collective-permute-start.37 = (bf16[384,128]{1,0:T(8,128)(2,1)S(1)}, bf16[384,128]{1,0:T(8,128)(2,1)S(1)}, u32[]{:S(2)}, u32[]{:S(2)}) collective-permute-start(bf16[384,128]{1,0:T(8,128)(2,1)S(1)} %get-tuple-element.181.after.ours), channel_id=1, source_target_pairs={{0,16},{4,20},{8,24},{12,28},{16,0},{20,4},{24,8},{28,12},{1,17},{... | collective-permute-start | bytes 294920 | tf_op jit(solution)/shard_map/ppermute | solution.py:33
  114.0 11.1 %collective-permute-start.41 = (bf16[72,768]{1,0:T(8,128)(2,1)S(1)}, bf16[72,768]{1,0:T(8,128)(2,1)S(1)}, u32[]{:S(2)}, u32[]{:S(2)}) collective-permute-start(bf16[72,768]{1,0:T(8,128)(2,1)S(1)} %get-tuple-element.182.after), channel_id=1, source_target_pairs={{0,16},{4,20},{8,24},{12,28},{16,0},{20,4},{24,8},{28,12},{1,17},{... | collective-permute-start | bytes 331784 | tf_op jit(solution)/shard_map/ppermute | solution.py:33
  (23 other events, 123.9 us)

commit v6 on v5

--- a/solution.py
+++ b/solution.py
@@ -1531,18 +1531,18 @@
     gp_parts, (gp, d_taps, d_w2, d_w1, gcb) = back[:4], back[4:]
     gp_got = trade_parts(gp_parts)
 
-    keep_a, give_a, keep_b, give_b = halve(
-        at, (2, 0), gp, keep_a[None], got_a[None], keep_b[None], got_b[None]
-    )
-    got_a = swap(give_a, "batch", 4)
-    got_b = swap(give_b, "batch", 1)
-
     proj = projection_grads(
-        at, gp, u1, n1, w_mine, keep_o, got_o, d_w2, d_w1, d_taps, gcb, condt, mu, mn, sums2, give_a, bs
+        at, gp, u1, n1, w_mine, keep_o, got_o, d_w2, d_w1, d_taps, gcb, condt, mu, mn, sums2, gcb, bs
     )
     p_keep_a, p_give_a, p_keep_b, p_give_b, packed = proj
     p_got_a = swap(p_give_a, "batch", 1)
     p_got_b = swap(p_give_b, "batch", 2)
+    keep_a, give_a, keep_b, give_b = halve(
+        at, (2, 0), p_give_a, keep_a[None], got_a[None], keep_b[None], got_b[None]
+    )
+    got_a = swap(give_a, "batch", 4)
+    got_b = swap(give_b, "batch", 1)
+
     p_keep_a, p_give_a, p_keep_b, p_give_b, packed = stage(
         at, p_give_a, pairs(p_keep_a), pairs(p_got_a), p_keep_b, p_got_b, packed
     )

time: 133 us -> 132 us (level)
  transfers between devices with their start and end apart: 42 -> 42, of which waited for: 17 -> 18; matrix products, arithmetic and copies ran while one was open for 3% -> 3% of each run, Pallas kernels for 49% -> 51%
where the time goes in v6:
time: 132 us; the launch traced here: 129 us
  Pallas kernels  68.4 us (52%)
  waiting for transfers between devices  27.8 us (21%)
  starting transfers between devices  27.6 us (21%)
  local copies, waits for them, and re-layouts  3.88 us (3%)
    ppermute x41, waiting for transfers between devices, swap(): return lax.ppermute(value, axis, [(i, i ^ mask) for i in range(count)])  27.8 us
    ppermute x41, starting transfers between devices, swap(): return lax.ppermute(value, axis, [(i, i ^ mask) for i in range(count)])  26.6 us
    pallas_call x1, Pallas kernels, feed_forward(): pl.pallas_call(functools.partial(feed_kernel, piece=piece, thin=thin), gr...  12.9 us
    pallas_call x1, Pallas kernels, backward_spectral(): pl.pallas_call(backward_kernel, in_specs=[SM, SM] + [VM] * 17 + [HBM], ou...  12.8 us
    pallas_call x1, Pallas kernels, hidden_grads(): pl.pallas_call(hidden_grads_kernel, grid_spec=pltpu.PrefetchScalarGridSpe...  10.8 us
    pallas_call x1, Pallas kernels, forward_spectral(): pl.pallas_call(forward_kernel, in_specs=[SM, SM] + [VM] * 12, out_specs=[...  10.5 us
    pallas_call x1, Pallas kernels, select_columns(): pl.pallas_call(functools.partial(select_kernel, fs=fs), grid_spec=pltpu.P...  4.82 us
    pallas_call x1, Pallas kernels, prepare(): pl.pallas_call(functools.partial(prepare_kernel, step=step, fs=fs), in_sp...  4.57 us
  transfers between devices with their start and end apart: 42, of which 18 were waited for; matrix products, arithmetic and copies ran while one was open for 3% of the time, Pallas kernels for 51%

profile of v6, /device:TPU:2, one launch (start us, length us, event | category | flops | bytes accessed | tf_op | source)
XLA Modules:
  0.0 129.3 jit_solution(9940259731753566326)
XLA Ops:
  0.8 2.0 %collective-permute-start.13 = (bf16[256,768]{1,0:T(8,128)(2,1)}, bf16[256,768]{1,0:T(8,128)(2,1)S(1)}, u32[]{:S(2)}, u32[]{:S(2)}) collective-permute-start(bf16[256,768]{1,0:T(8,128)(2,1)} %bitcast.33), channel_id=1, source_target_pairs={{0,8},{4,12},{8,0},{12,4},{16,24},{20,28},{24,16},{28,20},{1,9},{5... | collective-permute-start | bytes 1179656 | tf_op jit(solution)/shard_map/ppermute | solution.py:33
  4.3 4.6 %prepare.1 = (bf16[384,768]{1,0:T(8,128)(2,1)S(1)}, bf16[384,192]{1,0:T(8,128)(2,1)S(1)}, bf16[64,384]{1,0:T(8,128)(2,1)S(1)}, f32[384,8]{1,0:T(8,128)S(1)}, f32...) custom-call(s32[5]{0:T(128)S(1)} %stack.23.me_ref.at_ref, ...), custom_call_target="tpu_custom_call" | custom-call | flops 3000000000 | bytes 10500000 | tf_op jit(solution)/shard_map/prepare/pallas_call | solution.py:489
  8.9 2.9 %collective-permute-done.1.refs_0_ = bf16[256,768]{1,0:T(8,128)(2,1)S(1)} collective-permute-done((bf16[256,768]{1,0:T(8,128)(2,1)}, bf16[256,768]{1,0:T(8,128)(2,1)S(1)}, u32[]{:S(2)}, u32[]{:S(2)}) %collective-permute-start.1) | collective-permute-done | bytes 393248 | tf_op jit(solution)/shard_map/ppermute | solution.py:33
  13.5 10.5 %forward_spectral.1 = (bf16[192,256]{1,0:T(8,128)(2,1)S(1)}, bf16[192,256]{1,0:T(8,128)(2,1)S(1)}, bf16[192,256]{1,0:T(8,128)(2,1)S(1)}, bf16[192,256]{1,0:T(8,1...) custom-call(s32[5]{0:T(128)S(1)} %stack.23.me_ref.at_ref, ...), custom_call_target="tpu_custom_call" | custom-call | flops 15000000512 | bytes 52500000 | tf_op jit(solution)/shard_map/forward_spectral/pallas_call | solution.py:679
  24.1 1.6 %collective-permute-start.14 = (bf16[256,768]{1,0:T(8,128)(2,1)S(1)}, bf16[256,768]{1,0:T(8,128)(2,1)S(1)}, u32[]{:S(2)}, u32[]{:S(2)}) collective-permute-start(bf16[256,768]{1,0:T(8,128)(2,1)S(1)} %tie.6.refs_9_), channel_id=1, source_target_pairs={{0,8},{4,12},{8,0},{12,4},{16,24},{20,28},{24,16},{28,20},{1,9},{5... | collective-permute-start | bytes 1179656 | tf_op jit(solution)/shard_map/ppermute | solution.py:33
  27.6 4.8 %select_columns.1 = (bf16[384,768]{1,0:T(8,128)(2,1)S(1)}, bf16[384,768]{1,0:T(8,128)(2,1)S(1)}, bf16[384,768]{1,0:T(8,128)(2,1)S(1)}) custom-call(s32[5]{0:T(128)S(1)} %stack.23.me_ref.at_ref, f32[64,8]{1,0:T(8,128)S(1)} %get-tuple-element.118.after.refs_1_.cb, bf16[768,3072]{1,0:T(8,128)(2,1)} %gate.3, bf16[768,3072]{1,0:T(8,128)(2,1)} %up.3, ...), custom_call_target="tpu_custom_call" | custom-call | flops 5000000000 | bytes 17500000 | tf_op jit(solution)/shard_map/select_columns/pallas_call | solution.py:531
  32.6 1.3 %middle.1 = (f32[256,768]{1,0:T(8,128)S(1)}, bf16[256,768]{1,0:T(8,128)(2,1)S(1)}, bf16[768,256]{1,0:T(8,128)(2,1)S(1)}) custom-call(s32[5]{0:T(128)S(1)} %stack.23.me_ref.at_ref, bf16[192,256]{1,0:T(8,128)(2,1)S(1)} %get-tuple-element.113.z0, bf16[192,256]{1,0:T(8,128)(2,1)S(1)} %collective-permute-done.3.z1, ...), custom_call_target="tpu_custom_call" | custom-call | flops 2000000000 | bytes 7000000 | tf_op jit(solution)/shard_map/middle/pallas_call | solution.py:834
  35.0 1.6 %collective-permute-start.10 = (bf16[256,768]{1,0:T(8,128)(2,1)S(1)}, bf16[256,768]{1,0:T(8,128)(2,1)S(1)}, u32[]{:S(2)}, u32[]{:S(2)}) collective-permute-start(bf16[256,768]{1,0:T(8,128)(2,1)S(1)} %get-tuple-element.120.u2.refs_0_), channel_id=1, source_target_pairs={{0,8},{4,12},{8,0},{12,4},{16,24},{20,28},{24,16},{28,20},{1,9},{5... | collective-permute-start | bytes 1179656 | tf_op jit(solution)/shard_map/ppermute | solution.py:33
  37.5 12.9 %feed_forward.1 = (bf16[256,768]{1,0:T(8,128)(2,1)}, f32[256,768]{1,0:T(8,128)S(1)}, bf16[192,256]{1,0:T(8,128)(2,1)S(1)}, bf16[192,256]{1,0:T(8,128)(2,1)S(1)},...) custom-call(s32[5]{0:T(128)S(1)} %stack.23.me_ref.at_ref, ...), custom_call_target="tpu_custom_call" | custom-call | flops 12999999488 | bytes 45500000 | tf_op jit(solution)/shard_map/feed_forward/pallas_call | solution.py:909
  51.1 3.4 %collective-permute-done.10.refs_1_ = bf16[256,768]{1,0:T(8,128)(2,1)S(1)} collective-permute-done((bf16[256,768]{1,0:T(8,128)(2,1)S(1)}, bf16[256,768]{1,0:T(8,128)(2,1)S(1)}, u32[]{:S(2)}, u32[]{:S(2)}) %collective-permute-start.10) | collective-permute-done | bytes 393248 | tf_op jit(solution)/shard_map/ppermute | solution.py:33
  59.9 10.8 %hidden_grads.1 = (bf16[2,3,96,512]{3,2,1,0:T(8,128)(2,1)S(1)}, bf16[2,3,96,512]{3,2,1,0:T(8,128)(2,1)S(1)}, bf16[2,3,96,256]{3,2,1,0:T(8,128)(2,1)S(1)}, bf16[2...) custom-call(s32[5]{0:T(128)S(1)} %stack.23.me_ref.at_ref, ...), custom_call_target="tpu_custom_call" | custom-call | flops 14000000000 | bytes 49000000 | tf_op jit(solution)/shard_map/hidden_grads/pallas_call | solution.py:989
  71.7 2.6 %collective-permute-start.30 = (bf16[2,3,96,256]{3,2,1,0:T(8,128)(2,1)S(1)}, bf16[2,3,96,256]{3,2,1,0:T(8,128)(2,1)S(1)}, u32[]{:S(2)}, u32[]{:S(2)}) collective-permute-start(bf16[2,3,96,256]{3,2,1,0:T(8,128)(2,1)S(1)} %get-tuple-element.166), channel_id=1, source_target_pairs={{0,16},{4,20},{8,24},{12,28},{16,0},{20,4},{24,8},{28,12},{1,17},{... | collective-permute-start | bytes 884744 | tf_op jit(solution)/shard_map/ppermute | solution.py:33
  74.3 1.5 %collective-permute-start.29 = (bf16[2,3,96,512]{3,2,1,0:T(8,128)(2,1)S(1)}, bf16[2,3,96,512]{3,2,1,0:T(8,128)(2,1)S(1)}, u32[]{:S(2)}, u32[]{:S(2)}) collective-permute-start(bf16[2,3,96,512]{3,2,1,0:T(8,128)(2,1)S(1)} %get-tuple-element.146.after), channel_id=1, source_target_pairs={{0,4},{4,0},{8,12},{12,8},{16,20},{20,16},{24,28},{28,24},{1,5},{5... | collective-permute-start | bytes 1769480 | tf_op jit(solution)/shard_map/ppermute | solution.py:33
  75.9 12.8 %backward_spectral.1 = (bf16[400,256]{1,0:T(8,128)(2,1)S(1)}, bf16[400,256]{1,0:T(8,128)(2,1)S(1)}, bf16[400,256]{1,0:T(8,128)(2,1)S(1)}, bf16[400,256]{1,0:T(8,...) custom-call(s32[5]{0:T(128)S(1)} %stack.23.me_ref.at_ref, ...), custom_call_target="tpu_custom_call" | custom-call | flops 16999999488 | bytes 59500000 | tf_op jit(solution)/shard_map/backward_spectral/pallas_call | solution.py:800
  88.7 2.2 %projection_grads.1 = (bf16[4,72,384]{2,1,0:T(8,128)(2,1)S(1)}, bf16[4,112,384]{2,1,0:T(8,128)(2,1)S(1)}, bf16[2,2,72,384]{3,2,1,0:T(8,128)(2,1)S(1)}, bf16[2,2,...) custom-call(s32[5]{0:T(128)S(1)} %stack.23.me_ref.at_ref, bf16[384,1024]{1,0:T(8,128)(2,1)S(1)} %get-tuple-element.152.gp, ...), custom_call_target="tpu_custom_call" | custom-call | flops 2000000000 | bytes 7000000 | tf_op jit(solution)/shard_map/projection_grads/pallas_call | solution.py:1256
  93.2 1.5 %collective-permute-start.32 = (bf16[1,3,96,256]{3,2,1,0:T(8,128)(2,1)S(1)}, bf16[1,3,96,256]{3,2,1,0:T(8,128)(2,1)S(1)}, u32[]{:S(2)}, u32[]{:S(2)}) collective-permute-start(bf16[1,3,96,256]{3,2,1,0:T(8,128)(2,1)S(1)} %get-tuple-element.170), channel_id=1, source_target_pairs={{0,4},{4,0},{8,12},{12,8},{16,20},{20,16},{24,28},{28,24},{1,5},{5... | collective-permute-start | bytes 442376 | tf_op jit(solution)/shard_map/ppermute | solution.py:33
  94.7 6.2 %collective-permute-done.34.got_b = bf16[2,2,72,384]{3,2,1,0:T(8,128)(2,1)S(1)} collective-permute-done((bf16[2,2,72,384]{3,2,1,0:T(8,128)(2,1)S(1)}, bf16[2,2,72,384]{3,2,1,0:T(8,128)(2,1)S(1)}, u32[]{:S(2)}, u32[]{:S(2)}) %collective-permute-start.34) | collective-permute-done | bytes 221216 | tf_op jit(solution)/shard_map/ppermute | solution.py:33
  105.6 2.5 %collective-permute-done.31.got_a = bf16[1,3,96,512]{3,2,1,0:T(8,128)(2,1)S(1)} collective-permute-done((bf16[1,3,96,512]{3,2,1,0:T(8,128)(2,1)S(1)}, bf16[1,3,96,512]{3,2,1,0:T(8,128)(2,1)S(1)}, u32[]{:S(2)}, u32[]{:S(2)}) %collective-permute-start.31) | collective-permute-done | bytes 294944 | tf_op jit(solution)/shard_map/ppermute | solution.py:33
  109.2 2.0 %collective-permute-done.35.got_a = bf16[2,144,384]{2,1,0:T(8,128)(2,1)S(1)} collective-permute-done((bf16[2,144,384]{2,1,0:T(8,128)(2,1)S(1)}, bf16[2,144,384]{2,1,0:T(8,128)(2,1)S(1)}, u32[]{:S(2)}, u32[]{:S(2)}) %collective-permute-start.35) | collective-permute-done | bytes 221216 | tf_op jit(solution)/shard_map/ppermute | solution.py:33
  111.9 2.9 %collective-permute-start.41 = (bf16[72,768]{1,0:T(8,128)(2,1)S(1)}, bf16[72,768]{1,0:T(8,128)(2,1)S(1)}, u32[]{:S(2)}, u32[]{:S(2)}) collective-permute-start(bf16[72,768]{1,0:T(8,128)(2,1)S(1)} %get-tuple-element.182.after), channel_id=1, source_target_pairs={{0,16},{4,20},{8,24},{12,28},{16,0},{20,4},{24,8},{28,12},{1,17},{... | collective-permute-start | bytes 331784 | tf_op jit(solution)/shard_map/ppermute | solution.py:33
  115.6 3.1 %final.1.refs_0_ = f32[256,768]{1,0:T(8,128)S(1)} custom-call(s32[5]{0:T(128)S(1)} %stack.23.me_ref.at_ref, bf16[400,256]{1,0:T(8,128)(2,1)S(1)} %get-tuple-element.147.p0, bf16[400,256]{1,0:T(8,128)(2,1)S(1)} %collective-permute-done.25.p1, bf16[400,256]{1,0:T(8,128)(2,1)S(1)} %collective-permute-done.26.p2, ...), custom_call_target="tpu_custom_call" | custom-call | flops 300000000 | bytes 1050000 | tf_op jit(solution)/shard_map/final/pallas_call | solution.py:1311
  118.7 2.3 %collective-permute-done.37.theirs = bf16[384,128]{1,0:T(8,128)(2,1)S(1)} collective-permute-done((bf16[384,128]{1,0:T(8,128)(2,1)S(1)}, bf16[384,128]{1,0:T(8,128)(2,1)S(1)}, u32[]{:S(2)}, u32[]{:S(2)}) %collective-permute-start.37) | collective-permute-done | bytes 98336 | tf_op jit(solution)/shard_map/ppermute | solution.py:33
  122.1 1.7 %copy.46 = f32[256,1,768]{2,1,0:T(1,128)} copy(f32[256,1,768]{2,0,1:T(8,128)S(1)} %bitcast.26) | data formatting | bytes 1572864
  127.0 2.3 %small_grads.1 = (f32[64,1536]{1,0:T(8,128)}, f32[3,1536]{1,0:T(4,128)}, f32[768]{0:T(1024)}, f32[768]{0:T(1024)}, f32[768]{0:T(1024)}, /*index=5*/f32[768]{0:T(...) custom-call(s32[5]{0:T(128)S(1)} %stack.23.me_ref.at_ref, bf16[384,128]{1,0:T(8,128)(2,1)S(1)} %add.6.refs_1_.j0, ...), custom_call_target="tpu_custom_call" | custom-call | flops 3000000000 | bytes 10500000 | tf_op jit(solution)/shard_map/small_grads/pallas_call | solution.py:1400
  (101 shorter events, 28.3 us)
Async XLA Ops:
  0.6 11.1 %collective-permute-start.1 = (bf16[256,768]{1,0:T(8,128)(2,1)}, bf16[256,768]{1,0:T(8,128)(2,1)S(1)}, u32[]{:S(2)}, u32[]{:S(2)}) collective-permute-start(bf16[256,768]{1,0:T(8,128)(2,1)} %bitcast.29), channel_id=1, source_target_pairs={{0,2},{1,3},{2,0},{3,1},{4,6},{5,7},{6,4},{7,5},{8,10},{9,11},{10,... | collective-permute-start | bytes 1179656 | tf_op jit(solution)/shard_map/ppermute | solution.py:33
  0.7 12.1 %collective-permute-start = (bf16[256,768]{1,0:T(8,128)(2,1)}, bf16[256,768]{1,0:T(8,128)(2,1)S(1)}, u32[]{:S(2)}, u32[]{:S(2)}) collective-permute-start(bf16[256,768]{1,0:T(8,128)(2,1)} %bitcast.30), channel_id=1, source_target_pairs={{0,1},{1,0},{2,3},{3,2},{4,5},{5,4},{6,7},{7,6},{8,9},{9,8},{10,11... | collective-permute-start | bytes 1179656 | tf_op jit(solution)/shard_map/ppermute | solution.py:33
  0.8 12.0 %collective-permute-start.13 = (bf16[256,768]{1,0:T(8,128)(2,1)}, bf16[256,768]{1,0:T(8,128)(2,1)S(1)}, u32[]{:S(2)}, u32[]{:S(2)}) collective-permute-start(bf16[256,768]{1,0:T(8,128)(2,1)} %bitcast.33), channel_id=1, source_target_pairs={{0,8},{4,12},{8,0},{12,4},{16,24},{20,28},{24,16},{28,20},{1,9},{5... | collective-permute-start | bytes 1179656 | tf_op jit(solution)/shard_map/ppermute | solution.py:33
  11.8 12.2 %collective-permute-start.12 = (bf16[256,768]{1,0:T(8,128)(2,1)S(1)}, bf16[256,768]{1,0:T(8,128)(2,1)S(1)}, u32[]{:S(2)}, u32[]{:S(2)}) collective-permute-start(bf16[256,768]{1,0:T(8,128)(2,1)S(1)} %bitcast.34), channel_id=1, source_target_pairs={{0,2},{1,3},{2,0},{3,1},{4,6},{5,7},{6,4},{7,5},{8,10},{9,11},{10,... | collective-permute-start | bytes 1179656 | tf_op jit(solution)/shard_map/ppermute | solution.py:33
  24.1 26.3 %collective-permute-start.14 = (bf16[256,768]{1,0:T(8,128)(2,1)S(1)}, bf16[256,768]{1,0:T(8,128)(2,1)S(1)}, u32[]{:S(2)}, u32[]{:S(2)}) collective-permute-start(bf16[256,768]{1,0:T(8,128)(2,1)S(1)} %tie.6.refs_9_), channel_id=1, source_target_pairs={{0,8},{4,12},{8,0},{12,4},{16,24},{20,28},{24,16},{28,20},{1,9},{5... | collective-permute-start | bytes 1179656 | tf_op jit(solution)/shard_map/ppermute | solution.py:33
  34.0 17.1 %collective-permute-start.11 = (bf16[256,768]{1,0:T(8,128)(2,1)S(1)}, bf16[256,768]{1,0:T(8,128)(2,1)S(1)}, u32[]{:S(2)}, u32[]{:S(2)}) collective-permute-start(bf16[256,768]{1,0:T(8,128)(2,1)S(1)} %get-tuple-element.120.u2.refs_0_), channel_id=1, source_target_pairs={{0,10},{1,11},{2,8},{3,9},{4,14},{5,15},{6,12},{7,13},{8,2},{9,3},... | collective-permute-start | bytes 1179656 | tf_op jit(solution)/shard_map/ppermute | solution.py:1486
  35.0 19.5 %collective-permute-start.10 = (bf16[256,768]{1,0:T(8,128)(2,1)S(1)}, bf16[256,768]{1,0:T(8,128)(2,1)S(1)}, u32[]{:S(2)}, u32[]{:S(2)}) collective-permute-start(bf16[256,768]{1,0:T(8,128)(2,1)S(1)} %get-tuple-element.120.u2.refs_0_), channel_id=1, source_target_pairs={{0,8},{4,12},{8,0},{12,4},{16,24},{20,28},{24,16},{28,20},{1,9},{5... | collective-permute-start | bytes 1179656 | tf_op jit(solution)/shard_map/ppermute | solution.py:33
  36.5 18.3 %collective-permute-start.9 = (bf16[256,768]{1,0:T(8,128)(2,1)S(1)}, bf16[256,768]{1,0:T(8,128)(2,1)S(1)}, u32[]{:S(2)}, u32[]{:S(2)}) collective-permute-start(bf16[256,768]{1,0:T(8,128)(2,1)S(1)} %get-tuple-element.120.u2.refs_0_), channel_id=1, source_target_pairs={{0,2},{1,3},{2,0},{3,1},{4,6},{5,7},{6,4},{7,5},{8,10},{9,11},{10,... | collective-permute-start | bytes 1179656 | tf_op jit(solution)/shard_map/ppermute | solution.py:33
  57.6 16.8 %collective-permute-start.6 = (bf16[192,256]{1,0:T(8,128)(2,1)S(1)}, bf16[192,256]{1,0:T(8,128)(2,1)S(1)}, u32[]{:S(2)}, u32[]{:S(2)}) collective-permute-start(bf16[192,256]{1,0:T(8,128)(2,1)S(1)} %get-tuple-element.124), channel_id=1, source_target_pairs={{0,1},{1,0},{2,3},{3,2},{4,5},{5,4},{6,7},{7,6},{8,9},{9,8},{10,11... | collective-permute-start | bytes 294920 | tf_op jit(solution)/shard_map/ppermute | solution.py:33
  58.2 17.6 %collective-permute-start.7 = (bf16[192,256]{1,0:T(8,128)(2,1)S(1)}, bf16[192,256]{1,0:T(8,128)(2,1)S(1)}, u32[]{:S(2)}, u32[]{:S(2)}) collective-permute-start(bf16[192,256]{1,0:T(8,128)(2,1)S(1)} %get-tuple-element.125), channel_id=1, source_target_pairs={{0,2},{1,3},{2,0},{3,1},{4,6},{5,7},{6,4},{7,5},{8,10},{9,11},{10,... | collective-permute-start | bytes 294920 | tf_op jit(solution)/shard_map/ppermute | solution.py:33
  59.2 16.7 %collective-permute-start.8 = (bf16[192,256]{1,0:T(8,128)(2,1)S(1)}, bf16[192,256]{1,0:T(8,128)(2,1)S(1)}, u32[]{:S(2)}, u32[]{:S(2)}) collective-permute-start(bf16[192,256]{1,0:T(8,128)(2,1)S(1)} %get-tuple-element.126), channel_id=1, source_target_pairs={{0,3},{1,2},{2,1},{3,0},{4,7},{5,6},{6,5},{7,4},{8,11},{9,10},{10,... | collective-permute-start | bytes 294920 | tf_op jit(solution)/shard_map/ppermute | solution.py:33
  70.7 18.0 %collective-permute-start.28 = (bf16[192,768]{1,0:T(8,128)(2,1)S(1)}, bf16[192,768]{1,0:T(8,128)(2,1)S(1)}, u32[]{:S(2)}, u32[]{:S(2)}) collective-permute-start(bf16[192,768]{1,0:T(8,128)(2,1)S(1)} %get-tuple-element.156), channel_id=1, source_target_pairs={{0,2},{1,3},{2,0},{3,1},{4,6},{5,7},{6,4},{7,5},{8,10},{9,11},{10,... | collective-permute-start | bytes 884744 | tf_op jit(solution)/shard_map/ppermute | solution.py:33
  71.7 20.2 %collective-permute-start.30 = (bf16[2,3,96,256]{3,2,1,0:T(8,128)(2,1)S(1)}, bf16[2,3,96,256]{3,2,1,0:T(8,128)(2,1)S(1)}, u32[]{:S(2)}, u32[]{:S(2)}) collective-permute-start(bf16[2,3,96,256]{3,2,1,0:T(8,128)(2,1)S(1)} %get-tuple-element.166), channel_id=1, source_target_pairs={{0,16},{4,20},{8,24},{12,28},{16,0},{20,4},{24,8},{28,12},{1,17},{... | collective-permute-start | bytes 884744 | tf_op jit(solution)/shard_map/ppermute | solution.py:33
  74.3 17.6 %collective-permute-start.29 = (bf16[2,3,96,512]{3,2,1,0:T(8,128)(2,1)S(1)}, bf16[2,3,96,512]{3,2,1,0:T(8,128)(2,1)S(1)}, u32[]{:S(2)}, u32[]{:S(2)}) collective-permute-start(bf16[2,3,96,512]{3,2,1,0:T(8,128)(2,1)S(1)} %get-tuple-element.146.after), channel_id=1, source_target_pairs={{0,4},{4,0},{8,12},{12,8},{16,20},{20,16},{24,28},{28,24},{1,5},{5... | collective-permute-start | bytes 1769480 | tf_op jit(solution)/shard_map/ppermute | solution.py:33
  90.9 11.0 %collective-permute-start.33 = (bf16[4,112,384]{2,1,0:T(8,128)(2,1)S(1)}, bf16[4,112,384]{2,1,0:T(8,128)(2,1)S(1)}, u32[]{:S(2)}, u32[]{:S(2)}) collective-permute-start(bf16[4,112,384]{2,1,0:T(8,128)(2,1)S(1)} %get-tuple-element.163.after), channel_id=1, source_target_pairs={{0,4},{4,0},{8,12},{12,8},{16,20},{20,16},{24,28},{28,24},{1,5},{5... | collective-permute-start | bytes 1032200 | tf_op jit(solution)/shard_map/ppermute | solution.py:33
  91.5 9.4 %collective-permute-start.34 = (bf16[2,2,72,384]{3,2,1,0:T(8,128)(2,1)S(1)}, bf16[2,2,72,384]{3,2,1,0:T(8,128)(2,1)S(1)}, u32[]{:S(2)}, u32[]{:S(2)}) collective-permute-start(bf16[2,2,72,384]{3,2,1,0:T(8,128)(2,1)S(1)} %get-tuple-element.173), channel_id=1, source_target_pairs={{0,8},{4,12},{8,0},{12,4},{16,24},{20,28},{24,16},{28,20},{1,9},{5... | collective-permute-start | bytes 663560 | tf_op jit(solution)/shard_map/ppermute | solution.py:33
  92.7 15.5 %collective-permute-start.31 = (bf16[1,3,96,512]{3,2,1,0:T(8,128)(2,1)S(1)}, bf16[1,3,96,512]{3,2,1,0:T(8,128)(2,1)S(1)}, u32[]{:S(2)}, u32[]{:S(2)}) collective-permute-start(bf16[1,3,96,512]{3,2,1,0:T(8,128)(2,1)S(1)} %get-tuple-element.168), channel_id=1, source_target_pairs={{0,16},{4,20},{8,24},{12,28},{16,0},{20,4},{24,8},{28,12},{1,17},{... | collective-permute-start | bytes 884744 | tf_op jit(solution)/shard_map/ppermute | solution.py:33
  93.2 11.4 %collective-permute-start.32 = (bf16[1,3,96,256]{3,2,1,0:T(8,128)(2,1)S(1)}, bf16[1,3,96,256]{3,2,1,0:T(8,128)(2,1)S(1)}, u32[]{:S(2)}, u32[]{:S(2)}) collective-permute-start(bf16[1,3,96,256]{3,2,1,0:T(8,128)(2,1)S(1)} %get-tuple-element.170), channel_id=1, source_target_pairs={{0,4},{4,0},{8,12},{12,8},{16,20},{20,16},{24,28},{28,24},{1,5},{5... | collective-permute-start | bytes 442376 | tf_op jit(solution)/shard_map/ppermute | solution.py:33
  102.7 8.5 %collective-permute-start.35 = (bf16[2,144,384]{2,1,0:T(8,128)(2,1)S(1)}, bf16[2,144,384]{2,1,0:T(8,128)(2,1)S(1)}, u32[]{:S(2)}, u32[]{:S(2)}) collective-permute-start(bf16[2,144,384]{2,1,0:T(8,128)(2,1)S(1)} %get-tuple-element.178), channel_id=1, source_target_pairs={{0,8},{4,12},{8,0},{12,4},{16,24},{20,28},{24,16},{28,20},{1,9},{5... | collective-permute-start | bytes 663560 | tf_op jit(solution)/shard_map/ppermute | solution.py:33
  103.7 11.1 %collective-permute-start.25 = (bf16[400,256]{1,0:T(8,128)(2,1)S(1)}, bf16[400,256]{1,0:T(8,128)(2,1)S(1)}, u32[]{:S(2)}, u32[]{:S(2)}) collective-permute-start(bf16[400,256]{1,0:T(8,128)(2,1)S(1)} %get-tuple-element.148), channel_id=1, source_target_pairs={{0,1},{1,0},{2,3},{3,2},{4,5},{5,4},{6,7},{7,6},{8,9},{9,8},{10,11... | collective-permute-start | bytes 614408 | tf_op jit(solution)/shard_map/ppermute | solution.py:33
  104.6 10.2 %collective-permute-start.26 = (bf16[400,256]{1,0:T(8,128)(2,1)S(1)}, bf16[400,256]{1,0:T(8,128)(2,1)S(1)}, u32[]{:S(2)}, u32[]{:S(2)}) collective-permute-start(bf16[400,256]{1,0:T(8,128)(2,1)S(1)} %get-tuple-element.149), channel_id=1, source_target_pairs={{0,2},{1,3},{2,0},{3,1},{4,6},{5,7},{6,4},{7,5},{8,10},{9,11},{10,... | collective-permute-start | bytes 614408 | tf_op jit(solution)/shard_map/ppermute | solution.py:33
  108.2 7.4 %collective-permute-start.27 = (bf16[400,256]{1,0:T(8,128)(2,1)S(1)}, bf16[400,256]{1,0:T(8,128)(2,1)S(1)}, u32[]{:S(2)}, u32[]{:S(2)}) collective-permute-start(bf16[400,256]{1,0:T(8,128)(2,1)S(1)} %get-tuple-element.150), channel_id=1, source_target_pairs={{0,3},{1,2},{2,1},{3,0},{4,7},{5,6},{6,5},{7,4},{8,11},{9,10},{10,... | collective-permute-start | bytes 614408 | tf_op jit(solution)/shard_map/ppermute | solution.py:33
  111.8 9.2 %collective-permute-start.37 = (bf16[384,128]{1,0:T(8,128)(2,1)S(1)}, bf16[384,128]{1,0:T(8,128)(2,1)S(1)}, u32[]{:S(2)}, u32[]{:S(2)}) collective-permute-start(bf16[384,128]{1,0:T(8,128)(2,1)S(1)} %get-tuple-element.181.after.ours), channel_id=1, source_target_pairs={{0,16},{4,20},{8,24},{12,28},{16,0},{20,4},{24,8},{28,12},{1,17},{... | collective-permute-start | bytes 294920 | tf_op jit(solution)/shard_map/ppermute | solution.py:33
  111.9 11.9 %collective-permute-start.41 = (bf16[72,768]{1,0:T(8,128)(2,1)S(1)}, bf16[72,768]{1,0:T(8,128)(2,1)S(1)}, u32[]{:S(2)}, u32[]{:S(2)}) collective-permute-start(bf16[72,768]{1,0:T(8,128)(2,1)S(1)} %get-tuple-element.182.after), channel_id=1, source_target_pairs={{0,16},{4,20},{8,24},{12,28},{16,0},{20,4},{24,8},{28,12},{1,17},{... | collective-permute-start | bytes 331784 | tf_op jit(solution)/shard_map/ppermute | solution.py:33
  (23 other events, 121.9 us)

commit v7 on v6

--- a/solution.py
+++ b/solution.py
@@ -619,7 +619,7 @@
                 lo = j * width + (r - 2) * chunk
                 vm[lo : lo + chunk, :] = (mixed * member[j : j + 1, :]).astype(BF16)
 
-    span = 2 * quarter
+    span = 4 * quarter
 
     @pl.loop(0, length // span)
     def _(f):

time: 132 us -> 131 us (level)
  no operation moved by 1% of the time
where the time goes in v7:
time: 131 us; the launch traced here: 129 us
  Pallas kernels  68.1 us (52%)
  starting transfers between devices  27.7 us (21%)
  waiting for transfers between devices  27.7 us (21%)
  local copies, waits for them, and re-layouts  3.88 us (3%)
    ppermute x41, waiting for transfers between devices, swap(): return lax.ppermute(value, axis, [(i, i ^ mask) for i in range(count)])  27.7 us
    ppermute x41, starting transfers between devices, swap(): return lax.ppermute(value, axis, [(i, i ^ mask) for i in range(count)])  26.7 us
    pallas_call x1, Pallas kernels, feed_forward(): pl.pallas_call(functools.partial(feed_kernel, piece=piece, thin=thin), gr...  12.9 us
    pallas_call x1, Pallas kernels, backward_spectral(): pl.pallas_call(backward_kernel, in_specs=[SM, SM] + [VM] * 17 + [HBM], ou...  12.8 us
    pallas_call x1, Pallas kernels, hidden_grads(): pl.pallas_call(hidden_grads_kernel, grid_spec=pltpu.PrefetchScalarGridSpe...  10.8 us
    pallas_call x1, Pallas kernels, forward_spectral(): pl.pallas_call(forward_kernel, in_specs=[SM, SM] + [VM] * 12, out_specs=[...  10.3 us
    pallas_call x1, Pallas kernels, select_columns(): pl.pallas_call(functools.partial(select_kernel, fs=fs), grid_spec=pltpu.P...  4.82 us
    pallas_call x1, Pallas kernels, prepare(): pl.pallas_call(functools.partial(prepare_kernel, step=step, fs=fs), in_sp...  4.57 us
  transfers between devices with their start and end apart: 42, of which 18 were waited for; matrix products, arithmetic and copies ran while one was open for 3% of the time, Pallas kernels for 51%

profile of v7, /device:TPU:2, one launch (start us, length us, event | category | flops | bytes accessed | tf_op | source)
XLA Modules:
  0.0 129.1 jit_solution(11658717014190866983)
XLA Ops:
  0.8 2.0 %collective-permute-start.13 = (bf16[256,768]{1,0:T(8,128)(2,1)}, bf16[256,768]{1,0:T(8,128)(2,1)S(1)}, u32[]{:S(2)}, u32[]{:S(2)}) collective-permute-start(bf16[256,768]{1,0:T(8,128)(2,1)} %bitcast.33), channel_id=1, source_target_pairs={{0,8},{4,12},{8,0},{12,4},{16,24},{20,28},{24,16},{28,20},{1,9},{5... | collective-permute-start | bytes 1179656 | tf_op jit(solution)/shard_map/ppermute | solution.py:33
  4.3 4.6 %prepare.1 = (bf16[384,768]{1,0:T(8,128)(2,1)S(1)}, bf16[384,192]{1,0:T(8,128)(2,1)S(1)}, bf16[64,384]{1,0:T(8,128)(2,1)S(1)}, f32[384,8]{1,0:T(8,128)S(1)}, f32...) custom-call(s32[5]{0:T(128)S(1)} %stack.23.me_ref.at_ref, ...), custom_call_target="tpu_custom_call" | custom-call | flops 3000000000 | bytes 10500000 | tf_op jit(solution)/shard_map/prepare/pallas_call | solution.py:489
  8.9 2.9 %collective-permute-done.1.refs_0_ = bf16[256,768]{1,0:T(8,128)(2,1)S(1)} collective-permute-done((bf16[256,768]{1,0:T(8,128)(2,1)}, bf16[256,768]{1,0:T(8,128)(2,1)S(1)}, u32[]{:S(2)}, u32[]{:S(2)}) %collective-permute-start.1) | collective-permute-done | bytes 393248 | tf_op jit(solution)/shard_map/ppermute | solution.py:33
  13.5 10.3 %forward_spectral.1 = (bf16[192,256]{1,0:T(8,128)(2,1)S(1)}, bf16[192,256]{1,0:T(8,128)(2,1)S(1)}, bf16[192,256]{1,0:T(8,128)(2,1)S(1)}, bf16[192,256]{1,0:T(8,1...) custom-call(s32[5]{0:T(128)S(1)} %stack.23.me_ref.at_ref, ...), custom_call_target="tpu_custom_call" | custom-call | flops 15000000512 | bytes 52500000 | tf_op jit(solution)/shard_map/forward_spectral/pallas_call | solution.py:679
  23.8 1.6 %collective-permute-start.14 = (bf16[256,768]{1,0:T(8,128)(2,1)S(1)}, bf16[256,768]{1,0:T(8,128)(2,1)S(1)}, u32[]{:S(2)}, u32[]{:S(2)}) collective-permute-start(bf16[256,768]{1,0:T(8,128)(2,1)S(1)} %tie.6.refs_9_), channel_id=1, source_target_pairs={{0,8},{4,12},{8,0},{12,4},{16,24},{20,28},{24,16},{28,20},{1,9},{5... | collective-permute-start | bytes 1179656 | tf_op jit(solution)/shard_map/ppermute | solution.py:33
  27.3 4.8 %select_columns.1 = (bf16[384,768]{1,0:T(8,128)(2,1)S(1)}, bf16[384,768]{1,0:T(8,128)(2,1)S(1)}, bf16[384,768]{1,0:T(8,128)(2,1)S(1)}) custom-call(s32[5]{0:T(128)S(1)} %stack.23.me_ref.at_ref, f32[64,8]{1,0:T(8,128)S(1)} %get-tuple-element.118.after.refs_1_.cb, bf16[768,3072]{1,0:T(8,128)(2,1)} %gate.3, bf16[768,3072]{1,0:T(8,128)(2,1)} %up.3, ...), custom_call_target="tpu_custom_call" | custom-call | flops 5000000000 | bytes 17500000 | tf_op jit(solution)/shard_map/select_columns/pallas_call | solution.py:531
  32.4 1.3 %middle.1 = (f32[256,768]{1,0:T(8,128)S(1)}, bf16[256,768]{1,0:T(8,128)(2,1)S(1)}, bf16[768,256]{1,0:T(8,128)(2,1)S(1)}) custom-call(s32[5]{0:T(128)S(1)} %stack.23.me_ref.at_ref, bf16[192,256]{1,0:T(8,128)(2,1)S(1)} %get-tuple-element.113.z0, bf16[192,256]{1,0:T(8,128)(2,1)S(1)} %collective-permute-done.3.z1, ...), custom_call_target="tpu_custom_call" | custom-call | flops 2000000000 | bytes 7000000 | tf_op jit(solution)/shard_map/middle/pallas_call | solution.py:834
  34.7 1.6 %collective-permute-start.10 = (bf16[256,768]{1,0:T(8,128)(2,1)S(1)}, bf16[256,768]{1,0:T(8,128)(2,1)S(1)}, u32[]{:S(2)}, u32[]{:S(2)}) collective-permute-start(bf16[256,768]{1,0:T(8,128)(2,1)S(1)} %get-tuple-element.120.u2.refs_0_), channel_id=1, source_target_pairs={{0,8},{4,12},{8,0},{12,4},{16,24},{20,28},{24,16},{28,20},{1,9},{5... | collective-permute-start | bytes 1179656 | tf_op jit(solution)/shard_map/ppermute | solution.py:33
  37.3 12.9 %feed_forward.1 = (bf16[256,768]{1,0:T(8,128)(2,1)}, f32[256,768]{1,0:T(8,128)S(1)}, bf16[192,256]{1,0:T(8,128)(2,1)S(1)}, bf16[192,256]{1,0:T(8,128)(2,1)S(1)},...) custom-call(s32[5]{0:T(128)S(1)} %stack.23.me_ref.at_ref, ...), custom_call_target="tpu_custom_call" | custom-call | flops 12999999488 | bytes 45500000 | tf_op jit(solution)/shard_map/feed_forward/pallas_call | solution.py:909
  50.9 3.4 %collective-permute-done.10.refs_1_ = bf16[256,768]{1,0:T(8,128)(2,1)S(1)} collective-permute-done((bf16[256,768]{1,0:T(8,128)(2,1)S(1)}, bf16[256,768]{1,0:T(8,128)(2,1)S(1)}, u32[]{:S(2)}, u32[]{:S(2)}) %collective-permute-start.10) | collective-permute-done | bytes 393248 | tf_op jit(solution)/shard_map/ppermute | solution.py:33
  59.7 10.8 %hidden_grads.1 = (bf16[2,3,96,512]{3,2,1,0:T(8,128)(2,1)S(1)}, bf16[2,3,96,512]{3,2,1,0:T(8,128)(2,1)S(1)}, bf16[2,3,96,256]{3,2,1,0:T(8,128)(2,1)S(1)}, bf16[2...) custom-call(s32[5]{0:T(128)S(1)} %stack.23.me_ref.at_ref, ...), custom_call_target="tpu_custom_call" | custom-call | flops 14000000000 | bytes 49000000 | tf_op jit(solution)/shard_map/hidden_grads/pallas_call | solution.py:989
  71.5 2.6 %collective-permute-start.30 = (bf16[2,3,96,256]{3,2,1,0:T(8,128)(2,1)S(1)}, bf16[2,3,96,256]{3,2,1,0:T(8,128)(2,1)S(1)}, u32[]{:S(2)}, u32[]{:S(2)}) collective-permute-start(bf16[2,3,96,256]{3,2,1,0:T(8,128)(2,1)S(1)} %get-tuple-element.166), channel_id=1, source_target_pairs={{0,16},{4,20},{8,24},{12,28},{16,0},{20,4},{24,8},{28,12},{1,17},{... | collective-permute-start | bytes 884744 | tf_op jit(solution)/shard_map/ppermute | solution.py:33
  74.1 1.5 %collective-permute-start.29 = (bf16[2,3,96,512]{3,2,1,0:T(8,128)(2,1)S(1)}, bf16[2,3,96,512]{3,2,1,0:T(8,128)(2,1)S(1)}, u32[]{:S(2)}, u32[]{:S(2)}) collective-permute-start(bf16[2,3,96,512]{3,2,1,0:T(8,128)(2,1)S(1)} %get-tuple-element.146.after), channel_id=1, source_target_pairs={{0,4},{4,0},{8,12},{12,8},{16,20},{20,16},{24,28},{28,24},{1,5},{5... | collective-permute-start | bytes 1769480 | tf_op jit(solution)/shard_map/ppermute | solution.py:33
  75.6 12.8 %backward_spectral.1 = (bf16[400,256]{1,0:T(8,128)(2,1)S(1)}, bf16[400,256]{1,0:T(8,128)(2,1)S(1)}, bf16[400,256]{1,0:T(8,128)(2,1)S(1)}, bf16[400,256]{1,0:T(8,...) custom-call(s32[5]{0:T(128)S(1)} %stack.23.me_ref.at_ref, ...), custom_call_target="tpu_custom_call" | custom-call | flops 16999999488 | bytes 59500000 | tf_op jit(solution)/shard_map/backward_spectral/pallas_call | solution.py:800
  88.5 2.2 %projection_grads.1 = (bf16[4,72,384]{2,1,0:T(8,128)(2,1)S(1)}, bf16[4,112,384]{2,1,0:T(8,128)(2,1)S(1)}, bf16[2,2,72,384]{3,2,1,0:T(8,128)(2,1)S(1)}, bf16[2,2,...) custom-call(s32[5]{0:T(128)S(1)} %stack.23.me_ref.at_ref, bf16[384,1024]{1,0:T(8,128)(2,1)S(1)} %get-tuple-element.152.gp, ...), custom_call_target="tpu_custom_call" | custom-call | flops 2000000000 | bytes 7000000 | tf_op jit(solution)/shard_map/projection_grads/pallas_call | solution.py:1256
  92.9 1.5 %collective-permute-start.32 = (bf16[1,3,96,256]{3,2,1,0:T(8,128)(2,1)S(1)}, bf16[1,3,96,256]{3,2,1,0:T(8,128)(2,1)S(1)}, u32[]{:S(2)}, u32[]{:S(2)}) collective-permute-start(bf16[1,3,96,256]{3,2,1,0:T(8,128)(2,1)S(1)} %get-tuple-element.170), channel_id=1, source_target_pairs={{0,4},{4,0},{8,12},{12,8},{16,20},{20,16},{24,28},{28,24},{1,5},{5... | collective-permute-start | bytes 442376 | tf_op jit(solution)/shard_map/ppermute | solution.py:33
  94.4 6.2 %collective-permute-done.34.got_b = bf16[2,2,72,384]{3,2,1,0:T(8,128)(2,1)S(1)} collective-permute-done((bf16[2,2,72,384]{3,2,1,0:T(8,128)(2,1)S(1)}, bf16[2,2,72,384]{3,2,1,0:T(8,128)(2,1)S(1)}, u32[]{:S(2)}, u32[]{:S(2)}) %collective-permute-start.34) | collective-permute-done | bytes 221216 | tf_op jit(solution)/shard_map/ppermute | solution.py:33
  105.5 2.5 %collective-permute-done.31.got_a = bf16[1,3,96,512]{3,2,1,0:T(8,128)(2,1)S(1)} collective-permute-done((bf16[1,3,96,512]{3,2,1,0:T(8,128)(2,1)S(1)}, bf16[1,3,96,512]{3,2,1,0:T(8,128)(2,1)S(1)}, u32[]{:S(2)}, u32[]{:S(2)}) %collective-permute-start.31) | collective-permute-done | bytes 294944 | tf_op jit(solution)/shard_map/ppermute | solution.py:33
  108.9 2.0 %collective-permute-done.35.got_a = bf16[2,144,384]{2,1,0:T(8,128)(2,1)S(1)} collective-permute-done((bf16[2,144,384]{2,1,0:T(8,128)(2,1)S(1)}, bf16[2,144,384]{2,1,0:T(8,128)(2,1)S(1)}, u32[]{:S(2)}, u32[]{:S(2)}) %collective-permute-start.35) | collective-permute-done | bytes 221216 | tf_op jit(solution)/shard_map/ppermute | solution.py:33
  111.6 2.9 %collective-permute-start.41 = (bf16[72,768]{1,0:T(8,128)(2,1)S(1)}, bf16[72,768]{1,0:T(8,128)(2,1)S(1)}, u32[]{:S(2)}, u32[]{:S(2)}) collective-permute-start(bf16[72,768]{1,0:T(8,128)(2,1)S(1)} %get-tuple-element.182.after), channel_id=1, source_target_pairs={{0,16},{4,20},{8,24},{12,28},{16,0},{20,4},{24,8},{28,12},{1,17},{... | collective-permute-start | bytes 331784 | tf_op jit(solution)/shard_map/ppermute | solution.py:33
  115.3 3.1 %final.1.refs_0_ = f32[256,768]{1,0:T(8,128)S(1)} custom-call(s32[5]{0:T(128)S(1)} %stack.23.me_ref.at_ref, bf16[400,256]{1,0:T(8,128)(2,1)S(1)} %get-tuple-element.147.p0, bf16[400,256]{1,0:T(8,128)(2,1)S(1)} %collective-permute-done.25.p1, bf16[400,256]{1,0:T(8,128)(2,1)S(1)} %collective-permute-done.26.p2, ...), custom_call_target="tpu_custom_call" | custom-call | flops 300000000 | bytes 1050000 | tf_op jit(solution)/shard_map/final/pallas_call | solution.py:1311
  118.4 2.3 %collective-permute-done.37.theirs = bf16[384,128]{1,0:T(8,128)(2,1)S(1)} collective-permute-done((bf16[384,128]{1,0:T(8,128)(2,1)S(1)}, bf16[384,128]{1,0:T(8,128)(2,1)S(1)}, u32[]{:S(2)}, u32[]{:S(2)}) %collective-permute-start.37) | collective-permute-done | bytes 98336 | tf_op jit(solution)/shard_map/ppermute | solution.py:33
  121.9 1.7 %copy.46 = f32[256,1,768]{2,1,0:T(1,128)} copy(f32[256,1,768]{2,0,1:T(8,128)S(1)} %bitcast.26) | data formatting | bytes 1572864
  126.8 2.3 %small_grads.1 = (f32[64,1536]{1,0:T(8,128)}, f32[3,1536]{1,0:T(4,128)}, f32[768]{0:T(1024)}, f32[768]{0:T(1024)}, f32[768]{0:T(1024)}, /*index=5*/f32[768]{0:T(...) custom-call(s32[5]{0:T(128)S(1)} %stack.23.me_ref.at_ref, bf16[384,128]{1,0:T(8,128)(2,1)S(1)} %add.6.refs_1_.j0, ...), custom_call_target="tpu_custom_call" | custom-call | flops 3000000000 | bytes 10500000 | tf_op jit(solution)/shard_map/small_grads/pallas_call | solution.py:1400
  (101 shorter events, 28.3 us)
Async XLA Ops:
  0.6 11.1 %collective-permute-start.1 = (bf16[256,768]{1,0:T(8,128)(2,1)}, bf16[256,768]{1,0:T(8,128)(2,1)S(1)}, u32[]{:S(2)}, u32[]{:S(2)}) collective-permute-start(bf16[256,768]{1,0:T(8,128)(2,1)} %bitcast.29), channel_id=1, source_target_pairs={{0,2},{1,3},{2,0},{3,1},{4,6},{5,7},{6,4},{7,5},{8,10},{9,11},{10,... | collective-permute-start | bytes 1179656 | tf_op jit(solution)/shard_map/ppermute | solution.py:33
  0.7 12.1 %collective-permute-start = (bf16[256,768]{1,0:T(8,128)(2,1)}, bf16[256,768]{1,0:T(8,128)(2,1)S(1)}, u32[]{:S(2)}, u32[]{:S(2)}) collective-permute-start(bf16[256,768]{1,0:T(8,128)(2,1)} %bitcast.30), channel_id=1, source_target_pairs={{0,1},{1,0},{2,3},{3,2},{4,5},{5,4},{6,7},{7,6},{8,9},{9,8},{10,11... | collective-permute-start | bytes 1179656 | tf_op jit(solution)/shard_map/ppermute | solution.py:33
  0.8 12.0 %collective-permute-start.13 = (bf16[256,768]{1,0:T(8,128)(2,1)}, bf16[256,768]{1,0:T(8,128)(2,1)S(1)}, u32[]{:S(2)}, u32[]{:S(2)}) collective-permute-start(bf16[256,768]{1,0:T(8,128)(2,1)} %bitcast.33), channel_id=1, source_target_pairs={{0,8},{4,12},{8,0},{12,4},{16,24},{20,28},{24,16},{28,20},{1,9},{5... | collective-permute-start | bytes 1179656 | tf_op jit(solution)/shard_map/ppermute | solution.py:33
  11.8 12.0 %collective-permute-start.12 = (bf16[256,768]{1,0:T(8,128)(2,1)S(1)}, bf16[256,768]{1,0:T(8,128)(2,1)S(1)}, u32[]{:S(2)}, u32[]{:S(2)}) collective-permute-start(bf16[256,768]{1,0:T(8,128)(2,1)S(1)} %bitcast.34), channel_id=1, source_target_pairs={{0,2},{1,3},{2,0},{3,1},{4,6},{5,7},{6,4},{7,5},{8,10},{9,11},{10,... | collective-permute-start | bytes 1179656 | tf_op jit(solution)/shard_map/ppermute | solution.py:33
  23.8 26.4 %collective-permute-start.14 = (bf16[256,768]{1,0:T(8,128)(2,1)S(1)}, bf16[256,768]{1,0:T(8,128)(2,1)S(1)}, u32[]{:S(2)}, u32[]{:S(2)}) collective-permute-start(bf16[256,768]{1,0:T(8,128)(2,1)S(1)} %tie.6.refs_9_), channel_id=1, source_target_pairs={{0,8},{4,12},{8,0},{12,4},{16,24},{20,28},{24,16},{28,20},{1,9},{5... | collective-permute-start | bytes 1179656 | tf_op jit(solution)/shard_map/ppermute | solution.py:33
  33.7 17.1 %collective-permute-start.11 = (bf16[256,768]{1,0:T(8,128)(2,1)S(1)}, bf16[256,768]{1,0:T(8,128)(2,1)S(1)}, u32[]{:S(2)}, u32[]{:S(2)}) collective-permute-start(bf16[256,768]{1,0:T(8,128)(2,1)S(1)} %get-tuple-element.120.u2.refs_0_), channel_id=1, source_target_pairs={{0,10},{1,11},{2,8},{3,9},{4,14},{5,15},{6,12},{7,13},{8,2},{9,3},... | collective-permute-start | bytes 1179656 | tf_op jit(solution)/shard_map/ppermute | solution.py:1486
  34.7 19.5 %collective-permute-start.10 = (bf16[256,768]{1,0:T(8,128)(2,1)S(1)}, bf16[256,768]{1,0:T(8,128)(2,1)S(1)}, u32[]{:S(2)}, u32[]{:S(2)}) collective-permute-start(bf16[256,768]{1,0:T(8,128)(2,1)S(1)} %get-tuple-element.120.u2.refs_0_), channel_id=1, source_target_pairs={{0,8},{4,12},{8,0},{12,4},{16,24},{20,28},{24,16},{28,20},{1,9},{5... | collective-permute-start | bytes 1179656 | tf_op jit(solution)/shard_map/ppermute | solution.py:33
  36.3 18.3 %collective-permute-start.9 = (bf16[256,768]{1,0:T(8,128)(2,1)S(1)}, bf16[256,768]{1,0:T(8,128)(2,1)S(1)}, u32[]{:S(2)}, u32[]{:S(2)}) collective-permute-start(bf16[256,768]{1,0:T(8,128)(2,1)S(1)} %get-tuple-element.120.u2.refs_0_), channel_id=1, source_target_pairs={{0,2},{1,3},{2,0},{3,1},{4,6},{5,7},{6,4},{7,5},{8,10},{9,11},{10,... | collective-permute-start | bytes 1179656 | tf_op jit(solution)/shard_map/ppermute | solution.py:33
  57.3 16.8 %collective-permute-start.6 = (bf16[192,256]{1,0:T(8,128)(2,1)S(1)}, bf16[192,256]{1,0:T(8,128)(2,1)S(1)}, u32[]{:S(2)}, u32[]{:S(2)}) collective-permute-start(bf16[192,256]{1,0:T(8,128)(2,1)S(1)} %get-tuple-element.124), channel_id=1, source_target_pairs={{0,1},{1,0},{2,3},{3,2},{4,5},{5,4},{6,7},{7,6},{8,9},{9,8},{10,11... | collective-permute-start | bytes 294920 | tf_op jit(solution)/shard_map/ppermute | solution.py:33
  58.0 17.6 %collective-permute-start.7 = (bf16[192,256]{1,0:T(8,128)(2,1)S(1)}, bf16[192,256]{1,0:T(8,128)(2,1)S(1)}, u32[]{:S(2)}, u32[]{:S(2)}) collective-permute-start(bf16[192,256]{1,0:T(8,128)(2,1)S(1)} %get-tuple-element.125), channel_id=1, source_target_pairs={{0,2},{1,3},{2,0},{3,1},{4,6},{5,7},{6,4},{7,5},{8,10},{9,11},{10,... | collective-permute-start | bytes 294920 | tf_op jit(solution)/shard_map/ppermute | solution.py:33
  59.0 16.7 %collective-permute-start.8 = (bf16[192,256]{1,0:T(8,128)(2,1)S(1)}, bf16[192,256]{1,0:T(8,128)(2,1)S(1)}, u32[]{:S(2)}, u32[]{:S(2)}) collective-permute-start(bf16[192,256]{1,0:T(8,128)(2,1)S(1)} %get-tuple-element.126), channel_id=1, source_target_pairs={{0,3},{1,2},{2,1},{3,0},{4,7},{5,6},{6,5},{7,4},{8,11},{9,10},{10,... | collective-permute-start | bytes 294920 | tf_op jit(solution)/shard_map/ppermute | solution.py:33
  70.5 18.0 %collective-permute-start.28 = (bf16[192,768]{1,0:T(8,128)(2,1)S(1)}, bf16[192,768]{1,0:T(8,128)(2,1)S(1)}, u32[]{:S(2)}, u32[]{:S(2)}) collective-permute-start(bf16[192,768]{1,0:T(8,128)(2,1)S(1)} %get-tuple-element.156), channel_id=1, source_target_pairs={{0,2},{1,3},{2,0},{3,1},{4,6},{5,7},{6,4},{7,5},{8,10},{9,11},{10,... | collective-permute-start | bytes 884744 | tf_op jit(solution)/shard_map/ppermute | solution.py:33
  71.5 20.2 %collective-permute-start.30 = (bf16[2,3,96,256]{3,2,1,0:T(8,128)(2,1)S(1)}, bf16[2,3,96,256]{3,2,1,0:T(8,128)(2,1)S(1)}, u32[]{:S(2)}, u32[]{:S(2)}) collective-permute-start(bf16[2,3,96,256]{3,2,1,0:T(8,128)(2,1)S(1)} %get-tuple-element.166), channel_id=1, source_target_pairs={{0,16},{4,20},{8,24},{12,28},{16,0},{20,4},{24,8},{28,12},{1,17},{... | collective-permute-start | bytes 884744 | tf_op jit(solution)/shard_map/ppermute | solution.py:33
  74.1 17.6 %collective-permute-start.29 = (bf16[2,3,96,512]{3,2,1,0:T(8,128)(2,1)S(1)}, bf16[2,3,96,512]{3,2,1,0:T(8,128)(2,1)S(1)}, u32[]{:S(2)}, u32[]{:S(2)}) collective-permute-start(bf16[2,3,96,512]{3,2,1,0:T(8,128)(2,1)S(1)} %get-tuple-element.146.after), channel_id=1, source_target_pairs={{0,4},{4,0},{8,12},{12,8},{16,20},{20,16},{24,28},{28,24},{1,5},{5... | collective-permute-start | bytes 1769480 | tf_op jit(solution)/shard_map/ppermute | solution.py:33
  90.7 11.0 %collective-permute-start.33 = (bf16[4,112,384]{2,1,0:T(8,128)(2,1)S(1)}, bf16[4,112,384]{2,1,0:T(8,128)(2,1)S(1)}, u32[]{:S(2)}, u32[]{:S(2)}) collective-permute-start(bf16[4,112,384]{2,1,0:T(8,128)(2,1)S(1)} %get-tuple-element.163.after), channel_id=1, source_target_pairs={{0,4},{4,0},{8,12},{12,8},{16,20},{20,16},{24,28},{28,24},{1,5},{5... | collective-permute-start | bytes 1032200 | tf_op jit(solution)/shard_map/ppermute | solution.py:33
  91.3 9.4 %collective-permute-start.34 = (bf16[2,2,72,384]{3,2,1,0:T(8,128)(2,1)S(1)}, bf16[2,2,72,384]{3,2,1,0:T(8,128)(2,1)S(1)}, u32[]{:S(2)}, u32[]{:S(2)}) collective-permute-start(bf16[2,2,72,384]{3,2,1,0:T(8,128)(2,1)S(1)} %get-tuple-element.173), channel_id=1, source_target_pairs={{0,8},{4,12},{8,0},{12,4},{16,24},{20,28},{24,16},{28,20},{1,9},{5... | collective-permute-start | bytes 663560 | tf_op jit(solution)/shard_map/ppermute | solution.py:33
  92.5 15.5 %collective-permute-start.31 = (bf16[1,3,96,512]{3,2,1,0:T(8,128)(2,1)S(1)}, bf16[1,3,96,512]{3,2,1,0:T(8,128)(2,1)S(1)}, u32[]{:S(2)}, u32[]{:S(2)}) collective-permute-start(bf16[1,3,96,512]{3,2,1,0:T(8,128)(2,1)S(1)} %get-tuple-element.168), channel_id=1, source_target_pairs={{0,16},{4,20},{8,24},{12,28},{16,0},{20,4},{24,8},{28,12},{1,17},{... | collective-permute-start | bytes 884744 | tf_op jit(solution)/shard_map/ppermute | solution.py:33
  92.9 11.5 %collective-permute-start.32 = (bf16[1,3,96,256]{3,2,1,0:T(8,128)(2,1)S(1)}, bf16[1,3,96,256]{3,2,1,0:T(8,128)(2,1)S(1)}, u32[]{:S(2)}, u32[]{:S(2)}) collective-permute-start(bf16[1,3,96,256]{3,2,1,0:T(8,128)(2,1)S(1)} %get-tuple-element.170), channel_id=1, source_target_pairs={{0,4},{4,0},{8,12},{12,8},{16,20},{20,16},{24,28},{28,24},{1,5},{5... | collective-permute-start | bytes 442376 | tf_op jit(solution)/shard_map/ppermute | solution.py:33
  102.4 8.5 %collective-permute-start.35 = (bf16[2,144,384]{2,1,0:T(8,128)(2,1)S(1)}, bf16[2,144,384]{2,1,0:T(8,128)(2,1)S(1)}, u32[]{:S(2)}, u32[]{:S(2)}) collective-permute-start(bf16[2,144,384]{2,1,0:T(8,128)(2,1)S(1)} %get-tuple-element.178), channel_id=1, source_target_pairs={{0,8},{4,12},{8,0},{12,4},{16,24},{20,28},{24,16},{28,20},{1,9},{5... | collective-permute-start | bytes 663560 | tf_op jit(solution)/shard_map/ppermute | solution.py:33
  103.5 11.1 %collective-permute-start.25 = (bf16[400,256]{1,0:T(8,128)(2,1)S(1)}, bf16[400,256]{1,0:T(8,128)(2,1)S(1)}, u32[]{:S(2)}, u32[]{:S(2)}) collective-permute-start(bf16[400,256]{1,0:T(8,128)(2,1)S(1)} %get-tuple-element.148), channel_id=1, source_target_pairs={{0,1},{1,0},{2,3},{3,2},{4,5},{5,4},{6,7},{7,6},{8,9},{9,8},{10,11... | collective-permute-start | bytes 614408 | tf_op jit(solution)/shard_map/ppermute | solution.py:33
  104.4 10.2 %collective-permute-start.26 = (bf16[400,256]{1,0:T(8,128)(2,1)S(1)}, bf16[400,256]{1,0:T(8,128)(2,1)S(1)}, u32[]{:S(2)}, u32[]{:S(2)}) collective-permute-start(bf16[400,256]{1,0:T(8,128)(2,1)S(1)} %get-tuple-element.149), channel_id=1, source_target_pairs={{0,2},{1,3},{2,0},{3,1},{4,6},{5,7},{6,4},{7,5},{8,10},{9,11},{10,... | collective-permute-start | bytes 614408 | tf_op jit(solution)/shard_map/ppermute | solution.py:33
  108.0 7.4 %collective-permute-start.27 = (bf16[400,256]{1,0:T(8,128)(2,1)S(1)}, bf16[400,256]{1,0:T(8,128)(2,1)S(1)}, u32[]{:S(2)}, u32[]{:S(2)}) collective-permute-start(bf16[400,256]{1,0:T(8,128)(2,1)S(1)} %get-tuple-element.150), channel_id=1, source_target_pairs={{0,3},{1,2},{2,1},{3,0},{4,7},{5,6},{6,5},{7,4},{8,11},{9,10},{10,... | collective-permute-start | bytes 614408 | tf_op jit(solution)/shard_map/ppermute | solution.py:33
  111.5 9.2 %collective-permute-start.37 = (bf16[384,128]{1,0:T(8,128)(2,1)S(1)}, bf16[384,128]{1,0:T(8,128)(2,1)S(1)}, u32[]{:S(2)}, u32[]{:S(2)}) collective-permute-start(bf16[384,128]{1,0:T(8,128)(2,1)S(1)} %get-tuple-element.181.after.ours), channel_id=1, source_target_pairs={{0,16},{4,20},{8,24},{12,28},{16,0},{20,4},{24,8},{28,12},{1,17},{... | collective-permute-start | bytes 294920 | tf_op jit(solution)/shard_map/ppermute | solution.py:33
  111.6 12.0 %collective-permute-start.41 = (bf16[72,768]{1,0:T(8,128)(2,1)S(1)}, bf16[72,768]{1,0:T(8,128)(2,1)S(1)}, u32[]{:S(2)}, u32[]{:S(2)}) collective-permute-start(bf16[72,768]{1,0:T(8,128)(2,1)S(1)} %get-tuple-element.182.after), channel_id=1, source_target_pairs={{0,16},{4,20},{8,24},{12,28},{16,0},{20,4},{24,8},{28,12},{1,17},{... | collective-permute-start | bytes 331784 | tf_op jit(solution)/shard_map/ppermute | solution.py:33
  (23 other events, 121.8 us)
